TPU v7x, 32 devices: a whole 2x2x4 slice. The times are simulated.
32 devices in a mesh: section: 2 (over core), dp: 16 (over z, y, x).
Axes of the slice: x: 2, y: 2, z: 4, core: 2. Of those that a mesh axis runs over, the one named last changes fastest.
Arguments:
- bytes_in: bfloat16 [16, 1024, 768], P('dp', None, 'section'), may hold values from -6 to 6
- lengths: int32 [16], P('dp'), may hold values from 768 to 1024, as said below
- patch_index: int32 [16, 2, 96], P('dp'), may hold values from 0 to 1023, as said below
- patch_count: int32 [16, 2], P('dp'), may hold values from 1 to 96, as said below
- gain_l1: bfloat16 [768], P('dp'), may hold values from 0.099609375 to 1.8984375
- qkv_l: bfloat16 [768, 2304], P('dp'), may hold values from -0.21875 to 0.21875
- out_l: bfloat16 [768, 768], P('dp'), may hold values from -3.5 to 3.5
- gain_l2: bfloat16 [768], P('dp'), may hold values from 0.099609375 to 1.8984375
- up_l: bfloat16 [768, 3072], P('dp'), may hold values from -0.21875 to 0.21875
- down_l: bfloat16 [3072, 768], P('dp'), may hold values from -0.109375 to 0.109375
- patch_proj: bfloat16 [768, 1536], P('dp'), may hold values from -0.21875 to 0.21875
- gain_g1: bfloat16 [1536], P('dp'), may hold values from 0.099609375 to 1.8984375
- qkv_g: bfloat16 [1536, 4608], P('dp'), may hold values from -0.15625 to 0.15625
- out_g: bfloat16 [1536, 1536], P('dp'), may hold values from -1.25 to 1.25
- gain_g2: bfloat16 [1536], P('dp'), may hold values from 0.099609375 to 1.8984375
- up_g: bfloat16 [1536, 6144], P('dp'), may hold values from -0.15625 to 0.15625
- down_g: bfloat16 [6144, 1536], P('dp'), may hold values from -0.078125 to 0.078125
- out_grad: bfloat16 [16, 1024, 768], P('dp', None, 'section'), may hold values from -6 to 6
Outputs:
- hidden_out: bfloat16 [16, 1024, 768], P('dp', None, 'section')
- input_grad: bfloat16 [16, 1024, 768], P('dp', None, 'section')
- grad_gain_l1: float32 [768], P('dp')
- grad_qkv_l: float32 [768, 2304], P('dp')
- grad_out_l: float32 [768, 768], P('dp')
- grad_gain_l2: float32 [768], P('dp')
- grad_up_l: float32 [768, 3072], P('dp')
- grad_down_l: float32 [3072, 768], P('dp')
- grad_patch_proj: float32 [768, 1536], P('dp')
- grad_gain_g1: float32 [1536], P('dp')
- grad_qkv_g: float32 [1536, 4608], P('dp')
- grad_out_g: float32 [1536, 1536], P('dp')
- grad_gain_g2: float32 [1536], P('dp')
- grad_up_g: float32 [1536, 6144], P('dp')
- grad_down_g: float32 [6144, 1536], P('dp')
Inputs may be any that keep to these rules, and one draw needn't show every extreme that they name: `lengths`: each sequence's length; some sequence has exactly 1024. `patch_count`: live patch slots of block m of a sequence; some block of some sequence fills all 96. `patch_index`: in row (s, m) the first patch_count[s, m] entries are increasing byte positions from m * 512 to (m + 1) * 512 - 1 and below the sequence's length, the first of them m * 512; the remaining entries equal m * 512.
All inputs are finite; a program needn't handle non-finite values.
Results may differ from a plain program's by a relative error of at most 0.024.
Values may be sent and summed in bfloat16 or wider, within the bound.
No kernel may reach another device: no remote copies, remote signals or barrier semaphores. Data moves between devices by JAX's collectives and lax.ppermute only.
A program may use at most 576 MiB of HBM per device.

v0:
```python
import jax
import jax.numpy as jnp
from jax import lax
from jax.sharding import PartitionSpec as P

H_L = 12
H_G = 24
WINDOW = 1536


EPSILON = 1e-06


def from_behind(shard, axis, by):
    size = lax.axis_size(axis)
    pairs = [(i, i + by) for i in range(size) if 0 <= i + by < size]
    return lax.ppermute(shard, axis, pairs)


def shortened(shard):

    def short(part):
        return part.astype(jnp.bfloat16) if part.dtype == jnp.float32 else part

    return jax.tree.map(short, shard)


def rms_scale(values, gain):
    return values * lax.rsqrt(jnp.mean(values * values, axis=-1, keepdims=True) + EPSILON) * gain


def local_mask(length):

    def local_build_mask(query_pos, key_pos):
        causal = key_pos[None, :] <= query_pos[:, None]
        inside = query_pos[:, None] - key_pos[None, :] < WINDOW
        present = (key_pos[None, :] < length) | (key_pos[None, :] == query_pos[:, None])
        return causal & inside & present

    return local_build_mask


def global_mask(live_flat):

    def global_build_mask(query_pos, key_pos):
        causal = key_pos[None, :] <= query_pos[:, None]
        present = live_flat[key_pos][None, :] | (key_pos[None, :] == query_pos[:, None])
        return causal & present

    return global_build_mask


def head_groups(head_count, key_total):
    groups = max(1, key_total // 1024)
    while head_count % groups:
        groups -= 1
    return groups


def split_heads(rows, head_count, groups):
    total = rows.shape[0]
    head_dim = rows.shape[1] // head_count
    return jnp.moveaxis(rows.reshape(total, groups, head_count // groups, head_dim), 1, 0)


def join_heads(grouped):
    groups, total, per_group, head_dim = grouped.shape
    return jnp.moveaxis(grouped, 0, 1).reshape(total, groups * per_group * head_dim)


def attend_forward(queries, key_rows, value_rows, mask_fn, head_count, first_row):
    rows_total, model_width = queries.shape
    key_total = key_rows.shape[0]
    head_dim = model_width // head_count
    score_scale = head_dim ** (-0.5)
    block_count = rows_total // rows_total
    groups = head_groups(head_count, key_total)
    per_group = head_count // groups
    key_pos = jnp.arange(key_total)

    def one_group(operands):
        query_heads, key_heads, value_heads = operands

        def one_block(block_id):
            start = block_id * rows_total
            scores = (
                jnp.einsum(
                    "qhd,khd->hqk", query_heads, key_heads, preferred_element_type=jnp.float32
                )
                * score_scale
            )
            allowed = mask_fn(first_row + start + jnp.arange(rows_total), key_pos)
            scores = jnp.where(allowed[None], scores, -1e30)
            row_max = jnp.max(scores, axis=-1, keepdims=True)
            exponent = jnp.exp(scores - row_max)
            denominator = jnp.sum(exponent, axis=-1, keepdims=True)
            attention = (exponent / denominator).astype(jnp.bfloat16)
            mixture = jnp.einsum(
                "hqk,khd->qhd", attention, value_heads, preferred_element_type=jnp.float32
            )
            return (mixture, (row_max + jnp.log(denominator))[..., 0])

        mixture, log_total = lax.map(one_block, jnp.arange(block_count))
        return (
            mixture.reshape(rows_total, per_group, head_dim),
            jnp.moveaxis(log_total, 0, 1).reshape(per_group, rows_total),
        )

    operands = (
        split_heads(queries, head_count, groups),
        split_heads(key_rows, head_count, groups),
        split_heads(value_rows, head_count, groups),
    )
    mixture, log_total = lax.map(one_group, operands)
    return (join_heads(mixture), log_total.reshape(head_count, rows_total))


def attend_backward(
    queries, key_rows, value_rows, log_total, grad_mixture, mask_fn, head_count, first_row
):
    rows_total, model_width = queries.shape
    key_total = key_rows.shape[0]
    head_dim = model_width // head_count
    score_scale = head_dim ** (-0.5)
    block_count = rows_total // rows_total
    groups = head_groups(head_count, key_total)
    per_group = head_count // groups
    key_pos = jnp.arange(key_total)

    def one_group(operands):
        query_heads, key_heads, value_heads, total_heads, grad_heads = operands

        def one_block(carried, block_id):
            grad_keys, grad_values = carried
            start = block_id * rows_total
            scores = (
                jnp.einsum(
                    "qhd,khd->hqk", query_heads, key_heads, preferred_element_type=jnp.float32
                )
                * score_scale
            )
            allowed = mask_fn(first_row + start + jnp.arange(rows_total), key_pos)
            scores = jnp.where(allowed[None], scores, -1e30)
            attention = jnp.exp(scores - total_heads[..., None])
            grad_attention = jnp.einsum(
                "qhd,khd->hqk", grad_heads, value_heads, preferred_element_type=jnp.float32
            )
            grad_scores = attention * (
                grad_attention - jnp.sum(attention * grad_attention, axis=-1, keepdims=True)
            )
            grad_scores = grad_scores.astype(jnp.bfloat16)
            grad_query = (
                jnp.einsum(
                    "hqk,khd->qhd", grad_scores, key_heads, preferred_element_type=jnp.float32
                )
                * score_scale
            )
            grad_keys = (
                grad_keys
                + jnp.einsum(
                    "hqk,qhd->khd", grad_scores, query_heads, preferred_element_type=jnp.float32
                )
                * score_scale
            )
            grad_values = grad_values + jnp.einsum(
                "hqk,qhd->khd",
                attention.astype(jnp.bfloat16),
                grad_heads,
                preferred_element_type=jnp.float32,
            )
            return ((grad_keys, grad_values), grad_query)

        zero_heads = jnp.zeros((key_total, per_group, head_dim), jnp.float32)
        carried, grad_queries = lax.scan(
            one_block, (zero_heads, zero_heads), jnp.arange(block_count)
        )
        return (grad_queries.reshape(rows_total, per_group, head_dim), carried[0], carried[1])

    operands = (
        split_heads(queries, head_count, groups),
        split_heads(key_rows, head_count, groups),
        split_heads(value_rows, head_count, groups),
        log_total.reshape(groups, per_group, rows_total),
        split_heads(grad_mixture, head_count, groups),
    )
    grad_queries, grad_keys, grad_values = lax.map(one_group, operands)
    return (join_heads(grad_queries), join_heads(grad_keys), join_heads(grad_values))


def block_forward(inputs, weights, mask_fn, head_count, past_kv, first_row):
    gain_one, qkv_weight, out_weight, gain_two, up_weight, down_weight = weights
    model_width = inputs.shape[1]
    normed = rms_scale(inputs, gain_one.astype(jnp.float32)).astype(jnp.bfloat16)
    projected = jnp.dot(normed, qkv_weight, preferred_element_type=jnp.float32).astype(jnp.bfloat16)
    own_kv = projected[:, model_width:]
    all_kv = own_kv if past_kv is None else jnp.concatenate([past_kv, own_kv], axis=0)
    mixture, log_total = attend_forward(
        projected[:, :model_width],
        all_kv[:, :model_width],
        all_kv[:, model_width:],
        mask_fn,
        head_count,
        first_row,
    )
    mixture = mixture.astype(jnp.bfloat16)
    hidden = inputs + jnp.dot(mixture, out_weight, preferred_element_type=jnp.float32)
    normed_two = rms_scale(hidden, gain_two.astype(jnp.float32)).astype(jnp.bfloat16)
    upward = jnp.dot(normed_two, up_weight, preferred_element_type=jnp.float32)
    activated = jax.nn.gelu(upward).astype(jnp.bfloat16)
    result = hidden + jnp.dot(activated, down_weight, preferred_element_type=jnp.float32)
    return (result, (inputs, projected, mixture, log_total, hidden, upward))


def blank_saved(rows_total, model_width, hidden_units, head_count):
    return (
        jnp.zeros((rows_total, model_width), jnp.float32),
        jnp.zeros((rows_total, 3 * model_width), jnp.bfloat16),
        jnp.zeros((rows_total, model_width), jnp.bfloat16),
        jnp.zeros((head_count, rows_total), jnp.float32),
        jnp.zeros((rows_total, model_width), jnp.float32),
        jnp.zeros((rows_total, hidden_units), jnp.float32),
    )


def block_backward(grad_result, saved, weights, mask_fn, head_count, all_kv, pending_kv, first_row):
    gain_one, qkv_weight, out_weight, gain_two, up_weight, down_weight = weights
    inputs, projected, mixture, log_total, hidden, upward = saved
    model_width = inputs.shape[1]
    grad_branch = grad_result.astype(jnp.bfloat16)
    activated = jax.nn.gelu(upward).astype(jnp.bfloat16)
    grad_down = jnp.dot(activated.T, grad_branch, preferred_element_type=jnp.float32)
    grad_act = jnp.dot(grad_branch, down_weight.T, preferred_element_type=jnp.float32)
    grad_upward = jax.vjp(jax.nn.gelu, upward)[1](grad_act)[0].astype(jnp.bfloat16)
    normed_two, pull_two = jax.vjp(rms_scale, hidden, gain_two.astype(jnp.float32))
    grad_up = jnp.dot(
        normed_two.astype(jnp.bfloat16).T, grad_upward, preferred_element_type=jnp.float32
    )
    grad_normed_two = jnp.dot(grad_upward, up_weight.T, preferred_element_type=jnp.float32)
    grad_hidden_norm, grad_gain_two = pull_two(grad_normed_two)
    grad_hidden = grad_result + grad_hidden_norm
    grad_branch_att = grad_hidden.astype(jnp.bfloat16)
    grad_out = jnp.dot(mixture.T, grad_branch_att, preferred_element_type=jnp.float32)
    grad_mixture = jnp.dot(
        grad_branch_att, out_weight.T, preferred_element_type=jnp.float32
    ).astype(jnp.bfloat16)
    grad_query, grad_key, grad_value = attend_backward(
        projected[:, :model_width],
        all_kv[:, :model_width],
        all_kv[:, model_width:],
        log_total,
        grad_mixture,
        mask_fn,
        head_count,
        first_row,
    )
    kv_total = pending_kv + jnp.concatenate([grad_key, grad_value], axis=1)
    grad_projected = jnp.concatenate([grad_query, kv_total[first_row:]], axis=1).astype(
        jnp.bfloat16
    )
    normed, pull_one = jax.vjp(rms_scale, inputs, gain_one.astype(jnp.float32))
    grad_qkv = jnp.dot(
        normed.astype(jnp.bfloat16).T, grad_projected, preferred_element_type=jnp.float32
    )
    grad_normed = jnp.dot(grad_projected, qkv_weight.T, preferred_element_type=jnp.float32)
    grad_input_norm, grad_gain_one = pull_one(grad_normed)
    return (
        grad_hidden + grad_input_norm,
        (grad_gain_one, grad_qkv, grad_out, grad_gain_two, grad_up, grad_down),
        kv_total,
    )


def joined_kv(saved_list, model_width):
    if not saved_list:
        return None
    return jnp.concatenate([saved[1][:, model_width:] for saved in saved_list], axis=0)


def zero_tuple(arrays):
    return tuple((jnp.zeros(array.shape, jnp.float32) for array in arrays))


def add_tuple(left_set, right_set):
    return tuple((left + right for left, right in zip(left_set, right_set)))


def local(
    bytes_in,
    lengths,
    patch_index,
    patch_count,
    gain_l1,
    qkv_l,
    out_l,
    gain_l2,
    up_l,
    down_l,
    patch_proj,
    gain_g1,
    qkv_g,
    out_g,
    gain_g2,
    up_g,
    down_g,
    out_grad,
):
    is_first = lax.axis_index("section") == 0
    is_second = jnp.logical_not(is_first)
    gathered = (
        lax.all_gather(gain_l1, "dp", axis=0, tiled=True),
        lax.all_gather(qkv_l, "dp", axis=0, tiled=True),
        lax.all_gather(out_l, "dp", axis=0, tiled=True),
        lax.all_gather(gain_l2, "dp", axis=0, tiled=True),
        lax.all_gather(up_l, "dp", axis=0, tiled=True),
        lax.all_gather(down_l, "dp", axis=0, tiled=True),
        lax.all_gather(patch_proj, "dp", axis=0, tiled=True),
        lax.all_gather(gain_g1, "dp", axis=0, tiled=True),
        lax.all_gather(qkv_g, "dp", axis=0, tiled=True),
        lax.all_gather(out_g, "dp", axis=0, tiled=True),
        lax.all_gather(gain_g2, "dp", axis=0, tiled=True),
        lax.all_gather(up_g, "dp", axis=0, tiled=True),
        lax.all_gather(down_g, "dp", axis=0, tiled=True),
    )
    local_weights = gathered[0:6]
    proj_weight = gathered[6]
    global_weights = gathered[7:13]
    inputs_all, grads_all = (
        lax.all_gather(bytes_in, "section", axis=2, tiled=True),
        lax.all_gather(out_grad, "section", axis=2, tiled=True),
    )
    seq_inputs = inputs_all[0]
    seq_grads = grads_all[0]
    seq_rows, local_width = seq_inputs.shape
    micro_total = patch_index.shape[1]
    slot_total = patch_index.shape[2]
    block_tok = seq_rows // micro_total
    global_width = proj_weight.shape[1]
    local_units = local_weights[4].shape[1]
    global_units = global_weights[4].shape[1]
    slot_ids = jnp.arange(slot_total)
    live_rows = slot_ids[None, :] < patch_count[0][:, None]
    mask_local = local_mask(lengths[0])
    mask_global = global_mask(live_rows.reshape(micro_total * slot_total))
    saved_local = []
    saved_global = []
    saved_rows = []
    saved_arrived = []
    outputs = []
    for micro_id in range(micro_total):
        first_byte = micro_id * block_tok
        first_slot = micro_id * slot_total
        positions = patch_index[0, micro_id] - first_byte
        live_slot = live_rows[micro_id][:, None]

        def run_local(operands):
            source, past = operands
            result, saved = block_forward(
                source.astype(jnp.float32), local_weights, mask_local, H_L, past, first_byte
            )
            boundary_rows = result.astype(jnp.bfloat16)[positions]
            outgoing = jnp.dot(boundary_rows, proj_weight, preferred_element_type=jnp.float32)
            return (result, saved, boundary_rows, outgoing)

        def skip_local(operands):
            outgoing = jnp.zeros((slot_total, global_width), jnp.float32)
            return (
                jnp.zeros((block_tok, local_width), jnp.float32),
                blank_saved(block_tok, local_width, local_units, H_L),
                jnp.zeros((slot_total, local_width), jnp.bfloat16),
                outgoing,
            )

        result_local, saved, boundary_rows, outgoing = lax.cond(
            is_first,
            run_local,
            skip_local,
            (seq_inputs[first_byte : first_byte + block_tok], joined_kv(saved_local, local_width)),
        )
        arrived = from_behind(outgoing.astype(jnp.bfloat16), "section", 1).astype(outgoing.dtype)

        def run_global(operands):
            arrived_rows, past = operands
            result, saved_g = block_forward(
                arrived_rows, global_weights, mask_global, H_G, past, first_slot
            )
            return (jnp.where(live_slot, result[:, :local_width], 0.0), saved_g)

        def skip_global(operands):
            return (
                jnp.zeros((slot_total, local_width), jnp.float32),
                blank_saved(slot_total, global_width, global_units, H_G),
            )

        back_rows, saved_g = lax.cond(
            is_second, run_global, skip_global, (arrived, joined_kv(saved_global, global_width))
        )
        returned = from_behind(back_rows.astype(jnp.bfloat16), "section", -1).astype(
            back_rows.dtype
        )
        outputs.append(result_local.at[positions].add(returned))
        saved_local.append(saved)
        saved_global.append(saved_g)
        saved_rows.append(boundary_rows)
        saved_arrived.append(arrived)
    acc_local = zero_tuple(local_weights)
    acc_proj = jnp.zeros(proj_weight.shape, jnp.float32)
    acc_global = zero_tuple(global_weights)
    pending_local = jnp.zeros((seq_rows, 2 * local_width), jnp.float32)
    pending_global = jnp.zeros((micro_total * slot_total, 2 * global_width), jnp.float32)
    input_grads = [None] * micro_total
    for micro_id in reversed(range(micro_total)):
        first_byte = micro_id * block_tok
        first_slot = micro_id * slot_total
        last_byte = first_byte + block_tok
        last_slot = first_slot + slot_total
        positions = patch_index[0, micro_id] - first_byte
        live_slot = live_rows[micro_id][:, None]
        grad_micro = seq_grads[first_byte:last_byte].astype(jnp.float32)

        def back_global(operands):
            saved_g, arrived_rows, kv_rows, pending, acc_g, acc_p = operands
            top_grad = jnp.where(live_slot, grad_micro[positions], 0.0)
            grad_top = jnp.concatenate(
                [top_grad, jnp.zeros((slot_total, global_width - local_width), jnp.float32)], axis=1
            )
            grad_start, grad_set, pending = block_backward(
                grad_top, saved_g, global_weights, mask_global, H_G, kv_rows, pending, first_slot
            )
            grad_start = grad_start.astype(jnp.bfloat16)
            acc_g = add_tuple(acc_g, grad_set)
            return (acc_g, acc_p, pending, grad_start)

        def skip_back_global(operands):
            saved_g, arrived_rows, kv_rows, pending, acc_g, acc_p = operands
            outgoing = jnp.zeros((slot_total, global_width), jnp.bfloat16)
            return (acc_g, acc_p, pending, outgoing)

        acc_global, acc_proj, pending_part, outgoing = lax.cond(
            is_second,
            back_global,
            skip_back_global,
            (
                saved_global[micro_id],
                saved_arrived[micro_id],
                joined_kv(saved_global[: micro_id + 1], global_width),
                pending_global[:last_slot],
                acc_global,
                acc_proj,
            ),
        )
        pending_global = pending_global.at[:last_slot].set(pending_part)
        received = from_behind(outgoing, "section", -1)

        def back_local(operands):
            saved, boundary_rows, received_rows, kv_rows, pending, acc_l, acc_p = operands
            acc_p = acc_p + jnp.dot(
                boundary_rows.T, received_rows, preferred_element_type=jnp.float32
            )
            grad_rows = jnp.dot(received_rows, proj_weight.T, preferred_element_type=jnp.float32)
            grad_result = grad_micro.at[positions].add(grad_rows)
            grad_input, grad_set, pending = block_backward(
                grad_result, saved, local_weights, mask_local, H_L, kv_rows, pending, first_byte
            )
            return (add_tuple(acc_l, grad_set), acc_p, pending, grad_input.astype(jnp.bfloat16))

        def skip_back_local(operands):
            saved, boundary_rows, received_rows, kv_rows, pending, acc_l, acc_p = operands
            return (acc_l, acc_p, pending, jnp.zeros((block_tok, local_width), jnp.bfloat16))

        acc_local, acc_proj, pending_part, grad_input = lax.cond(
            is_first,
            back_local,
            skip_back_local,
            (
                saved_local[micro_id],
                saved_rows[micro_id],
                received,
                joined_kv(saved_local[: micro_id + 1], local_width),
                pending_local[:last_byte],
                acc_local,
                acc_proj,
            ),
        )
        pending_local = pending_local.at[:last_byte].set(pending_part)
        input_grads[micro_id] = grad_input
    shard_sums = lax.psum_scatter(
        acc_local + (acc_proj,) + acc_global, "dp", scatter_dimension=0, tiled=True
    )
    totals = jax.tree.map(
        lambda part: part.astype(jnp.float32), lax.psum(shortened(shard_sums), "section")
    )
    layer_out = jnp.concatenate(outputs, axis=0).astype(jnp.bfloat16)[None]
    layer_grad = jnp.concatenate(input_grads, axis=0)[None]
    half_width = local_width // 2
    upper_out, upper_grad = from_behind(
        (layer_out[..., half_width:], layer_grad[..., half_width:]), "section", 1
    )
    hidden_out = jnp.where(is_first, layer_out[..., :half_width], upper_out)
    input_grad = jnp.where(is_first, layer_grad[..., :half_width], upper_grad)
    return (hidden_out, input_grad) + tuple(totals)


def solution(mesh):
    in_specs = (
        P("dp", None, "section"),
        P("dp"),
        P("dp", None, None),
        P("dp", None),
        P("dp"),
        P("dp", None),
        P("dp", None),
        P("dp"),
        P("dp", None),
        P("dp", None),
        P("dp", None),
        P("dp"),
        P("dp", None),
        P("dp", None),
        P("dp"),
        P("dp", None),
        P("dp", None),
        P("dp", None, "section"),
    )
    out_specs = (
        P("dp", None, "section"),
        P("dp", None, "section"),
        P("dp"),
        P("dp", None),
        P("dp", None),
        P("dp"),
        P("dp", None),
        P("dp", None),
        P("dp", None),
        P("dp"),
        P("dp", None),
        P("dp", None),
        P("dp"),
        P("dp", None),
        P("dp", None),
    )
    return jax.shard_map(local, mesh=mesh, in_specs=in_specs, out_specs=out_specs, check_vma=False)
```

profile of v0, /device:TPU:1, one launch (start us, length us, event | category | flops | bytes accessed | tf_op | source)
XLA Modules:
  0.0 4252.5 jit_solution(16724482353643677667)
XLA Ops:
  17.9 64.1 %all-reduce.11 = (bf16[768]{0:T(1024)(128)(2,1)S(1)}, bf16[768]{0:T(1024)(128)(2,1)S(1)}, bf16[1536]{0:T(1024)(128)(2,1)S(1)}, bf16[1536]{0:T(1024)(128)(2,1)S(1)}) all-reduce(bf16[768]{0:T(1024)(128)(2,1)S(1)} %dynamic-update-slice.4, bf16[768]{0:T(1024)(128)(2,1)S(1)} %dynamic-update-slice.5, ...), channel_id=1, replica_groups=mesh['section'=2,'dp'=16] {'dp'}, use_global_device_ids=true, to_apply=%add.2 | all-reduce | flops 4608 | bytes 18432
  82.6 62.7 %all-gather.22.cloned.1.call-done = bf16[768,1536]{1,0:T(8,128)(2,1)} async-done(((bf16[48,1536]{1,0:T(8,128)(2,1)}), bf16[768,1536]{1,0:T(8,128)(2,1)}) %all-gather.22.cloned.1.call-update) | async-done | bytes 2359312 | tf_op jit(solution)/shard_map/all_gather | solution.py:316
  145.2 72.1 %all-gather.14.cloned.1.call-done = bf16[768,2304]{1,0:T(8,128)(2,1)} async-done(((bf16[48,2304]{1,0:T(8,128)(2,1)}), bf16[768,2304]{1,0:T(8,128)(2,1)}) %all-gather.14.cloned.1.call-update) | async-done | bytes 3538960 | tf_op jit(solution)/shard_map/all_gather | solution.py:311
  217.4 82.0 %all-gather.18.cloned.1.call-done = bf16[768,3072]{1,0:T(8,128)(2,1)} async-done(((bf16[48,3072]{1,0:T(8,128)(2,1)}), bf16[768,3072]{1,0:T(8,128)(2,1)}) %all-gather.18.cloned.1.call-update) | async-done | bytes 4718608 | tf_op jit(solution)/shard_map/all_gather | solution.py:314
  299.4 81.8 %all-gather.20.cloned.1.call-done = bf16[3072,768]{1,0:T(8,128)(2,1)} async-done(((bf16[192,768]{1,0:T(8,128)(2,1)}), bf16[3072,768]{1,0:T(8,128)(2,1)}) %all-gather.20.cloned.1.call-update) | async-done | bytes 4718608 | tf_op jit(solution)/shard_map/all_gather | solution.py:315
  381.2 14.1 conditional.8
  397.0 19.5 conditional.10
  424.1 6.9 collective-permute-done
  432.0 89.0 %collective-permute-done.2 = bf16[96,1536]{1,0:T(8,128)(2,1)S(1)} collective-permute-done((bf16[96,1536]{1,0:T(8,128)(2,1)}, bf16[96,1536]{1,0:T(8,128)(2,1)S(1)}, u32[]{:S(2)}, u32[]{:S(2)}) %collective-permute-start.2) | collective-permute-done | bytes 294944 | tf_op jit(solution)/shard_map/ppermute | solution.py:17
  521.1 123.3 %all-gather.24.cloned.1.call-done = bf16[1536,4608]{1,0:T(8,128)(2,1)} async-done(((bf16[96,4608]{1,0:T(8,128)(2,1)}), bf16[1536,4608]{1,0:T(8,128)(2,1)}) %all-gather.24.cloned.1.call-update) | async-done | bytes 14155792 | tf_op jit(solution)/shard_map/all_gather | solution.py:318
  644.4 212.3 %all-gather.28.cloned.1.call-done = bf16[1536,6144]{1,0:T(8,128)(2,1)} async-done(((bf16[96,6144]{1,0:T(8,128)(2,1)}), bf16[1536,6144]{1,0:T(8,128)(2,1)}) %all-gather.28.cloned.1.call-update) | async-done | bytes 18874384 | tf_op jit(solution)/shard_map/all_gather | solution.py:321
  856.7 212.5 %all-gather.30.cloned.1.call-done = bf16[6144,1536]{1,0:T(8,128)(2,1)} async-done(((bf16[384,1536]{1,0:T(8,128)(2,1)}), bf16[6144,1536]{1,0:T(8,128)(2,1)}) %all-gather.30.cloned.1.call-update) | async-done | bytes 18874384 | tf_op jit(solution)/shard_map/all_gather | solution.py:322
  1069.3 37.4 conditional.9
  1070.7 7.5 convolution_convert_fusion.1
  1088.5 11.3 fusion.48
  1107.7 43.1 %conditional.11 = (bf16[96,768]{1,0:T(8,128)(2,1)S(1)}, f32[96,1536]{1,0:T(8,128)S(1)}, bf16[96,4608]{1,0:T(8,128)(2,1)}, bf16[96,1536]{0,1:T(8,128)(2,1)}, f32[...) conditional(s32[]{:T(128)} %convert_element_type.445, ...), branch_computations={%region_19.20_spmd, %region_20.25_spmd} | conditional | flops 5564475392 | bytes 148469184 | solution.py:394
  1109.7 7.5 convolution_convert_fusion.4
  1132.7 11.5 fusion.110
  1144.2 5.2 fusion.102
  1152.8 111.6 %conditional.12 = (f32[1536]{0:T(1024)}, f32[1536,4608]{1,0:T(8,128)}, f32[1536,1536]{0,1:T(8,128)}, f32[1536]{0:T(1024)S(1)}, f32[1536,6144]{1,0:T(8,128)}, /*i...) conditional(s32[]{:T(128)} %convert_element_type.445, () %tuple.147, ...), branch_computations={%region_26.27_spmd, %region_27.35_spmd} | conditional | flops 11187487744 | bytes 237300384 | solution.py:438
  1162.3 10.4 fusion.130
  1172.8 13.6 multiply_reduce_fusion.10
  1201.4 10.2 multiply_reduce_fusion.9
  1219.4 11.9 fusion.141
  1231.3 16.9 fusion.134
  1248.1 15.8 fusion.145
  1264.5 137.7 %conditional.14 = (f32[1536]{0:T(1024)}, f32[1536,4608]{1,0:T(8,128)}, f32[1536,1536]{0,1:T(8,128)}, f32[1536]{0:T(1024)S(1)}, f32[1536,6144]{1,0:T(8,128)}, /*i...) conditional(s32[]{:T(128)} %convert_element_type.445, (f32[1536]{0:T(1024)}, f32[1536,4608]{1,0:T(8,128)}, ...), branch_computations={%region_45.46_spmd, %region_46.54_spmd} | conditional | flops 11071185920 | bytes 358444768 | solution.py:438
  1268.4 10.2 fusion.171
  1278.6 28.8 convolution_add_fusion.5
  1308.0 13.3 multiply_reduce_fusion.17
  1321.3 28.3 convolution_add_fusion.4
  1353.0 8.7 bitcast_add_fusion
  1372.2 9.6 multiply_reduce_fusion.16
  1381.9 17.9 convolution_add_fusion.6
  1409.0 29.5 conditional.13
  1438.5 11.4 conditional.15
  1454.3 9.7 copy.156
  1467.1 326.4 %reduce-scatter.12.cloned.1.call-done = f32[48,768]{1,0:T(8,128)} async-done(((f32[768,768]{1,0:T(8,128)}), f32[48,768]{1,0:T(8,128)}) %reduce-scatter.12.cloned.1.call-update) | async-done | bytes 147472 | tf_op jit(solution)/shard_map/reduce_scatter | solution.py:486
  1795.1 140.8 %reduce-scatter.18.cloned.1.call-done = f32[48,1536]{1,0:T(8,128)} async-done(((f32[768,1536]{1,0:T(8,128)}), f32[48,1536]{1,0:T(8,128)}) %reduce-scatter.18.cloned.1.call-update) | async-done | bytes 294928 | tf_op jit(solution)/shard_map/reduce_scatter | solution.py:486
  1937.5 154.6 %reduce-scatter.10.cloned.1.call-done = f32[48,2304]{1,0:T(8,128)} async-done(((f32[768,2304]{1,0:T(8,128)}), f32[48,2304]{1,0:T(8,128)}) %reduce-scatter.10.cloned.1.call-update) | async-done | bytes 442384 | tf_op jit(solution)/shard_map/reduce_scatter | solution.py:486
  2093.8 173.6 %reduce-scatter.22.cloned.1.call-done = f32[96,1536]{1,0:T(8,128)} async-done(((f32[1536,1536]{1,0:T(8,128)}), f32[96,1536]{1,0:T(8,128)}) %reduce-scatter.22.cloned.1.call-update) | async-done | bytes 589840 | tf_op jit(solution)/shard_map/reduce_scatter | solution.py:486
  2269.3 174.6 %reduce-scatter.14.cloned.1.call-done = f32[48,3072]{1,0:T(8,128)} async-done(((f32[768,3072]{1,0:T(8,128)}), f32[48,3072]{1,0:T(8,128)}) %reduce-scatter.14.cloned.1.call-update) | async-done | bytes 589840 | tf_op jit(solution)/shard_map/reduce_scatter | solution.py:486
  2445.7 173.9 %reduce-scatter.16.cloned.1.call-done = f32[192,768]{1,0:T(8,128)} async-done(((f32[3072,768]{1,0:T(8,128)}), f32[192,768]{1,0:T(8,128)}) %reduce-scatter.16.cloned.1.call-update) | async-done | bytes 589840 | tf_op jit(solution)/shard_map/reduce_scatter | solution.py:486
  2621.4 403.8 %reduce-scatter.20.cloned.1.call-done = f32[96,4608]{1,0:T(8,128)} async-done(((f32[1536,4608]{1,0:T(8,128)}), f32[96,4608]{1,0:T(8,128)}) %reduce-scatter.20.cloned.1.call-update) | async-done | bytes 1769488 | tf_op jit(solution)/shard_map/reduce_scatter | solution.py:486
  3027.7 545.8 %reduce-scatter.24.cloned.1.call-done = f32[96,6144]{1,0:T(8,128)} async-done(((f32[1536,6144]{1,0:T(8,128)}), f32[96,6144]{1,0:T(8,128)}) %reduce-scatter.24.cloned.1.call-update) | async-done | bytes 2359312 | tf_op jit(solution)/shard_map/reduce_scatter | solution.py:486
  3576.3 546.7 %reduce-scatter.26.cloned.1.call-done = f32[384,1536]{1,0:T(8,128)} async-done(((f32[6144,1536]{1,0:T(8,128)}), f32[384,1536]{1,0:T(8,128)}) %reduce-scatter.26.cloned.1.call-update) | async-done | bytes 2359312 | tf_op jit(solution)/shard_map/reduce_scatter | solution.py:486
  4145.4 60.7 %all-reduce.10 = (bf16[768]{0:T(1024)(128)(2,1)S(1)}, bf16[768]{0:T(1024)(128)(2,1)S(1)}, bf16[1536]{0:T(1024)(128)(2,1)S(1)}, bf16[1536]{0:T(1024)(128)(2,1)S(1)}) all-reduce(f32[768]{0:T(1024)S(1)} %get-tuple-element.1152, f32[768]{0:T(1024)S(1)} %get-tuple-element.1155, ...), channel_id=2, replica_groups=mesh['section'=2,'dp'=16] {'dp'}, use_global_device_ids=true, to_apply=%region_64.65.clone | all-reduce | flops 4608 | bytes 27648
  4206.4 19.1 all-reduce.12
  (449 shorter events, 221.1 us)
Async XLA Ops:
  7.2 75.4 %all-gather.12.cloned.1.call-start = ((), (), s32[]{:S(2)}) async-start(), calls=%async_computation.9 | async-start | bytes 2359296 | tf_op jit(solution)/shard_map/all_gather | solution.py:328
  7.9 74.7 %all-gather.16.cloned.1.call-start = ((), (), s32[]{:S(2)}) async-start(), calls=%async_computation.11 | async-start | bytes 1253376 | tf_op jit(solution)/shard_map/all_gather | solution.py:312
  8.7 136.6 %all-gather.22.cloned.1.call-start = ((), (), s32[]{:S(2)}) async-start(), calls=%async_computation.14 | async-start | bytes 2506752 | tf_op jit(solution)/shard_map/all_gather | solution.py:316
  9.4 208.0 %all-gather.14.cloned.1.call-start = ((), (), s32[]{:S(2)}) async-start(), calls=%async_computation.10 | async-start | bytes 3760128 | tf_op jit(solution)/shard_map/all_gather | solution.py:311
  10.0 289.4 %all-gather.18.cloned.1.call-start = ((), (), s32[]{:S(2)}) async-start(), calls=%async_computation.12 | async-start | bytes 5013504 | tf_op jit(solution)/shard_map/all_gather | solution.py:314
  10.6 71.9 %copy-start.113 = (s32[1,2,96]{2,1,0:T(2,128)S(1)}, s32[1,2,96]{2,1,0:T(2,128)}, u32[]{:S(2)}) copy-start(s32[1,2,96]{2,1,0:T(2,128)} %param.44) | copy-start | bytes 2308
  10.6 370.6 %all-gather.20.cloned.1.call-start = ((), (), s32[]{:S(2)}) async-start(), calls=%async_computation.13 | async-start | bytes 5013504 | tf_op jit(solution)/shard_map/all_gather | solution.py:315
  11.2 408.0 %all-gather.32.cloned.1.call-start = ((), (), s32[]{:S(2)}) async-start(), calls=%async_computation.19 | async-start | bytes 2359296 | tf_op jit(solution)/shard_map/all_gather | solution.py:329
  12.0 509.1 %all-gather.26.cloned.1.call-start = ((), (), s32[]{:S(2)}) async-start(), calls=%async_computation.16 | async-start | bytes 5013504 | tf_op jit(solution)/shard_map/all_gather | solution.py:319
  12.7 631.7 %all-gather.24.cloned.1.call-start = ((), (), s32[]{:S(2)}) async-start(), calls=%async_computation.15 | async-start | bytes 15040512 | tf_op jit(solution)/shard_map/all_gather | solution.py:318
  13.4 843.3 %all-gather.28.cloned.1.call-start = ((), (), s32[]{:S(2)}) async-start(), calls=%async_computation.17 | async-start | bytes 20054016 | tf_op jit(solution)/shard_map/all_gather | solution.py:321
  14.0 1055.2 %all-gather.30.cloned.1.call-start = ((), (), s32[]{:S(2)}) async-start(), calls=%async_computation.18 | async-start | bytes 20054016 | tf_op jit(solution)/shard_map/all_gather | solution.py:322
  14.8 1778.8 %reduce-scatter.12.cloned.1.call-start = ((), (), s32[]{:S(2)}) async-start(), calls=%async_computation.21 | async-start | bytes 2506752 | tf_op jit(solution)/shard_map/reduce_scatter | solution.py:486
  82.0 314.6 %copy-start.104 = (bf16[768]{0:T(1024)(128)(2,1)}, bf16[768]{0:T(1024)(128)(2,1)S(1)}, u32[]{:S(2)}) copy-start(bf16[768]{0:T(1024)(128)(2,1)S(1)} %get-tuple-element.1448) | copy-start | bytes 4612
  82.0 314.6 %copy-start.106 = (bf16[768]{0:T(1024)(128)(2,1)}, bf16[768]{0:T(1024)(128)(2,1)S(1)}, u32[]{:S(2)}) copy-start(bf16[768]{0:T(1024)(128)(2,1)S(1)} %get-tuple-element.1449) | copy-start | bytes 4612
  82.0 1025.1 %copy-start.95 = (bf16[1536]{0:T(1024)(128)(2,1)}, bf16[1536]{0:T(1024)(128)(2,1)S(1)}, u32[]{:S(2)}) copy-start(bf16[1536]{0:T(1024)(128)(2,1)S(1)} %get-tuple-element.1451) | copy-start | bytes 9220
  82.0 1070.8 %copy-start.93 = (bf16[1536]{0:T(1024)(128)(2,1)}, bf16[1536]{0:T(1024)(128)(2,1)S(1)}, u32[]{:S(2)}) copy-start(bf16[1536]{0:T(1024)(128)(2,1)S(1)} %get-tuple-element.1450) | copy-start | bytes 9220
  82.5 298.7 %copy-start.117 = (s32[96]{0:T(128)}, s32[96]{0:T(128)S(1)}, u32[]{:S(2)}) copy-start(s32[96]{0:T(128)S(1)} %get-tuple-element.1536) | copy-start | bytes 1156
  82.5 314.1 %copy-start.120 = (s32[96]{0:T(128)}, s32[96]{0:T(128)S(1)}, u32[]{:S(2)}) copy-start(s32[96]{0:T(128)S(1)} %get-tuple-element.1535) | copy-start | bytes 1156
  395.3 35.7 collective-permute-start
  417.6 103.4 %collective-permute-start.2 = (bf16[96,1536]{1,0:T(8,128)(2,1)}, bf16[96,1536]{1,0:T(8,128)(2,1)S(1)}, u32[]{:S(2)}, u32[]{:S(2)}) collective-permute-start(bf16[96,1536]{1,0:T(8,128)(2,1)} %get-tuple-element.1102), channel_id=1, source_target_pairs={{0,16},{1,17},{2,18},{3,19},{4,20},{5,21},{6,22},{7,23},{8,24},{9,... | collective-permute-start | bytes 884744 | tf_op jit(solution)/shard_map/ppermute | solution.py:17
  422.4 646.8 %copy-start.109 = (pred[96,1]{0,1:T(4,128)(4,1)S(1)}, pred[96,1]{0,1:T(4,128)(4,1)}, u32[]{:S(2)}) copy-start(pred[96,1]{0,1:T(4,128)(4,1)} %get-tuple-element.1539) | copy-start | bytes 292
  1152.8 111.7 %copy-start.1 = (f32[512,768]{1,0:T(8,128)S(1)}, f32[512,768]{1,0:T(8,128)}, u32[]{:S(2)}) copy-start(f32[512,768]{1,0:T(8,128)} %get-tuple-element.1531) | copy-start | bytes 4718596
  1152.8 111.7 %copy-start.110 = (pred[96,1]{0,1:T(4,128)(4,1)S(1)}, pred[96,1]{0,1:T(4,128)(4,1)}, u32[]{:S(2)}) copy-start(pred[96,1]{0,1:T(4,128)(4,1)} %get-tuple-element.1539) | copy-start | bytes 292
  1152.8 111.7 %copy-start.118 = (s32[96]{0:T(128)S(1)}, s32[96]{0:T(128)}, u32[]{:S(2)}) copy-start(s32[96]{0:T(128)} %copy-done.117) | copy-start | bytes 1156
  1278.6 29.5 copy-start.59
  1278.6 28.8 copy-start.94
  1308.0 43.4 %slice-start.10 = ((s8[4718592]{0:T(1024)(128)(4,1)}), s8[524288]{0:T(1024)(128)(4,1)S(1)}, s32[]{:S(2)}) async-start(s8[4718592]{0:T(1024)(128)(4,1)} %bitcast.245), calls=%async_computation.40 | async-start | bytes 1048576 | tf_op jit(solution)/shard_map/cond
  1321.3 30.1 slice-start.11
  1402.2 36.3 collective-permute-start.6
  1403.5 5.4 collective-permute-start.5
  1408.9 29.5 copy-start.2
  1409.0 29.5 copy-start.4
  1409.0 29.5 copy-start.87
  1409.0 29.5 copy-start.119
  1453.0 482.9 %reduce-scatter.18.cloned.1.call-start = ((), (), s32[]{:S(2)}) async-start(), calls=%async_computation.24 | async-start | bytes 5013504 | tf_op jit(solution)/shard_map/reduce_scatter | solution.py:486
  1453.7 638.4 %reduce-scatter.10.cloned.1.call-start = ((), (), s32[]{:S(2)}) async-start(), calls=%async_computation.20 | async-start | bytes 7520256 | tf_op jit(solution)/shard_map/reduce_scatter | solution.py:486
  1454.3 813.2 %reduce-scatter.22.cloned.1.call-start = ((), (), s32[]{:S(2)}) async-start(), calls=%async_computation.26 | async-start | bytes 10027008 | tf_op jit(solution)/shard_map/reduce_scatter | solution.py:486
  1464.0 979.9 %reduce-scatter.14.cloned.1.call-start = ((), (), s32[]{:S(2)}) async-start(), calls=%async_computation.22 | async-start | bytes 10027008 | tf_op jit(solution)/shard_map/reduce_scatter | solution.py:486
  1464.6 1155.0 %reduce-scatter.16.cloned.1.call-start = ((), (), s32[]{:S(2)}) async-start(), calls=%async_computation.23 | async-start | bytes 10027008 | tf_op jit(solution)/shard_map/reduce_scatter | solution.py:486
  1465.2 1560.0 %reduce-scatter.20.cloned.1.call-start = ((), (), s32[]{:S(2)}) async-start(), calls=%async_computation.25 | async-start | bytes 30081024 | tf_op jit(solution)/shard_map/reduce_scatter | solution.py:486
  1465.8 2107.7 %reduce-scatter.24.cloned.1.call-start = ((), (), s32[]{:S(2)}) async-start(), calls=%async_computation.27 | async-start | bytes 40108032 | tf_op jit(solution)/shard_map/reduce_scatter | solution.py:486
  1466.5 2656.5 %reduce-scatter.26.cloned.1.call-start = ((), (), s32[]{:S(2)}) async-start(), calls=%async_computation.28 | async-start | bytes 40108032 | tf_op jit(solution)/shard_map/reduce_scatter | solution.py:486
  1467.1 2764.8 %all-reduce.16.cloned.1.call-start = ((), (), s32[]{:S(2)}) async-start(), calls=%async_computation.29 | async-start | bytes 9142272 | tf_op jit(solution)/shard_map/psum | solution.py:490
  4125.9 4.8 collective-permute-start.1
  4129.4 3.2 collective-permute-start.3
  4139.3 88.3 %collective-permute-start.4 = (bf16[1,1024,384]{2,1,0:T(8,128)(2,1)}, bf16[1,1024,384]{2,1,0:T(8,128)(2,1)}, u32[]{:S(2)}, u32[]{:S(2)}) collective-permute-start(bf16[1,1024,384]{2,1,0:T(8,128)(2,1)} %pad_maximum_fusion.18), channel_id=1, source_target_pairs={{0,16},{1,17},{2,18},{3,19},{4,20},{5,21},{6,22},{7,23},{8,24},{9,... | collective-permute-start | bytes 2359304 | tf_op jit(solution)/shard_map/ppermute | solution.py:17
  4142.8 87.0 %collective-permute-start.7 = (bf16[1,1024,384]{2,1,0:T(8,128)(2,1)}, bf16[1,1024,384]{2,1,0:T(8,128)(2,1)}, u32[]{:S(2)}, u32[]{:S(2)}) collective-permute-start(bf16[1,1024,384]{2,1,0:T(8,128)(2,1)} %slice.271), channel_id=1, source_target_pairs={{0,16},{1,17},{2,18},{3,19},{4,20},{5,21},{6,22},{7,23},{8,24},{9,... | collective-permute-start | bytes 2359304 | tf_op jit(solution)/shard_map/ppermute | solution.py:17
  (76 other events, 468.1 us)
Sparse Core Ops, SparseCore 0:
  9.6 12.3 all-gather.11
  24.7 55.8 all-gather.15
  83.4 61.8 all-gather.21
  147.9 69.4 all-gather.13
  220.0 79.3 all-gather.17
  302.1 79.0 all-gather.19
  382.7 9.5 all-gather.31
  395.2 80.4 all-gather.25
  478.4 165.9 all-gather.23
  647.0 209.6 all-gather.27
  859.5 209.6 all-gather.29
  1453.1 340.3 reduce-scatter.11
  1799.5 136.3 reduce-scatter.17
  1941.1 150.9 reduce-scatter.9
  2097.6 169.7 reduce-scatter.21
  2273.9 169.9 reduce-scatter.13
  2449.4 170.1 reduce-scatter.15
  2626.2 398.9 reduce-scatter.19
  3032.2 541.2 reduce-scatter.23
  3580.4 542.5 reduce-scatter.25
  4128.3 31.0 all-reduce.15
where the time goes:
time: 4260 us; the launch traced here: 4250 us
  waiting for transfers between devices  3590 us (84%)
  matrix products  274 us (6%)
  blocking collectives  144 us (3%)
  local copies, waits for them, and re-layouts  92.2 us (2%)
  other arithmetic  78.9 us (2%)
    reduce_scatter x9, waiting for transfers between devices, local(): lax.psum_scatter(acc_local + (acc_proj,) + acc_global, 'dp', scatter_dime...  2640 us
    all_gather x1, waiting for transfers between devices, local(): lax.all_gather(down_g, 'dp', axis=0, tiled=True)  213 us
    all_gather x1, waiting for transfers between devices, local(): lax.all_gather(up_g, 'dp', axis=0, tiled=True)  212 us
    unnamed x2, blocking collectives  125 us
    all_gather x1, waiting for transfers between devices, local(): lax.all_gather(qkv_g, 'dp', axis=0, tiled=True)  123 us
    ppermute x8, waiting for transfers between devices, from_behind(): return lax.ppermute(shard, axis, pairs)  96 us
  transfers between devices with their start and end apart: 29, of which 18 were waited for; matrix products, arithmetic and copies ran while one was open for 2% of the time, Pallas kernels for 0%

commit v1 on v0

v1 whole, which is shorter than its diff:
```python
import functools

import jax
import jax.numpy as jnp
import numpy as np
from jax import lax
from jax.experimental import pallas as pl
from jax.experimental.pallas import tpu as pltpu
from jax.sharding import PartitionSpec as P

H_L = 12
H_G = 24
WINDOW = 1536
EPSILON = 1e-06
LANES = 128
NEG = -1e30
VMEM_LIMIT = 48 * 1024 * 1024
F32 = jnp.float32
BF16 = jnp.bfloat16


def mm(left, right):
    return jnp.dot(left, right, preferred_element_type=F32)


def mm_nt(left, right):
    return lax.dot_general(left, right, (((1,), (1,)), ((), ())), preferred_element_type=F32)


def mm_tn(left, right):
    return lax.dot_general(left, right, (((0,), (0,)), ((), ())), preferred_element_type=F32)


def row_scale(values):
    return lax.rsqrt(jnp.mean(values * values, axis=-1, keepdims=True) + EPSILON)


def norm_backward(grad_normed, values, scale, gain):
    grad_gain = jnp.sum(grad_normed * values * scale, axis=0)
    pulled = grad_normed * gain
    inner = jnp.mean(pulled * values, axis=-1, keepdims=True)
    return scale * pulled - values * (scale * scale * scale * inner), grad_gain


def query_block(rows):
    return 256 if rows % 256 == 0 else rows


def masked_scores(keys, query, bias, start, block, window):
    pos_k = lax.broadcasted_iota(jnp.int32, (block, block), 0)
    pos_q = lax.broadcasted_iota(jnp.int32, (block, block), 1)
    parts = []
    if start:
        before = mm_nt(keys[:start], query) + bias[:start]
        if window is not None:
            far = lax.broadcasted_iota(jnp.int32, (start, block), 0)
            own = lax.broadcasted_iota(jnp.int32, (start, block), 1) + start
            before = jnp.where(own - far < window, before, NEG)
        parts.append(before)
    diagonal = mm_nt(keys[start : start + block], query)
    diagonal = jnp.where(
        pos_k == pos_q,
        diagonal,
        jnp.where(pos_k < pos_q, diagonal + bias[start : start + block], NEG),
    )
    parts.append(diagonal)
    return parts


def attention_forward_kernel(rows, head_dim, window, q_ref, k_ref, v_ref, bias_ref, o_ref, lse_ref):
    block = query_block(rows)
    lane = lax.broadcasted_iota(jnp.int32, (block, LANES), 1)
    score_scale = head_dim ** (-0.5)
    for index in range(rows // block):
        start = index * block
        queries = q_ref[start : start + block, :] * score_scale
        out = jnp.zeros((block, LANES), F32)
        for head in range(LANES // head_dim):
            mine = (lane >= head * head_dim) & (lane < (head + 1) * head_dim)
            query = jnp.where(mine, queries, jnp.zeros_like(queries)).astype(BF16)
            parts = masked_scores(k_ref, query, bias_ref, start, block, window)
            top = functools.reduce(jnp.maximum, [jnp.max(p, axis=0, keepdims=True) for p in parts])
            parts = [jnp.exp(p - top) for p in parts]
            total = functools.reduce(jnp.add, [jnp.sum(p, axis=0, keepdims=True) for p in parts])
            inverse = 1.0 / total
            mixed = jnp.zeros((block, LANES), F32)
            low = 0
            for part in parts:
                high = low + part.shape[0]
                mixed += mm_tn((part * inverse).astype(BF16), v_ref[low:high, :])
                low = high
            out = jnp.where(mine, mixed, out)
            lse_ref[0, head : head + 1, start : start + block] = top + jnp.log(total)
        o_ref[start : start + block, :] = out.astype(BF16)


def attention_backward_kernel(
    rows, head_dim, window, q_ref, k_ref, v_ref, bias_ref, lse_ref, do_ref, dq_ref, dk_ref, dv_ref, dk_acc, dv_acc
):
    block = query_block(rows)
    lane = lax.broadcasted_iota(jnp.int32, (block, LANES), 1)
    score_scale = head_dim ** (-0.5)
    dk_acc[...] = jnp.zeros((rows, LANES), F32)
    dv_acc[...] = jnp.zeros((rows, LANES), F32)
    for index in range(rows // block):
        start = index * block
        queries = q_ref[start : start + block, :] * score_scale
        grads = do_ref[start : start + block, :]
        dq = jnp.zeros((block, LANES), F32)
        for head in range(LANES // head_dim):
            mine = (lane >= head * head_dim) & (lane < (head + 1) * head_dim)
            query = jnp.where(mine, queries, jnp.zeros_like(queries)).astype(BF16)
            grad = jnp.where(mine, grads, jnp.zeros_like(grads))
            lse = lse_ref[0, head : head + 1, start : start + block]
            parts = masked_scores(k_ref, query, bias_ref, start, block, window)
            parts = [jnp.exp(p - lse) for p in parts]
            grad_parts = []
            low = 0
            for part in parts:
                high = low + part.shape[0]
                grad_parts.append(mm_nt(v_ref[low:high, :], grad))
                low = high
            delta = functools.reduce(
                jnp.add,
                [jnp.sum(p * g, axis=0, keepdims=True) for p, g in zip(parts, grad_parts)],
            )
            mixed = jnp.zeros((block, LANES), F32)
            low = 0
            for part, grad_part in zip(parts, grad_parts):
                high = low + part.shape[0]
                grad_score = (part * (grad_part - delta)).astype(BF16)
                dv_acc[low:high, :] += mm(part.astype(BF16), grad)
                dk_acc[low:high, :] += mm(grad_score, query)
                mixed += mm_tn(grad_score, k_ref[low:high, :])
                low = high
            dq = jnp.where(mine, mixed, dq)
        dq_ref[start : start + block, :] = (dq * score_scale).astype(BF16)
    dk_ref[...] = dk_acc[...].astype(BF16)
    dv_ref[...] = dv_acc[...].astype(BF16)


def attention_specs(rows, width):
    pairs = width // LANES
    wide = lambda part: pl.BlockSpec((rows, LANES), lambda i, part=part: (0, part * pairs + i))
    bias = pl.BlockSpec((rows, 1), lambda i: (0, 0))
    return pairs, wide, bias


def attention_forward(projected, bias, head_dim):
    rows, width = projected.shape[0], projected.shape[1] // 3
    pairs, wide, bias_spec = attention_specs(rows, width)
    per = LANES // head_dim
    window = WINDOW if rows > WINDOW else None
    return pl.pallas_call(
        functools.partial(attention_forward_kernel, rows, head_dim, window),
        grid=(pairs,),
        in_specs=[wide(0), wide(1), wide(2), bias_spec],
        out_specs=[wide(0), pl.BlockSpec((1, per, rows), lambda i: (i, 0, 0))],
        out_shape=[
            jax.ShapeDtypeStruct((rows, width), BF16),
            jax.ShapeDtypeStruct((pairs, per, rows), F32),
        ],
        compiler_params=pltpu.CompilerParams(vmem_limit_bytes=VMEM_LIMIT),
        cost_estimate=pl.CostEstimate(
            flops=8 * rows * rows * width,
            bytes_accessed=8 * rows * width,
            transcendentals=rows * rows * width // head_dim,
        ),
    )(projected, projected, projected, bias)


def attention_backward(projected, bias, lse, grad_mixture, head_dim):
    rows, width = grad_mixture.shape
    pairs, wide, bias_spec = attention_specs(rows, width)
    per = LANES // head_dim
    window = WINDOW if rows > WINDOW else None
    shape = jax.ShapeDtypeStruct((rows, width), BF16)
    grads = pl.pallas_call(
        functools.partial(attention_backward_kernel, rows, head_dim, window),
        grid=(pairs,),
        in_specs=[
            wide(0),
            wide(1),
            wide(2),
            bias_spec,
            pl.BlockSpec((1, per, rows), lambda i: (i, 0, 0)),
            wide(0),
        ],
        out_specs=[wide(0), wide(0), wide(0)],
        out_shape=[shape, shape, shape],
        scratch_shapes=[pltpu.VMEM((rows, LANES), F32), pltpu.VMEM((rows, LANES), F32)],
        compiler_params=pltpu.CompilerParams(vmem_limit_bytes=VMEM_LIMIT),
        cost_estimate=pl.CostEstimate(
            flops=20 * rows * rows * width,
            bytes_accessed=16 * rows * width,
            transcendentals=rows * rows * width // head_dim,
        ),
    )(projected, projected, projected, bias, lse, grad_mixture)
    return jnp.concatenate(grads, axis=1)


def swap(array):
    return lax.ppermute(array, "section", [(0, 1), (1, 0)])


def exchange(array, bits, size, sends=None):
    pairs = [
        (core * size + i, core * size + (i ^ (1 << bit)))
        for core, bit in enumerate(bits)
        for i in range(size)
        if sends is None or sends(core, i)
    ]
    return lax.ppermute(array, ("section", "dp"), pairs)


def bit_count(size):
    return size.bit_length() - 1


def orders(size, middle):
    bits = bit_count(size)
    others = tuple(reversed(range(2, bits - 1)))
    result = []
    for core in range(2):
        lowest = (0, 1) if core == 0 else (1, 0)
        order = ()
        for entry in middle:
            order += others if entry is None else (lowest[0] if entry == -1 else lowest[1],)
        result.append(order)
    return result


def mask_of(index, order, places):
    return sum(((index >> t) & 1) << places.index(bit) for t, bit in enumerate(order))


def placement(order_pair, places):
    position = lax.axis_index("dp")
    own = sum(((position >> bit) & 1) << p for p, bit in enumerate(places))
    count = 1 << len(places)
    masks = [jnp.asarray([mask_of(j, order, places) for j in range(count)], jnp.int32) for order in order_pair]
    return (own ^ jnp.where(lax.axis_index("section") == 0, masks[0], masks[1])).astype(jnp.int32)


def aligned(rows, cuts=()):
    return rows % 16 == 0 and all(c % LANES == 0 and r % 16 == 0 for r0, r1, c0, c1 in cuts for r, c in ((r0, c0), (r1, c1)))


def assembly_kernel(half, cuts, table, low, high, *outs):
    step = pl.program_id(0)

    def store(ref):
        for (r0, r1, c0, c1), out in zip(cuts, outs):
            out[...] = ref[0, r0:r1, c0:c1]

    pl.when(step < half)(lambda: store(low))
    pl.when(step >= half)(lambda: store(high))


def assembled(low, high, table, cuts):
    half, rows, width = low.shape
    shapes = [(2 * half * (r1 - r0), c1 - c0) for r0, r1, c0, c1 in cuts]
    if not aligned(rows, cuts):
        stack = jnp.concatenate([low, high], axis=0)[jnp.argsort(table)]
        return [stack[:, r0:r1, c0:c1].reshape(s) for (r0, r1, c0, c1), s in zip(cuts, shapes)]
    return pl.pallas_call(
        functools.partial(assembly_kernel, half, cuts),
        grid_spec=pltpu.PrefetchScalarGridSpec(
            num_scalar_prefetch=1,
            grid=(2 * half,),
            in_specs=[
                pl.BlockSpec((1, rows, width), lambda j, t: (jnp.minimum(j, half - 1), 0, 0)),
                pl.BlockSpec((1, rows, width), lambda j, t: (jnp.maximum(j - half, 0), 0, 0)),
            ],
            out_specs=[pl.BlockSpec((r1 - r0, c1 - c0), lambda j, t: (t[j], 0)) for r0, r1, c0, c1 in cuts],
        ),
        out_shape=[jax.ShapeDtypeStruct(s, low.dtype) for s in shapes],
        compiler_params=pltpu.CompilerParams(vmem_limit_bytes=VMEM_LIMIT),
        cost_estimate=pl.CostEstimate(flops=0, bytes_accessed=8 * half * rows * width, transcendentals=0),
    )(table, low, high)


def split_kernel(half, table, *refs):
    step = pl.program_id(0)
    send, keep = refs[-2:]

    def store(out):
        base = 0
        for ref in refs[:-2]:
            width = ref.shape[1]
            out[0, :, base : base + width] = ref[...]
            base += width

    pl.when(step < half)(lambda: store(send))
    pl.when(step >= half)(lambda: store(keep))


def split_stack(grads, table, count):
    half, rows = count // 2, grads[0].shape[0] // count
    width = sum(grad.shape[1] for grad in grads)
    if not (aligned(rows) and all(grad.shape[1] % LANES == 0 for grad in grads)):
        stack = jnp.concatenate([grad.reshape(count, rows, grad.shape[1]) for grad in grads], axis=2)[table]
        return stack[half:], stack[:half]
    shape = jax.ShapeDtypeStruct((half, rows, width), BF16)
    return pl.pallas_call(
        functools.partial(split_kernel, half),
        grid_spec=pltpu.PrefetchScalarGridSpec(
            num_scalar_prefetch=1,
            grid=(count,),
            in_specs=[
                pl.BlockSpec((rows, grad.shape[1]), lambda j, t: (t[jnp.where(j < half, j + half, j - half)], 0))
                for grad in grads
            ],
            out_specs=[
                pl.BlockSpec((1, rows, width), lambda j, t: (jnp.minimum(j, half - 1), 0, 0)),
                pl.BlockSpec((1, rows, width), lambda j, t: (jnp.maximum(j - half, 0), 0, 0)),
            ],
        ),
        out_shape=[shape, shape],
        compiler_params=pltpu.CompilerParams(vmem_limit_bytes=VMEM_LIMIT),
        cost_estimate=pl.CostEstimate(flops=0, bytes_accessed=4 * count * rows * width, transcendentals=0),
    )(table, *grads)


class Stream:
    def __init__(self, size, steps):
        self.size, self.steps = size, steps
        self.arriving = None
        self.value = None
        self.done = False
        self.pending = None

    def begin(self, arrived=None):
        try:
            self.pending = self.steps.send(arrived)
        except StopIteration as stop:
            self.pending, self.value, self.done = None, stop.value, True

    def launch(self):
        outgoing, bits, sends = self.pending
        self.arriving, self.pending = exchange(outgoing, bits, self.size, sends), None

    def result(self):
        if self.arriving is None and self.pending is None and not self.done:
            self.begin()
        while not self.done:
            if self.arriving is None:
                self.launch()
            arrived, self.arriving = self.arriving, None
            self.begin(arrived)
        return self.value


def advance(streams, tied):
    for stream in streams:
        if stream.arriving is None and stream.pending is None and not stream.done:
            stream.begin()
    moving = [stream for stream in streams if not stream.done]
    ending = [stream for stream in moving if stream.arriving is not None]
    fresh = [stream for stream in moving if stream.arriving is None]
    arrived, outgoing, tied = lax.optimization_barrier(
        ([s.arriving for s in ending], [s.pending[0] for s in fresh], tied)
    )
    for stream, array in zip(fresh, outgoing):
        stream.pending = (array,) + stream.pending[1:]
    for stream, array in zip(ending, arrived):
        stream.arriving = None
        stream.begin(array)
    for stream in moving:
        if not stream.done:
            stream.launch()
    return tied


def top_sends(size):
    top = bit_count(size) - 1
    return lambda core, i: (i >> top) == core


def doubling(held, order_pair, first=0):
    steps = list(zip(*order_pair))[first:]
    for bits in steps[:-1]:
        arrived = yield held, bits, None
        held = jnp.concatenate([held, arrived], axis=0)
    arrived = yield held, steps[-1], None
    return held, arrived


def gather_all(packed, order_pair, places, cuts):
    low, high = yield from doubling(packed[None], order_pair)
    return assembled(low, high, placement(order_pair, places), cuts)


def gather_core(piece, order_pair, places, cuts, size):
    top = bit_count(size) - 1
    arrived = yield piece, (top, top), top_sends(size)
    mine = (lax.axis_index("dp") >> top) == lax.axis_index("section")
    low, high = yield from doubling(jnp.where(mine, piece, arrived)[None], order_pair)
    return assembled(low, high, placement(order_pair, places), cuts)


def own_bit(pair):
    position = lax.axis_index("dp")
    return (position >> jnp.where(lax.axis_index("section") == 0, pair[0], pair[1])) & 1


def gather_square(blocks, order_pair, places, cuts):
    first, second = list(zip(*order_pair))[:2]
    a, b = own_bit(first), own_bit(second)
    kept = lax.dynamic_index_in_dim(blocks, a, 0, keepdims=False)
    arrived = yield lax.dynamic_index_in_dim(blocks, 1 - a, 0, keepdims=False), first, None
    held = jnp.stack([kept, arrived])
    kept = lax.dynamic_index_in_dim(held, b, 1, keepdims=False)
    arrived = yield lax.dynamic_index_in_dim(held, 1 - b, 1, keepdims=False), second, None
    low, high = yield from doubling(jnp.concatenate([kept, arrived], axis=0), order_pair, 2)
    return assembled(low, high, placement(order_pair, places), cuts)


def total_of(terms):
    return sum(term.astype(F32) for term in terms)


def halving(grads, order_pair, places, last=0):
    steps = list(zip(*order_pair))
    count = 1 << len(steps)
    outgoing, kept = split_stack([grad.astype(BF16) for grad in grads], placement(order_pair, places), count)
    terms = [kept]
    for bits in reversed(steps[last:]):
        half = terms[0].shape[0]
        if outgoing is None:
            half //= 2
            outgoing = total_of([term[half:] for term in terms]).astype(BF16)
            terms = [term[:half] for term in terms]
        arrived = yield outgoing, bits, None
        terms, outgoing = terms + [arrived], None
    return terms


def scatter_all(grads, order_pair, places):
    terms = yield from halving(grads, order_pair, places)
    return total_of(terms)[0].astype(BF16)


def scatter_core(grads, order_pair, places, size):
    terms = yield from halving(grads, order_pair, places)
    top = bit_count(size) - 1
    sends = top_sends(size)
    arrived = yield total_of(terms)[0].astype(BF16), (top, top), lambda core, i: not sends(core, i)
    return (total_of(terms)[0] + arrived.astype(F32)).astype(BF16)


def scatter_square(grads, order_pair, places):
    terms = yield from halving(grads, order_pair, places, 2)
    held = total_of(terms).astype(BF16)
    first, second = list(zip(*order_pair))[:2]
    arrived = yield held[2:], second, None
    held = jnp.stack([held[:2], arrived])
    arrived = yield held[:, 1], first, None
    return jnp.stack([held[:, 0], arrived])


def scatter_small(vector, size):
    position = lax.axis_index("dp")
    held = vector
    for bit in reversed(range(bit_count(size))):
        half = held.shape[0] // 2
        own = (position >> bit) & 1
        arrived = yield lax.dynamic_slice_in_dim(held, (1 - own) * half, half, 0), (bit, bit), None
        held = lax.dynamic_slice_in_dim(held, own * half, half, 0) + arrived
    return held[0, 0]


def in_square(blocks):
    is_first = lax.axis_index("section") == 0
    middle = jnp.where(is_first, blocks[1:3], jnp.stack([blocks[2], blocks[1]]))
    return jnp.concatenate([blocks[:1], middle, blocks[3:]], axis=0)


SQUARE = ((0, 1), (1, 0))


def square_gather(rows, size):
    held = rows[None]
    for bits in SQUARE:
        held = jnp.concatenate([held, exchange(held, bits, size)], axis=0)
    return in_square(held)


def square_scatter(blocks, size):
    held = in_square(blocks)
    for bits in reversed(SQUARE):
        half = held.shape[0] // 2
        arrived = exchange(held[half:].astype(BF16), bits, size)
        held = held[:half] + arrived.astype(F32)
    return held[0]


def local(
    size,
    bytes_in,
    lengths,
    patch_index,
    patch_count,
    gain_l1,
    qkv_l,
    out_l,
    gain_l2,
    up_l,
    down_l,
    patch_proj,
    gain_g1,
    qkv_g,
    out_g,
    gain_g2,
    up_g,
    down_g,
    out_grad,
):
    core = lax.axis_index("section")
    position = lax.axis_index("dp")
    is_first = core == 0
    seq_rows, half_l = bytes_in.shape[1:]
    width_l, width_g = 2 * half_l, out_g.shape[1]
    half_g = width_g // 2
    rows_l, rows_g = out_l.shape[0], out_g.shape[0]
    units_l, units_g = down_l.shape[0], down_g.shape[0]
    head_l, head_g = width_l // H_L, width_g // H_G
    micro_total, slot_total = patch_index.shape[1:]
    slots = micro_total * slot_total
    bits = bit_count(size)
    every = tuple(range(bits))

    def joined(mine, theirs, axis=1):
        low = jnp.where(is_first, mine, theirs)
        high = jnp.where(is_first, theirs, mine)
        return jnp.concatenate([low, high], axis=axis)

    def shared(mine, axis=1):
        return joined(mine, swap(mine), axis)

    def half_of(array, which, axis=1):
        length = array.shape[axis] // 2
        return lax.dynamic_slice_in_dim(array, which * length, length, axis)

    def own_heads(weight):
        rows, width = weight.shape
        thirds = weight.reshape(rows, 3, 2, width // 6)
        return lax.dynamic_index_in_dim(thirds, core, 2, keepdims=False).reshape(rows, width // 2)

    def gain_block(one, two):
        return jnp.pad(jnp.stack([one, two], axis=1), ((0, 0), (0, LANES - 2)))

    top_first = [(bits - 1,) + o for o in orders(size, (None, -1, -2))]
    mixed = orders(size, (-1, None, -2))
    plane = [o[:2] + (bits - 1,) + o[2:] for o in orders(size, (-1, -2, None))]
    line = orders(size, (None,))
    below, beyond = tuple(range(bits - 1)), tuple(range(2, bits - 1))

    fresh = functools.partial(Stream, size)
    up_width, qkv_width = up_l.shape[1] // 2, 3 * half_g
    square_units = units_g * (size // 8)
    stream_qkv_l = fresh(
        gather_all(
            jnp.concatenate([own_heads(qkv_l), gain_block(gain_l1, gain_l2)], axis=1),
            top_first,
            every,
            [(0, rows_l, 0, 3 * half_l), (0, rows_l, 3 * half_l, 3 * half_l + LANES)],
        )
    )
    stream_up_l = fresh(
        gather_all(
            jnp.concatenate([half_of(up_l, core), half_of(out_l, core), half_of(patch_proj, core)], axis=1),
            top_first,
            every,
            [
                (0, rows_l, 0, up_width),
                (0, rows_l, up_width, up_width + half_l),
                (0, rows_l, up_width + half_l, up_width + half_l + half_g),
            ],
        )
    )
    stream_down_l = fresh(gather_core(down_l, mixed, below, [(0, units_l, 0, width_l)], size))
    stream_qkv_g = fresh(
        gather_all(
            jnp.concatenate([own_heads(qkv_g), half_of(out_g, core), gain_block(gain_g1, gain_g2)], axis=1),
            top_first,
            every,
            [
                (0, rows_g, 0, qkv_width),
                (0, rows_g, qkv_width, qkv_width + half_g),
                (0, rows_g, qkv_width + half_g, qkv_width + half_g + LANES),
            ],
        )
    )
    blocks = half_of(up_g, core).reshape(rows_g, size // 8, 2, 2, units_g)
    blocks = jnp.where(is_first, blocks.transpose(3, 2, 0, 1, 4), blocks.transpose(2, 3, 0, 1, 4))
    stream_up_g = fresh(
        gather_square(
            blocks.reshape(2, 2, rows_g, square_units), plane, every, [(0, rows_g, 0, square_units)]
        )
    )
    stream_down_g = fresh(
        gather_core(down_g[:, :width_l], line, beyond, [(0, units_g, 0, width_l)], size)
    )

    bias_l = jnp.where(jnp.arange(seq_rows) < lengths[0], 0.0, NEG).astype(F32)[:, None]
    live = (jnp.arange(slot_total)[None, :] < patch_count[0][:, None]).reshape(slots)
    bias_g = jnp.where(live, 0.0, NEG).astype(F32)[:, None]
    positions = patch_index[0].reshape(slots)
    picks = positions[:, None] == jnp.arange(seq_rows)[None, :]
    picks_live = (picks & live[:, None]).astype(BF16)
    picks = picks.astype(BF16)

    advance([stream_qkv_l, stream_up_g], ())
    seq_inputs = shared(bytes_in[0])
    inputs = seq_inputs.astype(F32)
    scale_l1 = row_scale(inputs)
    scale_l1 = advance([stream_qkv_l, stream_up_l, stream_up_g], scale_l1)
    seq_grads = shared(out_grad[0])
    grad_top_b = mm(picks_live, seq_grads).astype(BF16)
    grad_top_b = advance([stream_qkv_l, stream_up_l, stream_down_l, stream_up_g], grad_top_b)
    square_top = square_gather(half_of(grad_top_b, core), size).reshape(4 * slots, half_l)
    square_top = shared(square_top)
    square_top = advance([stream_qkv_l, stream_up_l, stream_down_l, stream_qkv_g], square_top)

    advance([stream_qkv_l, stream_up_l, stream_down_l, stream_qkv_g], ())
    qkv_wl, gains_l = stream_qkv_l.result()
    gain_one_l, gain_two_l = gains_l[:, 0].astype(F32), gains_l[:, 1].astype(F32)
    normed_l = (inputs * scale_l1 * gain_one_l).astype(BF16)
    projected_l = mm(normed_l, qkv_wl).astype(BF16)
    mixture_l, lse_l = attention_forward(projected_l, bias_l, head_l)
    mixture_l = shared(mixture_l)
    mixture_l = advance([stream_up_l, stream_down_l, stream_qkv_g], mixture_l)
    up_wl, out_wl, proj_w = stream_up_l.result()
    out_wl, proj_w = shared(out_wl), shared(proj_w)
    out_own_l = half_of(out_wl, core, 0)
    hidden_l = inputs + mm(mixture_l, out_wl)
    scale_l2 = row_scale(hidden_l)
    normed_l2 = (hidden_l * scale_l2 * gain_two_l).astype(BF16)
    upward_l = mm(normed_l2, up_wl)
    activated_l = jax.nn.gelu(upward_l).astype(BF16)
    activated_l = advance([stream_down_l, stream_qkv_g, stream_up_g, stream_down_g], activated_l)
    (down_wl,) = stream_down_l.result()
    partial_l = mm(activated_l, down_wl)
    local_out = half_of(hidden_l, core) + half_of(partial_l, core) + swap(half_of(partial_l, 1 - core))

    boundary = shared(mm(picks, local_out.astype(BF16)).astype(BF16))
    start_rows = mm(boundary, proj_w)
    scale_g1 = row_scale(start_rows)
    scale_g1 = advance([stream_qkv_g, stream_up_g, stream_down_g], scale_g1)
    qkv_wg, out_wg, gains_g = stream_qkv_g.result()
    gain_one_g, gain_two_g = gains_g[:, 0].astype(F32), gains_g[:, 1].astype(F32)
    normed_g = (start_rows * scale_g1 * gain_one_g).astype(BF16)
    out_theirs_g = swap(out_wg)
    projected_g = mm(normed_g, qkv_wg).astype(BF16)
    mixture_g, lse_g = attention_forward(projected_g, bias_g, head_g)
    mixture_g = shared(mixture_g)
    hidden_g = start_rows + joined(mm(mixture_g, out_wg), mm(mixture_g, out_theirs_g))
    scale_g2 = row_scale(hidden_g)
    normed_g2 = (hidden_g * scale_g2 * gain_two_g).astype(BF16)
    square_normed = square_gather(half_of(normed_g2, core), size).reshape(4 * slots, half_g)
    square_normed = shared(square_normed)
    square_normed = advance([stream_up_g, stream_down_g], square_normed)
    (up_wg,) = stream_up_g.result()
    (down_wg,) = stream_down_g.result()
    upward_g = mm(square_normed, up_wg)
    activated_g = jax.nn.gelu(upward_g).astype(BF16)

    def scattered(grads, order_pair, places):
        return fresh(scatter_all(grads, order_pair, places))

    grad_down_g = mm_tn(activated_g, square_top).astype(BF16)
    stream_down_g = fresh(scatter_core([grad_down_g], line, beyond, size))
    grad_act_g = mm_nt(square_top, down_wg)
    grad_up_g_rows = jax.vjp(jax.nn.gelu, upward_g)[1](grad_act_g)[0].astype(BF16)
    grad_up_g = mm_tn(square_normed, grad_up_g_rows).astype(BF16)
    stream_up_g = fresh(scatter_square([grad_up_g], plane, every))
    part = mm_nt(grad_up_g_rows, up_wg)
    part = half_of(part, core) + swap(half_of(part, 1 - core).astype(BF16)).astype(F32)
    part = advance([stream_down_g, stream_up_g], part)
    part = shared(square_scatter(part.reshape(4, slots, half_g), size))
    pulled, grad_gain_g2 = norm_backward(part, hidden_g, scale_g2, gain_two_g)
    grad_hidden_g = jnp.pad(grad_top_b.astype(F32), ((0, 0), (0, width_g - width_l))) + pulled
    grad_hidden_gb = grad_hidden_g.astype(BF16)
    mine_gb, theirs_gb = half_of(grad_hidden_gb, core), half_of(grad_hidden_gb, 1 - core)
    grad_out_g = mm_tn(mixture_g, mine_gb).astype(BF16)
    grad_mixture_g = (
        mm_nt(mine_gb, half_of(out_wg, core, 0)) + mm_nt(theirs_gb, half_of(out_theirs_g, core, 0))
    ).astype(BF16)
    grad_projected_g = attention_backward(projected_g, bias_g, lse_g, grad_mixture_g, head_g)
    grad_qkv_g = mm_tn(normed_g, grad_projected_g).astype(BF16)
    stream_qkv_g = scattered([grad_qkv_g, grad_out_g], top_first, every)
    grad_projected_g = advance([stream_down_g, stream_up_g, stream_qkv_g], grad_projected_g)
    part = mm_nt(grad_projected_g, qkv_wg)
    pulled, grad_gain_g1 = norm_backward(part + swap(part), start_rows, scale_g1, gain_one_g)
    grad_start = (grad_hidden_g + pulled).astype(BF16)
    grad_proj = mm_tn(boundary, half_of(grad_start, core)).astype(BF16)

    grad_rows = mm_nt(grad_start, proj_w).astype(BF16)
    grad_local = seq_grads.astype(F32) + mm_tn(picks, grad_rows)
    grad_local_b = grad_local.astype(BF16)
    grad_down_l = mm_tn(activated_l, grad_local_b).astype(BF16)
    stream_down_l = fresh(scatter_core([grad_down_l], mixed, below, size))
    grad_act_l = mm_nt(grad_local_b, down_wl)
    grad_up_l_rows = jax.vjp(jax.nn.gelu, upward_l)[1](grad_act_l)[0].astype(BF16)
    grad_up_l_rows = advance([stream_down_g, stream_up_g, stream_qkv_g, stream_down_l], grad_up_l_rows)
    grad_up_l = mm_tn(normed_l2, grad_up_l_rows).astype(BF16)
    part = mm_nt(grad_up_l_rows, up_wl)
    pulled, grad_gain_l2 = norm_backward(part + swap(part), hidden_l, scale_l2, gain_two_l)
    grad_hidden_l = grad_local + pulled
    grad_hidden_lb = grad_hidden_l.astype(BF16)
    grad_out_l = mm_tn(mixture_l, half_of(grad_hidden_lb, core)).astype(BF16)
    stream_up_l = scattered([grad_up_l, grad_out_l, grad_proj], top_first, every)
    grad_mixture_l = mm_nt(grad_hidden_lb, out_own_l).astype(BF16)
    grad_mixture_l = advance([stream_up_g, stream_qkv_g, stream_down_l, stream_up_l], grad_mixture_l)
    grad_projected_l = attention_backward(projected_l, bias_l, lse_l, grad_mixture_l, head_l)
    grad_qkv_l = mm_tn(normed_l, grad_projected_l).astype(BF16)
    stream_qkv_l = scattered([grad_qkv_l], top_first, every)
    grad_projected_l = advance(
        [stream_up_g, stream_qkv_g, stream_down_l, stream_up_l, stream_qkv_l], grad_projected_l
    )
    part = mm_nt(grad_projected_l, qkv_wl)
    pulled, grad_gain_l1 = norm_backward(part + swap(part), inputs, scale_l1, gain_one_l)
    input_grad = half_of(grad_hidden_l + pulled, core).astype(BF16)[None]
    gains = jnp.concatenate(
        [
            grad.reshape(size, 1, grad.shape[0] // size)
            for grad in (grad_gain_l1, grad_gain_l2, grad_gain_g1, grad_gain_g2)
        ],
        axis=2,
    )
    stream_gains = fresh(scatter_small(gains, size))

    partial_g = mm(activated_g, down_wg)
    partial_g = half_of(partial_g, core) + swap(half_of(partial_g, 1 - core).astype(BF16)).astype(F32)
    returned = half_of(hidden_g[:, :width_l], core) + square_scatter(partial_g.reshape(4, slots, half_l), size)
    hidden_out = (local_out + mm_tn(picks_live, returned.astype(BF16))).astype(BF16)[None]
    input_grad, hidden_out = advance(
        [stream_qkv_g, stream_down_l, stream_up_l, stream_qkv_l, stream_gains], (input_grad, hidden_out)
    )
    advance([stream_up_l, stream_qkv_l, stream_gains], ())
    advance([stream_up_l, stream_qkv_l, stream_gains], ())

    def joined_columns(mine, theirs):
        return joined(mine, theirs).astype(F32)

    def joined_heads(mine, theirs):
        rows, width = mine.shape
        thirds = [part.reshape(rows, 3, width // 3) for part in (mine, theirs)]
        return joined(*thirds, axis=2).reshape(rows, 2 * width).astype(F32)

    def from_owner(mine, theirs):
        return jnp.where((position >> (bits - 1)) == core, mine, theirs).astype(F32)

    def in_order(blocks):
        low = own_bit((0, 0)), own_bit((1, 1))
        rows, width = blocks.shape[2:]
        placed = []
        for y in range(2):
            for x in range(2):
                dx, dy = x ^ low[0], y ^ low[1]
                index = jnp.where(is_first, 2 * dx + dy, 2 * dy + dx)
                placed.append(lax.dynamic_index_in_dim(blocks.reshape(4, rows, width), index, 0, keepdims=False))
        stack = jnp.stack(placed).reshape(4, rows, size // 8, units_g)
        return stack.transpose(1, 2, 0, 3).reshape(rows, 4 * width)

    down_g_mine = stream_down_g.result()
    total_down_g = from_owner(down_g_mine, swap(down_g_mine))
    total_down_g = jnp.pad(total_down_g, ((0, 0), (0, width_g - width_l)))
    up_g_mine = in_order(stream_up_g.result())
    total_up_g = joined_columns(up_g_mine, swap(up_g_mine))
    g_mine = stream_qkv_g.result()
    g_theirs = swap(g_mine)
    total_qkv_g = joined_heads(g_mine[:, :qkv_width], g_theirs[:, :qkv_width])
    total_out_g = joined_columns(g_mine[:, qkv_width:], g_theirs[:, qkv_width:])
    down_l_mine = stream_down_l.result()
    total_down_l = from_owner(down_l_mine, swap(down_l_mine))
    l_mine = stream_up_l.result()
    l_theirs = swap(l_mine)
    cuts = [0, up_width, up_width + half_l, up_width + half_l + half_g]
    total_up_l, total_out_l, total_proj = (
        joined_columns(l_mine[:, low:high], l_theirs[:, low:high]) for low, high in zip(cuts, cuts[1:])
    )
    q_mine = stream_qkv_l.result()
    total_qkv_l = joined_heads(q_mine, swap(q_mine))
    gains = stream_gains.result()
    gains = jnp.where(is_first, gains, lax.ppermute(gains, "section", [(0, 1)]))
    total_gain_l1 = gains[:rows_l]
    total_gain_l2 = gains[rows_l : 2 * rows_l]
    total_gain_g1 = gains[2 * rows_l : 2 * rows_l + rows_g]
    total_gain_g2 = gains[2 * rows_l + rows_g :]
    return (
        hidden_out,
        input_grad,
        total_gain_l1,
        total_qkv_l,
        total_out_l,
        total_gain_l2,
        total_up_l,
        total_down_l,
        total_proj,
        total_gain_g1,
        total_qkv_g,
        total_out_g,
        total_gain_g2,
        total_up_g,
        total_down_g,
    )


def solution(mesh):
    rows, vector = P("dp", None), P("dp")
    features = P("dp", None, "section")
    in_specs = (
        features,
        vector,
        P("dp", None, None),
        rows,
        vector,
        rows,
        rows,
        vector,
        rows,
        rows,
        rows,
        vector,
        rows,
        rows,
        vector,
        rows,
        rows,
        features,
    )
    out_specs = (
        features,
        features,
        vector,
        rows,
        rows,
        vector,
        rows,
        rows,
        rows,
        vector,
        rows,
        rows,
        vector,
        rows,
        rows,
    )
    return jax.shard_map(
        functools.partial(local, mesh.shape["dp"]),
        mesh=mesh,
        in_specs=in_specs,
        out_specs=out_specs,
        check_vma=False,
    )
```

time: 4260 us -> 721 us (0.17)
  waiting for transfers between devices: 3590 us -> 256 us
  matrix products: 274 us -> 95.6 us
  blocking collectives: 144 us -> 0 us
  Pallas kernels: 0 us -> 104 us
  starting transfers between devices: 13.6 us -> 82.4 us
  local copies, waits for them, and re-layouts: 92.2 us -> 49.4 us
    reduce_scatter x9 -> x0, waiting for transfers between devices: 2640 us -> none  [local(): lax.psum_scatter(acc_local + (acc_proj,) + acc_global, 'dp', scatter_dime...]
    all_gather x11 -> x0, waiting for transfers between devices: 847 us -> none  [the longest x1 213 us: local(): lax.all_gather(down_g, 'dp', axis=0, tiled=True)]
    dot_general x38 -> x32, matrix products: 274 us -> 95.6 us  [the longest x9 38.3 us: mm_nt(): lax.dot_general(left, right, (((1,), (1,)), ((), ())), preferred_element_...]
    ppermute x8 -> x80, waiting for transfers between devices: 96 us -> 256 us  [the longest x56 251 us: exchange(): return lax.ppermute(array, ('section', 'dp'), pairs)]
    unnamed x2 -> x0, blocking collectives: 125 us -> none
    pallas_call x0 -> x16, Pallas kernels: none -> 104 us  [the longest x6 33.7 us: assembled(): pl.pallas_call(functools.partial(assembly_kernel, half, cuts), grid_spec=...]
    ppermute x8 -> x80, starting transfers between devices: 12.8 us -> 82.4 us  [the longest x56 48.9 us: exchange(): return lax.ppermute(array, ('section', 'dp'), pairs)]
  transfers between devices with their start and end apart: 29 -> 80, of which waited for: 18 -> 35; matrix products, arithmetic and copies ran while one was open for 2% -> 26% of each run, Pallas kernels for 0% -> 13%
where the time goes in v1:
time: 721 us; the launch traced here: 709 us
  waiting for transfers between devices  256 us (36%)
  other arithmetic  117 us (16%)
  Pallas kernels  104 us (14%)
  matrix products  95.6 us (13%)
  starting transfers between devices  82.4 us (11%)
  local copies, waits for them, and re-layouts  49.4 us (7%)
    ppermute x56, waiting for transfers between devices, exchange(): return lax.ppermute(array, ('section', 'dp'), pairs)  251 us
    ppermute x56, starting transfers between devices, exchange(): return lax.ppermute(array, ('section', 'dp'), pairs)  48.9 us
    dot_general x9, matrix products, mm_nt(): lax.dot_general(left, right, (((1,), (1,)), ((), ())), preferred_element_...  38.3 us
    pallas_call x6, Pallas kernels, assembled(): pl.pallas_call(functools.partial(assembly_kernel, half, cuts), grid_spec=...  33.7 us
    ppermute x23, starting transfers between devices, swap(): return lax.ppermute(array, 'section', [(0, 1), (1, 0)])  32.2 us
    dot_general x11, matrix products, mm_tn(): lax.dot_general(left, right, (((0,), (0,)), ((), ())), preferred_element_...  30.4 us
    pallas_call x6, Pallas kernels, split_stack(): pl.pallas_call(functools.partial(split_kernel, half), grid_spec=pltpu.Pre...  30.3 us
    dot_general x12, matrix products, mm(): return jnp.dot(left, right, preferred_element_type=F32)  27 us
  transfers between devices with their start and end apart: 80, of which 35 were waited for; matrix products, arithmetic and copies ran while one was open for 26% of the time, Pallas kernels for 13%

profile of v1, /device:TPU:1, one launch (start us, length us, event | category | flops | bytes accessed | tf_op | source)
XLA Modules:
  0.0 709.1 jit_solution(17477917545167355114)
XLA Ops:
  25.7 5.3 collective-permute-done.3
  31.0 4.1 collective-permute-done.4
  54.9 5.8 collective-permute-done.9
  60.7 7.2 %collective-permute-done.8 = bf16[2,48,2688]{2,1,0:T(8,128)(2,1)S(1)} collective-permute-done((bf16[2,48,2688]{2,1,0:T(8,128)(2,1)S(1)}, bf16[2,48,2688]{2,1,0:T(8,128)(2,1)S(1)}, u32[]{:S(2)}, u32[]{:S(2)}) %collective-permute-start.8) | collective-permute-done | bytes 516128 | tf_op jit(solution)/shard_map/ppermute | solution.py:213
  75.4 23.1 %collective-permute-done.15 = bf16[1,192,768]{2,1,0:T(8,128)(2,1)S(1)} collective-permute-done((bf16[1,192,768]{2,1,0:T(8,128)(2,1)S(1)}, bf16[1,192,768]{2,1,0:T(8,128)(2,1)S(1)}, u32[]{:S(2)}, u32[]{:S(2)}) %collective-permute-start.15) | collective-permute-done | bytes 294944 | tf_op jit(solution)/shard_map/ppermute | solution.py:213
  98.5 4.7 collective-permute-done.16
  110.4 12.9 %shard_map.506 = (bf16[1024,384]{1,0:T(8,128)(2,1)S(1)}, f32[3,2,1024]{2,1,0:T(2,128)S(1)}) custom-call(bf16[1024,1152]{1,0:T(8,128)(2,1)S(1)} %convolution_convert_fusion.1.q_ref.k_ref.v_ref, bf16[1024,1152]{1,0:T(8,128)(2,1)S(1)} %convolution_convert_fusion.1.q_ref.k_ref.v_ref, bf16[1024,1152]{1,0:T(8,128)(2,1)S(1)} %convolution_convert_fusion.1.q_ref.k_ref.v_ref, ...), custom_call_target="tpu_custom_call" | custom-call | flops 3221225472 | bytes 3145728 | tf_op jit(solution)/shard_map/pallas_call | solution.py:154
  126.8 38.8 %collective-permute-done.18 = bf16[2,192,768]{2,1,0:T(8,128)(2,1)S(1)} collective-permute-done((bf16[2,192,768]{2,1,0:T(8,128)(2,1)S(1)}, bf16[2,192,768]{2,1,0:T(8,128)(2,1)S(1)}, u32[]{:S(2)}, u32[]{:S(2)}) %collective-permute-start.18) | collective-permute-done | bytes 589856 | tf_op jit(solution)/shard_map/ppermute | solution.py:213
  170.8 6.1 shard_map.507
  182.5 6.1 multiply_convert_fusion
  188.6 19.4 %collective-permute-done.24 = bf16[4,96,768]{2,1,0:T(8,128)(2,1)S(1)} collective-permute-done((bf16[4,96,768]{2,1,0:T(8,128)(2,1)S(1)}, bf16[4,96,768]{2,1,0:T(8,128)(2,1)S(1)}, u32[]{:S(2)}, u32[]{:S(2)}) %collective-permute-start.24) | collective-permute-done | bytes 589856 | tf_op jit(solution)/shard_map/ppermute | solution.py:213
  211.3 5.0 pad_maximum_fusion.low
  217.3 11.8 %shard_map.508 = bf16[1536,768]{1,0:T(8,128)(2,1)S(1)} custom-call(s32[8]{0:T(128)S(1)} %fusion.103.table, bf16[4,192,768]{2,1,0:T(8,128)(2,1)S(1)} %pad_maximum_fusion.19.low, bf16[4,192,768]{2,1,0:T(8,128)(2,1)S(1)} %collective-permute-done.22.high), custom_call_target="tpu_custom_call" | custom-call | bytes 4718592 | tf_op jit(solution)/shard_map/pallas_call | solution.py:266
  243.4 8.5 %collective-permute-done.30 = bf16[384,768]{1,0:T(8,128)(2,1)S(1)} collective-permute-done((bf16[384,768]{1,0:T(8,128)(2,1)S(1)}, bf16[384,768]{1,0:T(8,128)(2,1)S(1)}, u32[]{:S(2)}, u32[]{:S(2)}) %collective-permute-start.30) | collective-permute-done | bytes 589856 | tf_op jit(solution)/shard_map/ppermute | solution.py:213
  252.0 16.4 %collective-permute-done.29.high = bf16[8,96,768]{2,1,0:T(8,128)(2,1)S(1)} collective-permute-done((bf16[8,96,768]{2,1,0:T(8,128)(2,1)S(1)}, bf16[8,96,768]{2,1,0:T(8,128)(2,1)S(1)}, u32[]{:S(2)}, u32[]{:S(2)}) %collective-permute-start.29) | collective-permute-done | bytes 1179680 | tf_op jit(solution)/shard_map/ppermute | solution.py:213
  272.1 12.9 %shard_map.509 = (bf16[1536,2304]{1,0:T(8,128)(2,1)}, bf16[1536,768]{1,0:T(8,128)(2,1)S(1)}, bf16[1536,128]{1,0:T(8,128)(2,1)S(1)}) custom-call(s32[16]{0:T(128)S(1)} %fusion.101.table, bf16[8,96,3200]{2,1,0:T(8,128)(2,1)} %pad_maximum_fusion.low, bf16[8,96,3200]{2,1,0:T(8,128)(2,1)} %collective-permute-done.28.high), custom_call_target="tpu_custom_call" | custom-call | bytes 19660800 | tf_op jit(solution)/shard_map/pallas_call | solution.py:266
  288.3 5.0 convolution_convert_fusion.2.q_ref.k_ref.v_ref
  293.3 5.1 shard_map.510
  306.4 4.6 collective-permute-done.34
  311.9 8.3 %collective-permute-done.35 = bf16[2,192,768]{2,1,0:T(8,128)(2,1)S(1)} collective-permute-done((bf16[2,192,768]{2,1,0:T(8,128)(2,1)S(1)}, bf16[2,192,768]{2,1,0:T(8,128)(2,1)S(1)}, u32[]{:S(2)}, u32[]{:S(2)}) %collective-permute-start.35) | collective-permute-done | bytes 589856 | tf_op jit(solution)/shard_map/ppermute | solution.py:213
  329.3 10.6 %collective-permute-done.33.high = bf16[1,384,768]{2,1,0:T(8,128)(2,1)S(1)} collective-permute-done((bf16[1,384,768]{2,1,0:T(8,128)(2,1)S(1)}, bf16[1,384,768]{2,1,0:T(8,128)(2,1)S(1)}, u32[]{:S(2)}, u32[]{:S(2)}) %collective-permute-start.33) | collective-permute-done | bytes 589856 | tf_op jit(solution)/shard_map/ppermute | solution.py:213
  363.7 5.1 collective-permute-done.38
  370.4 4.4 collective-permute-done.39
  384.5 5.2 shard_map.515
  391.0 5.1 convolution_convert_fusion.refs_0_
  396.0 12.6 %shard_map.516 = (bf16[8,96,3072]{2,1,0:T(8,128)(2,1)}, bf16[8,96,3072]{2,1,0:T(8,128)(2,1)}) custom-call(s32[16]{0:T(128)S(1)} %fusion.101.table, bf16[1536,2304]{1,0:T(8,128)(2,1)} %convolution_convert_fusion.refs_0_, bf16[1536,768]{1,0:T(8,128)(2,1)S(1)} %convolution_convert_fusion.6.refs_1_), custom_call_target="tpu_custom_call" | custom-call | bytes 18874368 | tf_op jit(solution)/shard_map/pallas_call | solution.py:305
  408.6 10.8 %collective-permute-done.42 = bf16[8,96,768]{2,1,0:T(8,128)(2,1)S(1)} collective-permute-done((bf16[8,96,768]{2,1,0:T(8,128)(2,1)S(1)}, bf16[8,96,768]{2,1,0:T(8,128)(2,1)S(1)}, u32[]{:S(2)}, u32[]{:S(2)}) %collective-permute-start.42) | collective-permute-done | bytes 1179680 | tf_op jit(solution)/shard_map/ppermute | solution.py:213
  419.4 6.9 fusion.135
  438.1 5.1 collective-permute-start.43
  448.7 5.1 fusion.29
  453.8 11.2 %fusion.6 = bf16[1024,1536]{1,0:T(8,128)(2,1)} fusion(f32[1024,1536]{1,0:T(8,128)} %get-tuple-element.305, bf16[1536,768]{1,0:T(8,128)(2,1)S(1)} %copy-done.5, f32[1024,768]{1,0:T(8,128)} %fusion.29, bf16[1024,384]{1,0:T(8,128)(2,1)} %copy-done.59, bf16[1024,384]{1,0:T(8,128)(2,1)} %copy-done.56), kind=kOutput, calls=%fused_computation.9 | convolution fusion | flops 2452094976 | bytes 16515072 | tf_op jit(solution)/shard_map/dot_general | solution.py:27
  472.2 14.0 %collective-permute-done.45 = bf16[8,96,3072]{2,1,0:T(8,128)(2,1)} collective-permute-done((bf16[8,96,3072]{2,1,0:T(8,128)(2,1)}, bf16[8,96,3072]{2,1,0:T(8,128)(2,1)}, u32[]{:S(2)}, u32[]{:S(2)}) %collective-permute-start.45) | collective-permute-done | bytes 4718624 | tf_op jit(solution)/shard_map/ppermute | solution.py:213
  486.2 7.0 fusion.136
  510.9 4.0 convolution_convert_fusion.3.refs_0_
  516.7 4.2 multiply_reduce_fusion
  520.9 4.9 fusion.124
  528.1 8.5 %shard_map.518 = (bf16[8,48,2688]{2,1,0:T(8,128)(2,1)S(1)}, bf16[8,48,2688]{2,1,0:T(8,128)(2,1)S(1)}) custom-call(s32[16]{0:T(128)S(1)} %fusion.101.table, bf16[768,1536]{1,0:T(8,128)(2,1)} %convolution_convert_fusion.3.refs_0_, bf16[768,384]{1,0:T(8,128)(2,1)S(1)} %convolution_convert_fusion.11.refs_1_, bf16[768,768]{1,0:T(8,128)(2,1)S(1)} %convolution_convert_fusion.8.refs_2_), custom_call_target="tpu_custom_call" | custom-call | bytes 8257536 | tf_op jit(solution)/shard_map/pallas_call | solution.py:305
  538.6 8.4 %collective-permute-done.48 = bf16[4,96,3072]{2,1,0:T(8,128)(2,1)} collective-permute-done((bf16[4,96,3072]{2,1,0:T(8,128)(2,1)S(1)}, bf16[4,96,3072]{2,1,0:T(8,128)(2,1)}, u32[]{:S(2)}, u32[]{:S(2)}) %collective-permute-start.48) | collective-permute-done | bytes 2359328 | tf_op jit(solution)/shard_map/ppermute | solution.py:213
  558.1 17.0 %shard_map.519 = (bf16[1024,384]{1,0:T(8,128)(2,1)S(1)}, bf16[1024,384]{1,0:T(8,128)(2,1)S(1)}, bf16[1024,384]{1,0:T(8,128)(2,1)S(1)}) custom-call(bf16[1024,1152]{1,0:T(8,128)(2,1)S(1)} %copy-done.24, bf16[1024,1152]{1,0:T(8,128)(2,1)S(1)} %copy-done.24, bf16[1024,1152]{1,0:T(8,128)(2,1)S(1)} %copy-done.24, f32[1024,1]{1,0:T(8,128)S(1)} %copy-done.18, ...), custom_call_target="tpu_custom_call" | custom-call | flops 8053063680 | bytes 6291456 | tf_op jit(solution)/shard_map/pallas_call | solution.py:178
  579.4 4.1 shard_map.520
  584.5 9.1 %collective-permute-done.52 = bf16[2,96,3072]{2,1,0:T(8,128)(2,1)S(1)} collective-permute-done((bf16[2,96,3072]{2,1,0:T(8,128)(2,1)S(1)}, bf16[2,96,3072]{2,1,0:T(8,128)(2,1)S(1)}, u32[]{:S(2)}, u32[]{:S(2)}) %collective-permute-start.52) | collective-permute-done | bytes 1179680 | tf_op jit(solution)/shard_map/ppermute | solution.py:213
  603.9 4.6 fusion.137
  626.0 3.7 fusion.35
  629.7 13.1 %collective-permute-done.55 = bf16[1,96,3072]{2,1,0:T(8,128)(2,1)} collective-permute-done((bf16[1,96,3072]{2,1,0:T(8,128)(2,1)}, bf16[1,96,3072]{2,1,0:T(8,128)(2,1)}, u32[]{:S(2)}, u32[]{:S(2)}) %collective-permute-start.55) | collective-permute-done | bytes 589856 | tf_op jit(solution)/shard_map/ppermute | solution.py:213
  657.0 4.4 collective-permute-done.65
  661.4 4.3 collective-permute-done.63
  678.5 7.2 %collective-permute-done.66 = bf16[1,48,2688]{2,1,0:T(8,128)(2,1)} collective-permute-done((bf16[1,48,2688]{2,1,0:T(8,128)(2,1)}, bf16[1,48,2688]{2,1,0:T(8,128)(2,1)}, u32[]{:S(2)}, u32[]{:S(2)}) %collective-permute-start.66) | collective-permute-done | bytes 258080 | tf_op jit(solution)/shard_map/ppermute | solution.py:213
  699.4 4.8 collective-permute-start.73
  (715 shorter events, 288.4 us)
Async XLA Ops:
  7.0 11.4 %collective-permute-start.1 = (bf16[1,48,1280]{2,1,0:T(8,128)(2,1)S(1)}, bf16[1,48,1280]{2,1,0:T(8,128)(2,1)}, u32[]{:S(2)}, u32[]{:S(2)}) collective-permute-start(bf16[1,48,1280]{2,1,0:T(8,128)(2,1)S(1)} %fusion.85), channel_id=1, source_target_pairs={{0,8},{1,9},{2,10},{3,11},{4,12},{5,13},{6,14},{7,15},{8,0},{9,1},... | collective-permute-start | bytes 368648 | tf_op jit(solution)/shard_map/ppermute | solution.py:213
  20.1 10.9 %collective-permute-start.3 = (bf16[2,48,1280]{2,1,0:T(8,128)(2,1)}, bf16[2,48,1280]{2,1,0:T(8,128)(2,1)}, u32[]{:S(2)}, u32[]{:S(2)}) collective-permute-start(bf16[2,48,1280]{2,1,0:T(8,128)(2,1)} %pad_maximum_fusion.45), channel_id=1, source_target_pairs={{0,4},{1,5},{2,6},{3,7},{4,0},{5,1},{6,2},{7,3},{8,12},{9,13},{10,... | collective-permute-start | bytes 737288 | tf_op jit(solution)/shard_map/ppermute | solution.py:213
  21.4 13.7 %collective-permute-start.4 = (bf16[1,48,2688]{2,1,0:T(8,128)(2,1)S(1)}, bf16[1,48,2688]{2,1,0:T(8,128)(2,1)}, u32[]{:S(2)}, u32[]{:S(2)}) collective-permute-start(bf16[1,48,2688]{2,1,0:T(8,128)(2,1)S(1)} %maximum_bitcast_fusion), channel_id=1, source_target_pairs={{0,8},{1,9},{2,10},{3,11},{4,12},{5,13},{6,14},{7,15},{8,0},{9,1},... | collective-permute-start | bytes 774152 | tf_op jit(solution)/shard_map/ppermute | solution.py:213
  23.8 11.3 %collective-permute-start.5 = (bf16[2,96,768]{2,1,0:T(8,128)(2,1)}, bf16[2,96,768]{2,1,0:T(8,128)(2,1)}, u32[]{:S(2)}, u32[]{:S(2)}) collective-permute-start(bf16[2,96,768]{2,1,0:T(8,128)(2,1)} %get-tuple-element.283), channel_id=1, source_target_pairs={{0,2},{1,3},{2,0},{3,1},{4,6},{5,7},{6,4},{7,5},{8,10},{9,11},{10,... | collective-permute-start | bytes 884744 | tf_op jit(solution)/shard_map/ppermute | solution.py:213
  45.4 15.3 %collective-permute-start.7 = (bf16[4,48,1280]{2,1,0:T(8,128)(2,1)S(1)}, bf16[4,48,1280]{2,1,0:T(8,128)(2,1)S(1)}, u32[]{:S(2)}, u32[]{:S(2)}) collective-permute-start(bf16[4,48,1280]{2,1,0:T(8,128)(2,1)S(1)} %pad_maximum_fusion.37), channel_id=1, source_target_pairs={{0,1},{1,0},{2,3},{3,2},{4,5},{5,4},{6,7},{7,6},{8,9},{9,8},{10,11... | collective-permute-start | bytes 1474568 | tf_op jit(solution)/shard_map/ppermute | solution.py:213
  51.3 16.6 %collective-permute-start.8 = (bf16[2,48,2688]{2,1,0:T(8,128)(2,1)S(1)}, bf16[2,48,2688]{2,1,0:T(8,128)(2,1)S(1)}, u32[]{:S(2)}, u32[]{:S(2)}) collective-permute-start(bf16[2,48,2688]{2,1,0:T(8,128)(2,1)S(1)} %pad_maximum_fusion.36), channel_id=1, source_target_pairs={{0,4},{1,5},{2,6},{3,7},{4,0},{5,1},{6,2},{7,3},{8,12},{9,13},{10,... | collective-permute-start | bytes 1548296 | tf_op jit(solution)/shard_map/ppermute | solution.py:213
  70.1 33.1 %collective-permute-start.14 = (bf16[4,48,2688]{2,1,0:T(8,128)(2,1)}, bf16[4,48,2688]{2,1,0:T(8,128)(2,1)}, u32[]{:S(2)}, u32[]{:S(2)}) collective-permute-start(bf16[4,48,2688]{2,1,0:T(8,128)(2,1)} %pad_maximum_fusion.23), channel_id=1, source_target_pairs={{0,1},{1,0},{2,3},{3,2},{4,5},{5,4},{6,7},{7,6},{8,9},{9,8},{10,11... | collective-permute-start | bytes 3096584 | tf_op jit(solution)/shard_map/ppermute | solution.py:213
  73.3 29.8 %collective-permute-start.13 = (bf16[8,48,1280]{2,1,0:T(8,128)(2,1)S(1)}, bf16[8,48,1280]{2,1,0:T(8,128)(2,1)S(1)}, u32[]{:S(2)}, u32[]{:S(2)}) collective-permute-start(bf16[8,48,1280]{2,1,0:T(8,128)(2,1)S(1)} %pad_maximum_fusion.24.low), channel_id=1, source_target_pairs={{0,2},{1,3},{2,0},{3,1},{4,6},{5,7},{6,4},{7,5},{8,10},{9,11},{10,... | collective-permute-start | bytes 2949128 | tf_op jit(solution)/shard_map/ppermute | solution.py:213
  73.5 29.7 %collective-permute-start.16 = (bf16[1,96,3200]{2,1,0:T(8,128)(2,1)}, bf16[1,96,3200]{2,1,0:T(8,128)(2,1)}, u32[]{:S(2)}, u32[]{:S(2)}) collective-permute-start(bf16[1,96,3200]{2,1,0:T(8,128)(2,1)} %fusion.42), channel_id=1, source_target_pairs={{0,8},{1,9},{2,10},{3,11},{4,12},{5,13},{6,14},{7,15},{8,0},{9,1},... | collective-permute-start | bytes 1843208 | tf_op jit(solution)/shard_map/ppermute | solution.py:213
  75.2 23.3 %collective-permute-start.15 = (bf16[1,192,768]{2,1,0:T(8,128)(2,1)S(1)}, bf16[1,192,768]{2,1,0:T(8,128)(2,1)S(1)}, u32[]{:S(2)}, u32[]{:S(2)}) collective-permute-start(bf16[1,192,768]{2,1,0:T(8,128)(2,1)S(1)} %select_bitcast_fusion.1), channel_id=1, source_target_pairs={{0,1},{1,0},{2,3},{3,2},{4,5},{5,4},{6,7},{7,6},{8,9},{9,8},{10,11... | collective-permute-start | bytes 884744 | tf_op jit(solution)/shard_map/ppermute | solution.py:213
  106.5 59.0 %collective-permute-start.17 = (bf16[8,48,2688]{2,1,0:T(8,128)(2,1)S(1)}, bf16[8,48,2688]{2,1,0:T(8,128)(2,1)S(1)}, u32[]{:S(2)}, u32[]{:S(2)}) collective-permute-start(bf16[8,48,2688]{2,1,0:T(8,128)(2,1)S(1)} %pad_maximum_fusion.4.low), channel_id=1, source_target_pairs={{0,2},{1,3},{2,0},{3,1},{4,6},{5,7},{6,4},{7,5},{8,10},{9,11},{10,... | collective-permute-start | bytes 6193160 | tf_op jit(solution)/shard_map/ppermute | solution.py:213
  124.8 40.8 %collective-permute-start.19 = (bf16[2,96,3200]{2,1,0:T(8,128)(2,1)S(1)}, bf16[2,96,3200]{2,1,0:T(8,128)(2,1)S(1)}, u32[]{:S(2)}, u32[]{:S(2)}) collective-permute-start(bf16[2,96,3200]{2,1,0:T(8,128)(2,1)S(1)} %pad_maximum_fusion.11), channel_id=1, source_target_pairs={{0,4},{1,5},{2,6},{3,7},{4,0},{5,1},{6,2},{7,3},{8,12},{9,13},{10,... | collective-permute-start | bytes 3686408 | tf_op jit(solution)/shard_map/ppermute | solution.py:213
  124.9 40.7 %collective-permute-start.18 = (bf16[2,192,768]{2,1,0:T(8,128)(2,1)S(1)}, bf16[2,192,768]{2,1,0:T(8,128)(2,1)S(1)}, u32[]{:S(2)}, u32[]{:S(2)}) collective-permute-start(bf16[2,192,768]{2,1,0:T(8,128)(2,1)S(1)} %pad_maximum_fusion.31), channel_id=1, source_target_pairs={{0,4},{1,5},{2,6},{3,7},{4,0},{5,1},{6,2},{7,3},{8,12},{9,13},{10,... | collective-permute-start | bytes 1769480 | tf_op jit(solution)/shard_map/ppermute | solution.py:213
  168.9 42.5 %collective-permute-start.23 = (bf16[4,96,3200]{2,1,0:T(8,128)(2,1)}, bf16[4,96,3200]{2,1,0:T(8,128)(2,1)}, u32[]{:S(2)}, u32[]{:S(2)}) collective-permute-start(bf16[4,96,3200]{2,1,0:T(8,128)(2,1)} %pad_maximum_fusion.1), channel_id=1, source_target_pairs={{0,1},{1,0},{2,3},{3,2},{4,5},{5,4},{6,7},{7,6},{8,9},{9,8},{10,11... | collective-permute-start | bytes 7372808 | tf_op jit(solution)/shard_map/ppermute | solution.py:213
  179.3 28.6 %collective-permute-start.24 = (bf16[4,96,768]{2,1,0:T(8,128)(2,1)S(1)}, bf16[4,96,768]{2,1,0:T(8,128)(2,1)S(1)}, u32[]{:S(2)}, u32[]{:S(2)}) collective-permute-start(bf16[4,96,768]{2,1,0:T(8,128)(2,1)S(1)} %pad_maximum_fusion.32), channel_id=1, source_target_pairs={{0,8},{1,9},{2,10},{3,11},{4,12},{5,13},{6,14},{7,15},{8,0},{9,1},... | collective-permute-start | bytes 1769480 | tf_op jit(solution)/shard_map/ppermute | solution.py:213
  179.5 28.4 %collective-permute-start.22 = (bf16[4,192,768]{2,1,0:T(8,128)(2,1)S(1)}, bf16[4,192,768]{2,1,0:T(8,128)(2,1)S(1)}, u32[]{:S(2)}, u32[]{:S(2)}) collective-permute-start(bf16[4,192,768]{2,1,0:T(8,128)(2,1)S(1)} %pad_maximum_fusion.19.low), channel_id=1, source_target_pairs={{0,2},{1,3},{2,0},{3,1},{4,6},{5,7},{6,4},{7,5},{8,10},{9,11},{10,... | collective-permute-start | bytes 3538952 | tf_op jit(solution)/shard_map/ppermute | solution.py:213
  216.4 55.7 %collective-permute-start.28 = (bf16[8,96,3200]{2,1,0:T(8,128)(2,1)}, bf16[8,96,3200]{2,1,0:T(8,128)(2,1)}, u32[]{:S(2)}, u32[]{:S(2)}) collective-permute-start(bf16[8,96,3200]{2,1,0:T(8,128)(2,1)} %pad_maximum_fusion.low), channel_id=1, source_target_pairs={{0,2},{1,3},{2,0},{3,1},{4,6},{5,7},{6,4},{7,5},{8,10},{9,11},{10,... | collective-permute-start | bytes 14745608 | tf_op jit(solution)/shard_map/ppermute | solution.py:213
  236.2 32.1 %collective-permute-start.29 = (bf16[8,96,768]{2,1,0:T(8,128)(2,1)S(1)}, bf16[8,96,768]{2,1,0:T(8,128)(2,1)S(1)}, u32[]{:S(2)}, u32[]{:S(2)}) collective-permute-start(bf16[8,96,768]{2,1,0:T(8,128)(2,1)S(1)} %pad_maximum_fusion.20.low), channel_id=1, source_target_pairs={{0,4},{1,5},{2,6},{3,7},{4,0},{5,1},{6,2},{7,3},{8,12},{9,13},{10,... | collective-permute-start | bytes 3538952 | tf_op jit(solution)/shard_map/ppermute | solution.py:213
  240.3 11.6 %collective-permute-start.30 = (bf16[384,768]{1,0:T(8,128)(2,1)S(1)}, bf16[384,768]{1,0:T(8,128)(2,1)S(1)}, u32[]{:S(2)}, u32[]{:S(2)}) collective-permute-start(bf16[384,768]{1,0:T(8,128)(2,1)S(1)} %copy-done.120), channel_id=1, source_target_pairs={{0,8},{1,9},{2,10},{3,11},{4,12},{5,13},{6,14},{7,15},{24,16},{25,... | collective-permute-start | bytes 1769480 | tf_op jit(solution)/shard_map/ppermute | solution.py:213
  285.0 15.2 %collective-permute-start.32 = (bf16[1536,768]{1,0:T(8,128)(2,1)S(1)}, bf16[1536,768]{1,0:T(8,128)(2,1)}, u32[]{:S(2)}, u32[]{:S(2)}) collective-permute-start(bf16[1536,768]{1,0:T(8,128)(2,1)S(1)} %get-tuple-element.156), channel_id=1, source_target_pairs={{0,16},{16,0},{1,17},{17,1},{2,18},{18,2},{3,19},{19,3},{4,20},{20... | collective-permute-start | bytes 7077896 | tf_op jit(solution)/shard_map/ppermute | solution.py:203
  324.8 15.1 %collective-permute-start.33 = (bf16[1,384,768]{2,1,0:T(8,128)(2,1)S(1)}, bf16[1,384,768]{2,1,0:T(8,128)(2,1)S(1)}, u32[]{:S(2)}, u32[]{:S(2)}) collective-permute-start(bf16[1,384,768]{2,1,0:T(8,128)(2,1)S(1)} %select_bitcast_fusion.low), channel_id=1, source_target_pairs={{0,4},{1,5},{2,6},{3,7},{4,0},{5,1},{6,2},{7,3},{8,12},{9,13},{10,... | collective-permute-start | bytes 1769480 | tf_op jit(solution)/shard_map/ppermute | solution.py:213
  379.1 29.5 %collective-permute-start.41 = (bf16[1,384,768]{2,1,0:T(8,128)(2,1)S(1)}, bf16[1,384,768]{2,1,0:T(8,128)(2,1)S(1)}, u32[]{:S(2)}, u32[]{:S(2)}) collective-permute-start(bf16[1,384,768]{2,1,0:T(8,128)(2,1)S(1)} %get-tuple-element.170), channel_id=1, source_target_pairs={{0,4},{1,5},{2,6},{3,7},{4,0},{5,1},{6,2},{7,3},{8,12},{9,13},{10,... | collective-permute-start | bytes 1769480 | tf_op jit(solution)/shard_map/ppermute | solution.py:213
  379.2 40.2 %collective-permute-start.42 = (bf16[8,96,768]{2,1,0:T(8,128)(2,1)S(1)}, bf16[8,96,768]{2,1,0:T(8,128)(2,1)S(1)}, u32[]{:S(2)}, u32[]{:S(2)}) collective-permute-start(bf16[8,96,768]{2,1,0:T(8,128)(2,1)S(1)} %get-tuple-element.171), channel_id=1, source_target_pairs={{0,4},{1,5},{2,6},{3,7},{4,0},{5,1},{6,2},{7,3},{8,12},{9,13},{10,... | collective-permute-start | bytes 3538952 | tf_op jit(solution)/shard_map/ppermute | solution.py:213
  426.3 16.8 %collective-permute-start.46 = (f32[192,1536]{1,0:T(8,128)}, f32[192,1536]{1,0:T(8,128)}, u32[]{:S(2)}, u32[]{:S(2)}) collective-permute-start(f32[192,1536]{1,0:T(8,128)} %fusion.135), channel_id=1, source_target_pairs={{0,16},{16,0},{1,17},{17,1},{2,18},{18,2},{3,19},{19,3},{4,20},{20... | collective-permute-start | bytes 3538952 | tf_op jit(solution)/shard_map/ppermute | solution.py:203
  428.6 57.5 %collective-permute-start.45 = (bf16[8,96,3072]{2,1,0:T(8,128)(2,1)}, bf16[8,96,3072]{2,1,0:T(8,128)(2,1)}, u32[]{:S(2)}, u32[]{:S(2)}) collective-permute-start(bf16[8,96,3072]{2,1,0:T(8,128)(2,1)} %get-tuple-element.176), channel_id=1, source_target_pairs={{0,2},{1,3},{2,0},{3,1},{4,6},{5,7},{6,4},{7,5},{8,10},{9,11},{10,... | collective-permute-start | bytes 14155784 | tf_op jit(solution)/shard_map/ppermute | solution.py:213
  434.7 59.4 %collective-permute-start.62 = (bf16[1,192,384]{2,1,0:T(8,128)(2,1)}, bf16[1,192,384]{2,1,0:T(8,128)(2,1)}, u32[]{:S(2)}, u32[]{:S(2)}) collective-permute-start(bf16[1,192,384]{2,1,0:T(8,128)(2,1)} %slice.651), channel_id=1, source_target_pairs={{0,1},{1,0},{2,3},{3,2},{4,5},{5,4},{6,7},{7,6},{8,9},{9,8},{10,11... | collective-permute-start | bytes 442376 | tf_op jit(solution)/shard_map/ppermute | solution.py:213
  437.0 35.2 %collective-permute-start.44 = (bf16[4,96,768]{2,1,0:T(8,128)(2,1)}, bf16[4,96,768]{2,1,0:T(8,128)(2,1)}, u32[]{:S(2)}, u32[]{:S(2)}) collective-permute-start(bf16[4,96,768]{2,1,0:T(8,128)(2,1)} %add_convert_fusion.9), channel_id=1, source_target_pairs={{0,8},{1,9},{2,10},{3,11},{4,12},{5,13},{6,14},{7,15},{8,0},{9,1},... | collective-permute-start | bytes 1769480 | tf_op jit(solution)/shard_map/ppermute | solution.py:213
  438.1 34.1 %collective-permute-start.43 = (bf16[384,768]{1,0:T(8,128)(2,1)}, bf16[384,768]{1,0:T(8,128)(2,1)}, u32[]{:S(2)}, u32[]{:S(2)}) collective-permute-start(bf16[384,768]{1,0:T(8,128)(2,1)} %bitcast_convert_fusion), channel_id=1, source_target_pairs={{8,0},{9,1},{10,2},{11,3},{12,4},{13,5},{14,6},{15,7},{16,24},{17,... | collective-permute-start | bytes 1769480 | tf_op jit(solution)/shard_map/ppermute | solution.py:213
  493.3 23.4 %collective-permute-start.50 = (f32[1024,768]{1,0:T(8,128)}, f32[1024,768]{1,0:T(8,128)}, u32[]{:S(2)}, u32[]{:S(2)}) collective-permute-start(f32[1024,768]{1,0:T(8,128)} %fusion.136), channel_id=1, source_target_pairs={{0,16},{16,0},{1,17},{17,1},{2,18},{18,2},{3,19},{19,3},{4,20},{20... | collective-permute-start | bytes 9437192 | tf_op jit(solution)/shard_map/ppermute | solution.py:203
  502.8 35.8 %collective-permute-start.47 = (bf16[2,96,768]{2,1,0:T(8,128)(2,1)}, bf16[2,96,768]{2,1,0:T(8,128)(2,1)}, u32[]{:S(2)}, u32[]{:S(2)}) collective-permute-start(bf16[2,96,768]{2,1,0:T(8,128)(2,1)} %get-tuple-element.276), channel_id=1, source_target_pairs={{0,2},{1,3},{2,0},{3,1},{4,6},{5,7},{6,4},{7,5},{8,10},{9,11},{10,... | collective-permute-start | bytes 884744 | tf_op jit(solution)/shard_map/ppermute | solution.py:213
  505.7 32.9 %collective-permute-start.49 = (bf16[4,192,768]{2,1,0:T(8,128)(2,1)}, bf16[4,192,768]{2,1,0:T(8,128)(2,1)}, u32[]{:S(2)}, u32[]{:S(2)}) collective-permute-start(bf16[4,192,768]{2,1,0:T(8,128)(2,1)} %get-tuple-element.181), channel_id=1, source_target_pairs={{0,2},{1,3},{2,0},{3,1},{4,6},{5,7},{6,4},{7,5},{8,10},{9,11},{10,... | collective-permute-start | bytes 3538952 | tf_op jit(solution)/shard_map/ppermute | solution.py:213
  510.1 37.0 %collective-permute-start.48 = (bf16[4,96,3072]{2,1,0:T(8,128)(2,1)S(1)}, bf16[4,96,3072]{2,1,0:T(8,128)(2,1)}, u32[]{:S(2)}, u32[]{:S(2)}) collective-permute-start(bf16[4,96,3072]{2,1,0:T(8,128)(2,1)S(1)} %add_convert_fusion), channel_id=1, source_target_pairs={{0,1},{1,0},{2,3},{3,2},{4,5},{5,4},{6,7},{7,6},{8,9},{9,8},{10,11... | collective-permute-start | bytes 7077896 | tf_op jit(solution)/shard_map/ppermute | solution.py:213
  549.7 34.8 %collective-permute-start.51 = (bf16[2,96,768]{2,1,0:T(8,128)(2,1)}, bf16[2,96,768]{2,1,0:T(8,128)(2,1)}, u32[]{:S(2)}, u32[]{:S(2)}) collective-permute-start(bf16[2,96,768]{2,1,0:T(8,128)(2,1)} %get-tuple-element.275), channel_id=1, source_target_pairs={{0,1},{1,0},{2,3},{3,2},{4,5},{5,4},{6,7},{7,6},{8,9},{9,8},{10,11... | collective-permute-start | bytes 884744 | tf_op jit(solution)/shard_map/ppermute | solution.py:213
  553.0 31.4 %collective-permute-start.53 = (bf16[2,192,768]{2,1,0:T(8,128)(2,1)}, bf16[2,192,768]{2,1,0:T(8,128)(2,1)S(1)}, u32[]{:S(2)}, u32[]{:S(2)}) collective-permute-start(bf16[2,192,768]{2,1,0:T(8,128)(2,1)} %add_convert_fusion.6), channel_id=1, source_target_pairs={{0,4},{1,5},{2,6},{3,7},{4,0},{5,1},{6,2},{7,3},{8,12},{9,13},{10,... | collective-permute-start | bytes 1769480 | tf_op jit(solution)/shard_map/ppermute | solution.py:213
  553.2 40.4 %collective-permute-start.54 = (bf16[8,48,2688]{2,1,0:T(8,128)(2,1)S(1)}, bf16[8,48,2688]{2,1,0:T(8,128)(2,1)S(1)}, u32[]{:S(2)}, u32[]{:S(2)}) collective-permute-start(bf16[8,48,2688]{2,1,0:T(8,128)(2,1)S(1)} %copy-done.20), channel_id=1, source_target_pairs={{0,2},{1,3},{2,0},{3,1},{4,6},{5,7},{6,4},{7,5},{8,10},{9,11},{10,... | collective-permute-start | bytes 6193160 | tf_op jit(solution)/shard_map/ppermute | solution.py:213
  556.7 36.8 %collective-permute-start.52 = (bf16[2,96,3072]{2,1,0:T(8,128)(2,1)S(1)}, bf16[2,96,3072]{2,1,0:T(8,128)(2,1)S(1)}, u32[]{:S(2)}, u32[]{:S(2)}) collective-permute-start(bf16[2,96,3072]{2,1,0:T(8,128)(2,1)S(1)} %add_convert_fusion.1), channel_id=1, source_target_pairs={{0,4},{1,5},{2,6},{3,7},{4,0},{5,1},{6,2},{7,3},{8,12},{9,13},{10,... | collective-permute-start | bytes 3538952 | tf_op jit(solution)/shard_map/ppermute | solution.py:213
  611.2 18.5 %collective-permute-start.56 = (bf16[1,192,768]{2,1,0:T(8,128)(2,1)}, bf16[1,192,768]{2,1,0:T(8,128)(2,1)S(1)}, u32[]{:S(2)}, u32[]{:S(2)}) collective-permute-start(bf16[1,192,768]{2,1,0:T(8,128)(2,1)} %add_convert_fusion.12), channel_id=1, source_target_pairs={{0,1},{1,0},{2,3},{3,2},{4,5},{5,4},{6,7},{7,6},{8,9},{9,8},{10,11... | collective-permute-start | bytes 884744 | tf_op jit(solution)/shard_map/ppermute | solution.py:213
  613.9 28.8 %collective-permute-start.55 = (bf16[1,96,3072]{2,1,0:T(8,128)(2,1)}, bf16[1,96,3072]{2,1,0:T(8,128)(2,1)}, u32[]{:S(2)}, u32[]{:S(2)}) collective-permute-start(bf16[1,96,3072]{2,1,0:T(8,128)(2,1)} %add_convert_fusion.5), channel_id=1, source_target_pairs={{0,8},{1,9},{2,10},{3,11},{4,12},{5,13},{6,14},{7,15},{8,0},{9,1},... | collective-permute-start | bytes 1769480 | tf_op jit(solution)/shard_map/ppermute | solution.py:213
  615.2 27.6 %collective-permute-start.58 = (bf16[8,48,1152]{2,1,0:T(8,128)(2,1)}, bf16[8,48,1152]{2,1,0:T(8,128)(2,1)}, u32[]{:S(2)}, u32[]{:S(2)}) collective-permute-start(bf16[8,48,1152]{2,1,0:T(8,128)(2,1)} %get-tuple-element.199), channel_id=1, source_target_pairs={{0,2},{1,3},{2,0},{3,1},{4,6},{5,7},{6,4},{7,5},{8,10},{9,11},{10,... | collective-permute-start | bytes 2654216 | tf_op jit(solution)/shard_map/ppermute | solution.py:213
  616.9 25.8 %collective-permute-start.57 = (bf16[4,48,2688]{2,1,0:T(8,128)(2,1)}, bf16[4,48,2688]{2,1,0:T(8,128)(2,1)}, u32[]{:S(2)}, u32[]{:S(2)}) collective-permute-start(bf16[4,48,2688]{2,1,0:T(8,128)(2,1)} %add_convert_fusion.2), channel_id=1, source_target_pairs={{0,1},{1,0},{2,3},{3,2},{4,5},{5,4},{6,7},{7,6},{8,9},{9,8},{10,11... | collective-permute-start | bytes 3096584 | tf_op jit(solution)/shard_map/ppermute | solution.py:213
  643.9 11.2 %collective-permute-start.75 = (bf16[192,768]{1,0:T(8,128)(2,1)S(1)}, bf16[192,768]{1,0:T(8,128)(2,1)S(1)}, u32[]{:S(2)}, u32[]{:S(2)}) collective-permute-start(bf16[192,768]{1,0:T(8,128)(2,1)S(1)} %bitcast_convert_fusion.1), channel_id=1, source_target_pairs={{8,0},{9,1},{10,2},{11,3},{12,4},{13,5},{14,6},{15,7},{16,24},{17,... | collective-permute-start | bytes 884744 | tf_op jit(solution)/shard_map/ppermute | solution.py:213
  646.4 15.1 %collective-permute-start.64 = (bf16[4,48,1152]{2,1,0:T(8,128)(2,1)S(1)}, bf16[4,48,1152]{2,1,0:T(8,128)(2,1)S(1)}, u32[]{:S(2)}, u32[]{:S(2)}) collective-permute-start(bf16[4,48,1152]{2,1,0:T(8,128)(2,1)S(1)} %add_convert_fusion.11), channel_id=1, source_target_pairs={{0,1},{1,0},{2,3},{3,2},{4,5},{5,4},{6,7},{7,6},{8,9},{9,8},{10,11... | collective-permute-start | bytes 1327112 | tf_op jit(solution)/shard_map/ppermute | solution.py:213
  649.2 16.5 %collective-permute-start.63 = (bf16[2,48,2688]{2,1,0:T(8,128)(2,1)S(1)}, bf16[2,48,2688]{2,1,0:T(8,128)(2,1)S(1)}, u32[]{:S(2)}, u32[]{:S(2)}) collective-permute-start(bf16[2,48,2688]{2,1,0:T(8,128)(2,1)S(1)} %add_convert_fusion.10), channel_id=1, source_target_pairs={{0,4},{1,5},{2,6},{3,7},{4,0},{5,1},{6,2},{7,3},{8,12},{9,13},{10,... | collective-permute-start | bytes 1548296 | tf_op jit(solution)/shard_map/ppermute | solution.py:213
  653.2 18.4 %collective-permute-start.77 = (bf16[96,3072]{1,0:T(8,128)(2,1)S(1)}, bf16[96,3072]{1,0:T(8,128)(2,1)S(1)}, u32[]{:S(2)}, u32[]{:S(2)}) collective-permute-start(bf16[96,3072]{1,0:T(8,128)(2,1)S(1)} %fusion.44), channel_id=1, source_target_pairs={{0,16},{16,0},{1,17},{17,1},{2,18},{18,2},{3,19},{19,3},{4,20},{20... | collective-permute-start | bytes 1769480 | tf_op jit(solution)/shard_map/ppermute | solution.py:203
  657.0 29.4 %collective-permute-start.76 = (bf16[192,768]{1,0:T(8,128)(2,1)}, bf16[192,768]{1,0:T(8,128)(2,1)S(1)}, u32[]{:S(2)}, u32[]{:S(2)}) collective-permute-start(bf16[192,768]{1,0:T(8,128)(2,1)} %fusion.51), channel_id=1, source_target_pairs={{0,16},{16,0},{1,17},{17,1},{2,18},{18,2},{3,19},{19,3},{4,20},{20... | collective-permute-start | bytes 884744 | tf_op jit(solution)/shard_map/ppermute | solution.py:203
  666.5 12.0 %collective-permute-start.68 = (f32[4,1,288]{2,1,0:T(1,128)}, f32[4,1,288]{2,1,0:T(1,128)}, u32[]{:S(2)}, u32[]{:S(2)}) collective-permute-start(f32[4,1,288]{2,1,0:T(1,128)} %constant_dynamic-slice_fusion.7), channel_id=1, source_target_pairs={{0,4},{1,5},{2,6},{3,7},{4,0},{5,1},{6,2},{7,3},{8,12},{9,13},{10,... | collective-permute-start | bytes 13832 | tf_op jit(solution)/shard_map/ppermute | solution.py:213
  671.6 14.1 %collective-permute-start.66 = (bf16[1,48,2688]{2,1,0:T(8,128)(2,1)}, bf16[1,48,2688]{2,1,0:T(8,128)(2,1)}, u32[]{:S(2)}, u32[]{:S(2)}) collective-permute-start(bf16[1,48,2688]{2,1,0:T(8,128)(2,1)} %add_convert_fusion.14), channel_id=1, source_target_pairs={{0,8},{1,9},{2,10},{3,11},{4,12},{5,13},{6,14},{7,15},{8,0},{9,1},... | collective-permute-start | bytes 774152 | tf_op jit(solution)/shard_map/ppermute | solution.py:213
  693.9 12.5 %collective-permute-start.74 = (bf16[48,2688]{1,0:T(8,128)(2,1)S(1)}, bf16[48,2688]{1,0:T(8,128)(2,1)S(1)}, u32[]{:S(2)}, u32[]{:S(2)}) collective-permute-start(bf16[48,2688]{1,0:T(8,128)(2,1)S(1)} %fusion.78), channel_id=1, source_target_pairs={{0,16},{16,0},{1,17},{17,1},{2,18},{18,2},{3,19},{19,3},{4,20},{20... | collective-permute-start | bytes 774152 | tf_op jit(solution)/shard_map/ppermute | solution.py:203
  (215 other events, 2379.7 us)

commit v2 on v1

--- a/solution.py
+++ b/solution.py
@@ -13,8 +13,12 @@
 WINDOW = 1536
 EPSILON = 1e-06
 LANES = 128
+GELU_SCALE = (2.0 / np.pi) ** 0.5
+GELU_CUBE = 0.044715
 NEG = -1e30
 VMEM_LIMIT = 48 * 1024 * 1024
+FREE = pl.CostEstimate(flops=0, bytes_accessed=0, transcendentals=0)
+LONG = pl.CostEstimate(flops=10**11, bytes_accessed=0, transcendentals=0)
 F32 = jnp.float32
 BF16 = jnp.bfloat16
 
@@ -161,11 +165,7 @@
             jax.ShapeDtypeStruct((pairs, per, rows), F32),
         ],
         compiler_params=pltpu.CompilerParams(vmem_limit_bytes=VMEM_LIMIT),
-        cost_estimate=pl.CostEstimate(
-            flops=8 * rows * rows * width,
-            bytes_accessed=8 * rows * width,
-            transcendentals=rows * rows * width // head_dim,
-        ),
+        cost_estimate=FREE,
     )(projected, projected, projected, bias)
 
 
@@ -190,13 +190,9 @@
         out_shape=[shape, shape, shape],
         scratch_shapes=[pltpu.VMEM((rows, LANES), F32), pltpu.VMEM((rows, LANES), F32)],
         compiler_params=pltpu.CompilerParams(vmem_limit_bytes=VMEM_LIMIT),
-        cost_estimate=pl.CostEstimate(
-            flops=20 * rows * rows * width,
-            bytes_accessed=16 * rows * width,
-            transcendentals=rows * rows * width // head_dim,
-        ),
+        cost_estimate=LONG,
     )(projected, projected, projected, bias, lse, grad_mixture)
-    return jnp.concatenate(grads, axis=1)
+    return grads
 
 
 def swap(array):
@@ -204,13 +200,17 @@
 
 
 def exchange(array, bits, size, sends=None):
+    if sends == "flips":
+        return tuple(
+            lax.ppermute(part, "dp", [(i, i ^ flip) for i in range(size)]) for part, flip in zip(array, bits)
+        )
     pairs = [
         (core * size + i, core * size + (i ^ (1 << bit)))
         for core, bit in enumerate(bits)
         for i in range(size)
         if sends is None or sends(core, i)
     ]
-    return lax.ppermute(array, ("section", "dp"), pairs)
+    return jax.tree.map(lambda part: lax.ppermute(part, ("section", "dp"), pairs), array)
 
 
 def bit_count(size):
@@ -246,47 +246,97 @@
     return rows % 16 == 0 and all(c % LANES == 0 and r % 16 == 0 for r0, r1, c0, c1 in cuts for r, c in ((r0, c0), (r1, c1)))
 
 
-def assembly_kernel(half, cuts, table, low, high, *outs):
+def assembly_kernel(bounds, cuts, table, *refs):
     step = pl.program_id(0)
+    parts, outs = refs[: len(bounds)], refs[len(bounds) :]
 
     def store(ref):
         for (r0, r1, c0, c1), out in zip(cuts, outs):
             out[...] = ref[0, r0:r1, c0:c1]
 
-    pl.when(step < half)(lambda: store(low))
-    pl.when(step >= half)(lambda: store(high))
-
-
-def assembled(low, high, table, cuts):
-    half, rows, width = low.shape
-    shapes = [(2 * half * (r1 - r0), c1 - c0) for r0, r1, c0, c1 in cuts]
+    for (low, high), ref in zip(bounds, parts):
+        pl.when((step >= low) & (step < high))(functools.partial(store, ref))
+
+
+def assembled(parts, table, cuts, offset=0, width=None):
+    rows = parts[0].shape[1]
+    width = width or parts[0].shape[2]
+    ends = np.cumsum([part.shape[0] for part in parts])
+    count = int(ends[-1])
+    bounds = [(int(end) - part.shape[0], int(end)) for end, part in zip(ends, parts)]
+    shapes = [(count * (r1 - r0), c1 - c0) for r0, r1, c0, c1 in cuts]
     if not aligned(rows, cuts):
-        stack = jnp.concatenate([low, high], axis=0)[jnp.argsort(table)]
+        stack = jnp.concatenate(parts, axis=0)[jnp.argsort(table)][..., offset : offset + width]
         return [stack[:, r0:r1, c0:c1].reshape(s) for (r0, r1, c0, c1), s in zip(cuts, shapes)]
     return pl.pallas_call(
-        functools.partial(assembly_kernel, half, cuts),
+        functools.partial(assembly_kernel, bounds, cuts),
         grid_spec=pltpu.PrefetchScalarGridSpec(
             num_scalar_prefetch=1,
-            grid=(2 * half,),
+            grid=(count,),
             in_specs=[
-                pl.BlockSpec((1, rows, width), lambda j, t: (jnp.minimum(j, half - 1), 0, 0)),
-                pl.BlockSpec((1, rows, width), lambda j, t: (jnp.maximum(j - half, 0), 0, 0)),
+                pl.BlockSpec(
+                    (1, rows, width),
+                    lambda j, t, low=low, high=high: (jnp.clip(j, low, high - 1) - low, 0, offset // width),
+                )
+                for low, high in bounds
             ],
             out_specs=[pl.BlockSpec((r1 - r0, c1 - c0), lambda j, t: (t[j], 0)) for r0, r1, c0, c1 in cuts],
         ),
-        out_shape=[jax.ShapeDtypeStruct(s, low.dtype) for s in shapes],
+        out_shape=[jax.ShapeDtypeStruct(s, parts[0].dtype) for s in shapes],
         compiler_params=pltpu.CompilerParams(vmem_limit_bytes=VMEM_LIMIT),
-        cost_estimate=pl.CostEstimate(flops=0, bytes_accessed=8 * half * rows * width, transcendentals=0),
-    )(table, low, high)
-
-
-def split_kernel(half, table, *refs):
+        cost_estimate=FREE,
+    )(table, *parts)
+
+
+def quarters(parts):
+    if len(parts) == 4:
+        return [(part, 0) for part in parts]
+    return [(part, k) for part in parts for k in range(2)]
+
+
+def grouped_kernel(cuts, table, *refs):
+    step = pl.program_id(0)
+    for index, part in enumerate(refs[:4]):
+        place = table[step + index * pl.num_programs(0)] % 4
+        for (r0, r1, c0, c1), out in zip(cuts, refs[4:]):
+            rows = r1 - r0
+            out[pl.ds(pl.multiple_of(place * rows, 16), rows), :] = part[0, r0:r1, c0:c1]
+
+
+def assembled_fours(parts, table, cuts, width=None, cost=FREE):
+    rows = parts[0].shape[1]
+    width = width or parts[0].shape[2]
+    count = sum(part.shape[0] for part in parts)
+    shapes = [(count * (r1 - r0), c1 - c0) for r0, r1, c0, c1 in cuts]
+    if not aligned(rows, cuts):
+        stack = jnp.concatenate(parts, axis=0)[jnp.argsort(table)]
+        return [stack[:, r0:r1, c0:c1].reshape(s) for (r0, r1, c0, c1), s in zip(cuts, shapes)]
+    steps = count // 4
+    return pl.pallas_call(
+        functools.partial(grouped_kernel, cuts),
+        grid_spec=pltpu.PrefetchScalarGridSpec(
+            num_scalar_prefetch=1,
+            grid=(steps,),
+            in_specs=[
+                pl.BlockSpec((1, rows, width), lambda j, t, k=k: (k * steps + j, 0, 0)) for _, k in quarters(parts)
+            ],
+            out_specs=[
+                pl.BlockSpec((4 * (r1 - r0), c1 - c0), lambda j, t: (t[j] // 4, 0)) for r0, r1, c0, c1 in cuts
+            ],
+        ),
+        out_shape=[jax.ShapeDtypeStruct(s, parts[0].dtype) for s in shapes],
+        compiler_params=pltpu.CompilerParams(vmem_limit_bytes=VMEM_LIMIT),
+        cost_estimate=cost,
+    )(table, *[part for part, _ in quarters(parts)])
+
+
+def split_kernel(half, count, table, *refs):
     step = pl.program_id(0)
     send, keep = refs[-2:]
 
     def store(out):
         base = 0
-        for ref in refs[:-2]:
+        for ref in refs[:count]:
             width = ref.shape[1]
             out[0, :, base : base + width] = ref[...]
             base += width
@@ -295,31 +345,169 @@
     pl.when(step >= half)(lambda: store(keep))
 
 
-def split_stack(grads, table, count):
+def split_stack(grads, table, count, into=None):
     half, rows = count // 2, grads[0].shape[0] // count
     width = sum(grad.shape[1] for grad in grads)
     if not (aligned(rows) and all(grad.shape[1] % LANES == 0 for grad in grads)):
         stack = jnp.concatenate([grad.reshape(count, rows, grad.shape[1]) for grad in grads], axis=2)[table]
-        return stack[half:], stack[:half]
-    shape = jax.ShapeDtypeStruct((half, rows, width), BF16)
+        halves = [stack[half:], stack[:half]]
+        if into is not None:
+            halves = [jnp.concatenate([part, old[..., width:]], axis=2) for part, old in zip(halves, into)]
+        return halves
+    full = width if into is None else into[0].shape[2]
+    shape = jax.ShapeDtypeStruct((half, rows, full), BF16)
+    into = [] if into is None else list(into)
     return pl.pallas_call(
-        functools.partial(split_kernel, half),
+        functools.partial(split_kernel, half, len(grads)),
         grid_spec=pltpu.PrefetchScalarGridSpec(
             num_scalar_prefetch=1,
             grid=(count,),
             in_specs=[
                 pl.BlockSpec((rows, grad.shape[1]), lambda j, t: (t[jnp.where(j < half, j + half, j - half)], 0))
                 for grad in grads
-            ],
+            ]
+            + [pl.BlockSpec(memory_space=pl.ANY) for _ in into],
             out_specs=[
                 pl.BlockSpec((1, rows, width), lambda j, t: (jnp.minimum(j, half - 1), 0, 0)),
                 pl.BlockSpec((1, rows, width), lambda j, t: (jnp.maximum(j - half, 0), 0, 0)),
             ],
         ),
         out_shape=[shape, shape],
+        input_output_aliases={1 + len(grads) + k: k for k in range(len(into))},
         compiler_params=pltpu.CompilerParams(vmem_limit_bytes=VMEM_LIMIT),
-        cost_estimate=pl.CostEstimate(flops=0, bytes_accessed=4 * count * rows * width, transcendentals=0),
-    )(table, *grads)
+        cost_estimate=FREE,
+    )(table, *grads, *into)
+
+
+def write_rows(target, parts, table, rows):
+    index = 0
+    for part in parts:
+        for k in range(part.shape[0]):
+            target[pl.ds(pl.multiple_of(table[index] * rows, 16), rows), :] = part[k]
+            index += 1
+
+
+def product_kernel(rows, count, gelu, table, x_ref, *refs):
+    parts, outs, weight = refs[:count], refs[count:-1], refs[-1]
+    write_rows(weight, parts, table, rows)
+    result = jnp.dot(x_ref[...], weight[...], preferred_element_type=F32)
+    if not gelu:
+        outs[0][...] = result.astype(outs[0].dtype)
+        return
+    square = result * result
+    bend = jnp.tanh(GELU_SCALE * (result + GELU_CUBE * (result * square)))
+    outs[0][...] = (0.5 * result * (1.0 + bend)).astype(outs[0].dtype)
+    slope = 0.5 * (1.0 + bend)
+    slope += (0.5 * GELU_SCALE) * result * (1.0 - bend * bend) * (1.0 + (3.0 * GELU_CUBE) * square)
+    outs[1][...] = slope.astype(outs[1].dtype)
+
+
+def pullback_kernel(rows, count, bounds, table, places, x_ref, *refs):
+    parts, grads = refs[:count], refs[count : count + len(bounds)]
+    dx_ref, send, keep, weight, turned, total = refs[count + len(bounds) :]
+    step = pl.program_id(0)
+
+    @pl.when(step == 0)
+    def _():
+        turned[...] = x_ref[...].T
+        total[...] = jnp.zeros_like(total)
+
+    write_rows(weight, parts, table, rows)
+    grad = grads[-1][...]
+    for (low, high), ref in list(zip(bounds, grads))[:-1]:
+        grad = jnp.where((step >= low) & (step < high), ref[...], grad)
+    total[...] += lax.dot_general(grad, weight[...], (((1,), (1,)), ((), ())), preferred_element_type=F32)
+    weight[...] = jnp.dot(turned[...], grad, preferred_element_type=F32).astype(BF16)
+    half = keep.shape[0]
+    for index in range(2 * half):
+        block = weight[pl.ds(pl.multiple_of(places[index] * rows, 16), rows), :]
+        (keep if index < half else send)[index % half] = block
+
+    @pl.when(step == pl.num_programs(0) - 1)
+    def _():
+        dx_ref[...] = total[...].astype(BF16)
+
+
+TILE = 384
+
+
+class Weight:
+    def __init__(self, parts, table, offset, width):
+        self.parts, self.table, self.offset, self.width = parts, table, offset, width
+        self.rows = parts[0].shape[1]
+        self.count = sum(part.shape[0] for part in parts)
+        self.aligned = aligned(self.rows) and offset % TILE == 0 and width % TILE == 0
+
+    def whole(self):
+        cut = (0, self.rows, 0, self.width)
+        stack = jnp.concatenate(self.parts, axis=0)[jnp.argsort(self.table)]
+        return stack[..., self.offset : self.offset + self.width].reshape(-1, self.width)
+
+    def part_specs(self):
+        first = self.offset // TILE
+        return [
+            pl.BlockSpec((self.count // 4, self.rows, TILE), lambda i, *tables, k=k: (k, 0, first + i))
+            for _, k in quarters(self.parts)
+        ]
+
+    def product(self, x, gelu=False):
+        if not self.aligned:
+            result = mm(x, self.whole())
+            if not gelu:
+                return result.astype(BF16)
+            slope = jax.vjp(jax.nn.gelu, result)[1](jnp.ones_like(result))[0]
+            return jax.nn.gelu(result).astype(BF16), slope.astype(BF16)
+        tokens, depth = x.shape
+        outs = 2 if gelu else 1
+        shape = jax.ShapeDtypeStruct((tokens, self.width), BF16)
+        results = pl.pallas_call(
+            functools.partial(product_kernel, self.rows, 4, gelu),
+            grid_spec=pltpu.PrefetchScalarGridSpec(
+                num_scalar_prefetch=1,
+                grid=(self.width // TILE,),
+                in_specs=[pl.BlockSpec((tokens, depth), lambda i, t: (0, 0))] + self.part_specs(),
+                out_specs=[pl.BlockSpec((tokens, TILE), lambda i, t: (0, i))] * outs,
+                scratch_shapes=[pltpu.VMEM((depth, TILE), BF16)],
+            ),
+            out_shape=[shape] * outs,
+            compiler_params=pltpu.CompilerParams(vmem_limit_bytes=VMEM_LIMIT),
+            cost_estimate=LONG if gelu else FREE,
+        )(self.table, x, *[part for part, _ in quarters(self.parts)])
+        return results if gelu else results[0]
+
+    def pullback(self, x, grads, places, lead=0):
+        if not self.aligned:
+            grad = jnp.concatenate(grads, axis=1)
+            halves = split_stack([mm_tn(x, grad).astype(BF16)], places, self.count)
+            return mm_nt(grad, self.whole()).astype(BF16), [jnp.pad(h, ((0, 0), (0, 0), (lead, 0))) for h in halves]
+        tokens, depth = x.shape
+        ends = np.cumsum([grad.shape[1] // TILE for grad in grads])
+        bounds = [(int(end) - grad.shape[1] // TILE, int(end)) for end, grad in zip(ends, grads)]
+        half = jax.ShapeDtypeStruct((self.count // 2, self.rows, lead + self.width), BF16)
+        half_spec = pl.BlockSpec((self.count // 2, self.rows, TILE), lambda i, t, p: (0, 0, lead // TILE + i))
+        result = pl.pallas_call(
+            functools.partial(pullback_kernel, self.rows, 4, bounds),
+            grid_spec=pltpu.PrefetchScalarGridSpec(
+                num_scalar_prefetch=2,
+                grid=(self.width // TILE,),
+                in_specs=[pl.BlockSpec((tokens, depth), lambda i, t, p: (0, 0))]
+                + self.part_specs()
+                + [
+                    pl.BlockSpec((tokens, TILE), lambda i, t, p, low=low, high=high: (0, jnp.clip(i, low, high - 1) - low))
+                    for low, high in bounds
+                ],
+                out_specs=[pl.BlockSpec((tokens, depth), lambda i, t, p: (0, 0)), half_spec, half_spec],
+                scratch_shapes=[
+                    pltpu.VMEM((depth, TILE), BF16),
+                    pltpu.VMEM((depth, tokens), BF16),
+                    pltpu.VMEM((tokens, depth), F32),
+                ],
+            ),
+            out_shape=[jax.ShapeDtypeStruct((tokens, depth), BF16), half, half],
+            compiler_params=pltpu.CompilerParams(vmem_limit_bytes=VMEM_LIMIT),
+            cost_estimate=FREE,
+        )(self.table, places, x, *[part for part, _ in quarters(self.parts)], *grads)
+        return result[0], result[1:]
 
 
 class Stream:
@@ -351,7 +539,7 @@
         return self.value
 
 
-def advance(streams, tied):
+def advance(streams, tied, hold=()):
     for stream in streams:
         if stream.arriving is None and stream.pending is None and not stream.done:
             stream.begin()
@@ -367,7 +555,7 @@
         stream.arriving = None
         stream.begin(array)
     for stream in moving:
-        if not stream.done:
+        if not stream.done and stream not in hold:
             stream.launch()
     return tied
 
@@ -377,26 +565,29 @@
     return lambda core, i: (i >> top) == core
 
 
-def doubling(held, order_pair, first=0):
+def doubling(held, order_pair, first=0, twice=False):
+    parts = (held,)
     steps = list(zip(*order_pair))[first:]
-    for bits in steps[:-1]:
-        arrived = yield held, bits, None
-        held = jnp.concatenate([held, arrived], axis=0)
-    arrived = yield held, steps[-1], None
-    return held, arrived
-
-
-def gather_all(packed, order_pair, places, cuts):
-    low, high = yield from doubling(packed[None], order_pair)
-    return assembled(low, high, placement(order_pair, places), cuts)
-
-
-def gather_core(piece, order_pair, places, cuts, size):
+    for index, bits in enumerate(steps):
+        if len(parts) > 1 and not (twice and index == len(steps) - 1):
+            parts = (jnp.concatenate(parts, axis=0),)
+        arrived = yield lax.optimization_barrier(parts), bits, None
+        parts = parts + arrived
+    return parts
+
+
+def gather_all(packed, order_pair, twice):
+    return (yield from doubling(packed[None], order_pair, 0, twice))
+
+
+def gather_core(piece, order_pair, places):
+    size = lax.axis_size("dp")
     top = bit_count(size) - 1
     arrived = yield piece, (top, top), top_sends(size)
     mine = (lax.axis_index("dp") >> top) == lax.axis_index("section")
-    low, high = yield from doubling(jnp.where(mine, piece, arrived)[None], order_pair)
-    return assembled(low, high, placement(order_pair, places), cuts)
+    parts = yield from doubling(jnp.where(mine, piece, arrived)[None], order_pair)
+    table, cuts = placement(order_pair, places), [(0, piece.shape[0], 0, piece.shape[1])]
+    return assembled_fours(parts, table, cuts) if len(places) > 1 else assembled(parts, table, cuts)
 
 
 def own_bit(pair):
@@ -412,23 +603,19 @@
     held = jnp.stack([kept, arrived])
     kept = lax.dynamic_index_in_dim(held, b, 1, keepdims=False)
     arrived = yield lax.dynamic_index_in_dim(held, 1 - b, 1, keepdims=False), second, None
-    low, high = yield from doubling(jnp.concatenate([kept, arrived], axis=0), order_pair, 2)
-    return assembled(low, high, placement(order_pair, places), cuts)
+    parts = yield from doubling(jnp.concatenate([kept, arrived], axis=0), order_pair, 2)
+    return assembled(parts, placement(order_pair, places), cuts)
 
 
 def total_of(terms):
     return sum(term.astype(F32) for term in terms)
 
 
-def halving(grads, order_pair, places, last=0):
-    steps = list(zip(*order_pair))
-    count = 1 << len(steps)
-    outgoing, kept = split_stack([grad.astype(BF16) for grad in grads], placement(order_pair, places), count)
-    terms = [kept]
-    for bits in reversed(steps[last:]):
-        half = terms[0].shape[0]
+def halving(send, kept, order_pair, last=0):
+    terms, outgoing = [kept], send
+    for bits in reversed(list(zip(*order_pair))[last:]):
         if outgoing is None:
-            half //= 2
+            half = terms[0].shape[0] // 2
             outgoing = total_of([term[half:] for term in terms]).astype(BF16)
             terms = [term[:half] for term in terms]
         arrived = yield outgoing, bits, None
@@ -436,21 +623,23 @@
     return terms
 
 
-def scatter_all(grads, order_pair, places):
-    terms = yield from halving(grads, order_pair, places)
+def scatter_all(halves, order_pair):
+    terms = yield from halving(*halves, order_pair)
     return total_of(terms)[0].astype(BF16)
 
 
-def scatter_core(grads, order_pair, places, size):
-    terms = yield from halving(grads, order_pair, places)
+def scatter_core(grad, order_pair, places, size):
+    halves = split_stack([grad], placement(order_pair, places), 1 << len(places))
+    terms = yield from halving(*halves, order_pair)
     top = bit_count(size) - 1
     sends = top_sends(size)
     arrived = yield total_of(terms)[0].astype(BF16), (top, top), lambda core, i: not sends(core, i)
     return (total_of(terms)[0] + arrived.astype(F32)).astype(BF16)
 
 
-def scatter_square(grads, order_pair, places):
-    terms = yield from halving(grads, order_pair, places, 2)
+def scatter_square(grad, order_pair, places):
+    halves = split_stack([grad], placement(order_pair, places), 1 << len(places))
+    terms = yield from halving(*halves, order_pair, 2)
     held = total_of(terms).astype(BF16)
     first, second = list(zip(*order_pair))[:2]
     arrived = yield held[2:], second, None
@@ -461,13 +650,17 @@
 
 def scatter_small(vector, size):
     position = lax.axis_index("dp")
-    held = vector
-    for bit in reversed(range(bit_count(size))):
-        half = held.shape[0] // 2
-        own = (position >> bit) & 1
-        arrived = yield lax.dynamic_slice_in_dim(held, (1 - own) * half, half, 0), (bit, bit), None
-        held = lax.dynamic_slice_in_dim(held, own * half, half, 0) + arrived
-    return held[0, 0]
+    held = vector.reshape(size // 4, 4, vector.shape[2])
+    for count, low in ((4, 0), (size // 4, 2)):
+        own = (position >> low) & (count - 1)
+
+        def part(index):
+            return lax.dynamic_index_in_dim(held, index, 1 if low == 0 else 0, keepdims=False)
+
+        outgoing = tuple(part(own ^ other) for other in range(1, count))
+        arrived = yield outgoing, tuple(other << low for other in range(1, count)), "flips"
+        held = part(own) + sum(arrived)
+    return held
 
 
 def in_square(blocks):
@@ -479,18 +672,19 @@
 SQUARE = ((0, 1), (1, 0))
 
 
-def square_gather(rows, size):
+def gather_in_square(rows):
     held = rows[None]
     for bits in SQUARE:
-        held = jnp.concatenate([held, exchange(held, bits, size)], axis=0)
+        arrived = yield held, bits, None
+        held = jnp.concatenate([held, arrived], axis=0)
     return in_square(held)
 
 
-def square_scatter(blocks, size):
+def scatter_in_square(blocks):
     held = in_square(blocks)
     for bits in reversed(SQUARE):
         half = held.shape[0] // 2
-        arrived = exchange(held[half:].astype(BF16), bits, size)
+        arrived = yield held[half:].astype(BF16), bits, None
         held = held[:half] + arrived.astype(F32)
     return held[0]
 
@@ -542,16 +736,28 @@
         length = array.shape[axis] // 2
         return lax.dynamic_slice_in_dim(array, which * length, length, axis)
 
+    def slope_of(upward):
+        return jax.vjp(jax.nn.gelu, upward)[1](jnp.ones_like(upward))[0]
+
+    def summed_cores(part):
+        part = part.astype(BF16)
+        return part.astype(F32) + swap(part).astype(F32)
+
     def own_heads(weight):
-        rows, width = weight.shape
-        thirds = weight.reshape(rows, 3, 2, width // 6)
-        return lax.dynamic_index_in_dim(thirds, core, 2, keepdims=False).reshape(rows, width // 2)
-
-    def gain_block(one, two):
-        return jnp.pad(jnp.stack([one, two], axis=1), ((0, 0), (0, LANES - 2)))
+        return jnp.concatenate([half_of(third, core) for third in jnp.split(weight, 3, axis=1)], axis=1)
+
+    def square_columns(weight):
+        pieces = jnp.split(weight, size // 2, axis=1)
+        return [jnp.concatenate(pieces[k::4], axis=1) for k in range(4)]
+
+    def gain_block():
+        columns = [gain.reshape(rows_l, -1) for gain in (gain_l1, gain_l2, gain_g1, gain_g2)]
+        block = jnp.concatenate(columns, axis=1)
+        return jnp.pad(block, ((0, 0), (0, TILE - block.shape[1])))
 
     top_first = [(bits - 1,) + o for o in orders(size, (None, -1, -2))]
     mixed = orders(size, (-1, None, -2))
+    lows_last = orders(size, (None, -1, -2))
     plane = [o[:2] + (bits - 1,) + o[2:] for o in orders(size, (-1, -2, None))]
     line = orders(size, (None,))
     below, beyond = tuple(range(bits - 1)), tuple(range(2, bits - 1))
@@ -559,48 +765,32 @@
     fresh = functools.partial(Stream, size)
     up_width, qkv_width = up_l.shape[1] // 2, 3 * half_g
     square_units = units_g * (size // 8)
-    stream_qkv_l = fresh(
+    table = placement(top_first, every)
+    between = [
+        (bits - 1,) + orders(size, middle)[which] for which, middle in enumerate(((None, -1, -2), (-1, None, -2)))
+    ]
+    places_g = placement(between, every)
+    side_l = half_l + half_g
+    stream_l = fresh(
         gather_all(
-            jnp.concatenate([own_heads(qkv_l), gain_block(gain_l1, gain_l2)], axis=1),
+            jnp.concatenate(
+                [half_of(out_l, core), half_of(patch_proj, core), gain_block(), own_heads(qkv_l), half_of(up_l, core)],
+                axis=1,
+            ),
             top_first,
-            every,
-            [(0, rows_l, 0, 3 * half_l), (0, rows_l, 3 * half_l, 3 * half_l + LANES)],
+            True,
         )
     )
-    stream_up_l = fresh(
-        gather_all(
-            jnp.concatenate([half_of(up_l, core), half_of(out_l, core), half_of(patch_proj, core)], axis=1),
-            top_first,
-            every,
-            [
-                (0, rows_l, 0, up_width),
-                (0, rows_l, up_width, up_width + half_l),
-                (0, rows_l, up_width + half_l, up_width + half_l + half_g),
-            ],
-        )
-    )
-    stream_down_l = fresh(gather_core(down_l, mixed, below, [(0, units_l, 0, width_l)], size))
-    stream_qkv_g = fresh(
-        gather_all(
-            jnp.concatenate([own_heads(qkv_g), half_of(out_g, core), gain_block(gain_g1, gain_g2)], axis=1),
-            top_first,
-            every,
-            [
-                (0, rows_g, 0, qkv_width),
-                (0, rows_g, qkv_width, qkv_width + half_g),
-                (0, rows_g, qkv_width + half_g, qkv_width + half_g + LANES),
-            ],
-        )
-    )
-    blocks = half_of(up_g, core).reshape(rows_g, size // 8, 2, 2, units_g)
-    blocks = jnp.where(is_first, blocks.transpose(3, 2, 0, 1, 4), blocks.transpose(2, 3, 0, 1, 4))
-    stream_up_g = fresh(
-        gather_square(
-            blocks.reshape(2, 2, rows_g, square_units), plane, every, [(0, rows_g, 0, square_units)]
-        )
-    )
+    stream_down_l = fresh(gather_core(down_l, lows_last, below))
+    stream_g = fresh(gather_all(own_heads(qkv_g), top_first, False))
+    stream_out_g = fresh(gather_all(half_of(out_g, core), top_first, False))
+    square = square_columns(half_of(up_g, core))
+    one_two = jnp.where(is_first, square[2], square[1])
+    two_one = jnp.where(is_first, square[1], square[2])
+    blocks = jnp.stack([square[0], one_two, two_one, square[3]]).reshape(2, 2, rows_g, square_units)
+    stream_up_g = fresh(gather_square(blocks, plane, every, [(0, rows_g, 0, square_units)]))
     stream_down_g = fresh(
-        gather_core(down_g[:, :width_l], line, beyond, [(0, units_g, 0, width_l)], size)
+        gather_core(down_g[:, :width_l], line, beyond)
     )
 
     bias_l = jnp.where(jnp.arange(seq_rows) < lengths[0], 0.0, NEG).astype(F32)[:, None]
@@ -611,35 +801,51 @@
     picks_live = (picks & live[:, None]).astype(BF16)
     picks = picks.astype(BF16)
 
-    advance([stream_qkv_l, stream_up_g], ())
+    advance([stream_l], ())
     seq_inputs = shared(bytes_in[0])
     inputs = seq_inputs.astype(F32)
     scale_l1 = row_scale(inputs)
-    scale_l1 = advance([stream_qkv_l, stream_up_l, stream_up_g], scale_l1)
     seq_grads = shared(out_grad[0])
     grad_top_b = mm(picks_live, seq_grads).astype(BF16)
-    grad_top_b = advance([stream_qkv_l, stream_up_l, stream_down_l, stream_up_g], grad_top_b)
-    square_top = square_gather(half_of(grad_top_b, core), size).reshape(4 * slots, half_l)
-    square_top = shared(square_top)
-    square_top = advance([stream_qkv_l, stream_up_l, stream_down_l, stream_qkv_g], square_top)
-
-    advance([stream_qkv_l, stream_up_l, stream_down_l, stream_qkv_g], ())
-    qkv_wl, gains_l = stream_qkv_l.result()
-    gain_one_l, gain_two_l = gains_l[:, 0].astype(F32), gains_l[:, 1].astype(F32)
+    scale_l1 = advance([stream_l, stream_up_g, stream_down_l, stream_g], scale_l1)
+    stream_top = fresh(gather_in_square(half_of(grad_top_b, core)))
+    grad_top_b = advance([stream_l, stream_up_g, stream_down_l, stream_top], grad_top_b)
+    advance([stream_l, stream_g, stream_top, stream_out_g], ())
+
+    advance([stream_l, stream_g, stream_down_l, stream_up_g, stream_down_g, stream_top, stream_out_g], ())
+    parts = stream_l.result()
+    front = side_l + TILE
+    out_wl, proj_w, gains = assembled_fours(
+        parts,
+        table,
+        [(0, rows_l, 0, half_l), (0, rows_l, half_l, side_l), (0, rows_l, side_l, side_l + LANES)],
+        front,
+        LONG,
+    )
+    qkv_wl = Weight(parts, table, front, 3 * half_l)
+    up_wl = Weight(parts, table, front + 3 * half_l, up_width)
+    gain_one_l, gain_two_l = gains[:, 0].astype(F32), gains[:, 1].astype(F32)
+    per = width_g // width_l
+    gain_one_g, gain_two_g = (
+        gains[:, low : low + per].reshape(width_g).astype(F32) for low in (2, 2 + per)
+    )
     normed_l = (inputs * scale_l1 * gain_one_l).astype(BF16)
-    projected_l = mm(normed_l, qkv_wl).astype(BF16)
+    projected_l = qkv_wl.product(normed_l)
     mixture_l, lse_l = attention_forward(projected_l, bias_l, head_l)
-    mixture_l = shared(mixture_l)
-    mixture_l = advance([stream_up_l, stream_down_l, stream_qkv_g], mixture_l)
-    up_wl, out_wl, proj_w = stream_up_l.result()
-    out_wl, proj_w = shared(out_wl), shared(proj_w)
+    mixture_l, out_wl, proj_w = advance(
+        [stream_down_l, stream_up_g, stream_down_g, stream_out_g], (mixture_l, out_wl, proj_w), [stream_up_g]
+    )
+    mixture_l = advance([stream_g], mixture_l)
+    mixture_l, out_wl = shared(mixture_l), shared(out_wl)
     out_own_l = half_of(out_wl, core, 0)
     hidden_l = inputs + mm(mixture_l, out_wl)
     scale_l2 = row_scale(hidden_l)
     normed_l2 = (hidden_l * scale_l2 * gain_two_l).astype(BF16)
-    upward_l = mm(normed_l2, up_wl)
-    activated_l = jax.nn.gelu(upward_l).astype(BF16)
-    activated_l = advance([stream_down_l, stream_qkv_g, stream_up_g, stream_down_g], activated_l)
+    activated_l, slope_l = up_wl.product(normed_l2, gelu=True)
+    activated_l, proj_w = advance(
+        [stream_down_l, stream_down_g, stream_out_g, stream_up_g], (activated_l, proj_w), [stream_out_g]
+    )
+    proj_w = shared(proj_w)
     (down_wl,) = stream_down_l.result()
     partial_l = mm(activated_l, down_wl)
     local_out = half_of(hidden_l, core) + half_of(partial_l, core) + swap(half_of(partial_l, 1 - core))
@@ -647,52 +853,55 @@
     boundary = shared(mm(picks, local_out.astype(BF16)).astype(BF16))
     start_rows = mm(boundary, proj_w)
     scale_g1 = row_scale(start_rows)
-    scale_g1 = advance([stream_qkv_g, stream_up_g, stream_down_g], scale_g1)
-    qkv_wg, out_wg, gains_g = stream_qkv_g.result()
-    gain_one_g, gain_two_g = gains_g[:, 0].astype(F32), gains_g[:, 1].astype(F32)
+    square_top = shared(stream_top.result().reshape(4 * slots, half_l))
+    scale_g1, square_top = advance([stream_g, stream_out_g, stream_up_g], (scale_g1, square_top))
+    qkv_wg = Weight(stream_g.result(), table, 0, qkv_width)
     normed_g = (start_rows * scale_g1 * gain_one_g).astype(BF16)
+    projected_g = qkv_wg.product(normed_g)
+    mixture_g, lse_g = attention_forward(projected_g, bias_g, head_g)
+    mixture_g = advance([stream_out_g], mixture_g)
+    (out_wg,) = assembled_fours(stream_out_g.result(), table, [(0, rows_g, 0, half_g)])
     out_theirs_g = swap(out_wg)
-    projected_g = mm(normed_g, qkv_wg).astype(BF16)
-    mixture_g, lse_g = attention_forward(projected_g, bias_g, head_g)
     mixture_g = shared(mixture_g)
     hidden_g = start_rows + joined(mm(mixture_g, out_wg), mm(mixture_g, out_theirs_g))
     scale_g2 = row_scale(hidden_g)
     normed_g2 = (hidden_g * scale_g2 * gain_two_g).astype(BF16)
-    square_normed = square_gather(half_of(normed_g2, core), size).reshape(4 * slots, half_g)
-    square_normed = shared(square_normed)
-    square_normed = advance([stream_up_g, stream_down_g], square_normed)
+    square_normed = fresh(gather_in_square(half_of(normed_g2, core))).result()
+    square_normed = shared(square_normed.reshape(4 * slots, half_g))
     (up_wg,) = stream_up_g.result()
     (down_wg,) = stream_down_g.result()
     upward_g = mm(square_normed, up_wg)
     activated_g = jax.nn.gelu(upward_g).astype(BF16)
 
-    def scattered(grads, order_pair, places):
-        return fresh(scatter_all(grads, order_pair, places))
-
     grad_down_g = mm_tn(activated_g, square_top).astype(BF16)
-    stream_down_g = fresh(scatter_core([grad_down_g], line, beyond, size))
+    stream_down_g = fresh(scatter_core(grad_down_g, line, beyond, size))
     grad_act_g = mm_nt(square_top, down_wg)
     grad_up_g_rows = jax.vjp(jax.nn.gelu, upward_g)[1](grad_act_g)[0].astype(BF16)
     grad_up_g = mm_tn(square_normed, grad_up_g_rows).astype(BF16)
-    stream_up_g = fresh(scatter_square([grad_up_g], plane, every))
+    stream_up_g = fresh(scatter_square(grad_up_g, plane, every))
     part = mm_nt(grad_up_g_rows, up_wg)
     part = half_of(part, core) + swap(half_of(part, 1 - core).astype(BF16)).astype(F32)
     part = advance([stream_down_g, stream_up_g], part)
-    part = shared(square_scatter(part.reshape(4, slots, half_g), size))
+    part = shared(fresh(scatter_in_square(part.reshape(4, slots, half_g))).result())
     pulled, grad_gain_g2 = norm_backward(part, hidden_g, scale_g2, gain_two_g)
     grad_hidden_g = jnp.pad(grad_top_b.astype(F32), ((0, 0), (0, width_g - width_l))) + pulled
     grad_hidden_gb = grad_hidden_g.astype(BF16)
     mine_gb, theirs_gb = half_of(grad_hidden_gb, core), half_of(grad_hidden_gb, 1 - core)
     grad_out_g = mm_tn(mixture_g, mine_gb).astype(BF16)
+    stream_out_g = fresh(scatter_all(split_stack([grad_out_g], table, size), top_first))
     grad_mixture_g = (
         mm_nt(mine_gb, half_of(out_wg, core, 0)) + mm_nt(theirs_gb, half_of(out_theirs_g, core, 0))
     ).astype(BF16)
+    partial_g = mm(activated_g, down_wg)
+    partial_g = half_of(partial_g, core) + swap(half_of(partial_g, 1 - core).astype(BF16)).astype(F32)
+    stream_out = fresh(scatter_in_square(partial_g.reshape(4, slots, half_l)))
+    grad_mixture_g = advance([stream_down_g, stream_out_g, stream_out], grad_mixture_g)
     grad_projected_g = attention_backward(projected_g, bias_g, lse_g, grad_mixture_g, head_g)
-    grad_qkv_g = mm_tn(normed_g, grad_projected_g).astype(BF16)
-    stream_qkv_g = scattered([grad_qkv_g, grad_out_g], top_first, every)
-    grad_projected_g = advance([stream_down_g, stream_up_g, stream_qkv_g], grad_projected_g)
-    part = mm_nt(grad_projected_g, qkv_wg)
-    pulled, grad_gain_g1 = norm_backward(part + swap(part), start_rows, scale_g1, gain_one_g)
+    part, halves = qkv_wg.pullback(normed_g, grad_projected_g, places_g)
+    stream_g = fresh(scatter_all(halves, between))
+    part = advance([stream_g, stream_out, stream_out_g, stream_up_g], part)
+    part = summed_cores(part)
+    pulled, grad_gain_g1 = norm_backward(part, start_rows, scale_g1, gain_one_g)
     grad_start = (grad_hidden_g + pulled).astype(BF16)
     grad_proj = mm_tn(boundary, half_of(grad_start, core)).astype(BF16)
 
@@ -700,27 +909,26 @@
     grad_local = seq_grads.astype(F32) + mm_tn(picks, grad_rows)
     grad_local_b = grad_local.astype(BF16)
     grad_down_l = mm_tn(activated_l, grad_local_b).astype(BF16)
-    stream_down_l = fresh(scatter_core([grad_down_l], mixed, below, size))
+    stream_down_l = fresh(scatter_core(grad_down_l, mixed, below, size))
     grad_act_l = mm_nt(grad_local_b, down_wl)
-    grad_up_l_rows = jax.vjp(jax.nn.gelu, upward_l)[1](grad_act_l)[0].astype(BF16)
-    grad_up_l_rows = advance([stream_down_g, stream_up_g, stream_qkv_g, stream_down_l], grad_up_l_rows)
-    grad_up_l = mm_tn(normed_l2, grad_up_l_rows).astype(BF16)
-    part = mm_nt(grad_up_l_rows, up_wl)
-    pulled, grad_gain_l2 = norm_backward(part + swap(part), hidden_l, scale_l2, gain_two_l)
+    grad_up_l_rows = (slope_l.astype(F32) * grad_act_l).astype(BF16)
+    part, up_halves = up_wl.pullback(normed_l2, [grad_up_l_rows], table, side_l)
+    part, up_halves = advance([stream_down_g, stream_up_g, stream_g, stream_out_g], (part, up_halves))
+    part = summed_cores(part)
+    pulled, grad_gain_l2 = norm_backward(part, hidden_l, scale_l2, gain_two_l)
     grad_hidden_l = grad_local + pulled
     grad_hidden_lb = grad_hidden_l.astype(BF16)
     grad_out_l = mm_tn(mixture_l, half_of(grad_hidden_lb, core)).astype(BF16)
-    stream_up_l = scattered([grad_up_l, grad_out_l, grad_proj], top_first, every)
+    stream_up_l = fresh(scatter_all(split_stack([grad_out_l, grad_proj], table, size, up_halves), top_first))
     grad_mixture_l = mm_nt(grad_hidden_lb, out_own_l).astype(BF16)
-    grad_mixture_l = advance([stream_up_g, stream_qkv_g, stream_down_l, stream_up_l], grad_mixture_l)
+    grad_mixture_l = advance([stream_g, stream_down_l, stream_up_l], grad_mixture_l)
     grad_projected_l = attention_backward(projected_l, bias_l, lse_l, grad_mixture_l, head_l)
-    grad_qkv_l = mm_tn(normed_l, grad_projected_l).astype(BF16)
-    stream_qkv_l = scattered([grad_qkv_l], top_first, every)
-    grad_projected_l = advance(
-        [stream_up_g, stream_qkv_g, stream_down_l, stream_up_l, stream_qkv_l], grad_projected_l
-    )
-    part = mm_nt(grad_projected_l, qkv_wl)
-    pulled, grad_gain_l1 = norm_backward(part + swap(part), inputs, scale_l1, gain_one_l)
+    grad_projected_l = advance([stream_g, stream_out_g, stream_up_g], grad_projected_l)
+    part, halves = qkv_wl.pullback(normed_l, grad_projected_l, table)
+    stream_qkv_l = fresh(scatter_all(halves, top_first))
+    part = advance([stream_up_l, stream_down_l, stream_qkv_l], part)
+    part = summed_cores(part)
+    pulled, grad_gain_l1 = norm_backward(part, inputs, scale_l1, gain_one_l)
     input_grad = half_of(grad_hidden_l + pulled, core).astype(BF16)[None]
     gains = jnp.concatenate(
         [
@@ -729,25 +937,24 @@
         ],
         axis=2,
     )
+    returned = half_of(hidden_g[:, :width_l], core) + stream_out.result()
+    hidden_out = (local_out + mm_tn(picks_live, returned.astype(BF16))).astype(BF16)[None]
+    input_grad, gains = advance(
+        [stream_qkv_l, stream_up_l, stream_down_l, stream_up_g, stream_out_g, stream_g], (input_grad, gains)
+    )
     stream_gains = fresh(scatter_small(gains, size))
-
-    partial_g = mm(activated_g, down_wg)
-    partial_g = half_of(partial_g, core) + swap(half_of(partial_g, 1 - core).astype(BF16)).astype(F32)
-    returned = half_of(hidden_g[:, :width_l], core) + square_scatter(partial_g.reshape(4, slots, half_l), size)
-    hidden_out = (local_out + mm_tn(picks_live, returned.astype(BF16))).astype(BF16)[None]
-    input_grad, hidden_out = advance(
-        [stream_qkv_g, stream_down_l, stream_up_l, stream_qkv_l, stream_gains], (input_grad, hidden_out)
-    )
-    advance([stream_up_l, stream_qkv_l, stream_gains], ())
-    advance([stream_up_l, stream_qkv_l, stream_gains], ())
+    advance([stream_qkv_l, stream_gains], ())
+    advance([stream_up_l, stream_down_l, stream_gains], ())
+    advance([stream_qkv_l, stream_gains], ())
+    advance([stream_up_l, stream_qkv_l, stream_down_l], ())
 
     def joined_columns(mine, theirs):
         return joined(mine, theirs).astype(F32)
 
     def joined_heads(mine, theirs):
-        rows, width = mine.shape
-        thirds = [part.reshape(rows, 3, width // 3) for part in (mine, theirs)]
-        return joined(*thirds, axis=2).reshape(rows, 2 * width).astype(F32)
+        low, high = jnp.where(is_first, mine, theirs), jnp.where(is_first, theirs, mine)
+        thirds = [jnp.split(part, 3, axis=1) for part in (low, high)]
+        return jnp.concatenate([part for pair in zip(*thirds) for part in pair], axis=1).astype(F32)
 
     def from_owner(mine, theirs):
         return jnp.where((position >> (bits - 1)) == core, mine, theirs).astype(F32)
@@ -761,24 +968,24 @@
                 dx, dy = x ^ low[0], y ^ low[1]
                 index = jnp.where(is_first, 2 * dx + dy, 2 * dy + dx)
                 placed.append(lax.dynamic_index_in_dim(blocks.reshape(4, rows, width), index, 0, keepdims=False))
-        stack = jnp.stack(placed).reshape(4, rows, size // 8, units_g)
-        return stack.transpose(1, 2, 0, 3).reshape(rows, 4 * width)
+        pieces = [jnp.split(part, size // 8, axis=1) for part in placed]
+        return jnp.concatenate([piece for group in zip(*pieces) for piece in group], axis=1)
 
     down_g_mine = stream_down_g.result()
     total_down_g = from_owner(down_g_mine, swap(down_g_mine))
     total_down_g = jnp.pad(total_down_g, ((0, 0), (0, width_g - width_l)))
     up_g_mine = in_order(stream_up_g.result())
     total_up_g = joined_columns(up_g_mine, swap(up_g_mine))
-    g_mine = stream_qkv_g.result()
-    g_theirs = swap(g_mine)
-    total_qkv_g = joined_heads(g_mine[:, :qkv_width], g_theirs[:, :qkv_width])
-    total_out_g = joined_columns(g_mine[:, qkv_width:], g_theirs[:, qkv_width:])
+    g_mine = stream_g.result()
+    total_qkv_g = joined_heads(g_mine, swap(g_mine))
+    out_g_mine = stream_out_g.result()
+    total_out_g = joined_columns(out_g_mine, swap(out_g_mine))
     down_l_mine = stream_down_l.result()
     total_down_l = from_owner(down_l_mine, swap(down_l_mine))
     l_mine = stream_up_l.result()
     l_theirs = swap(l_mine)
-    cuts = [0, up_width, up_width + half_l, up_width + half_l + half_g]
-    total_up_l, total_out_l, total_proj = (
+    cuts = [0, half_l, side_l, side_l + up_width]
+    total_out_l, total_proj, total_up_l = (
         joined_columns(l_mine[:, low:high], l_theirs[:, low:high]) for low, high in zip(cuts, cuts[1:])
     )
     q_mine = stream_qkv_l.result()

time: 721 us -> 629 us (0.87)
  waiting for transfers between devices: 256 us -> 167 us
  matrix products: 95.6 us -> 55.9 us
  starting transfers between devices: 82.4 us -> 114 us
  Pallas kernels: 104 us -> 117 us
    ppermute x56 -> x63, waiting for transfers between devices: 251 us -> 160 us  [the longest x57 160 us: exchange(): lax.ppermute(part, ('section', 'dp'), pairs)]
    ppermute x56 -> x63, starting transfers between devices: 48.9 us -> 79 us  [the longest x57 72.7 us: exchange(): lax.ppermute(part, ('section', 'dp'), pairs)]
    dot_general x9 -> x6, matrix products: 38.3 us -> 15.7 us  [mm_nt(): lax.dot_general(left, right, (((1,), (1,)), ((), ())), preferred_element_...]
    pallas_call x12 -> x16, Pallas kernels: 64 us -> 76.6 us  [the longest x3 33.7 us: pullback(): pl.pallas_call(functools.partial(pullback_kernel, self.rows, 4, bounds),...]
    dot_general x12 -> x9, matrix products: 27 us -> 16.9 us  [mm(): return jnp.dot(left, right, preferred_element_type=F32)]
    unnamed x374 -> x410, local copies, waits for them, and re-layouts: 17.7 us -> 25.3 us
    convert_element_type x4 -> x7, other arithmetic: 1.32 us -> 8.73 us  [the longest x1 2.37 us: local(): normed_l2 = (hidden_l * scale_l2 * gain_two_l).astype(BF16)]
    reshape x8 -> x5, local copies, waits for them, and re-layouts: 11.8 us -> 4.53 us  [the longest x4 3.18 us: gain_block(): gain.reshape(rows_l, -1)]
  transfers between devices with their start and end apart: 80 -> 88, of which waited for: 35 -> 29; matrix products, arithmetic and copies ran while one was open for 26% -> 26% of each run, Pallas kernels for 13% -> 18%
where the time goes in v2:
time: 629 us; the launch traced here: 622 us
  waiting for transfers between devices  167 us (27%)
  Pallas kernels  117 us (19%)
  other arithmetic  116 us (18%)
  starting transfers between devices  114 us (18%)
  matrix products  55.9 us (9%)
  local copies, waits for them, and re-layouts  47 us (7%)
    ppermute x57, waiting for transfers between devices, exchange(): lax.ppermute(part, ('section', 'dp'), pairs)  160 us
    ppermute x57, starting transfers between devices, exchange(): lax.ppermute(part, ('section', 'dp'), pairs)  72.7 us
    pallas_call x3, Pallas kernels, pullback(): pl.pallas_call(functools.partial(pullback_kernel, self.rows, 4, bounds),...  33.7 us
    ppermute x24, starting transfers between devices, swap(): return lax.ppermute(array, 'section', [(0, 1), (1, 0)])  33.6 us
    convert_element_type x15, other arithmetic, halving(): outgoing = total_of([term[half:] for term in terms]).astype(BF16)  26.2 us
    unnamed x410, local copies, waits for them, and re-layouts  25.3 us
    dot_general x8, matrix products, mm_tn(): lax.dot_general(left, right, (((0,), (0,)), ((), ())), preferred_element_...  23.2 us
    pallas_call x2, Pallas kernels, attention_backward(): pl.pallas_call(functools.partial(attention_backward_kernel, rows, head_di...  22.9 us
  transfers between devices with their start and end apart: 88, of which 29 were waited for; matrix products, arithmetic and copies ran while one was open for 26% of the time, Pallas kernels for 18%

profile of v2, /device:TPU:1, one launch (start us, length us, event | category | flops | bytes accessed | tf_op | source)
XLA Modules:
  0.0 621.8 jit_solution(9676073154703182449)
XLA Ops:
  7.6 3.2 collective-permute-start.1
  17.5 11.2 %collective-permute-done.1 = bf16[1,48,4224]{2,1,0:T(8,128)(2,1)S(1)} collective-permute-done((bf16[1,48,4224]{2,1,0:T(8,128)(2,1)S(1)}, bf16[1,48,4224]{2,1,0:T(8,128)(2,1)S(1)}, u32[]{:S(2)}, u32[]{:S(2)}) %collective-permute-start.1) | collective-permute-done | bytes 405536 | tf_op jit(solution)/shard_map/ppermute | solution.py:213
  37.1 4.0 collective-permute-done.4
  41.8 9.5 %collective-permute-done.2 = bf16[2,48,4224]{2,1,0:T(8,128)(2,1)S(1)} collective-permute-done((bf16[2,48,4224]{2,1,0:T(8,128)(2,1)}, bf16[2,48,4224]{2,1,0:T(8,128)(2,1)S(1)}, u32[]{:S(2)}, u32[]{:S(2)}) %collective-permute-start.2) | collective-permute-done | bytes 811040 | tf_op jit(solution)/shard_map/ppermute | solution.py:213
  52.3 3.5 collective-permute-start.7
  56.7 16.8 %collective-permute-done.7 = bf16[1,96,2304]{2,1,0:T(8,128)(2,1)S(1)} collective-permute-done((bf16[1,96,2304]{2,1,0:T(8,128)(2,1)S(1)}, bf16[1,96,2304]{2,1,0:T(8,128)(2,1)S(1)}, u32[]{:S(2)}, u32[]{:S(2)}) %collective-permute-start.7) | collective-permute-done | bytes 442400 | tf_op jit(solution)/shard_map/ppermute | solution.py:213
  78.8 3.3 collective-permute-start.11
  86.7 21.1 %collective-permute-done.12 = bf16[1,192,768]{2,1,0:T(8,128)(2,1)S(1)} collective-permute-done((bf16[1,192,768]{2,1,0:T(8,128)(2,1)S(1)}, bf16[1,192,768]{2,1,0:T(8,128)(2,1)S(1)}, u32[]{:S(2)}, u32[]{:S(2)}) %collective-permute-start.12) | collective-permute-done | bytes 294944 | tf_op jit(solution)/shard_map/ppermute | solution.py:213
  108.4 7.3 %collective-permute-done.13 = bf16[2,96,768]{2,1,0:T(8,128)(2,1)S(1)} collective-permute-done((bf16[2,96,768]{2,1,0:T(8,128)(2,1)S(1)}, bf16[2,96,768]{2,1,0:T(8,128)(2,1)S(1)}, u32[]{:S(2)}, u32[]{:S(2)}) %collective-permute-start.13) | collective-permute-done | bytes 294944 | tf_op jit(solution)/shard_map/ppermute | solution.py:213
  128.3 4.5 collective-permute-start.20
  140.9 5.8 shard_map.434.q_ref.k_ref.v_ref
  149.5 12.8 %shard_map.435 = (bf16[1024,384]{1,0:T(8,128)(2,1)S(1)}, f32[3,2,1024]{2,1,0:T(2,128)S(1)}) custom-call(bf16[1024,1152]{1,0:T(8,128)(2,1)S(1)} %copy-done.3, bf16[1024,1152]{1,0:T(8,128)(2,1)S(1)} %copy-done.3, bf16[1024,1152]{1,0:T(8,128)(2,1)S(1)} %copy-done.3, f32[1024,1]{1,0:T(8,128)S(1)} %fusion.45.bias_ref), custom_call_target="tpu_custom_call" | custom-call | tf_op jit(solution)/shard_map/pallas_call | solution.py:158
  173.7 8.7 %collective-permute-start.25 = (bf16[4,96,768]{2,1,0:T(8,128)(2,1)}, bf16[4,96,768]{2,1,0:T(8,128)(2,1)}, u32[]{:S(2)}, u32[]{:S(2)}) collective-permute-start(bf16[4,96,768]{2,1,0:T(8,128)(2,1)} %pad_maximum_fusion.37), channel_id=1, source_target_pairs={{0,1},{1,0},{2,3},{3,2},{4,5},{5,4},{6,7},{7,6},{8,9},{9,8},{10,11... | collective-permute-start | bytes 1769480 | tf_op jit(solution)/shard_map/ppermute | solution.py:213
  185.7 3.2 multiply_reduce_fusion.2
  191.7 10.0 %shard_map.436 = (bf16[1024,1536]{1,0:T(8,128)(2,1)}, bf16[1024,1536]{1,0:T(8,128)(2,1)}) custom-call(s32[16]{0:T(128)S(1)} %get-tuple-element.399.table.places, bf16[1024,768]{1,0:T(8,128)(2,1)S(1)} %multiply_convert_fusion.1.x_ref, bf16[4,48,4224]{2,1,0:T(8,128)(2,1)S(1)} %copy-done.6, bf16[4,48,4224]{2,1,0:T(8,128)(2,1)S(1)} %copy-done.9, ...), custom_call_target="tpu_custom_call" | custom-call | flops 99999997952 | tf_op jit(solution)/shard_map/pallas_call | solution.py:463
  223.3 17.1 %collective-permute-done.30.refs_1_ = bf16[8,96,768]{2,1,0:T(8,128)(2,1)S(1)} collective-permute-done((bf16[8,96,768]{2,1,0:T(8,128)(2,1)S(1)}, bf16[8,96,768]{2,1,0:T(8,128)(2,1)S(1)}, u32[]{:S(2)}, u32[]{:S(2)}) %collective-permute-start.30) | collective-permute-done | bytes 1179680 | tf_op jit(solution)/shard_map/ppermute | solution.py:213
  248.3 6.5 %shard_map.438.q_ref.k_ref.v_ref = bf16[192,2304]{1,0:T(8,128)(2,1)S(1)} custom-call(s32[16]{0:T(128)S(1)} %get-tuple-element.399.table.places, bf16[192,1536]{1,0:T(8,128)(2,1)S(1)} %multiply_convert_fusion.3.x_ref, bf16[8,96,2304]{2,1,0:T(8,128)(2,1)S(1)} %pad_maximum_fusion.refs_0_.refs_1_, bf16[8,96,2304]{2,1,0:T(8,128)(2,1)S(1)} %pad_maximum_fusion.refs_0_.refs_1_, ...), custom_call_target="tpu_custom_call" | custom-call | tf_op jit(solution)/shard_map/pallas_call | solution.py:463
  254.8 5.1 shard_map.439
  260.5 3.1 shard_map.440
  265.7 4.1 collective-permute-done.33
  275.0 5.8 collective-permute-done.35
  281.0 8.9 %collective-permute-done.36 = bf16[2,192,768]{2,1,0:T(8,128)(2,1)S(1)} collective-permute-done((bf16[2,192,768]{2,1,0:T(8,128)(2,1)S(1)}, bf16[2,192,768]{2,1,0:T(8,128)(2,1)S(1)}, u32[]{:S(2)}, u32[]{:S(2)}) %collective-permute-start.36) | collective-permute-done | bytes 589856 | tf_op jit(solution)/shard_map/ppermute | solution.py:213
  311.7 3.5 convolution_convert_fusion.4.refs_0_
  318.0 4.4 shard_map.444
  336.0 4.8 collective-permute-done.42
  349.4 4.2 shard_map.445
  356.1 3.6 collective-permute-done.40
  364.4 5.6 shard_map.446
  370.7 11.8 %shard_map.447 = (bf16[192,1536]{1,0:T(8,128)(2,1)S(1)}, bf16[8,96,2304]{2,1,0:T(8,128)(2,1)}, bf16[8,96,2304]{2,1,0:T(8,128)(2,1)}) custom-call(s32[16]{0:T(128)S(1)} %get-tuple-element.399.table.places, s32[16]{0:T(128)S(1)} %get-tuple-element.398.places, bf16[192,1536]{1,0:T(8,128)(2,1)S(1)} %copy-done.17, bf16[8,96,2304]{2,1,0:T(8,128)(2,1)} %copy-done.2, ...), custom_call_target="tpu_custom_call" | custom-call | tf_op jit(solution)/shard_map/pallas_call | solution.py:488
  382.5 8.9 %collective-permute-done.46 = bf16[8,96,768]{2,1,0:T(8,128)(2,1)} collective-permute-done((bf16[8,96,768]{2,1,0:T(8,128)(2,1)}, bf16[8,96,768]{2,1,0:T(8,128)(2,1)}, u32[]{:S(2)}, u32[]{:S(2)}) %collective-permute-start.46) | collective-permute-done | bytes 1179680 | tf_op jit(solution)/shard_map/ppermute | solution.py:213
  399.5 3.1 fusion.21
  404.8 5.0 fusion.24
  409.9 8.0 %multiply_convert_fusion.refs_4_ = bf16[1024,1536]{1,0:T(8,128)(2,1)} fusion(bf16[1024,1536]{1,0:T(8,128)(2,1)} %get-tuple-element.228, bf16[1536,768]{1,0:T(8,128)(2,1)} %copy-done.22, f32[1024,768]{1,0:T(8,128)} %fusion.24, bf16[1024,384]{1,0:T(8,128)(2,1)S(1)} %copy-done.81, bf16[1024,384]{1,0:T(8,128)(2,1)S(1)} %copy-done.79), kind=kOutput, calls=%fused_computation | convolution fusion | flops 2425356288 | bytes 13369344 | tf_op jit(solution)/shard_map/dot_general | solution.py:31
  417.8 11.8 %shard_map.448 = (bf16[1024,768]{1,0:T(8,128)(2,1)S(1)}, bf16[8,48,2688]{2,1,0:T(8,128)(2,1)}, bf16[8,48,2688]{2,1,0:T(8,128)(2,1)}) custom-call(s32[16]{0:T(128)S(1)} %get-tuple-element.399.table.places, s32[16]{0:T(128)S(1)} %get-tuple-element.399.table.places, bf16[1024,768]{1,0:T(8,128)(2,1)S(1)} %copy-done.15, bf16[4,48,4224]{2,1,0:T(8,128)(2,1)S(1)} %copy-done.7, ...), custom_call_target="tpu_custom_call" | custom-call | tf_op jit(solution)/shard_map/pallas_call | solution.py:488
  430.3 6.0 convolution_convert_fusion.refs_0_
  439.0 4.1 collective-permute-done.50
  443.2 3.2 add_convert_fusion
  461.6 5.1 fusion.123
  476.7 17.2 %shard_map.451 = (bf16[1024,384]{1,0:T(8,128)(2,1)S(1)}, bf16[1024,384]{1,0:T(8,128)(2,1)S(1)}, bf16[1024,384]{1,0:T(8,128)(2,1)S(1)}) custom-call(bf16[1024,1152]{1,0:T(8,128)(2,1)S(1)} %copy-done.4, bf16[1024,1152]{1,0:T(8,128)(2,1)S(1)} %copy-done.4, bf16[1024,1152]{1,0:T(8,128)(2,1)S(1)} %copy-done.4, f32[1024,1]{1,0:T(8,128)S(1)} %copy-done.28, ...), custom_call_target="tpu_custom_call" | custom-call | flops 99999997952 | tf_op jit(solution)/shard_map/pallas_call | solution.py:178
  494.0 3.4 collective-permute-done.57
  501.4 10.2 %shard_map.452 = (bf16[1024,768]{1,0:T(8,128)(2,1)S(1)}, bf16[8,48,1152]{2,1,0:T(8,128)(2,1)}, bf16[8,48,1152]{2,1,0:T(8,128)(2,1)S(1)}) custom-call(s32[16]{0:T(128)S(1)} %get-tuple-element.399.table.places, s32[16]{0:T(128)S(1)} %get-tuple-element.399.table.places, bf16[1024,768]{1,0:T(8,128)(2,1)} %copy-done.10, bf16[4,48,4224]{2,1,0:T(8,128)(2,1)} %copy-done.5, ...), custom_call_target="tpu_custom_call" | custom-call | tf_op jit(solution)/shard_map/pallas_call | solution.py:488
  511.7 9.5 %collective-permute-start.66 = (bf16[1024,768]{1,0:T(8,128)(2,1)S(1)}, bf16[1024,768]{1,0:T(8,128)(2,1)S(1)}, u32[]{:S(2)}, u32[]{:S(2)}) collective-permute-start(bf16[1024,768]{1,0:T(8,128)(2,1)S(1)} %get-tuple-element.262), channel_id=1, source_target_pairs={{0,16},{16,0},{1,17},{17,1},{2,18},{18,2},{3,19},{19,3},{4,20},{20... | collective-permute-start | bytes 4718600 | tf_op jit(solution)/shard_map/ppermute | solution.py:199
  540.0 3.6 fusion.31
  543.6 12.1 %collective-permute-done.63 = bf16[2,96,768]{2,1,0:T(8,128)(2,1)} collective-permute-done((bf16[2,96,768]{2,1,0:T(8,128)(2,1)}, bf16[2,96,768]{2,1,0:T(8,128)(2,1)}, u32[]{:S(2)}, u32[]{:S(2)}) %collective-permute-start.63) | collective-permute-done | bytes 294944 | tf_op jit(solution)/shard_map/ppermute | solution.py:213
  577.3 3.3 collective-permute-start.86
  590.0 4.3 collective-permute-start.80
  598.6 8.7 %collective-permute-done.78 = bf16[1,48,2688]{2,1,0:T(8,128)(2,1)S(1)} collective-permute-done((bf16[1,48,2688]{2,1,0:T(8,128)(2,1)S(1)}, bf16[1,48,2688]{2,1,0:T(8,128)(2,1)S(1)}, u32[]{:S(2)}, u32[]{:S(2)}) %collective-permute-start.78) | collective-permute-done | bytes 258080 | tf_op jit(solution)/shard_map/ppermute | solution.py:213
  610.7 3.7 collective-permute-start.81
  (755 shorter events, 273.0 us)
Async XLA Ops:
  7.6 21.0 %collective-permute-start.1 = (bf16[1,48,4224]{2,1,0:T(8,128)(2,1)S(1)}, bf16[1,48,4224]{2,1,0:T(8,128)(2,1)S(1)}, u32[]{:S(2)}, u32[]{:S(2)}) collective-permute-start(bf16[1,48,4224]{2,1,0:T(8,128)(2,1)S(1)} %bitcast.160), channel_id=1, source_target_pairs={{0,8},{1,9},{2,10},{3,11},{4,12},{5,13},{6,14},{7,15},{8,0},{9,1},... | collective-permute-start | bytes 1216520 | tf_op jit(solution)/shard_map/ppermute | solution.py:213
  29.6 21.7 %collective-permute-start.2 = (bf16[2,48,4224]{2,1,0:T(8,128)(2,1)}, bf16[2,48,4224]{2,1,0:T(8,128)(2,1)S(1)}, u32[]{:S(2)}, u32[]{:S(2)}) collective-permute-start(bf16[2,48,4224]{2,1,0:T(8,128)(2,1)} %pad_maximum_fusion.28), channel_id=1, source_target_pairs={{0,4},{1,5},{2,6},{3,7},{4,0},{5,1},{6,2},{7,3},{8,12},{9,13},{10,... | collective-permute-start | bytes 2433032 | tf_op jit(solution)/shard_map/ppermute | solution.py:213
  51.5 22.1 %collective-permute-start.6 = (bf16[4,48,4224]{2,1,0:T(8,128)(2,1)S(1)}, bf16[4,48,4224]{2,1,0:T(8,128)(2,1)S(1)}, u32[]{:S(2)}, u32[]{:S(2)}) collective-permute-start(bf16[4,48,4224]{2,1,0:T(8,128)(2,1)S(1)} %pad_maximum_fusion.4.refs_0_), channel_id=1, source_target_pairs={{0,1},{1,0},{2,3},{3,2},{4,5},{5,4},{6,7},{7,6},{8,9},{9,8},{10,11... | collective-permute-start | bytes 4866056 | tf_op jit(solution)/shard_map/ppermute | solution.py:213
  52.3 21.3 %collective-permute-start.7 = (bf16[1,96,2304]{2,1,0:T(8,128)(2,1)S(1)}, bf16[1,96,2304]{2,1,0:T(8,128)(2,1)S(1)}, u32[]{:S(2)}, u32[]{:S(2)}) collective-permute-start(bf16[1,96,2304]{2,1,0:T(8,128)(2,1)S(1)} %copy-done.69), channel_id=1, source_target_pairs={{0,8},{1,9},{2,10},{3,11},{4,12},{5,13},{6,14},{7,15},{8,0},{9,1},... | collective-permute-start | bytes 1327112 | tf_op jit(solution)/shard_map/ppermute | solution.py:213
  55.8 17.8 %collective-permute-start.8 = (bf16[1,192,384]{2,1,0:T(8,128)(2,1)S(1)}, bf16[1,192,384]{2,1,0:T(8,128)(2,1)S(1)}, u32[]{:S(2)}, u32[]{:S(2)}) collective-permute-start(bf16[1,192,384]{2,1,0:T(8,128)(2,1)S(1)} %dynamic-slice_bitcast_fusion.7), channel_id=1, source_target_pairs={{0,1},{1,0},{2,3},{3,2},{4,5},{5,4},{6,7},{7,6},{8,9},{9,8},{10,11... | collective-permute-start | bytes 442376 | tf_op jit(solution)/shard_map/ppermute | solution.py:213
  74.3 47.3 %collective-permute-start.9 = (bf16[4,48,4224]{2,1,0:T(8,128)(2,1)S(1)}, bf16[4,48,4224]{2,1,0:T(8,128)(2,1)}, u32[]{:S(2)}, u32[]{:S(2)}) collective-permute-start(bf16[4,48,4224]{2,1,0:T(8,128)(2,1)S(1)} %pad_maximum_fusion.4.refs_0_), channel_id=1, source_target_pairs={{0,2},{1,3},{2,0},{3,1},{4,6},{5,7},{6,4},{7,5},{8,10},{9,11},{10,... | collective-permute-start | bytes 4866056 | tf_op jit(solution)/shard_map/ppermute | solution.py:213
  76.5 45.1 %collective-permute-start.10 = (bf16[4,48,4224]{2,1,0:T(8,128)(2,1)S(1)}, bf16[4,48,4224]{2,1,0:T(8,128)(2,1)}, u32[]{:S(2)}, u32[]{:S(2)}) collective-permute-start(bf16[4,48,4224]{2,1,0:T(8,128)(2,1)S(1)} %collective-permute-done.6.refs_1_), channel_id=1, source_target_pairs={{0,2},{1,3},{2,0},{3,1},{4,6},{5,7},{6,4},{7,5},{8,10},{9,11},{10,... | collective-permute-start | bytes 4866056 | tf_op jit(solution)/shard_map/ppermute | solution.py:213
  78.8 42.8 %collective-permute-start.11 = (bf16[2,96,2304]{2,1,0:T(8,128)(2,1)}, bf16[2,96,2304]{2,1,0:T(8,128)(2,1)}, u32[]{:S(2)}, u32[]{:S(2)}) collective-permute-start(bf16[2,96,2304]{2,1,0:T(8,128)(2,1)} %pad_maximum_fusion.27), channel_id=1, source_target_pairs={{0,4},{1,5},{2,6},{3,7},{4,0},{5,1},{6,2},{7,3},{8,12},{9,13},{10,... | collective-permute-start | bytes 2654216 | tf_op jit(solution)/shard_map/ppermute | solution.py:213
  83.1 24.7 %collective-permute-start.12 = (bf16[1,192,768]{2,1,0:T(8,128)(2,1)S(1)}, bf16[1,192,768]{2,1,0:T(8,128)(2,1)S(1)}, u32[]{:S(2)}, u32[]{:S(2)}) collective-permute-start(bf16[1,192,768]{2,1,0:T(8,128)(2,1)S(1)} %select_bitcast_fusion.1), channel_id=1, source_target_pairs={{0,4},{1,5},{2,6},{3,7},{4,0},{5,1},{6,2},{7,3},{8,12},{9,13},{10,... | collective-permute-start | bytes 884744 | tf_op jit(solution)/shard_map/ppermute | solution.py:213
  85.0 30.6 %collective-permute-start.13 = (bf16[2,96,768]{2,1,0:T(8,128)(2,1)S(1)}, bf16[2,96,768]{2,1,0:T(8,128)(2,1)S(1)}, u32[]{:S(2)}, u32[]{:S(2)}) collective-permute-start(bf16[2,96,768]{2,1,0:T(8,128)(2,1)S(1)} %get-tuple-element.366), channel_id=1, source_target_pairs={{0,2},{1,3},{2,0},{3,1},{4,6},{5,7},{6,4},{7,5},{8,10},{9,11},{10,... | collective-permute-start | bytes 884744 | tf_op jit(solution)/shard_map/ppermute | solution.py:213
  107.8 13.8 %collective-permute-start.14 = (bf16[2,192,384]{2,1,0:T(8,128)(2,1)}, bf16[2,192,384]{2,1,0:T(8,128)(2,1)}, u32[]{:S(2)}, u32[]{:S(2)}) collective-permute-start(bf16[2,192,384]{2,1,0:T(8,128)(2,1)} %pad_maximum_fusion.43), channel_id=1, source_target_pairs={{0,2},{1,3},{2,0},{3,1},{4,6},{5,7},{6,4},{7,5},{8,10},{9,11},{10,... | collective-permute-start | bytes 884744 | tf_op jit(solution)/shard_map/ppermute | solution.py:213
  122.6 39.8 %collective-permute-start.17 = (bf16[2,192,768]{2,1,0:T(8,128)(2,1)S(1)}, bf16[2,192,768]{2,1,0:T(8,128)(2,1)S(1)}, u32[]{:S(2)}, u32[]{:S(2)}) collective-permute-start(bf16[2,192,768]{2,1,0:T(8,128)(2,1)S(1)} %pad_maximum_fusion.35), channel_id=1, source_target_pairs={{0,1},{1,0},{2,3},{3,2},{4,5},{5,4},{6,7},{7,6},{8,9},{9,8},{10,11... | collective-permute-start | bytes 1769480 | tf_op jit(solution)/shard_map/ppermute | solution.py:213
  123.3 39.1 %collective-permute-start.18 = (bf16[4,96,768]{2,1,0:T(8,128)(2,1)S(1)}, bf16[4,96,768]{2,1,0:T(8,128)(2,1)S(1)}, u32[]{:S(2)}, u32[]{:S(2)}) collective-permute-start(bf16[4,96,768]{2,1,0:T(8,128)(2,1)S(1)} %pad_maximum_fusion.36), channel_id=1, source_target_pairs={{0,8},{1,9},{2,10},{3,11},{4,12},{5,13},{6,14},{7,15},{8,0},{9,1},... | collective-permute-start | bytes 1769480 | tf_op jit(solution)/shard_map/ppermute | solution.py:213
  125.5 39.8 %collective-permute-start.19 = (bf16[384,768]{1,0:T(8,128)(2,1)S(1)}, bf16[384,768]{1,0:T(8,128)(2,1)S(1)}, u32[]{:S(2)}, u32[]{:S(2)}) collective-permute-start(bf16[384,768]{1,0:T(8,128)(2,1)S(1)} %copy-done.132), channel_id=1, source_target_pairs={{0,8},{1,9},{2,10},{3,11},{4,12},{5,13},{6,14},{7,15},{24,16},{25,... | collective-permute-start | bytes 1769480 | tf_op jit(solution)/shard_map/ppermute | solution.py:213
  128.3 34.1 %collective-permute-start.20 = (bf16[2,96,768]{2,1,0:T(8,128)(2,1)S(1)}, bf16[2,96,768]{2,1,0:T(8,128)(2,1)S(1)}, u32[]{:S(2)}, u32[]{:S(2)}) collective-permute-start(bf16[2,96,768]{2,1,0:T(8,128)(2,1)S(1)} %pad_maximum_fusion.47), channel_id=1, source_target_pairs={{0,4},{1,5},{2,6},{3,7},{4,0},{5,1},{6,2},{7,3},{8,12},{9,13},{10,... | collective-permute-start | bytes 884744 | tf_op jit(solution)/shard_map/ppermute | solution.py:213
  135.4 47.0 %collective-permute-start.16 = (bf16[4,96,2304]{2,1,0:T(8,128)(2,1)}, bf16[4,96,2304]{2,1,0:T(8,128)(2,1)}, u32[]{:S(2)}, u32[]{:S(2)}) collective-permute-start(bf16[4,96,2304]{2,1,0:T(8,128)(2,1)} %pad_maximum_fusion.3), channel_id=1, source_target_pairs={{0,1},{1,0},{2,3},{3,2},{4,5},{5,4},{6,7},{7,6},{8,9},{9,8},{10,11... | collective-permute-start | bytes 5308424 | tf_op jit(solution)/shard_map/ppermute | solution.py:213
  165.3 17.3 %collective-permute-start.22 = (bf16[768,384]{1,0:T(8,128)(2,1)S(1)}, bf16[768,384]{1,0:T(8,128)(2,1)S(1)}, u32[]{:S(2)}, u32[]{:S(2)}) collective-permute-start(bf16[768,384]{1,0:T(8,128)(2,1)S(1)} %get-tuple-element.180), channel_id=1, source_target_pairs={{0,16},{16,0},{1,17},{17,1},{2,18},{18,2},{3,19},{19,3},{4,20},{20... | collective-permute-start | bytes 1769480 | tf_op jit(solution)/shard_map/ppermute | solution.py:199
  167.6 34.1 %collective-permute-start.23 = (bf16[4,192,768]{2,1,0:T(8,128)(2,1)S(1)}, bf16[4,192,768]{2,1,0:T(8,128)(2,1)S(1)}, u32[]{:S(2)}, u32[]{:S(2)}) collective-permute-start(bf16[4,192,768]{2,1,0:T(8,128)(2,1)S(1)} %pad_maximum_fusion.19.refs_0_.refs_1_), channel_id=1, source_target_pairs={{0,2},{1,3},{2,0},{3,1},{4,6},{5,7},{6,4},{7,5},{8,10},{9,11},{10,... | collective-permute-start | bytes 3538952 | tf_op jit(solution)/shard_map/ppermute | solution.py:213
  170.0 31.7 %collective-permute-start.24 = (bf16[1,384,768]{2,1,0:T(8,128)(2,1)S(1)}, bf16[1,384,768]{2,1,0:T(8,128)(2,1)S(1)}, u32[]{:S(2)}, u32[]{:S(2)}) collective-permute-start(bf16[1,384,768]{2,1,0:T(8,128)(2,1)S(1)} %select_bitcast_fusion.refs_0_), channel_id=1, source_target_pairs={{0,4},{1,5},{2,6},{3,7},{4,0},{5,1},{6,2},{7,3},{8,12},{9,13},{10,... | collective-permute-start | bytes 1769480 | tf_op jit(solution)/shard_map/ppermute | solution.py:213
  173.7 28.1 %collective-permute-start.25 = (bf16[4,96,768]{2,1,0:T(8,128)(2,1)}, bf16[4,96,768]{2,1,0:T(8,128)(2,1)}, u32[]{:S(2)}, u32[]{:S(2)}) collective-permute-start(bf16[4,96,768]{2,1,0:T(8,128)(2,1)} %pad_maximum_fusion.37), channel_id=1, source_target_pairs={{0,1},{1,0},{2,3},{3,2},{4,5},{5,4},{6,7},{7,6},{8,9},{9,8},{10,11... | collective-permute-start | bytes 1769480 | tf_op jit(solution)/shard_map/ppermute | solution.py:213
  185.3 56.2 %collective-permute-start.29 = (bf16[8,96,2304]{2,1,0:T(8,128)(2,1)S(1)}, bf16[8,96,2304]{2,1,0:T(8,128)(2,1)}, u32[]{:S(2)}, u32[]{:S(2)}) collective-permute-start(bf16[8,96,2304]{2,1,0:T(8,128)(2,1)S(1)} %pad_maximum_fusion.refs_0_.refs_1_), channel_id=1, source_target_pairs={{0,2},{1,3},{2,0},{3,1},{4,6},{5,7},{6,4},{7,5},{8,10},{9,11},{10,... | collective-permute-start | bytes 10616840 | tf_op jit(solution)/shard_map/ppermute | solution.py:213
  213.2 27.3 %collective-permute-start.30 = (bf16[8,96,768]{2,1,0:T(8,128)(2,1)S(1)}, bf16[8,96,768]{2,1,0:T(8,128)(2,1)S(1)}, u32[]{:S(2)}, u32[]{:S(2)}) collective-permute-start(bf16[8,96,768]{2,1,0:T(8,128)(2,1)S(1)} %pad_maximum_fusion.20.refs_0_), channel_id=1, source_target_pairs={{0,4},{1,5},{2,6},{3,7},{4,0},{5,1},{6,2},{7,3},{8,12},{9,13},{10,... | collective-permute-start | bytes 3538952 | tf_op jit(solution)/shard_map/ppermute | solution.py:213
  241.5 19.0 %collective-permute-start.32 = (bf16[8,96,768]{2,1,0:T(8,128)(2,1)}, bf16[8,96,768]{2,1,0:T(8,128)(2,1)}, u32[]{:S(2)}, u32[]{:S(2)}) collective-permute-start(bf16[8,96,768]{2,1,0:T(8,128)(2,1)} %pad_maximum_fusion.21.refs_0_.refs_1_), channel_id=1, source_target_pairs={{0,2},{1,3},{2,0},{3,1},{4,6},{5,7},{6,4},{7,5},{8,10},{9,11},{10,... | collective-permute-start | bytes 3538952 | tf_op jit(solution)/shard_map/ppermute | solution.py:213
  344.7 14.9 %collective-permute-start.40 = (bf16[1,384,768]{2,1,0:T(8,128)(2,1)S(1)}, bf16[1,384,768]{2,1,0:T(8,128)(2,1)S(1)}, u32[]{:S(2)}, u32[]{:S(2)}) collective-permute-start(bf16[1,384,768]{2,1,0:T(8,128)(2,1)S(1)} %get-tuple-element.205), channel_id=1, source_target_pairs={{0,4},{1,5},{2,6},{3,7},{4,0},{5,1},{6,2},{7,3},{8,12},{9,13},{10,... | collective-permute-start | bytes 1769480 | tf_op jit(solution)/shard_map/ppermute | solution.py:213
  346.0 45.3 %collective-permute-start.46 = (bf16[8,96,768]{2,1,0:T(8,128)(2,1)}, bf16[8,96,768]{2,1,0:T(8,128)(2,1)}, u32[]{:S(2)}, u32[]{:S(2)}) collective-permute-start(bf16[8,96,768]{2,1,0:T(8,128)(2,1)} %get-tuple-element.211), channel_id=1, source_target_pairs={{0,4},{1,5},{2,6},{3,7},{4,0},{5,1},{6,2},{7,3},{8,12},{9,13},{10,... | collective-permute-start | bytes 3538952 | tf_op jit(solution)/shard_map/ppermute | solution.py:213
  359.7 31.7 %collective-permute-start.44 = (bf16[2,192,384]{2,1,0:T(8,128)(2,1)}, bf16[2,192,384]{2,1,0:T(8,128)(2,1)}, u32[]{:S(2)}, u32[]{:S(2)}) collective-permute-start(bf16[2,192,384]{2,1,0:T(8,128)(2,1)} %pad_maximum_fusion.45), channel_id=1, source_target_pairs={{0,2},{1,3},{2,0},{3,1},{4,6},{5,7},{6,4},{7,5},{8,10},{9,11},{10,... | collective-permute-start | bytes 884744 | tf_op jit(solution)/shard_map/ppermute | solution.py:213
  359.8 31.6 %collective-permute-start.45 = (bf16[8,96,768]{2,1,0:T(8,128)(2,1)}, bf16[8,96,768]{2,1,0:T(8,128)(2,1)}, u32[]{:S(2)}, u32[]{:S(2)}) collective-permute-start(bf16[8,96,768]{2,1,0:T(8,128)(2,1)} %get-tuple-element.210), channel_id=1, source_target_pairs={{0,2},{1,3},{2,0},{3,1},{4,6},{5,7},{6,4},{7,5},{8,10},{9,11},{10,... | collective-permute-start | bytes 3538952 | tf_op jit(solution)/shard_map/ppermute | solution.py:213
  362.1 76.9 %collective-permute-start.48 = (bf16[384,768]{1,0:T(8,128)(2,1)}, bf16[384,768]{1,0:T(8,128)(2,1)}, u32[]{:S(2)}, u32[]{:S(2)}) collective-permute-start(bf16[384,768]{1,0:T(8,128)(2,1)} %bitcast_convert_fusion), channel_id=1, source_target_pairs={{8,0},{9,1},{10,2},{11,3},{12,4},{13,5},{14,6},{15,7},{16,24},{17,... | collective-permute-start | bytes 1769480 | tf_op jit(solution)/shard_map/ppermute | solution.py:213
  395.9 43.1 %collective-permute-start.49 = (bf16[4,96,768]{2,1,0:T(8,128)(2,1)}, bf16[4,96,768]{2,1,0:T(8,128)(2,1)}, u32[]{:S(2)}, u32[]{:S(2)}) collective-permute-start(bf16[4,96,768]{2,1,0:T(8,128)(2,1)} %add_convert_fusion.8), channel_id=1, source_target_pairs={{0,8},{1,9},{2,10},{3,11},{4,12},{5,13},{6,14},{7,15},{8,0},{9,1},... | collective-permute-start | bytes 1769480 | tf_op jit(solution)/shard_map/ppermute | solution.py:213
  395.9 47.3 %collective-permute-start.50 = (bf16[8,96,2304]{2,1,0:T(8,128)(2,1)}, bf16[8,96,2304]{2,1,0:T(8,128)(2,1)}, u32[]{:S(2)}, u32[]{:S(2)}) collective-permute-start(bf16[8,96,2304]{2,1,0:T(8,128)(2,1)} %get-tuple-element.225), channel_id=1, source_target_pairs={{0,2},{1,3},{2,0},{3,1},{4,6},{5,7},{6,4},{7,5},{8,10},{9,11},{10,... | collective-permute-start | bytes 10616840 | tf_op jit(solution)/shard_map/ppermute | solution.py:213
  399.3 39.7 %collective-permute-start.51 = (bf16[4,96,768]{2,1,0:T(8,128)(2,1)}, bf16[4,96,768]{2,1,0:T(8,128)(2,1)}, u32[]{:S(2)}, u32[]{:S(2)}) collective-permute-start(bf16[4,96,768]{2,1,0:T(8,128)(2,1)} %add_convert_fusion.7), channel_id=1, source_target_pairs={{0,1},{1,0},{2,3},{3,2},{4,5},{5,4},{6,7},{7,6},{8,9},{9,8},{10,11... | collective-permute-start | bytes 1769480 | tf_op jit(solution)/shard_map/ppermute | solution.py:213
  446.4 25.4 %collective-permute-start.53 = (bf16[4,96,2304]{2,1,0:T(8,128)(2,1)}, bf16[4,96,2304]{2,1,0:T(8,128)(2,1)}, u32[]{:S(2)}, u32[]{:S(2)}) collective-permute-start(bf16[4,96,2304]{2,1,0:T(8,128)(2,1)} %add_convert_fusion), channel_id=1, source_target_pairs={{0,1},{1,0},{2,3},{3,2},{4,5},{5,4},{6,7},{7,6},{8,9},{9,8},{10,11... | collective-permute-start | bytes 5308424 | tf_op jit(solution)/shard_map/ppermute | solution.py:213
  452.3 41.6 %collective-permute-start.58 = (bf16[2,96,768]{2,1,0:T(8,128)(2,1)}, bf16[2,96,768]{2,1,0:T(8,128)(2,1)S(1)}, u32[]{:S(2)}, u32[]{:S(2)}) collective-permute-start(bf16[2,96,768]{2,1,0:T(8,128)(2,1)} %add_convert_fusion.14), channel_id=1, source_target_pairs={{0,4},{1,5},{2,6},{3,7},{4,0},{5,1},{6,2},{7,3},{8,12},{9,13},{10,... | collective-permute-start | bytes 884744 | tf_op jit(solution)/shard_map/ppermute | solution.py:213
  455.9 38.1 %collective-permute-start.59 = (bf16[2,96,768]{2,1,0:T(8,128)(2,1)}, bf16[2,96,768]{2,1,0:T(8,128)(2,1)}, u32[]{:S(2)}, u32[]{:S(2)}) collective-permute-start(bf16[2,96,768]{2,1,0:T(8,128)(2,1)} %get-tuple-element.360), channel_id=1, source_target_pairs={{0,2},{1,3},{2,0},{3,1},{4,6},{5,7},{6,4},{7,5},{8,10},{9,11},{10,... | collective-permute-start | bytes 884744 | tf_op jit(solution)/shard_map/ppermute | solution.py:213
  471.9 39.8 %collective-permute-start.55 = (bf16[8,48,2688]{2,1,0:T(8,128)(2,1)S(1)}, bf16[8,48,2688]{2,1,0:T(8,128)(2,1)}, u32[]{:S(2)}, u32[]{:S(2)}) collective-permute-start(bf16[8,48,2688]{2,1,0:T(8,128)(2,1)S(1)} %get-tuple-element.239), channel_id=1, source_target_pairs={{0,2},{1,3},{2,0},{3,1},{4,6},{5,7},{6,4},{7,5},{8,10},{9,11},{10,... | collective-permute-start | bytes 6193160 | tf_op jit(solution)/shard_map/ppermute | solution.py:213
  473.1 38.6 %collective-permute-start.56 = (bf16[4,192,768]{2,1,0:T(8,128)(2,1)S(1)}, bf16[4,192,768]{2,1,0:T(8,128)(2,1)S(1)}, u32[]{:S(2)}, u32[]{:S(2)}) collective-permute-start(bf16[4,192,768]{2,1,0:T(8,128)(2,1)S(1)} %copy-done.47), channel_id=1, source_target_pairs={{0,2},{1,3},{2,0},{3,1},{4,6},{5,7},{6,4},{7,5},{8,10},{9,11},{10,... | collective-permute-start | bytes 3538952 | tf_op jit(solution)/shard_map/ppermute | solution.py:213
  475.4 21.9 %collective-permute-start.57 = (bf16[2,96,2304]{2,1,0:T(8,128)(2,1)S(1)}, bf16[2,96,2304]{2,1,0:T(8,128)(2,1)S(1)}, u32[]{:S(2)}, u32[]{:S(2)}) collective-permute-start(bf16[2,96,2304]{2,1,0:T(8,128)(2,1)S(1)} %add_convert_fusion.2), channel_id=1, source_target_pairs={{0,4},{1,5},{2,6},{3,7},{4,0},{5,1},{6,2},{7,3},{8,12},{9,13},{10,... | collective-permute-start | bytes 2654216 | tf_op jit(solution)/shard_map/ppermute | solution.py:213
  499.4 38.1 %collective-permute-start.64 = (bf16[1,96,768]{2,1,0:T(8,128)(2,1)}, bf16[1,96,768]{2,1,0:T(8,128)(2,1)}, u32[]{:S(2)}, u32[]{:S(2)}) collective-permute-start(bf16[1,96,768]{2,1,0:T(8,128)(2,1)} %add_convert_fusion.19), channel_id=1, source_target_pairs={{0,8},{1,9},{2,10},{3,11},{4,12},{5,13},{6,14},{7,15},{8,0},{9,1},... | collective-permute-start | bytes 442376 | tf_op jit(solution)/shard_map/ppermute | solution.py:213
  511.7 21.1 %collective-permute-start.66 = (bf16[1024,768]{1,0:T(8,128)(2,1)S(1)}, bf16[1024,768]{1,0:T(8,128)(2,1)S(1)}, u32[]{:S(2)}, u32[]{:S(2)}) collective-permute-start(bf16[1024,768]{1,0:T(8,128)(2,1)S(1)} %get-tuple-element.262), channel_id=1, source_target_pairs={{0,16},{16,0},{1,17},{17,1},{2,18},{18,2},{3,19},{19,3},{4,20},{20... | collective-permute-start | bytes 4718600 | tf_op jit(solution)/shard_map/ppermute | solution.py:199
  523.4 32.3 %collective-permute-start.65 = (bf16[1,96,2304]{2,1,0:T(8,128)(2,1)}, bf16[1,96,2304]{2,1,0:T(8,128)(2,1)}, u32[]{:S(2)}, u32[]{:S(2)}) collective-permute-start(bf16[1,96,2304]{2,1,0:T(8,128)(2,1)} %add_convert_fusion.12), channel_id=1, source_target_pairs={{0,8},{1,9},{2,10},{3,11},{4,12},{5,13},{6,14},{7,15},{8,0},{9,1},... | collective-permute-start | bytes 1327112 | tf_op jit(solution)/shard_map/ppermute | solution.py:213
  527.8 27.9 %collective-permute-start.60 = (bf16[8,48,1152]{2,1,0:T(8,128)(2,1)}, bf16[8,48,1152]{2,1,0:T(8,128)(2,1)}, u32[]{:S(2)}, u32[]{:S(2)}) collective-permute-start(bf16[8,48,1152]{2,1,0:T(8,128)(2,1)} %get-tuple-element.254), channel_id=1, source_target_pairs={{0,2},{1,3},{2,0},{3,1},{4,6},{5,7},{6,4},{7,5},{8,10},{9,11},{10,... | collective-permute-start | bytes 2654216 | tf_op jit(solution)/shard_map/ppermute | solution.py:213
  531.6 24.1 %collective-permute-start.61 = (bf16[4,48,2688]{2,1,0:T(8,128)(2,1)}, bf16[4,48,2688]{2,1,0:T(8,128)(2,1)}, u32[]{:S(2)}, u32[]{:S(2)}) collective-permute-start(bf16[4,48,2688]{2,1,0:T(8,128)(2,1)} %add_convert_fusion.1), channel_id=1, source_target_pairs={{0,1},{1,0},{2,3},{3,2},{4,5},{5,4},{6,7},{7,6},{8,9},{9,8},{10,11... | collective-permute-start | bytes 3096584 | tf_op jit(solution)/shard_map/ppermute | solution.py:213
  532.8 23.0 %collective-permute-start.62 = (bf16[2,192,768]{2,1,0:T(8,128)(2,1)}, bf16[2,192,768]{2,1,0:T(8,128)(2,1)}, u32[]{:S(2)}, u32[]{:S(2)}) collective-permute-start(bf16[2,192,768]{2,1,0:T(8,128)(2,1)} %add_convert_fusion.4), channel_id=1, source_target_pairs={{0,4},{1,5},{2,6},{3,7},{4,0},{5,1},{6,2},{7,3},{8,12},{9,13},{10,... | collective-permute-start | bytes 1769480 | tf_op jit(solution)/shard_map/ppermute | solution.py:213
  537.5 18.2 %collective-permute-start.63 = (bf16[2,96,768]{2,1,0:T(8,128)(2,1)}, bf16[2,96,768]{2,1,0:T(8,128)(2,1)}, u32[]{:S(2)}, u32[]{:S(2)}) collective-permute-start(bf16[2,96,768]{2,1,0:T(8,128)(2,1)} %get-tuple-element.358), channel_id=1, source_target_pairs={{0,1},{1,0},{2,3},{3,2},{4,5},{5,4},{6,7},{7,6},{8,9},{9,8},{10,11... | collective-permute-start | bytes 884744 | tf_op jit(solution)/shard_map/ppermute | solution.py:213
  560.1 22.2 %collective-permute-start.67 = (bf16[2,48,2688]{2,1,0:T(8,128)(2,1)S(1)}, bf16[2,48,2688]{2,1,0:T(8,128)(2,1)S(1)}, u32[]{:S(2)}, u32[]{:S(2)}) collective-permute-start(bf16[2,48,2688]{2,1,0:T(8,128)(2,1)S(1)} %add_convert_fusion.9), channel_id=1, source_target_pairs={{0,4},{1,5},{2,6},{3,7},{4,0},{5,1},{6,2},{7,3},{8,12},{9,13},{10,... | collective-permute-start | bytes 1548296 | tf_op jit(solution)/shard_map/ppermute | solution.py:213
  561.3 16.0 %collective-permute-start.68 = (bf16[1,192,768]{2,1,0:T(8,128)(2,1)S(1)}, bf16[1,192,768]{2,1,0:T(8,128)(2,1)S(1)}, u32[]{:S(2)}, u32[]{:S(2)}) collective-permute-start(bf16[1,192,768]{2,1,0:T(8,128)(2,1)S(1)} %add_convert_fusion.13), channel_id=1, source_target_pairs={{0,1},{1,0},{2,3},{3,2},{4,5},{5,4},{6,7},{7,6},{8,9},{9,8},{10,11... | collective-permute-start | bytes 884744 | tf_op jit(solution)/shard_map/ppermute | solution.py:213
  588.3 19.1 %collective-permute-start.78 = (bf16[1,48,2688]{2,1,0:T(8,128)(2,1)S(1)}, bf16[1,48,2688]{2,1,0:T(8,128)(2,1)S(1)}, u32[]{:S(2)}, u32[]{:S(2)}) collective-permute-start(bf16[1,48,2688]{2,1,0:T(8,128)(2,1)S(1)} %add_convert_fusion.16), channel_id=1, source_target_pairs={{0,8},{1,9},{2,10},{3,11},{4,12},{5,13},{6,14},{7,15},{8,0},{9,1},... | collective-permute-start | bytes 774152 | tf_op jit(solution)/shard_map/ppermute | solution.py:213
  590.0 19.6 %collective-permute-start.80 = (bf16[192,768]{1,0:T(8,128)(2,1)S(1)}, bf16[192,768]{1,0:T(8,128)(2,1)S(1)}, u32[]{:S(2)}, u32[]{:S(2)}) collective-permute-start(bf16[192,768]{1,0:T(8,128)(2,1)S(1)} %bitcast_convert_fusion.1), channel_id=1, source_target_pairs={{8,0},{9,1},{10,2},{11,3},{12,4},{13,5},{14,6},{15,7},{16,24},{17,... | collective-permute-start | bytes 884744 | tf_op jit(solution)/shard_map/ppermute | solution.py:213
  (232 other events, 1979.8 us)

commit v3 on v2

--- a/solution.py
+++ b/solution.py
@@ -8,8 +8,6 @@
 from jax.experimental.pallas import tpu as pltpu
 from jax.sharding import PartitionSpec as P
 
-H_L = 12
-H_G = 24
 WINDOW = 1536
 EPSILON = 1e-06
 LANES = 128
@@ -50,95 +48,150 @@
     return 256 if rows % 256 == 0 else rows
 
 
-def masked_scores(keys, query, bias, start, block, window):
-    pos_k = lax.broadcasted_iota(jnp.int32, (block, block), 0)
-    pos_q = lax.broadcasted_iota(jnp.int32, (block, block), 1)
+def head_masks(block):
+    lane = lax.broadcasted_iota(jnp.int32, (block, LANES), 1)
+    return [lane < LANES // 2, lane >= LANES // 2]
+
+
+def stacked(values, masks):
+    return jnp.concatenate([jnp.where(mask, values, jnp.zeros_like(values)) for mask in masks], axis=0)
+
+
+def first_lanes(values):
+    lane = lax.broadcasted_iota(jnp.int32, (values[0].shape[0], LANES), 1)
+    result = jnp.zeros(lane.shape, F32)
+    for index, value in enumerate(values):
+        result = jnp.where(lane == index, value, result)
+    return result.astype(BF16)
+
+
+def masked_scores(keys, biased, query, extended, bias, start, block, window):
+    key_at = lax.broadcasted_iota(jnp.int32, (block, 2 * block), 0)
+    query_at = lax.broadcasted_iota(jnp.int32, (block, 2 * block), 1)
+    query_at = jnp.where(query_at < block, query_at, query_at - block)
     parts = []
     if start:
-        before = mm_nt(keys[:start], query) + bias[:start]
+        before = mm_nt(biased[:start], extended)
         if window is not None:
-            far = lax.broadcasted_iota(jnp.int32, (start, block), 0)
-            own = lax.broadcasted_iota(jnp.int32, (start, block), 1) + start
+            far = lax.broadcasted_iota(jnp.int32, (start, 2 * block), 0)
+            own = lax.broadcasted_iota(jnp.int32, (start, 2 * block), 1)
+            own = jnp.where(own < block, own, own - block) + start
             before = jnp.where(own - far < window, before, NEG)
         parts.append(before)
     diagonal = mm_nt(keys[start : start + block], query)
-    diagonal = jnp.where(
-        pos_k == pos_q,
-        diagonal,
-        jnp.where(pos_k < pos_q, diagonal + bias[start : start + block], NEG),
-    )
-    parts.append(diagonal)
+    masked = jnp.where(key_at < query_at, diagonal + bias[start : start + block], NEG)
+    parts.append(jnp.where(key_at == query_at, diagonal, masked))
     return parts
 
 
-def attention_forward_kernel(rows, head_dim, window, q_ref, k_ref, v_ref, bias_ref, o_ref, lse_ref):
+def ranges(parts):
+    low = 0
+    for part in parts:
+        yield low, low + part.shape[0], part
+        low += part.shape[0]
+
+
+def extend_keys(biased, k_ref, bias_ref):
+    biased[:, :LANES] = k_ref[...]
+    biased[:, LANES:] = first_lanes([bias_ref[...]])
+
+
+def attention_forward_kernel(rows, window, q_ref, k_ref, v_ref, bias_ref, o_ref, lse_ref, biased, counted):
     block = query_block(rows)
+    masks = head_masks(block)
+    score_scale = (LANES // 2) ** (-0.5)
     lane = lax.broadcasted_iota(jnp.int32, (block, LANES), 1)
-    score_scale = head_dim ** (-0.5)
+    extend_keys(biased, k_ref, bias_ref)
+    for head, mask in enumerate(head_masks(rows)):
+        counted[head] = jnp.where(mask, v_ref[...], jnp.ones_like(v_ref))
+    one = first_lanes([jnp.ones((2 * block, 1), F32)])
+    query_at = lax.broadcasted_iota(jnp.int32, (2 * block, block), 0)
+    query_at = jnp.where(query_at < block, query_at, query_at - block)
+    key_at = lax.broadcasted_iota(jnp.int32, (2 * block, block), 1)
     for index in range(rows // block):
         start = index * block
-        queries = q_ref[start : start + block, :] * score_scale
-        out = jnp.zeros((block, LANES), F32)
-        for head in range(LANES // head_dim):
-            mine = (lane >= head * head_dim) & (lane < (head + 1) * head_dim)
-            query = jnp.where(mine, queries, jnp.zeros_like(queries)).astype(BF16)
-            parts = masked_scores(k_ref, query, bias_ref, start, block, window)
-            top = functools.reduce(jnp.maximum, [jnp.max(p, axis=0, keepdims=True) for p in parts])
-            parts = [jnp.exp(p - top) for p in parts]
-            total = functools.reduce(jnp.add, [jnp.sum(p, axis=0, keepdims=True) for p in parts])
-            inverse = 1.0 / total
-            mixed = jnp.zeros((block, LANES), F32)
-            low = 0
+        query = stacked((q_ref[start : start + block, :] * score_scale).astype(BF16), masks)
+        extended = jnp.concatenate([query, one], axis=1)
+        parts = []
+        if start:
+            before = mm_nt(extended, biased[:start, :])
+            if window is not None:
+                far = lax.broadcasted_iota(jnp.int32, (2 * block, start), 1)
+                own = lax.broadcasted_iota(jnp.int32, (2 * block, start), 0)
+                own = jnp.where(own < block, own, own - block) + start
+                before = jnp.where(own - far < window, before, NEG)
+            parts.append(before)
+        masked = jnp.where(key_at < query_at, mm_nt(extended, biased[start : start + block, :]), NEG)
+        parts.append(jnp.where(key_at == query_at, mm_nt(query, k_ref[start : start + block, :]), masked))
+        top = functools.reduce(jnp.maximum, [jnp.max(p, axis=1, keepdims=True) for p in parts])
+        parts = [jnp.exp(p - top).astype(BF16) for p in parts]
+        out, logs = jnp.zeros((block, LANES), F32), jnp.zeros((block, LANES), F32)
+        for head, mask in enumerate(masks):
+            span = slice(head * block, (head + 1) * block)
+            mixed, low = jnp.zeros((block, LANES), F32), 0
             for part in parts:
-                high = low + part.shape[0]
-                mixed += mm_tn((part * inverse).astype(BF16), v_ref[low:high, :])
+                high = low + part.shape[1]
+                mixed += mm(part[span], counted[head, low:high, :])
                 low = high
-            out = jnp.where(mine, mixed, out)
-            lse_ref[0, head : head + 1, start : start + block] = top + jnp.log(total)
+            other = LANES // 2 if head == 0 else 0
+            total = mixed[:, other : other + 1]
+            out = jnp.where(mask, mixed * (1.0 / total), out)
+            logs = jnp.where(lane == head, top[span] + jnp.log(total), logs)
         o_ref[start : start + block, :] = out.astype(BF16)
+        lse_ref[0, :, start : start + block] = logs.T[:2]
 
 
 def attention_backward_kernel(
-    rows, head_dim, window, q_ref, k_ref, v_ref, bias_ref, lse_ref, do_ref, dq_ref, dk_ref, dv_ref, dk_acc, dv_acc
+    rows,
+    window,
+    q_ref,
+    k_ref,
+    v_ref,
+    bias_ref,
+    lse_ref,
+    o_ref,
+    do_ref,
+    dq_ref,
+    dk_ref,
+    dv_ref,
+    dk_acc,
+    dv_acc,
+    biased,
+    reduced,
 ):
     block = query_block(rows)
-    lane = lax.broadcasted_iota(jnp.int32, (block, LANES), 1)
-    score_scale = head_dim ** (-0.5)
-    dk_acc[...] = jnp.zeros((rows, LANES), F32)
-    dv_acc[...] = jnp.zeros((rows, LANES), F32)
-    for index in range(rows // block):
+    masks = head_masks(block)
+    score_scale = (LANES // 2) ** (-0.5)
+    extend_keys(biased, k_ref, bias_ref)
+    reduced[:, :LANES] = v_ref[...]
+    reduced[:, LANES:] = first_lanes([jnp.full((rows, 1), -1.0, F32)] * 2)
+    one = first_lanes([jnp.ones((2 * block, 1), F32)])
+    for index in reversed(range(rows // block)):
         start = index * block
-        queries = q_ref[start : start + block, :] * score_scale
-        grads = do_ref[start : start + block, :]
-        dq = jnp.zeros((block, LANES), F32)
-        for head in range(LANES // head_dim):
-            mine = (lane >= head * head_dim) & (lane < (head + 1) * head_dim)
-            query = jnp.where(mine, queries, jnp.zeros_like(queries)).astype(BF16)
-            grad = jnp.where(mine, grads, jnp.zeros_like(grads))
-            lse = lse_ref[0, head : head + 1, start : start + block]
-            parts = masked_scores(k_ref, query, bias_ref, start, block, window)
-            parts = [jnp.exp(p - lse) for p in parts]
-            grad_parts = []
-            low = 0
-            for part in parts:
-                high = low + part.shape[0]
-                grad_parts.append(mm_nt(v_ref[low:high, :], grad))
-                low = high
-            delta = functools.reduce(
-                jnp.add,
-                [jnp.sum(p * g, axis=0, keepdims=True) for p, g in zip(parts, grad_parts)],
-            )
-            mixed = jnp.zeros((block, LANES), F32)
-            low = 0
-            for part, grad_part in zip(parts, grad_parts):
-                high = low + part.shape[0]
-                grad_score = (part * (grad_part - delta)).astype(BF16)
-                dv_acc[low:high, :] += mm(part.astype(BF16), grad)
-                dk_acc[low:high, :] += mm(grad_score, query)
-                mixed += mm_tn(grad_score, k_ref[low:high, :])
-                low = high
-            dq = jnp.where(mine, mixed, dq)
-        dq_ref[start : start + block, :] = (dq * score_scale).astype(BF16)
+        query = stacked((q_ref[start : start + block, :] * score_scale).astype(BF16), masks)
+        extended = jnp.concatenate([query, one], axis=1)
+        grad = stacked(do_ref[start : start + block, :], masks)
+        mixed = o_ref[start : start + block, :].astype(F32)
+        delta = jnp.sum(grad.astype(F32) * jnp.concatenate([mixed, mixed], axis=0), axis=1, keepdims=True)
+        near = delta.astype(BF16).astype(F32)
+        grad_extended = jnp.concatenate([grad, first_lanes([near, delta - near])], axis=1)
+        lse = jnp.concatenate([lse_ref[0, head : head + 1, start : start + block] for head in range(2)], axis=1)
+        parts = masked_scores(k_ref, biased, query, extended, bias_ref, start, block, window)
+        turned = jnp.zeros((2 * block, LANES), F32)
+        for low, high, part in ranges(parts):
+            weights = jnp.exp(part - lse)
+            change = (weights * mm_nt(reduced[low:high, :], grad_extended)).astype(BF16)
+            dv = mm(weights.astype(BF16), grad)
+            dk = mm(change, query)
+            if index == rows // block - 1:
+                dv_acc[low:high, :] = dv
+                dk_acc[low:high, :] = dk
+            else:
+                dv_acc[low:high, :] += dv
+                dk_acc[low:high, :] += dk
+            turned += mm_tn(change, k_ref[low:high, :])
+        dq = jnp.where(masks[0], turned[:block], turned[block:]) * score_scale
+        dq_ref[start : start + block, :] = dq.astype(BF16)
     dk_ref[...] = dk_acc[...].astype(BF16)
     dv_ref[...] = dv_acc[...].astype(BF16)
 
@@ -150,49 +203,53 @@
     return pairs, wide, bias
 
 
-def attention_forward(projected, bias, head_dim):
+def attention_forward(projected, bias):
     rows, width = projected.shape[0], projected.shape[1] // 3
     pairs, wide, bias_spec = attention_specs(rows, width)
-    per = LANES // head_dim
     window = WINDOW if rows > WINDOW else None
     return pl.pallas_call(
-        functools.partial(attention_forward_kernel, rows, head_dim, window),
+        functools.partial(attention_forward_kernel, rows, window),
         grid=(pairs,),
         in_specs=[wide(0), wide(1), wide(2), bias_spec],
-        out_specs=[wide(0), pl.BlockSpec((1, per, rows), lambda i: (i, 0, 0))],
+        out_specs=[wide(0), pl.BlockSpec((1, 2, rows), lambda i: (i, 0, 0))],
         out_shape=[
             jax.ShapeDtypeStruct((rows, width), BF16),
-            jax.ShapeDtypeStruct((pairs, per, rows), F32),
+            jax.ShapeDtypeStruct((pairs, 2, rows), F32),
         ],
+        scratch_shapes=[pltpu.VMEM((rows, 2 * LANES), BF16), pltpu.VMEM((2, rows, LANES), BF16)],
         compiler_params=pltpu.CompilerParams(vmem_limit_bytes=VMEM_LIMIT),
         cost_estimate=FREE,
     )(projected, projected, projected, bias)
 
 
-def attention_backward(projected, bias, lse, grad_mixture, head_dim):
+def attention_backward(projected, bias, lse, mixture, grad_mixture):
     rows, width = grad_mixture.shape
     pairs, wide, bias_spec = attention_specs(rows, width)
-    per = LANES // head_dim
     window = WINDOW if rows > WINDOW else None
     shape = jax.ShapeDtypeStruct((rows, width), BF16)
-    grads = pl.pallas_call(
-        functools.partial(attention_backward_kernel, rows, head_dim, window),
+    return pl.pallas_call(
+        functools.partial(attention_backward_kernel, rows, window),
         grid=(pairs,),
         in_specs=[
             wide(0),
             wide(1),
             wide(2),
             bias_spec,
-            pl.BlockSpec((1, per, rows), lambda i: (i, 0, 0)),
+            pl.BlockSpec((1, 2, rows), lambda i: (i, 0, 0)),
+            wide(0),
             wide(0),
         ],
         out_specs=[wide(0), wide(0), wide(0)],
         out_shape=[shape, shape, shape],
-        scratch_shapes=[pltpu.VMEM((rows, LANES), F32), pltpu.VMEM((rows, LANES), F32)],
+        scratch_shapes=[
+            pltpu.VMEM((rows, LANES), F32),
+            pltpu.VMEM((rows, LANES), F32),
+            pltpu.VMEM((rows, 2 * LANES), BF16),
+            pltpu.VMEM((rows, 2 * LANES), BF16),
+        ],
         compiler_params=pltpu.CompilerParams(vmem_limit_bytes=VMEM_LIMIT),
         cost_estimate=LONG,
-    )(projected, projected, projected, bias, lse, grad_mixture)
-    return grads
+    )(projected, projected, projected, bias, lse, mixture, grad_mixture)
 
 
 def swap(array):
@@ -294,13 +351,13 @@
     return [(part, k) for part in parts for k in range(2)]
 
 
-def grouped_kernel(cuts, table, *refs):
-    step = pl.program_id(0)
-    for index, part in enumerate(refs[:4]):
-        place = table[step + index * pl.num_programs(0)] % 4
+def whole_kernel(cuts, table, *refs):
+    quarter = refs[0].shape[0]
+    for index in range(4 * quarter):
+        part, place = refs[index // quarter], table[index]
         for (r0, r1, c0, c1), out in zip(cuts, refs[4:]):
             rows = r1 - r0
-            out[pl.ds(pl.multiple_of(place * rows, 16), rows), :] = part[0, r0:r1, c0:c1]
+            out[pl.ds(pl.multiple_of(place * rows, 16), rows), :] = part[index % quarter, r0:r1, c0:c1]
 
 
 def assembled_fours(parts, table, cuts, width=None, cost=FREE):
@@ -311,18 +368,13 @@
     if not aligned(rows, cuts):
         stack = jnp.concatenate(parts, axis=0)[jnp.argsort(table)]
         return [stack[:, r0:r1, c0:c1].reshape(s) for (r0, r1, c0, c1), s in zip(cuts, shapes)]
-    steps = count // 4
     return pl.pallas_call(
-        functools.partial(grouped_kernel, cuts),
+        functools.partial(whole_kernel, cuts),
         grid_spec=pltpu.PrefetchScalarGridSpec(
             num_scalar_prefetch=1,
-            grid=(steps,),
-            in_specs=[
-                pl.BlockSpec((1, rows, width), lambda j, t, k=k: (k * steps + j, 0, 0)) for _, k in quarters(parts)
-            ],
-            out_specs=[
-                pl.BlockSpec((4 * (r1 - r0), c1 - c0), lambda j, t: (t[j] // 4, 0)) for r0, r1, c0, c1 in cuts
-            ],
+            grid=(1,),
+            in_specs=[pl.BlockSpec((count // 4, rows, width), lambda j, t, k=k: (k, 0, 0)) for _, k in quarters(parts)],
+            out_specs=[pl.BlockSpec(shape, lambda j, t: (0, 0)) for shape in shapes],
         ),
         out_shape=[jax.ShapeDtypeStruct(s, parts[0].dtype) for s in shapes],
         compiler_params=pltpu.CompilerParams(vmem_limit_bytes=VMEM_LIMIT),
@@ -402,6 +454,43 @@
     outs[1][...] = slope.astype(outs[1].dtype)
 
 
+def outer_kernel(rows, bounds, places, x_ref, *refs):
+    grads, (send, keep, weight, turned) = refs[: len(bounds)], refs[len(bounds) :]
+    step = pl.program_id(0)
+
+    @pl.when(step == 0)
+    def _():
+        turned[...] = x_ref[...].T
+
+    grad = grads[-1][...]
+    for (low, high), ref in list(zip(bounds, grads))[:-1]:
+        grad = jnp.where((step >= low) & (step < high), ref[...], grad)
+    weight[...] = mm(turned[...], grad).astype(BF16)
+    half = keep.shape[0]
+    for index in range(2 * half):
+        block = weight[pl.ds(pl.multiple_of(places[index] * rows, 16), rows), :]
+        (keep if index < half else send)[index % half] = block
+
+
+def inner_kernel(rows, bounds, table, *refs):
+    parts, grads, (dx_ref, weight, total) = refs[:4], refs[4 : 4 + len(bounds)], refs[4 + len(bounds) :]
+    step = pl.program_id(0)
+
+    @pl.when(step == 0)
+    def _():
+        total[...] = jnp.zeros_like(total)
+
+    write_rows(weight, parts, table, rows)
+    grad = grads[-1][...]
+    for (low, high), ref in list(zip(bounds, grads))[:-1]:
+        grad = jnp.where((step >= low) & (step < high), ref[...], grad)
+    total[...] += mm_nt(grad, weight[...])
+
+    @pl.when(step == pl.num_programs(0) - 1)
+    def _():
+        dx_ref[...] = total[...].astype(BF16)
+
+
 def pullback_kernel(rows, count, bounds, table, places, x_ref, *refs):
     parts, grads = refs[:count], refs[count : count + len(bounds)]
     dx_ref, send, keep, weight, turned, total = refs[count + len(bounds) :]
@@ -418,6 +507,31 @@
         grad = jnp.where((step >= low) & (step < high), ref[...], grad)
     total[...] += lax.dot_general(grad, weight[...], (((1,), (1,)), ((), ())), preferred_element_type=F32)
     weight[...] = jnp.dot(turned[...], grad, preferred_element_type=F32).astype(BF16)
+    half = keep.shape[0]
+    for index in range(2 * half):
+        block = weight[pl.ds(pl.multiple_of(places[index] * rows, 16), rows), :]
+        (keep if index < half else send)[index % half] = block
+
+    @pl.when(step == pl.num_programs(0) - 1)
+    def _():
+        dx_ref[...] = total[...].astype(BF16)
+
+
+def feed_forward_kernel(rows, table, places, x_ref, grad_ref, down_ref, slope_ref, act_ref, *refs):
+    parts, (dx_ref, down_out, send, keep, weight, turned, total) = refs[:4], refs[4:]
+    step = pl.program_id(0)
+
+    @pl.when(step == 0)
+    def _():
+        turned[...] = x_ref[...].T
+        total[...] = jnp.zeros_like(total)
+
+    grad = grad_ref[...]
+    change = (mm_nt(grad, down_ref[...]) * slope_ref[...].astype(F32)).astype(BF16)
+    down_out[...] = mm_tn(act_ref[...], grad).astype(BF16)
+    write_rows(weight, parts, table, rows)
+    total[...] += mm_nt(change, weight[...])
+    weight[...] = mm(turned[...], change).astype(BF16)
     half = keep.shape[0]
     for index in range(2 * half):
         block = weight[pl.ds(pl.multiple_of(places[index] * rows, 16), rows), :]
@@ -474,6 +588,85 @@
             cost_estimate=LONG if gelu else FREE,
         )(self.table, x, *[part for part, _ in quarters(self.parts)])
         return results if gelu else results[0]
+
+    def feed_forward_pullback(self, x, grad, down, slope, activated, places, lead):
+        if not self.aligned or down.shape[0] != self.width:
+            change = (slope.astype(F32) * mm_nt(grad, down)).astype(BF16)
+            dx, halves = self.pullback(x, [change], places, lead)
+            return dx, mm_tn(activated, grad).astype(BF16), halves
+        tokens, depth = x.shape
+        half = jax.ShapeDtypeStruct((self.count // 2, self.rows, lead + self.width), BF16)
+        half_spec = pl.BlockSpec((self.count // 2, self.rows, TILE), lambda i, t, p: (0, 0, lead // TILE + i))
+        full = pl.BlockSpec((tokens, depth), lambda i, t, p: (0, 0))
+        units = pl.BlockSpec((tokens, TILE), lambda i, t, p: (0, i))
+        unit_rows = pl.BlockSpec((TILE, depth), lambda i, t, p: (i, 0))
+        result = pl.pallas_call(
+            functools.partial(feed_forward_kernel, self.rows),
+            grid_spec=pltpu.PrefetchScalarGridSpec(
+                num_scalar_prefetch=2,
+                grid=(self.width // TILE,),
+                in_specs=[full, full, unit_rows, units, units] + self.part_specs(),
+                out_specs=[full, unit_rows, half_spec, half_spec],
+                scratch_shapes=[
+                    pltpu.VMEM((depth, TILE), BF16),
+                    pltpu.VMEM((depth, tokens), BF16),
+                    pltpu.VMEM((tokens, depth), F32),
+                ],
+            ),
+            out_shape=[jax.ShapeDtypeStruct((tokens, depth), BF16), jax.ShapeDtypeStruct(down.shape, BF16), half, half],
+            compiler_params=pltpu.CompilerParams(vmem_limit_bytes=VMEM_LIMIT),
+            cost_estimate=FREE,
+        )(self.table, places, x, grad, down, slope, activated, *[part for part, _ in quarters(self.parts)])
+        return result[0], result[1], result[2:]
+
+    def grad_specs(self, tokens, grads):
+        ends = np.cumsum([grad.shape[1] // TILE for grad in grads])
+        bounds = [(int(end) - grad.shape[1] // TILE, int(end)) for end, grad in zip(ends, grads)]
+        specs = [
+            pl.BlockSpec((tokens, TILE), lambda i, t, low=low, high=high: (0, jnp.clip(i, low, high - 1) - low))
+            for low, high in bounds
+        ]
+        return bounds, specs
+
+    def outer(self, x, grads, places):
+        if not self.aligned:
+            return split_stack([mm_tn(x, jnp.concatenate(grads, axis=1)).astype(BF16)], places, self.count)
+        tokens, depth = x.shape
+        bounds, specs = self.grad_specs(tokens, grads)
+        half = jax.ShapeDtypeStruct((self.count // 2, self.rows, self.width), BF16)
+        half_spec = pl.BlockSpec((self.count // 2, self.rows, TILE), lambda i, t: (0, 0, i))
+        return pl.pallas_call(
+            functools.partial(outer_kernel, self.rows, bounds),
+            grid_spec=pltpu.PrefetchScalarGridSpec(
+                num_scalar_prefetch=1,
+                grid=(self.width // TILE,),
+                in_specs=[pl.BlockSpec((tokens, depth), lambda i, t: (0, 0))] + specs,
+                out_specs=[half_spec, half_spec],
+                scratch_shapes=[pltpu.VMEM((depth, TILE), BF16), pltpu.VMEM((depth, tokens), BF16)],
+            ),
+            out_shape=[half, half],
+            compiler_params=pltpu.CompilerParams(vmem_limit_bytes=VMEM_LIMIT),
+            cost_estimate=FREE,
+        )(places, x, *grads)
+
+    def inner(self, grads):
+        if not self.aligned:
+            return mm_nt(jnp.concatenate(grads, axis=1), self.whole()).astype(BF16)
+        tokens, depth = grads[0].shape[0], self.rows * self.count
+        bounds, specs = self.grad_specs(tokens, grads)
+        return pl.pallas_call(
+            functools.partial(inner_kernel, self.rows, bounds),
+            grid_spec=pltpu.PrefetchScalarGridSpec(
+                num_scalar_prefetch=1,
+                grid=(self.width // TILE,),
+                in_specs=self.part_specs() + specs,
+                out_specs=pl.BlockSpec((tokens, depth), lambda i, t: (0, 0)),
+                scratch_shapes=[pltpu.VMEM((depth, TILE), BF16), pltpu.VMEM((tokens, depth), F32)],
+            ),
+            out_shape=jax.ShapeDtypeStruct((tokens, depth), BF16),
+            compiler_params=pltpu.CompilerParams(vmem_limit_bytes=VMEM_LIMIT),
+            cost_estimate=FREE,
+        )(self.table, *[part for part, _ in quarters(self.parts)], *grads)
 
     def pullback(self, x, grads, places, lead=0):
         if not self.aligned:
@@ -718,7 +911,6 @@
     half_g = width_g // 2
     rows_l, rows_g = out_l.shape[0], out_g.shape[0]
     units_l, units_g = down_l.shape[0], down_g.shape[0]
-    head_l, head_g = width_l // H_L, width_g // H_G
     micro_total, slot_total = patch_index.shape[1:]
     slots = micro_total * slot_total
     bits = bit_count(size)
@@ -755,8 +947,7 @@
         block = jnp.concatenate(columns, axis=1)
         return jnp.pad(block, ((0, 0), (0, TILE - block.shape[1])))
 
-    top_first = [(bits - 1,) + o for o in orders(size, (None, -1, -2))]
-    mixed = orders(size, (-1, None, -2))
+    lows_first = orders(size, (-1, -2, None))
     lows_last = orders(size, (None, -1, -2))
     plane = [o[:2] + (bits - 1,) + o[2:] for o in orders(size, (-1, -2, None))]
     line = orders(size, (None,))
@@ -765,11 +956,10 @@
     fresh = functools.partial(Stream, size)
     up_width, qkv_width = up_l.shape[1] // 2, 3 * half_g
     square_units = units_g * (size // 8)
-    table = placement(top_first, every)
-    between = [
-        (bits - 1,) + orders(size, middle)[which] for which, middle in enumerate(((None, -1, -2), (-1, None, -2)))
-    ]
-    places_g = placement(between, every)
+    rises, falls = (None, -1, -2), (-1, None, -2)
+    order_l = [(bits - 1,) + orders(size, middle)[which] for which, middle in enumerate((falls, rises))]
+    order_g = [(bits - 1,) + orders(size, middle)[which] for which, middle in enumerate((rises, falls))]
+    table, table_g = placement(order_l, every), placement(order_g, every)
     side_l = half_l + half_g
     stream_l = fresh(
         gather_all(
@@ -777,13 +967,13 @@
                 [half_of(out_l, core), half_of(patch_proj, core), gain_block(), own_heads(qkv_l), half_of(up_l, core)],
                 axis=1,
             ),
-            top_first,
+            order_l,
             True,
         )
     )
     stream_down_l = fresh(gather_core(down_l, lows_last, below))
-    stream_g = fresh(gather_all(own_heads(qkv_g), top_first, False))
-    stream_out_g = fresh(gather_all(half_of(out_g, core), top_first, False))
+    stream_g = fresh(gather_all(own_heads(qkv_g), order_g, False))
+    stream_out_g = fresh(gather_all(half_of(out_g, core), order_g, False))
     square = square_columns(half_of(up_g, core))
     one_two = jnp.where(is_first, square[2], square[1])
     two_one = jnp.where(is_first, square[1], square[2])
@@ -810,7 +1000,7 @@
     scale_l1 = advance([stream_l, stream_up_g, stream_down_l, stream_g], scale_l1)
     stream_top = fresh(gather_in_square(half_of(grad_top_b, core)))
     grad_top_b = advance([stream_l, stream_up_g, stream_down_l, stream_top], grad_top_b)
-    advance([stream_l, stream_g, stream_top, stream_out_g], ())
+    advance([stream_l, stream_g, stream_top, stream_up_g], (), [stream_up_g])
 
     advance([stream_l, stream_g, stream_down_l, stream_up_g, stream_down_g, stream_top, stream_out_g], ())
     parts = stream_l.result()
@@ -831,7 +1021,8 @@
     )
     normed_l = (inputs * scale_l1 * gain_one_l).astype(BF16)
     projected_l = qkv_wl.product(normed_l)
-    mixture_l, lse_l = attention_forward(projected_l, bias_l, head_l)
+    own_mixture_l, lse_l = attention_forward(projected_l, bias_l)
+    mixture_l = own_mixture_l
     mixture_l, out_wl, proj_w = advance(
         [stream_down_l, stream_up_g, stream_down_g, stream_out_g], (mixture_l, out_wl, proj_w), [stream_up_g]
     )
@@ -843,7 +1034,7 @@
     normed_l2 = (hidden_l * scale_l2 * gain_two_l).astype(BF16)
     activated_l, slope_l = up_wl.product(normed_l2, gelu=True)
     activated_l, proj_w = advance(
-        [stream_down_l, stream_down_g, stream_out_g, stream_up_g], (activated_l, proj_w), [stream_out_g]
+        [stream_down_l, stream_down_g, stream_out_g, stream_up_g], (activated_l, proj_w)
     )
     proj_w = shared(proj_w)
     (down_wl,) = stream_down_l.result()
@@ -855,12 +1046,13 @@
     scale_g1 = row_scale(start_rows)
     square_top = shared(stream_top.result().reshape(4 * slots, half_l))
     scale_g1, square_top = advance([stream_g, stream_out_g, stream_up_g], (scale_g1, square_top))
-    qkv_wg = Weight(stream_g.result(), table, 0, qkv_width)
+    qkv_wg = Weight(stream_g.result(), table_g, 0, qkv_width)
     normed_g = (start_rows * scale_g1 * gain_one_g).astype(BF16)
     projected_g = qkv_wg.product(normed_g)
-    mixture_g, lse_g = attention_forward(projected_g, bias_g, head_g)
+    own_mixture_g, lse_g = attention_forward(projected_g, bias_g)
+    mixture_g = own_mixture_g
     mixture_g = advance([stream_out_g], mixture_g)
-    (out_wg,) = assembled_fours(stream_out_g.result(), table, [(0, rows_g, 0, half_g)])
+    (out_wg,) = assembled_fours(stream_out_g.result(), table_g, [(0, rows_g, 0, half_g)])
     out_theirs_g = swap(out_wg)
     mixture_g = shared(mixture_g)
     hidden_g = start_rows + joined(mm(mixture_g, out_wg), mm(mixture_g, out_theirs_g))
@@ -888,19 +1080,20 @@
     grad_hidden_gb = grad_hidden_g.astype(BF16)
     mine_gb, theirs_gb = half_of(grad_hidden_gb, core), half_of(grad_hidden_gb, 1 - core)
     grad_out_g = mm_tn(mixture_g, mine_gb).astype(BF16)
-    stream_out_g = fresh(scatter_all(split_stack([grad_out_g], table, size), top_first))
+    stream_out_g = fresh(scatter_all(split_stack([grad_out_g], table_g, size), order_g))
     grad_mixture_g = (
         mm_nt(mine_gb, half_of(out_wg, core, 0)) + mm_nt(theirs_gb, half_of(out_theirs_g, core, 0))
     ).astype(BF16)
     partial_g = mm(activated_g, down_wg)
     partial_g = half_of(partial_g, core) + swap(half_of(partial_g, 1 - core).astype(BF16)).astype(F32)
     stream_out = fresh(scatter_in_square(partial_g.reshape(4, slots, half_l)))
-    grad_mixture_g = advance([stream_down_g, stream_out_g, stream_out], grad_mixture_g)
-    grad_projected_g = attention_backward(projected_g, bias_g, lse_g, grad_mixture_g, head_g)
-    part, halves = qkv_wg.pullback(normed_g, grad_projected_g, places_g)
-    stream_g = fresh(scatter_all(halves, between))
-    part = advance([stream_g, stream_out, stream_out_g, stream_up_g], part)
+    grad_mixture_g = advance([stream_out_g, stream_out], grad_mixture_g)
+    grad_projected_g = attention_backward(projected_g, bias_g, lse_g, own_mixture_g, grad_mixture_g)
+    part, halves = qkv_wg.pullback(normed_g, grad_projected_g, table_g)
+    stream_g = fresh(scatter_all(halves, order_g))
+    part = advance([stream_g, stream_out, stream_out_g, stream_down_g], part)
     part = summed_cores(part)
+    part = advance([stream_up_g], part)
     pulled, grad_gain_g1 = norm_backward(part, start_rows, scale_g1, gain_one_g)
     grad_start = (grad_hidden_g + pulled).astype(BF16)
     grad_proj = mm_tn(boundary, half_of(grad_start, core)).astype(BF16)
@@ -908,25 +1101,24 @@
     grad_rows = mm_nt(grad_start, proj_w).astype(BF16)
     grad_local = seq_grads.astype(F32) + mm_tn(picks, grad_rows)
     grad_local_b = grad_local.astype(BF16)
-    grad_down_l = mm_tn(activated_l, grad_local_b).astype(BF16)
-    stream_down_l = fresh(scatter_core(grad_down_l, mixed, below, size))
-    grad_act_l = mm_nt(grad_local_b, down_wl)
-    grad_up_l_rows = (slope_l.astype(F32) * grad_act_l).astype(BF16)
-    part, up_halves = up_wl.pullback(normed_l2, [grad_up_l_rows], table, side_l)
-    part, up_halves = advance([stream_down_g, stream_up_g, stream_g, stream_out_g], (part, up_halves))
+    part, grad_down_l, up_halves = up_wl.feed_forward_pullback(
+        normed_l2, grad_local_b, down_wl, slope_l, activated_l, table, side_l
+    )
+    stream_down_l = fresh(scatter_core(grad_down_l, lows_first, below, size))
+    part, up_halves = advance([stream_g, stream_down_g, stream_up_g, stream_out_g], (part, up_halves))
     part = summed_cores(part)
     pulled, grad_gain_l2 = norm_backward(part, hidden_l, scale_l2, gain_two_l)
     grad_hidden_l = grad_local + pulled
     grad_hidden_lb = grad_hidden_l.astype(BF16)
     grad_out_l = mm_tn(mixture_l, half_of(grad_hidden_lb, core)).astype(BF16)
-    stream_up_l = fresh(scatter_all(split_stack([grad_out_l, grad_proj], table, size, up_halves), top_first))
+    stream_up_l = fresh(scatter_all(split_stack([grad_out_l, grad_proj], table, size, up_halves), order_l))
     grad_mixture_l = mm_nt(grad_hidden_lb, out_own_l).astype(BF16)
     grad_mixture_l = advance([stream_g, stream_down_l, stream_up_l], grad_mixture_l)
-    grad_projected_l = attention_backward(projected_l, bias_l, lse_l, grad_mixture_l, head_l)
-    grad_projected_l = advance([stream_g, stream_out_g, stream_up_g], grad_projected_l)
-    part, halves = qkv_wl.pullback(normed_l, grad_projected_l, table)
-    stream_qkv_l = fresh(scatter_all(halves, top_first))
-    part = advance([stream_up_l, stream_down_l, stream_qkv_l], part)
+    grad_projected_l = attention_backward(projected_l, bias_l, lse_l, own_mixture_l, grad_mixture_l)
+    grad_projected_l = advance([stream_out_g, stream_up_g], grad_projected_l)
+    stream_qkv_l = fresh(scatter_all(qkv_wl.outer(normed_l, grad_projected_l, table), order_l))
+    grad_projected_l = advance([stream_qkv_l], grad_projected_l)
+    part = advance([stream_up_l, stream_up_g, stream_g, stream_down_l], qkv_wl.inner(grad_projected_l))
     part = summed_cores(part)
     pulled, grad_gain_l1 = norm_backward(part, inputs, scale_l1, gain_one_l)
     input_grad = half_of(grad_hidden_l + pulled, core).astype(BF16)[None]
@@ -939,13 +1131,11 @@
     )
     returned = half_of(hidden_g[:, :width_l], core) + stream_out.result()
     hidden_out = (local_out + mm_tn(picks_live, returned.astype(BF16))).astype(BF16)[None]
-    input_grad, gains = advance(
-        [stream_qkv_l, stream_up_l, stream_down_l, stream_up_g, stream_out_g, stream_g], (input_grad, gains)
-    )
     stream_gains = fresh(scatter_small(gains, size))
-    advance([stream_qkv_l, stream_gains], ())
-    advance([stream_up_l, stream_down_l, stream_gains], ())
-    advance([stream_qkv_l, stream_gains], ())
+    input_grad = advance([stream_qkv_l, stream_up_l, stream_down_l, stream_gains], input_grad)
+    advance([stream_qkv_l, stream_gains, stream_down_l, stream_out_g, stream_g], ())
+    advance([stream_up_l, stream_gains], ())
+    advance([stream_qkv_l], ())
     advance([stream_up_l, stream_qkv_l, stream_down_l], ())
 
     def joined_columns(mine, theirs):

time: 629 us -> 600 us (0.954)
  matrix products: 55.9 us -> 39 us
  starting transfers between devices: 114 us -> 101 us
  local copies, waits for them, and re-layouts: 47 us -> 55.9 us
    pallas_call x3 -> x1, Pallas kernels: 33.7 us -> 12 us  [pullback(): pl.pallas_call(functools.partial(pullback_kernel, self.rows, 4, bounds),...]
    pallas_call x7 -> x10, Pallas kernels: 47.8 us -> 65.8 us  [the longest x2 18.2 us: attention_backward(): pl.pallas_call(functools.partial(attention_backward_kernel, rows, window)...]
    ppermute x24, starting transfers between devices: 33.6 us -> 22.1 us  [swap(): return lax.ppermute(array, 'section', [(0, 1), (1, 0)])]
    unnamed x410 -> x412, local copies, waits for them, and re-layouts: 25.3 us -> 36.7 us
    dot_general x8 -> x7, matrix products: 23.2 us -> 14.9 us  [mm_tn(): lax.dot_general(left, right, (((0,), (0,)), ((), ())), preferred_element_...]
    dot_general x6 -> x5, matrix products: 15.7 us -> 8.06 us  [mm_nt(): lax.dot_general(left, right, (((1,), (1,)), ((), ())), preferred_element_...]
  transfers between devices with their start and end apart: 88 -> 88, of which waited for: 29 -> 27; matrix products, arithmetic and copies ran while one was open for 26% -> 24% of each run, Pallas kernels for 18% -> 20%
where the time goes in v3:
time: 600 us; the launch traced here: 593 us
  waiting for transfers between devices  163 us (27%)
  Pallas kernels  120 us (20%)
  other arithmetic  110 us (18%)
  starting transfers between devices  101 us (17%)
  local copies, waits for them, and re-layouts  55.9 us (9%)
  matrix products  39 us (6%)
    ppermute x57, waiting for transfers between devices, exchange(): lax.ppermute(part, ('section', 'dp'), pairs)  156 us
    ppermute x57, starting transfers between devices, exchange(): lax.ppermute(part, ('section', 'dp'), pairs)  71.2 us
    unnamed x412, local copies, waits for them, and re-layouts  36.7 us
    convert_element_type x15, other arithmetic, halving(): outgoing = total_of([term[half:] for term in terms]).astype(BF16)  28.5 us
    pallas_call x3, Pallas kernels, product(): pl.pallas_call(functools.partial(product_kernel, self.rows, 4, gelu), gri...  22.4 us
    ppermute x24, starting transfers between devices, swap(): return lax.ppermute(array, 'section', [(0, 1), (1, 0)])  22.1 us
    pallas_call x2, Pallas kernels, attention_backward(): pl.pallas_call(functools.partial(attention_backward_kernel, rows, window)...  18.2 us
    pallas_call x1, Pallas kernels, feed_forward_pullback(): pl.pallas_call(functools.partial(feed_forward_kernel, self.rows), grid_sp...  17.7 us
  transfers between devices with their start and end apart: 88, of which 27 were waited for; matrix products, arithmetic and copies ran while one was open for 24% of the time, Pallas kernels for 20%

profile of v3, /device:TPU:1, one launch (start us, length us, event | category | flops | bytes accessed | tf_op | source)
XLA Modules:
  0.0 593.1 jit_solution(13109367322723093668)
XLA Ops:
  7.6 3.2 collective-permute-start.1
  17.5 11.2 %collective-permute-done.1 = bf16[1,48,4224]{2,1,0:T(8,128)(2,1)S(1)} collective-permute-done((bf16[1,48,4224]{2,1,0:T(8,128)(2,1)S(1)}, bf16[1,48,4224]{2,1,0:T(8,128)(2,1)S(1)}, u32[]{:S(2)}, u32[]{:S(2)}) %collective-permute-start.1) | collective-permute-done | bytes 405536 | tf_op jit(solution)/shard_map/ppermute | solution.py:270
  37.1 4.0 collective-permute-done.4
  51.4 7.0 %collective-permute-done.7 = bf16[1,96,2304]{2,1,0:T(8,128)(2,1)} collective-permute-done((bf16[1,96,2304]{2,1,0:T(8,128)(2,1)}, bf16[1,96,2304]{2,1,0:T(8,128)(2,1)}, u32[]{:S(2)}, u32[]{:S(2)}) %collective-permute-start.7) | collective-permute-done | bytes 442400 | tf_op jit(solution)/shard_map/ppermute | solution.py:270
  58.4 11.0 %collective-permute-done.8 = bf16[1,192,384]{2,1,0:T(8,128)(2,1)S(1)} collective-permute-done((bf16[1,192,384]{2,1,0:T(8,128)(2,1)}, bf16[1,192,384]{2,1,0:T(8,128)(2,1)S(1)}, u32[]{:S(2)}, u32[]{:S(2)}) %collective-permute-start.8) | collective-permute-done | bytes 147488 | tf_op jit(solution)/shard_map/ppermute | solution.py:270
  77.0 3.2 collective-permute-start.13
  86.9 24.1 %collective-permute-done.14 = bf16[2,192,384]{2,1,0:T(8,128)(2,1)} collective-permute-done((bf16[2,192,384]{2,1,0:T(8,128)(2,1)}, bf16[2,192,384]{2,1,0:T(8,128)(2,1)}, u32[]{:S(2)}, u32[]{:S(2)}) %collective-permute-start.14) | collective-permute-done | bytes 294944 | tf_op jit(solution)/shard_map/ppermute | solution.py:270
  117.4 3.1 collective-permute-start.19
  128.5 5.8 shard_map.434.q_ref.k_ref.v_ref
  137.2 9.5 %shard_map.435 = (bf16[1024,384]{1,0:T(8,128)(2,1)S(1)}, f32[3,2,1024]{2,1,0:T(2,128)S(1)}) custom-call(bf16[1024,1152]{1,0:T(8,128)(2,1)S(1)} %copy-done.3, bf16[1024,1152]{1,0:T(8,128)(2,1)S(1)} %copy-done.3, bf16[1024,1152]{1,0:T(8,128)(2,1)S(1)} %copy-done.3, f32[1024,1]{1,0:T(8,128)S(1)} %fusion.44.bias_ref), custom_call_target="tpu_custom_call" | custom-call | tf_op jit(solution)/shard_map/pallas_call | solution.py:210
  146.7 13.4 %collective-permute-done.19 = bf16[1,96,768]{2,1,0:T(8,128)(2,1)S(1)} collective-permute-done((bf16[1,96,768]{2,1,0:T(8,128)(2,1)S(1)}, bf16[1,96,768]{2,1,0:T(8,128)(2,1)S(1)}, u32[]{:S(2)}, u32[]{:S(2)}) %collective-permute-start.19) | collective-permute-done | bytes 147488 | tf_op jit(solution)/shard_map/ppermute | solution.py:270
  161.0 4.4 collective-permute-start.21
  168.9 3.6 collective-permute-start.23
  183.5 10.1 %shard_map.436 = (bf16[1024,1536]{1,0:T(8,128)(2,1)}, bf16[1024,1536]{1,0:T(8,128)(2,1)}) custom-call(s32[16]{0:T(128)S(1)} %fusion.98.table.places, bf16[1024,768]{1,0:T(8,128)(2,1)S(1)} %multiply_convert_fusion.x_ref, bf16[4,48,4224]{2,1,0:T(8,128)(2,1)S(1)} %copy-done.5, bf16[4,48,4224]{2,1,0:T(8,128)(2,1)S(1)} %copy-done.8, ...), custom_call_target="tpu_custom_call" | custom-call | flops 99999997952 | tf_op jit(solution)/shard_map/pallas_call | solution.py:577
  194.5 5.3 fusion.130
  213.1 7.4 %collective-permute-done.29 = bf16[4,96,768]{2,1,0:T(8,128)(2,1)S(1)} collective-permute-done((bf16[4,96,768]{2,1,0:T(8,128)(2,1)S(1)}, bf16[4,96,768]{2,1,0:T(8,128)(2,1)S(1)}, u32[]{:S(2)}, u32[]{:S(2)}) %collective-permute-start.29) | collective-permute-done | bytes 589856 | tf_op jit(solution)/shard_map/ppermute | solution.py:270
  220.5 20.1 %collective-permute-done.30.refs_1_ = bf16[8,96,768]{2,1,0:T(8,128)(2,1)S(1)} collective-permute-done((bf16[8,96,768]{2,1,0:T(8,128)(2,1)S(1)}, bf16[8,96,768]{2,1,0:T(8,128)(2,1)S(1)}, u32[]{:S(2)}, u32[]{:S(2)}) %collective-permute-start.30) | collective-permute-done | bytes 1179680 | tf_op jit(solution)/shard_map/ppermute | solution.py:270
  249.0 6.5 %shard_map.438.q_ref.k_ref.v_ref = bf16[192,2304]{1,0:T(8,128)(2,1)S(1)} custom-call(s32[16]{0:T(128)S(1)} %fusion.99.table.places, bf16[192,1536]{1,0:T(8,128)(2,1)S(1)} %multiply_convert_fusion.2.x_ref, bf16[8,96,2304]{2,1,0:T(8,128)(2,1)S(1)} %pad_maximum_fusion.refs_0_.refs_1_, bf16[8,96,2304]{2,1,0:T(8,128)(2,1)S(1)} %pad_maximum_fusion.refs_0_.refs_1_, ...), custom_call_target="tpu_custom_call" | custom-call | tf_op jit(solution)/shard_map/pallas_call | solution.py:577
  255.5 4.6 shard_map.439
  264.4 3.3 collective-permute-done.33
  274.2 4.7 collective-permute-done.35
  280.1 8.0 %collective-permute-done.36 = bf16[2,192,768]{2,1,0:T(8,128)(2,1)S(1)} collective-permute-done((bf16[2,192,768]{2,1,0:T(8,128)(2,1)S(1)}, bf16[2,192,768]{2,1,0:T(8,128)(2,1)S(1)}, u32[]{:S(2)}, u32[]{:S(2)}) %collective-permute-start.36) | collective-permute-done | bytes 589856 | tf_op jit(solution)/shard_map/ppermute | solution.py:270
  310.0 3.2 convolution_convert_fusion.3.refs_0_
  316.8 4.6 shard_map.444
  335.4 3.8 collective-permute-done.41
  348.0 4.2 shard_map.445
  356.1 4.5 shard_map.446
  361.3 12.0 %shard_map.447 = (bf16[192,1536]{1,0:T(8,128)(2,1)S(1)}, bf16[8,96,2304]{2,1,0:T(8,128)(2,1)}, bf16[8,96,2304]{2,1,0:T(8,128)(2,1)}) custom-call(s32[16]{0:T(128)S(1)} %fusion.99.table.places, s32[16]{0:T(128)S(1)} %fusion.99.table.places, bf16[192,1536]{1,0:T(8,128)(2,1)S(1)} %copy-done.20, bf16[8,96,2304]{2,1,0:T(8,128)(2,1)} %copy-done.2, ...), custom_call_target="tpu_custom_call" | custom-call | tf_op jit(solution)/shard_map/pallas_call | solution.py:681
  380.7 5.7 collective-permute-start.48
  397.8 5.7 fusion.15
  405.0 17.7 %shard_map.448 = (bf16[1024,768]{1,0:T(8,128)(2,1)S(1)}, bf16[1536,768]{1,0:T(8,128)(2,1)}, bf16[8,48,2688]{2,1,0:T(8,128)(2,1)}, bf16[8,48,2688]{2,1,0:T(8,128)(2,1)}) custom-call(s32[16]{0:T(128)S(1)} %fusion.98.table.places, s32[16]{0:T(128)S(1)} %fusion.98.table.places, bf16[1024,768]{1,0:T(8,128)(2,1)S(1)} %copy-done.18, ...), custom_call_target="tpu_custom_call" | custom-call | tf_op jit(solution)/shard_map/pallas_call | solution.py:603
  424.4 2.9 shard_map.449
  436.3 3.3 add_convert_fusion
  447.5 4.3 shard_map.450
  453.2 8.3 %collective-permute-done.55 = bf16[4,96,2304]{2,1,0:T(8,128)(2,1)S(1)} collective-permute-done((bf16[4,96,2304]{2,1,0:T(8,128)(2,1)}, bf16[4,96,2304]{2,1,0:T(8,128)(2,1)S(1)}, u32[]{:S(2)}, u32[]{:S(2)}) %collective-permute-start.55) | collective-permute-done | bytes 1769504 | tf_op jit(solution)/shard_map/ppermute | solution.py:270
  461.9 3.3 add_convert_fusion.2
  465.8 13.7 %shard_map.451 = (bf16[1024,384]{1,0:T(8,128)(2,1)S(1)}, bf16[1024,384]{1,0:T(8,128)(2,1)S(1)}, bf16[1024,384]{1,0:T(8,128)(2,1)S(1)}) custom-call(bf16[1024,1152]{1,0:T(8,128)(2,1)} %shard_map.434.q_ref.k_ref.v_ref, bf16[1024,1152]{1,0:T(8,128)(2,1)} %shard_map.434.q_ref.k_ref.v_ref, bf16[1024,1152]{1,0:T(8,128)(2,1)} %shard_map.434.q_ref.k_ref.v_ref, ...), custom_call_target="tpu_custom_call" | custom-call | flops 99999997952 | tf_op jit(solution)/shard_map/pallas_call | solution.py:230
  486.6 5.1 shard_map.452
  492.2 5.6 shard_map.453
  515.6 3.0 fusion.5
  518.9 3.7 fusion.30
  522.6 3.9 collective-permute-done.62
  531.8 4.5 collective-permute-done.71
  538.4 3.8 collective-permute-done.69
  551.3 4.8 collective-permute-start.80
  560.1 3.3 collective-permute-start.78
  566.5 10.6 %collective-permute-done.78 = bf16[1,48,2688]{2,1,0:T(8,128)(2,1)S(1)} collective-permute-done((bf16[1,48,2688]{2,1,0:T(8,128)(2,1)S(1)}, bf16[1,48,2688]{2,1,0:T(8,128)(2,1)S(1)}, u32[]{:S(2)}, u32[]{:S(2)}) %collective-permute-start.78) | collective-permute-done | bytes 258080 | tf_op jit(solution)/shard_map/ppermute | solution.py:270
  580.4 3.5 collective-permute-start.81
  (757 shorter events, 266.3 us)
Async XLA Ops:
  7.6 21.0 %collective-permute-start.1 = (bf16[1,48,4224]{2,1,0:T(8,128)(2,1)S(1)}, bf16[1,48,4224]{2,1,0:T(8,128)(2,1)S(1)}, u32[]{:S(2)}, u32[]{:S(2)}) collective-permute-start(bf16[1,48,4224]{2,1,0:T(8,128)(2,1)S(1)} %bitcast.160), channel_id=1, source_target_pairs={{0,8},{1,9},{2,10},{3,11},{4,12},{5,13},{6,14},{7,15},{8,0},{9,1},... | collective-permute-start | bytes 1216520 | tf_op jit(solution)/shard_map/ppermute | solution.py:270
  29.6 14.8 %collective-permute-start.2 = (bf16[2,48,4224]{2,1,0:T(8,128)(2,1)}, bf16[2,48,4224]{2,1,0:T(8,128)(2,1)S(1)}, u32[]{:S(2)}, u32[]{:S(2)}) collective-permute-start(bf16[2,48,4224]{2,1,0:T(8,128)(2,1)} %pad_maximum_fusion.28), channel_id=1, source_target_pairs={{0,1},{1,0},{2,3},{3,2},{4,5},{5,4},{6,7},{7,6},{8,9},{9,8},{10,11... | collective-permute-start | bytes 2433032 | tf_op jit(solution)/shard_map/ppermute | solution.py:270
  44.6 24.9 %collective-permute-start.6 = (bf16[4,48,4224]{2,1,0:T(8,128)(2,1)S(1)}, bf16[4,48,4224]{2,1,0:T(8,128)(2,1)S(1)}, u32[]{:S(2)}, u32[]{:S(2)}) collective-permute-start(bf16[4,48,4224]{2,1,0:T(8,128)(2,1)S(1)} %pad_maximum_fusion.4.refs_0_), channel_id=1, source_target_pairs={{0,4},{1,5},{2,6},{3,7},{4,0},{5,1},{6,2},{7,3},{8,12},{9,13},{10,... | collective-permute-start | bytes 4866056 | tf_op jit(solution)/shard_map/ppermute | solution.py:270
  50.0 19.5 %collective-permute-start.9 = (bf16[2,96,768]{2,1,0:T(8,128)(2,1)S(1)}, bf16[2,96,768]{2,1,0:T(8,128)(2,1)S(1)}, u32[]{:S(2)}, u32[]{:S(2)}) collective-permute-start(bf16[2,96,768]{2,1,0:T(8,128)(2,1)S(1)} %get-tuple-element.370), channel_id=1, source_target_pairs={{0,2},{1,3},{2,0},{3,1},{4,6},{5,7},{6,4},{7,5},{8,10},{9,11},{10,... | collective-permute-start | bytes 884744 | tf_op jit(solution)/shard_map/ppermute | solution.py:270
  51.2 18.3 %collective-permute-start.8 = (bf16[1,192,384]{2,1,0:T(8,128)(2,1)}, bf16[1,192,384]{2,1,0:T(8,128)(2,1)S(1)}, u32[]{:S(2)}, u32[]{:S(2)}) collective-permute-start(bf16[1,192,384]{2,1,0:T(8,128)(2,1)} %dynamic-slice_bitcast_fusion.7), channel_id=1, source_target_pairs={{0,1},{1,0},{2,3},{3,2},{4,5},{5,4},{6,7},{7,6},{8,9},{9,8},{10,11... | collective-permute-start | bytes 442376 | tf_op jit(solution)/shard_map/ppermute | solution.py:270
  70.2 40.7 %collective-permute-start.10 = (bf16[4,48,4224]{2,1,0:T(8,128)(2,1)S(1)}, bf16[4,48,4224]{2,1,0:T(8,128)(2,1)}, u32[]{:S(2)}, u32[]{:S(2)}) collective-permute-start(bf16[4,48,4224]{2,1,0:T(8,128)(2,1)S(1)} %pad_maximum_fusion.4.refs_0_), channel_id=1, source_target_pairs={{0,2},{1,3},{2,0},{3,1},{4,6},{5,7},{6,4},{7,5},{8,10},{9,11},{10,... | collective-permute-start | bytes 4866056 | tf_op jit(solution)/shard_map/ppermute | solution.py:270
  71.2 39.8 %collective-permute-start.11 = (bf16[4,48,4224]{2,1,0:T(8,128)(2,1)S(1)}, bf16[4,48,4224]{2,1,0:T(8,128)(2,1)}, u32[]{:S(2)}, u32[]{:S(2)}) collective-permute-start(bf16[4,48,4224]{2,1,0:T(8,128)(2,1)S(1)} %collective-permute-done.6.refs_1_), channel_id=1, source_target_pairs={{0,2},{1,3},{2,0},{3,1},{4,6},{5,7},{6,4},{7,5},{8,10},{9,11},{10,... | collective-permute-start | bytes 4866056 | tf_op jit(solution)/shard_map/ppermute | solution.py:270
  74.6 36.4 %collective-permute-start.12 = (bf16[2,96,2304]{2,1,0:T(8,128)(2,1)}, bf16[2,96,2304]{2,1,0:T(8,128)(2,1)}, u32[]{:S(2)}, u32[]{:S(2)}) collective-permute-start(bf16[2,96,2304]{2,1,0:T(8,128)(2,1)} %pad_maximum_fusion.27), channel_id=1, source_target_pairs={{0,4},{1,5},{2,6},{3,7},{4,0},{5,1},{6,2},{7,3},{8,12},{9,13},{10,... | collective-permute-start | bytes 2654216 | tf_op jit(solution)/shard_map/ppermute | solution.py:270
  81.0 30.0 %collective-permute-start.14 = (bf16[2,192,384]{2,1,0:T(8,128)(2,1)}, bf16[2,192,384]{2,1,0:T(8,128)(2,1)}, u32[]{:S(2)}, u32[]{:S(2)}) collective-permute-start(bf16[2,192,384]{2,1,0:T(8,128)(2,1)} %pad_maximum_fusion.43), channel_id=1, source_target_pairs={{0,2},{1,3},{2,0},{3,1},{4,6},{5,7},{6,4},{7,5},{8,10},{9,11},{10,... | collective-permute-start | bytes 884744 | tf_op jit(solution)/shard_map/ppermute | solution.py:270
  112.1 48.1 %collective-permute-start.16 = (bf16[2,192,768]{2,1,0:T(8,128)(2,1)S(1)}, bf16[2,192,768]{2,1,0:T(8,128)(2,1)S(1)}, u32[]{:S(2)}, u32[]{:S(2)}) collective-permute-start(bf16[2,192,768]{2,1,0:T(8,128)(2,1)S(1)} %pad_maximum_fusion.36), channel_id=1, source_target_pairs={{0,1},{1,0},{2,3},{3,2},{4,5},{5,4},{6,7},{7,6},{8,9},{9,8},{10,11... | collective-permute-start | bytes 1769480 | tf_op jit(solution)/shard_map/ppermute | solution.py:270
  113.1 47.1 %collective-permute-start.17 = (bf16[4,96,768]{2,1,0:T(8,128)(2,1)S(1)}, bf16[4,96,768]{2,1,0:T(8,128)(2,1)S(1)}, u32[]{:S(2)}, u32[]{:S(2)}) collective-permute-start(bf16[4,96,768]{2,1,0:T(8,128)(2,1)S(1)} %pad_maximum_fusion.35), channel_id=1, source_target_pairs={{0,8},{1,9},{2,10},{3,11},{4,12},{5,13},{6,14},{7,15},{8,0},{9,1},... | collective-permute-start | bytes 1769480 | tf_op jit(solution)/shard_map/ppermute | solution.py:270
  115.6 44.6 %collective-permute-start.18 = (bf16[384,768]{1,0:T(8,128)(2,1)S(1)}, bf16[384,768]{1,0:T(8,128)(2,1)S(1)}, u32[]{:S(2)}, u32[]{:S(2)}) collective-permute-start(bf16[384,768]{1,0:T(8,128)(2,1)S(1)} %copy-done.139), channel_id=1, source_target_pairs={{0,8},{1,9},{2,10},{3,11},{4,12},{5,13},{6,14},{7,15},{24,16},{25,... | collective-permute-start | bytes 1769480 | tf_op jit(solution)/shard_map/ppermute | solution.py:270
  117.4 42.8 %collective-permute-start.19 = (bf16[1,96,768]{2,1,0:T(8,128)(2,1)S(1)}, bf16[1,96,768]{2,1,0:T(8,128)(2,1)S(1)}, u32[]{:S(2)}, u32[]{:S(2)}) collective-permute-start(bf16[1,96,768]{2,1,0:T(8,128)(2,1)S(1)} %copy-done.97), channel_id=1, source_target_pairs={{0,8},{1,9},{2,10},{3,11},{4,12},{5,13},{6,14},{7,15},{8,0},{9,1},... | collective-permute-start | bytes 442376 | tf_op jit(solution)/shard_map/ppermute | solution.py:270
  123.3 50.9 %collective-permute-start.15 = (bf16[4,96,2304]{2,1,0:T(8,128)(2,1)}, bf16[4,96,2304]{2,1,0:T(8,128)(2,1)}, u32[]{:S(2)}, u32[]{:S(2)}) collective-permute-start(bf16[4,96,2304]{2,1,0:T(8,128)(2,1)} %pad_maximum_fusion.3), channel_id=1, source_target_pairs={{0,1},{1,0},{2,3},{3,2},{4,5},{5,4},{6,7},{7,6},{8,9},{9,8},{10,11... | collective-permute-start | bytes 5308424 | tf_op jit(solution)/shard_map/ppermute | solution.py:270
  166.7 27.0 %collective-permute-start.22 = (bf16[4,192,768]{2,1,0:T(8,128)(2,1)S(1)}, bf16[4,192,768]{2,1,0:T(8,128)(2,1)S(1)}, u32[]{:S(2)}, u32[]{:S(2)}) collective-permute-start(bf16[4,192,768]{2,1,0:T(8,128)(2,1)S(1)} %pad_maximum_fusion.19.refs_0_.refs_1_), channel_id=1, source_target_pairs={{0,2},{1,3},{2,0},{3,1},{4,6},{5,7},{6,4},{7,5},{8,10},{9,11},{10,... | collective-permute-start | bytes 3538952 | tf_op jit(solution)/shard_map/ppermute | solution.py:270
  168.9 24.7 %collective-permute-start.23 = (bf16[1,384,768]{2,1,0:T(8,128)(2,1)S(1)}, bf16[1,384,768]{2,1,0:T(8,128)(2,1)S(1)}, u32[]{:S(2)}, u32[]{:S(2)}) collective-permute-start(bf16[1,384,768]{2,1,0:T(8,128)(2,1)S(1)} %select_bitcast_fusion.refs_0_), channel_id=1, source_target_pairs={{0,4},{1,5},{2,6},{3,7},{4,0},{5,1},{6,2},{7,3},{8,12},{9,13},{10,... | collective-permute-start | bytes 1769480 | tf_op jit(solution)/shard_map/ppermute | solution.py:270
  173.2 20.4 %collective-permute-start.24 = (bf16[2,96,768]{2,1,0:T(8,128)(2,1)}, bf16[2,96,768]{2,1,0:T(8,128)(2,1)S(1)}, u32[]{:S(2)}, u32[]{:S(2)}) collective-permute-start(bf16[2,96,768]{2,1,0:T(8,128)(2,1)} %pad_maximum_fusion.47), channel_id=1, source_target_pairs={{0,4},{1,5},{2,6},{3,7},{4,0},{5,1},{6,2},{7,3},{8,12},{9,13},{10,... | collective-permute-start | bytes 884744 | tf_op jit(solution)/shard_map/ppermute | solution.py:270
  177.3 64.4 %collective-permute-start.28 = (bf16[8,96,2304]{2,1,0:T(8,128)(2,1)S(1)}, bf16[8,96,2304]{2,1,0:T(8,128)(2,1)}, u32[]{:S(2)}, u32[]{:S(2)}) collective-permute-start(bf16[8,96,2304]{2,1,0:T(8,128)(2,1)S(1)} %pad_maximum_fusion.refs_0_.refs_1_), channel_id=1, source_target_pairs={{0,2},{1,3},{2,0},{3,1},{4,6},{5,7},{6,4},{7,5},{8,10},{9,11},{10,... | collective-permute-start | bytes 10616840 | tf_op jit(solution)/shard_map/ppermute | solution.py:270
  206.5 13.9 %collective-permute-start.29 = (bf16[4,96,768]{2,1,0:T(8,128)(2,1)S(1)}, bf16[4,96,768]{2,1,0:T(8,128)(2,1)S(1)}, u32[]{:S(2)}, u32[]{:S(2)}) collective-permute-start(bf16[4,96,768]{2,1,0:T(8,128)(2,1)S(1)} %pad_maximum_fusion.37), channel_id=1, source_target_pairs={{0,1},{1,0},{2,3},{3,2},{4,5},{5,4},{6,7},{7,6},{8,9},{9,8},{10,11... | collective-permute-start | bytes 1769480 | tf_op jit(solution)/shard_map/ppermute | solution.py:270
  207.0 33.6 %collective-permute-start.30 = (bf16[8,96,768]{2,1,0:T(8,128)(2,1)S(1)}, bf16[8,96,768]{2,1,0:T(8,128)(2,1)S(1)}, u32[]{:S(2)}, u32[]{:S(2)}) collective-permute-start(bf16[8,96,768]{2,1,0:T(8,128)(2,1)S(1)} %pad_maximum_fusion.20.refs_0_), channel_id=1, source_target_pairs={{0,4},{1,5},{2,6},{3,7},{4,0},{5,1},{6,2},{7,3},{8,12},{9,13},{10,... | collective-permute-start | bytes 3538952 | tf_op jit(solution)/shard_map/ppermute | solution.py:270
  242.8 17.9 %collective-permute-start.32 = (bf16[8,96,768]{2,1,0:T(8,128)(2,1)}, bf16[8,96,768]{2,1,0:T(8,128)(2,1)}, u32[]{:S(2)}, u32[]{:S(2)}) collective-permute-start(bf16[8,96,768]{2,1,0:T(8,128)(2,1)} %pad_maximum_fusion.22.refs_0_.refs_1_), channel_id=1, source_target_pairs={{0,2},{1,3},{2,0},{3,1},{4,6},{5,7},{6,4},{7,5},{8,10},{9,11},{10,... | collective-permute-start | bytes 3538952 | tf_op jit(solution)/shard_map/ppermute | solution.py:270
  342.8 30.5 %collective-permute-start.45 = (bf16[1,384,768]{2,1,0:T(8,128)(2,1)}, bf16[1,384,768]{2,1,0:T(8,128)(2,1)}, u32[]{:S(2)}, u32[]{:S(2)}) collective-permute-start(bf16[1,384,768]{2,1,0:T(8,128)(2,1)} %get-tuple-element.212), channel_id=1, source_target_pairs={{0,4},{1,5},{2,6},{3,7},{4,0},{5,1},{6,2},{7,3},{8,12},{9,13},{10,... | collective-permute-start | bytes 1769480 | tf_op jit(solution)/shard_map/ppermute | solution.py:270
  343.5 48.2 %collective-permute-start.49 = (bf16[8,96,768]{2,1,0:T(8,128)(2,1)}, bf16[8,96,768]{2,1,0:T(8,128)(2,1)}, u32[]{:S(2)}, u32[]{:S(2)}) collective-permute-start(bf16[8,96,768]{2,1,0:T(8,128)(2,1)} %get-tuple-element.227), channel_id=1, source_target_pairs={{0,4},{1,5},{2,6},{3,7},{4,0},{5,1},{6,2},{7,3},{8,12},{9,13},{10,... | collective-permute-start | bytes 3538952 | tf_op jit(solution)/shard_map/ppermute | solution.py:270
  354.5 18.8 %collective-permute-start.43 = (bf16[2,192,384]{2,1,0:T(8,128)(2,1)}, bf16[2,192,384]{2,1,0:T(8,128)(2,1)}, u32[]{:S(2)}, u32[]{:S(2)}) collective-permute-start(bf16[2,192,384]{2,1,0:T(8,128)(2,1)} %pad_maximum_fusion.45), channel_id=1, source_target_pairs={{0,2},{1,3},{2,0},{3,1},{4,6},{5,7},{6,4},{7,5},{8,10},{9,11},{10,... | collective-permute-start | bytes 884744 | tf_op jit(solution)/shard_map/ppermute | solution.py:270
  355.6 17.8 %collective-permute-start.44 = (bf16[8,96,768]{2,1,0:T(8,128)(2,1)}, bf16[8,96,768]{2,1,0:T(8,128)(2,1)}, u32[]{:S(2)}, u32[]{:S(2)}) collective-permute-start(bf16[8,96,768]{2,1,0:T(8,128)(2,1)} %get-tuple-element.211), channel_id=1, source_target_pairs={{0,2},{1,3},{2,0},{3,1},{4,6},{5,7},{6,4},{7,5},{8,10},{9,11},{10,... | collective-permute-start | bytes 3538952 | tf_op jit(solution)/shard_map/ppermute | solution.py:270
  373.4 54.5 %collective-permute-start.47 = (bf16[8,96,2304]{2,1,0:T(8,128)(2,1)}, bf16[8,96,2304]{2,1,0:T(8,128)(2,1)}, u32[]{:S(2)}, u32[]{:S(2)}) collective-permute-start(bf16[8,96,2304]{2,1,0:T(8,128)(2,1)} %get-tuple-element.223), channel_id=1, source_target_pairs={{0,2},{1,3},{2,0},{3,1},{4,6},{5,7},{6,4},{7,5},{8,10},{9,11},{10,... | collective-permute-start | bytes 10616840 | tf_op jit(solution)/shard_map/ppermute | solution.py:270
  376.5 15.0 %collective-permute-start.50 = (bf16[192,1536]{1,0:T(8,128)(2,1)S(1)}, bf16[192,1536]{1,0:T(8,128)(2,1)S(1)}, u32[]{:S(2)}, u32[]{:S(2)}) collective-permute-start(bf16[192,1536]{1,0:T(8,128)(2,1)S(1)} %get-tuple-element.228), channel_id=1, source_target_pairs={{0,16},{16,0},{1,17},{17,1},{2,18},{18,2},{3,19},{19,3},{4,20},{20... | collective-permute-start | bytes 1769480 | tf_op jit(solution)/shard_map/ppermute | solution.py:256
  380.7 47.2 %collective-permute-start.48 = (bf16[384,768]{1,0:T(8,128)(2,1)}, bf16[384,768]{1,0:T(8,128)(2,1)}, u32[]{:S(2)}, u32[]{:S(2)}) collective-permute-start(bf16[384,768]{1,0:T(8,128)(2,1)} %bitcast_convert_fusion), channel_id=1, source_target_pairs={{8,0},{9,1},{10,2},{11,3},{12,4},{13,5},{14,6},{15,7},{16,24},{17,... | collective-permute-start | bytes 1769480 | tf_op jit(solution)/shard_map/ppermute | solution.py:270
  388.4 39.5 %collective-permute-start.52 = (bf16[4,96,768]{2,1,0:T(8,128)(2,1)}, bf16[4,96,768]{2,1,0:T(8,128)(2,1)}, u32[]{:S(2)}, u32[]{:S(2)}) collective-permute-start(bf16[4,96,768]{2,1,0:T(8,128)(2,1)} %add_convert_fusion.7), channel_id=1, source_target_pairs={{0,1},{1,0},{2,3},{3,2},{4,5},{5,4},{6,7},{7,6},{8,9},{9,8},{10,11... | collective-permute-start | bytes 1769480 | tf_op jit(solution)/shard_map/ppermute | solution.py:270
  394.8 33.1 %collective-permute-start.51 = (bf16[4,96,768]{2,1,0:T(8,128)(2,1)}, bf16[4,96,768]{2,1,0:T(8,128)(2,1)}, u32[]{:S(2)}, u32[]{:S(2)}) collective-permute-start(bf16[4,96,768]{2,1,0:T(8,128)(2,1)} %add_convert_fusion.8), channel_id=1, source_target_pairs={{0,8},{1,9},{2,10},{3,11},{4,12},{5,13},{6,14},{7,15},{8,0},{9,1},... | collective-permute-start | bytes 1769480 | tf_op jit(solution)/shard_map/ppermute | solution.py:270
  430.1 49.4 %collective-permute-start.53 = (bf16[2,96,768]{2,1,0:T(8,128)(2,1)}, bf16[2,96,768]{2,1,0:T(8,128)(2,1)}, u32[]{:S(2)}, u32[]{:S(2)}) collective-permute-start(bf16[2,96,768]{2,1,0:T(8,128)(2,1)} %add_convert_fusion.14), channel_id=1, source_target_pairs={{0,4},{1,5},{2,6},{3,7},{4,0},{5,1},{6,2},{7,3},{8,12},{9,13},{10,... | collective-permute-start | bytes 884744 | tf_op jit(solution)/shard_map/ppermute | solution.py:270
  432.9 46.7 %collective-permute-start.54 = (bf16[2,96,768]{2,1,0:T(8,128)(2,1)}, bf16[2,96,768]{2,1,0:T(8,128)(2,1)}, u32[]{:S(2)}, u32[]{:S(2)}) collective-permute-start(bf16[2,96,768]{2,1,0:T(8,128)(2,1)} %get-tuple-element.364), channel_id=1, source_target_pairs={{0,2},{1,3},{2,0},{3,1},{4,6},{5,7},{6,4},{7,5},{8,10},{9,11},{10,... | collective-permute-start | bytes 884744 | tf_op jit(solution)/shard_map/ppermute | solution.py:270
  439.6 21.9 %collective-permute-start.55 = (bf16[4,96,2304]{2,1,0:T(8,128)(2,1)}, bf16[4,96,2304]{2,1,0:T(8,128)(2,1)S(1)}, u32[]{:S(2)}, u32[]{:S(2)}) collective-permute-start(bf16[4,96,2304]{2,1,0:T(8,128)(2,1)} %add_convert_fusion), channel_id=1, source_target_pairs={{0,1},{1,0},{2,3},{3,2},{4,5},{5,4},{6,7},{7,6},{8,9},{9,8},{10,11... | collective-permute-start | bytes 5308424 | tf_op jit(solution)/shard_map/ppermute | solution.py:270
  461.4 39.6 %collective-permute-start.58 = (bf16[8,48,2688]{2,1,0:T(8,128)(2,1)}, bf16[8,48,2688]{2,1,0:T(8,128)(2,1)}, u32[]{:S(2)}, u32[]{:S(2)}) collective-permute-start(bf16[8,48,2688]{2,1,0:T(8,128)(2,1)} %get-tuple-element.256), channel_id=1, source_target_pairs={{0,2},{1,3},{2,0},{3,1},{4,6},{5,7},{6,4},{7,5},{8,10},{9,11},{10,... | collective-permute-start | bytes 6193160 | tf_op jit(solution)/shard_map/ppermute | solution.py:270
  465.2 35.8 %collective-permute-start.60 = (bf16[2,96,2304]{2,1,0:T(8,128)(2,1)}, bf16[2,96,2304]{2,1,0:T(8,128)(2,1)}, u32[]{:S(2)}, u32[]{:S(2)}) collective-permute-start(bf16[2,96,2304]{2,1,0:T(8,128)(2,1)} %add_convert_fusion.2), channel_id=1, source_target_pairs={{0,4},{1,5},{2,6},{3,7},{4,0},{5,1},{6,2},{7,3},{8,12},{9,13},{10,... | collective-permute-start | bytes 2654216 | tf_op jit(solution)/shard_map/ppermute | solution.py:270
  465.8 35.3 %collective-permute-start.61 = (bf16[4,192,768]{2,1,0:T(8,128)(2,1)}, bf16[4,192,768]{2,1,0:T(8,128)(2,1)}, u32[]{:S(2)}, u32[]{:S(2)}) collective-permute-start(bf16[4,192,768]{2,1,0:T(8,128)(2,1)} %get-tuple-element.259), channel_id=1, source_target_pairs={{0,4},{1,5},{2,6},{3,7},{4,0},{5,1},{6,2},{7,3},{8,12},{9,13},{10,... | collective-permute-start | bytes 3538952 | tf_op jit(solution)/shard_map/ppermute | solution.py:270
  481.7 18.1 %collective-permute-start.59 = (bf16[2,96,768]{2,1,0:T(8,128)(2,1)}, bf16[2,96,768]{2,1,0:T(8,128)(2,1)S(1)}, u32[]{:S(2)}, u32[]{:S(2)}) collective-permute-start(bf16[2,96,768]{2,1,0:T(8,128)(2,1)} %get-tuple-element.362), channel_id=1, source_target_pairs={{0,1},{1,0},{2,3},{3,2},{4,5},{5,4},{6,7},{7,6},{8,9},{9,8},{10,11... | collective-permute-start | bytes 884744 | tf_op jit(solution)/shard_map/ppermute | solution.py:270
  491.7 30.8 %collective-permute-start.57 = (bf16[8,48,1152]{2,1,0:T(8,128)(2,1)}, bf16[8,48,1152]{2,1,0:T(8,128)(2,1)}, u32[]{:S(2)}, u32[]{:S(2)}) collective-permute-start(bf16[8,48,1152]{2,1,0:T(8,128)(2,1)} %get-tuple-element.254), channel_id=1, source_target_pairs={{0,2},{1,3},{2,0},{3,1},{4,6},{5,7},{6,4},{7,5},{8,10},{9,11},{10,... | collective-permute-start | bytes 2654216 | tf_op jit(solution)/shard_map/ppermute | solution.py:270
  499.8 30.8 %collective-permute-start.70 = (bf16[1,96,768]{2,1,0:T(8,128)(2,1)}, bf16[1,96,768]{2,1,0:T(8,128)(2,1)}, u32[]{:S(2)}, u32[]{:S(2)}) collective-permute-start(bf16[1,96,768]{2,1,0:T(8,128)(2,1)} %add_convert_fusion.19), channel_id=1, source_target_pairs={{0,8},{1,9},{2,10},{3,11},{4,12},{5,13},{6,14},{7,15},{8,0},{9,1},... | collective-permute-start | bytes 442376 | tf_op jit(solution)/shard_map/ppermute | solution.py:270
  503.5 23.0 %collective-permute-start.62 = (bf16[4,48,2688]{2,1,0:T(8,128)(2,1)}, bf16[4,48,2688]{2,1,0:T(8,128)(2,1)}, u32[]{:S(2)}, u32[]{:S(2)}) collective-permute-start(bf16[4,48,2688]{2,1,0:T(8,128)(2,1)} %add_convert_fusion.1), channel_id=1, source_target_pairs={{0,4},{1,5},{2,6},{3,7},{4,0},{5,1},{6,2},{7,3},{8,12},{9,13},{10,... | collective-permute-start | bytes 3096584 | tf_op jit(solution)/shard_map/ppermute | solution.py:270
  514.5 21.9 %collective-permute-start.71 = (bf16[1,96,2304]{2,1,0:T(8,128)(2,1)}, bf16[1,96,2304]{2,1,0:T(8,128)(2,1)}, u32[]{:S(2)}, u32[]{:S(2)}) collective-permute-start(bf16[1,96,2304]{2,1,0:T(8,128)(2,1)} %add_convert_fusion.11), channel_id=1, source_target_pairs={{0,8},{1,9},{2,10},{3,11},{4,12},{5,13},{6,14},{7,15},{8,0},{9,1},... | collective-permute-start | bytes 1327112 | tf_op jit(solution)/shard_map/ppermute | solution.py:270
  527.6 14.6 %collective-permute-start.65 = (bf16[4,48,1152]{2,1,0:T(8,128)(2,1)S(1)}, bf16[4,48,1152]{2,1,0:T(8,128)(2,1)S(1)}, u32[]{:S(2)}, u32[]{:S(2)}) collective-permute-start(bf16[4,48,1152]{2,1,0:T(8,128)(2,1)S(1)} %add_convert_fusion.12), channel_id=1, source_target_pairs={{0,4},{1,5},{2,6},{3,7},{4,0},{5,1},{6,2},{7,3},{8,12},{9,13},{10,... | collective-permute-start | bytes 1327112 | tf_op jit(solution)/shard_map/ppermute | solution.py:270
  538.3 18.7 %collective-permute-start.72 = (bf16[2,48,2688]{2,1,0:T(8,128)(2,1)S(1)}, bf16[2,48,2688]{2,1,0:T(8,128)(2,1)S(1)}, u32[]{:S(2)}, u32[]{:S(2)}) collective-permute-start(bf16[2,48,2688]{2,1,0:T(8,128)(2,1)S(1)} %add_convert_fusion.9), channel_id=1, source_target_pairs={{0,1},{1,0},{2,3},{3,2},{4,5},{5,4},{6,7},{7,6},{8,9},{9,8},{10,11... | collective-permute-start | bytes 1548296 | tf_op jit(solution)/shard_map/ppermute | solution.py:270
  546.9 17.7 %collective-permute-start.77 = (bf16[2,48,1152]{2,1,0:T(8,128)(2,1)S(1)}, bf16[2,48,1152]{2,1,0:T(8,128)(2,1)S(1)}, u32[]{:S(2)}, u32[]{:S(2)}) collective-permute-start(bf16[2,48,1152]{2,1,0:T(8,128)(2,1)S(1)} %add_convert_fusion.17), channel_id=1, source_target_pairs={{0,1},{1,0},{2,3},{3,2},{4,5},{5,4},{6,7},{7,6},{8,9},{9,8},{10,11... | collective-permute-start | bytes 663560 | tf_op jit(solution)/shard_map/ppermute | solution.py:270
  551.3 15.2 %collective-permute-start.80 = (bf16[192,768]{1,0:T(8,128)(2,1)S(1)}, bf16[192,768]{1,0:T(8,128)(2,1)S(1)}, u32[]{:S(2)}, u32[]{:S(2)}) collective-permute-start(bf16[192,768]{1,0:T(8,128)(2,1)S(1)} %bitcast_convert_fusion.1), channel_id=1, source_target_pairs={{8,0},{9,1},{10,2},{11,3},{12,4},{13,5},{14,6},{15,7},{16,24},{17,... | collective-permute-start | bytes 884744 | tf_op jit(solution)/shard_map/ppermute | solution.py:270
  556.1 31.1 %collective-permute-start.84 = (bf16[96,2304]{1,0:T(8,128)(2,1)S(1)}, bf16[96,2304]{1,0:T(8,128)(2,1)S(1)}, u32[]{:S(2)}, u32[]{:S(2)}) collective-permute-start(bf16[96,2304]{1,0:T(8,128)(2,1)S(1)} %fusion.45), channel_id=1, source_target_pairs={{0,16},{16,0},{1,17},{17,1},{2,18},{18,2},{3,19},{19,3},{4,20},{20... | collective-permute-start | bytes 1327112 | tf_op jit(solution)/shard_map/ppermute | solution.py:256
  560.1 17.0 %collective-permute-start.78 = (bf16[1,48,2688]{2,1,0:T(8,128)(2,1)S(1)}, bf16[1,48,2688]{2,1,0:T(8,128)(2,1)S(1)}, u32[]{:S(2)}, u32[]{:S(2)}) collective-permute-start(bf16[1,48,2688]{2,1,0:T(8,128)(2,1)S(1)} %add_convert_fusion.16), channel_id=1, source_target_pairs={{0,8},{1,9},{2,10},{3,11},{4,12},{5,13},{6,14},{7,15},{8,0},{9,1},... | collective-permute-start | bytes 774152 | tf_op jit(solution)/shard_map/ppermute | solution.py:270
  565.6 13.9 %collective-permute-start.79 = (bf16[1,48,1152]{2,1,0:T(8,128)(2,1)S(1)}, bf16[1,48,1152]{2,1,0:T(8,128)(2,1)S(1)}, u32[]{:S(2)}, u32[]{:S(2)}) collective-permute-start(bf16[1,48,1152]{2,1,0:T(8,128)(2,1)S(1)} %add_convert_fusion.21), channel_id=1, source_target_pairs={{0,8},{1,9},{2,10},{3,11},{4,12},{5,13},{6,14},{7,15},{8,0},{9,1},... | collective-permute-start | bytes 331784 | tf_op jit(solution)/shard_map/ppermute | solution.py:270
  (233 other events, 1923.8 us)

commit v4 on v3

--- a/solution.py
+++ b/solution.py
@@ -383,18 +383,14 @@
 
 
 def split_kernel(half, count, table, *refs):
-    step = pl.program_id(0)
     send, keep = refs[-2:]
-
-    def store(out):
-        base = 0
+    rows = refs[0].shape[0] // (2 * half)
+    for index in range(2 * half):
+        place, base = table[index], 0
         for ref in refs[:count]:
-            width = ref.shape[1]
-            out[0, :, base : base + width] = ref[...]
-            base += width
-
-    pl.when(step < half)(lambda: store(send))
-    pl.when(step >= half)(lambda: store(keep))
+            block = ref[pl.ds(pl.multiple_of(place * rows, 16), rows), :]
+            (keep if index < half else send)[index % half, :, base : base + ref.shape[1]] = block
+            base += ref.shape[1]
 
 
 def split_stack(grads, table, count, into=None):
@@ -409,20 +405,15 @@
     full = width if into is None else into[0].shape[2]
     shape = jax.ShapeDtypeStruct((half, rows, full), BF16)
     into = [] if into is None else list(into)
+    half_spec = pl.BlockSpec((half, rows, width), lambda j, t: (0, 0, 0))
     return pl.pallas_call(
         functools.partial(split_kernel, half, len(grads)),
         grid_spec=pltpu.PrefetchScalarGridSpec(
             num_scalar_prefetch=1,
-            grid=(count,),
-            in_specs=[
-                pl.BlockSpec((rows, grad.shape[1]), lambda j, t: (t[jnp.where(j < half, j + half, j - half)], 0))
-                for grad in grads
-            ]
+            grid=(1,),
+            in_specs=[pl.BlockSpec(grad.shape, lambda j, t: (0, 0)) for grad in grads]
             + [pl.BlockSpec(memory_space=pl.ANY) for _ in into],
-            out_specs=[
-                pl.BlockSpec((1, rows, width), lambda j, t: (jnp.minimum(j, half - 1), 0, 0)),
-                pl.BlockSpec((1, rows, width), lambda j, t: (jnp.maximum(j - half, 0), 0, 0)),
-            ],
+            out_specs=[half_spec, half_spec],
         ),
         out_shape=[shape, shape],
         input_output_aliases={1 + len(grads) + k: k for k in range(len(into))},
@@ -959,7 +950,8 @@
     rises, falls = (None, -1, -2), (-1, None, -2)
     order_l = [(bits - 1,) + orders(size, middle)[which] for which, middle in enumerate((falls, rises))]
     order_g = [(bits - 1,) + orders(size, middle)[which] for which, middle in enumerate((rises, falls))]
-    table, table_g = placement(order_l, every), placement(order_g, every)
+    gather_g = [(bits - 1,) + order for order in orders(size, rises)]
+    table, table_g, places_g = (placement(order, every) for order in (order_l, gather_g, order_g))
     side_l = half_l + half_g
     stream_l = fresh(
         gather_all(
@@ -972,8 +964,8 @@
         )
     )
     stream_down_l = fresh(gather_core(down_l, lows_last, below))
-    stream_g = fresh(gather_all(own_heads(qkv_g), order_g, False))
-    stream_out_g = fresh(gather_all(half_of(out_g, core), order_g, False))
+    stream_g = fresh(gather_all(own_heads(qkv_g), gather_g, False))
+    stream_out_g = fresh(gather_all(half_of(out_g, core), gather_g, False))
     square = square_columns(half_of(up_g, core))
     one_two = jnp.where(is_first, square[2], square[1])
     two_one = jnp.where(is_first, square[1], square[2])
@@ -1080,7 +1072,7 @@
     grad_hidden_gb = grad_hidden_g.astype(BF16)
     mine_gb, theirs_gb = half_of(grad_hidden_gb, core), half_of(grad_hidden_gb, 1 - core)
     grad_out_g = mm_tn(mixture_g, mine_gb).astype(BF16)
-    stream_out_g = fresh(scatter_all(split_stack([grad_out_g], table_g, size), order_g))
+    stream_out_g = fresh(scatter_all(split_stack([grad_out_g], places_g, size), order_g))
     grad_mixture_g = (
         mm_nt(mine_gb, half_of(out_wg, core, 0)) + mm_nt(theirs_gb, half_of(out_theirs_g, core, 0))
     ).astype(BF16)
@@ -1089,7 +1081,7 @@
     stream_out = fresh(scatter_in_square(partial_g.reshape(4, slots, half_l)))
     grad_mixture_g = advance([stream_out_g, stream_out], grad_mixture_g)
     grad_projected_g = attention_backward(projected_g, bias_g, lse_g, own_mixture_g, grad_mixture_g)
-    part, halves = qkv_wg.pullback(normed_g, grad_projected_g, table_g)
+    part, halves = qkv_wg.pullback(normed_g, grad_projected_g, places_g)
     stream_g = fresh(scatter_all(halves, order_g))
     part = advance([stream_g, stream_out, stream_out_g, stream_down_g], part)
     part = summed_cores(part)

time: 600 us -> 585 us (0.975)
  Pallas kernels: 120 us -> 111 us
  starting transfers between devices: 101 us -> 94.1 us
    pallas_call x5, Pallas kernels: 17.5 us -> 8.26 us  [split_stack(): pl.pallas_call(functools.partial(split_kernel, half, len(grads)), grid_sp...]
    unnamed x412 -> x410, local copies, waits for them, and re-layouts: 36.7 us -> 37.4 us
  transfers between devices with their start and end apart: 88 -> 88, of which waited for: 27 -> 28; matrix products, arithmetic and copies ran while one was open for 24% -> 25% of each run, Pallas kernels for 20% -> 19%
where the time goes in v4:
time: 585 us; the launch traced here: 578 us
  waiting for transfers between devices  161 us (28%)
  other arithmetic  111 us (19%)
  Pallas kernels  111 us (19%)
  starting transfers between devices  94.1 us (16%)
  local copies, waits for them, and re-layouts  57.8 us (10%)
  matrix products  39 us (7%)
    ppermute x57, waiting for transfers between devices, exchange(): lax.ppermute(part, ('section', 'dp'), pairs)  154 us
    ppermute x57, starting transfers between devices, exchange(): lax.ppermute(part, ('section', 'dp'), pairs)  66.8 us
    unnamed x410, local copies, waits for them, and re-layouts  37.4 us
    convert_element_type x15, other arithmetic, halving(): outgoing = total_of([term[half:] for term in terms]).astype(BF16)  27.9 us
    pallas_call x3, Pallas kernels, product(): pl.pallas_call(functools.partial(product_kernel, self.rows, 4, gelu), gri...  22.5 us
    ppermute x24, starting transfers between devices, swap(): return lax.ppermute(array, 'section', [(0, 1), (1, 0)])  19.7 us
    pallas_call x2, Pallas kernels, attention_backward(): pl.pallas_call(functools.partial(attention_backward_kernel, rows, window)...  18.2 us
    pallas_call x1, Pallas kernels, feed_forward_pullback(): pl.pallas_call(functools.partial(feed_forward_kernel, self.rows), grid_sp...  17.8 us
  transfers between devices with their start and end apart: 88, of which 28 were waited for; matrix products, arithmetic and copies ran while one was open for 25% of the time, Pallas kernels for 19%

profile of v4, /device:TPU:1, one launch (start us, length us, event | category | flops | bytes accessed | tf_op | source)
XLA Modules:
  0.0 578.2 jit_solution(16887862773473409679)
XLA Ops:
  7.6 3.2 collective-permute-start.1
  18.4 10.2 %collective-permute-done.1 = bf16[1,48,4224]{2,1,0:T(8,128)(2,1)S(1)} collective-permute-done((bf16[1,48,4224]{2,1,0:T(8,128)(2,1)S(1)}, bf16[1,48,4224]{2,1,0:T(8,128)(2,1)S(1)}, u32[]{:S(2)}, u32[]{:S(2)}) %collective-permute-start.1) | collective-permute-done | bytes 405536 | tf_op jit(solution)/shard_map/ppermute | solution.py:270
  37.1 4.0 collective-permute-done.4
  51.4 7.0 %collective-permute-done.7 = bf16[1,96,2304]{2,1,0:T(8,128)(2,1)} collective-permute-done((bf16[1,96,2304]{2,1,0:T(8,128)(2,1)}, bf16[1,96,2304]{2,1,0:T(8,128)(2,1)}, u32[]{:S(2)}, u32[]{:S(2)}) %collective-permute-start.7) | collective-permute-done | bytes 442400 | tf_op jit(solution)/shard_map/ppermute | solution.py:270
  58.4 11.0 %collective-permute-done.8 = bf16[1,192,384]{2,1,0:T(8,128)(2,1)S(1)} collective-permute-done((bf16[1,192,384]{2,1,0:T(8,128)(2,1)}, bf16[1,192,384]{2,1,0:T(8,128)(2,1)S(1)}, u32[]{:S(2)}, u32[]{:S(2)}) %collective-permute-start.8) | collective-permute-done | bytes 147488 | tf_op jit(solution)/shard_map/ppermute | solution.py:270
  74.6 3.2 collective-permute-start.12
  85.9 10.3 %collective-permute-done.13 = bf16[1,192,768]{2,1,0:T(8,128)(2,1)} collective-permute-done((bf16[1,192,768]{2,1,0:T(8,128)(2,1)}, bf16[1,192,768]{2,1,0:T(8,128)(2,1)}, u32[]{:S(2)}, u32[]{:S(2)}) %collective-permute-start.13) | collective-permute-done | bytes 294944 | tf_op jit(solution)/shard_map/ppermute | solution.py:270
  96.3 14.7 %collective-permute-done.14 = bf16[2,192,384]{2,1,0:T(8,128)(2,1)} collective-permute-done((bf16[2,192,384]{2,1,0:T(8,128)(2,1)}, bf16[2,192,384]{2,1,0:T(8,128)(2,1)}, u32[]{:S(2)}, u32[]{:S(2)}) %collective-permute-start.14) | collective-permute-done | bytes 294944 | tf_op jit(solution)/shard_map/ppermute | solution.py:270
  117.1 3.1 collective-permute-start.19
  120.1 2.8 pad_maximum_fusion.3
  126.3 5.8 %shard_map.452.q_ref.k_ref.v_ref = bf16[1024,1152]{1,0:T(8,128)(2,1)} custom-call(s32[16]{0:T(128)S(1)} %get-tuple-element.404.table.places, bf16[1024,768]{1,0:T(8,128)(2,1)S(1)} %fusion.2.x_ref, bf16[4,48,4224]{2,1,0:T(8,128)(2,1)S(1)} %pad_maximum_fusion.4.refs_0_, bf16[4,48,4224]{2,1,0:T(8,128)(2,1)S(1)} %collective-permute-done.6.refs_1_, ...), custom_call_target="tpu_custom_call" | custom-call | tf_op jit(solution)/shard_map/pallas_call | solution.py:568
  135.0 9.5 %shard_map.453 = (bf16[1024,384]{1,0:T(8,128)(2,1)S(1)}, f32[3,2,1024]{2,1,0:T(2,128)S(1)}) custom-call(bf16[1024,1152]{1,0:T(8,128)(2,1)S(1)} %copy-done.3, bf16[1024,1152]{1,0:T(8,128)(2,1)S(1)} %copy-done.3, bf16[1024,1152]{1,0:T(8,128)(2,1)S(1)} %copy-done.3, f32[1024,1]{1,0:T(8,128)S(1)} %fusion.44.bias_ref), custom_call_target="tpu_custom_call" | custom-call | tf_op jit(solution)/shard_map/pallas_call | solution.py:210
  144.5 16.2 %collective-permute-done.19 = bf16[1,96,768]{2,1,0:T(8,128)(2,1)S(1)} collective-permute-done((bf16[1,96,768]{2,1,0:T(8,128)(2,1)S(1)}, bf16[1,96,768]{2,1,0:T(8,128)(2,1)S(1)}, u32[]{:S(2)}, u32[]{:S(2)}) %collective-permute-start.19) | collective-permute-done | bytes 147488 | tf_op jit(solution)/shard_map/ppermute | solution.py:270
  168.1 2.8 pad_maximum_fusion.refs_0_.refs_1_
  176.6 10.2 %shard_map.454 = (bf16[1024,1536]{1,0:T(8,128)(2,1)}, bf16[1024,1536]{1,0:T(8,128)(2,1)}) custom-call(s32[16]{0:T(128)S(1)} %get-tuple-element.404.table.places, bf16[1024,768]{1,0:T(8,128)(2,1)S(1)} %multiply_convert_fusion.x_ref, bf16[4,48,4224]{2,1,0:T(8,128)(2,1)S(1)} %copy-done.5, bf16[4,48,4224]{2,1,0:T(8,128)(2,1)S(1)} %copy-done.8, ...), custom_call_target="tpu_custom_call" | custom-call | flops 99999997952 | tf_op jit(solution)/shard_map/pallas_call | solution.py:568
  187.7 5.3 fusion.131
  206.5 9.0 %collective-permute-done.29 = bf16[4,96,768]{2,1,0:T(8,128)(2,1)S(1)} collective-permute-done((bf16[4,96,768]{2,1,0:T(8,128)(2,1)S(1)}, bf16[4,96,768]{2,1,0:T(8,128)(2,1)S(1)}, u32[]{:S(2)}, u32[]{:S(2)}) %collective-permute-start.29) | collective-permute-done | bytes 589856 | tf_op jit(solution)/shard_map/ppermute | solution.py:270
  215.5 13.1 %collective-permute-done.30.refs_1_ = bf16[8,96,768]{2,1,0:T(8,128)(2,1)S(1)} collective-permute-done((bf16[8,96,768]{2,1,0:T(8,128)(2,1)S(1)}, bf16[8,96,768]{2,1,0:T(8,128)(2,1)S(1)}, u32[]{:S(2)}, u32[]{:S(2)}) %collective-permute-start.30) | collective-permute-done | bytes 1179680 | tf_op jit(solution)/shard_map/ppermute | solution.py:270
  238.3 6.5 %shard_map.456.q_ref.k_ref.v_ref = bf16[192,2304]{1,0:T(8,128)(2,1)S(1)} custom-call(s32[16]{0:T(128)S(1)} %get-tuple-element.403.table, bf16[192,1536]{1,0:T(8,128)(2,1)S(1)} %multiply_convert_fusion.2.x_ref, bf16[8,96,2304]{2,1,0:T(8,128)(2,1)S(1)} %pad_maximum_fusion.refs_0_.refs_1_, bf16[8,96,2304]{2,1,0:T(8,128)(2,1)S(1)} %pad_maximum_fusion.refs_0_.refs_1_, ...), custom_call_target="tpu_custom_call" | custom-call | tf_op jit(solution)/shard_map/pallas_call | solution.py:568
  244.9 4.6 shard_map.457
  254.8 3.6 collective-permute-done.33
  264.8 4.6 collective-permute-done.35
  270.4 8.2 %collective-permute-done.36 = bf16[2,192,768]{2,1,0:T(8,128)(2,1)S(1)} collective-permute-done((bf16[2,192,768]{2,1,0:T(8,128)(2,1)S(1)}, bf16[2,192,768]{2,1,0:T(8,128)(2,1)S(1)}, u32[]{:S(2)}, u32[]{:S(2)}) %collective-permute-start.36) | collective-permute-done | bytes 589856 | tf_op jit(solution)/shard_map/ppermute | solution.py:270
  301.0 3.2 convolution_convert_fusion.3.refs_0_
  318.4 2.7 collective-permute-done.40
  323.6 3.7 collective-permute-done.41
  341.8 4.5 shard_map.464
  347.0 12.0 %shard_map.465 = (bf16[192,1536]{1,0:T(8,128)(2,1)S(1)}, bf16[8,96,2304]{2,1,0:T(8,128)(2,1)}, bf16[8,96,2304]{2,1,0:T(8,128)(2,1)}) custom-call(s32[16]{0:T(128)S(1)} %get-tuple-element.403.table, s32[16]{0:T(128)S(1)} %get-tuple-element.402.table.places, bf16[192,1536]{1,0:T(8,128)(2,1)S(1)} %copy-done.20, bf16[8,96,2304]{2,1,0:T(8,128)(2,1)} %copy-done.2, ...), custom_call_target="tpu_custom_call" | custom-call | tf_op jit(solution)/shard_map/pallas_call | solution.py:672
  366.1 5.8 %collective-permute-start.48 = (bf16[384,768]{1,0:T(8,128)(2,1)}, bf16[384,768]{1,0:T(8,128)(2,1)}, u32[]{:S(2)}, u32[]{:S(2)}) collective-permute-start(bf16[384,768]{1,0:T(8,128)(2,1)} %bitcast_convert_fusion), channel_id=1, source_target_pairs={{8,0},{9,1},{10,2},{11,3},{12,4},{13,5},{14,6},{15,7},{16,24},{17,... | collective-permute-start | bytes 1769480 | tf_op jit(solution)/shard_map/ppermute | solution.py:270
  383.4 5.7 fusion.15
  390.6 17.8 %shard_map.466 = (bf16[1024,768]{1,0:T(8,128)(2,1)S(1)}, bf16[1536,768]{1,0:T(8,128)(2,1)}, bf16[8,48,2688]{2,1,0:T(8,128)(2,1)}, bf16[8,48,2688]{2,1,0:T(8,128)(2,1)}) custom-call(s32[16]{0:T(128)S(1)} %get-tuple-element.404.table.places, s32[16]{0:T(128)S(1)} %get-tuple-element.404.table.places, bf16[1024,768]{1,0:T(8,128)(2,1)S(1)} %copy-done.18, ...), custom_call_target="tpu_custom_call" | custom-call | tf_op jit(solution)/shard_map/pallas_call | solution.py:594
  420.7 3.3 add_convert_fusion
  435.3 10.6 %collective-permute-done.55 = bf16[4,96,2304]{2,1,0:T(8,128)(2,1)S(1)} collective-permute-done((bf16[4,96,2304]{2,1,0:T(8,128)(2,1)}, bf16[4,96,2304]{2,1,0:T(8,128)(2,1)S(1)}, u32[]{:S(2)}, u32[]{:S(2)}) %collective-permute-start.55) | collective-permute-done | bytes 1769504 | tf_op jit(solution)/shard_map/ppermute | solution.py:270
  447.1 2.7 add_convert_fusion.2
  450.8 13.7 %shard_map.469 = (bf16[1024,384]{1,0:T(8,128)(2,1)S(1)}, bf16[1024,384]{1,0:T(8,128)(2,1)S(1)}, bf16[1024,384]{1,0:T(8,128)(2,1)S(1)}) custom-call(bf16[1024,1152]{1,0:T(8,128)(2,1)} %shard_map.452.q_ref.k_ref.v_ref, bf16[1024,1152]{1,0:T(8,128)(2,1)} %shard_map.452.q_ref.k_ref.v_ref, bf16[1024,1152]{1,0:T(8,128)(2,1)} %shard_map.452.q_ref.k_ref.v_ref, ...), custom_call_target="tpu_custom_call" | custom-call | flops 99999997952 | tf_op jit(solution)/shard_map/pallas_call | solution.py:230
  471.3 5.1 shard_map.470
  477.4 5.7 shard_map.471
  489.2 2.9 collective-permute-start.64
  500.4 3.0 fusion.5
  503.7 3.7 fusion.30
  507.4 2.9 collective-permute-done.62
  516.9 4.3 collective-permute-done.71
  523.5 3.6 collective-permute-done.69
  527.2 2.8 collective-permute-start.74
  536.2 4.7 collective-permute-start.80
  545.1 3.3 collective-permute-start.78
  551.5 10.5 %collective-permute-done.78 = bf16[1,48,2688]{2,1,0:T(8,128)(2,1)S(1)} collective-permute-done((bf16[1,48,2688]{2,1,0:T(8,128)(2,1)S(1)}, bf16[1,48,2688]{2,1,0:T(8,128)(2,1)S(1)}, u32[]{:S(2)}, u32[]{:S(2)}) %collective-permute-start.78) | collective-permute-done | bytes 258080 | tf_op jit(solution)/shard_map/ppermute | solution.py:270
  565.3 3.5 collective-permute-start.81
  (754 shorter events, 263.1 us)
Async XLA Ops:
  7.6 21.0 %collective-permute-start.1 = (bf16[1,48,4224]{2,1,0:T(8,128)(2,1)S(1)}, bf16[1,48,4224]{2,1,0:T(8,128)(2,1)S(1)}, u32[]{:S(2)}, u32[]{:S(2)}) collective-permute-start(bf16[1,48,4224]{2,1,0:T(8,128)(2,1)S(1)} %bitcast.160), channel_id=1, source_target_pairs={{0,8},{1,9},{2,10},{3,11},{4,12},{5,13},{6,14},{7,15},{8,0},{9,1},... | collective-permute-start | bytes 1216520 | tf_op jit(solution)/shard_map/ppermute | solution.py:270
  29.6 14.8 %collective-permute-start.2 = (bf16[2,48,4224]{2,1,0:T(8,128)(2,1)}, bf16[2,48,4224]{2,1,0:T(8,128)(2,1)S(1)}, u32[]{:S(2)}, u32[]{:S(2)}) collective-permute-start(bf16[2,48,4224]{2,1,0:T(8,128)(2,1)} %pad_maximum_fusion.28), channel_id=1, source_target_pairs={{0,1},{1,0},{2,3},{3,2},{4,5},{5,4},{6,7},{7,6},{8,9},{9,8},{10,11... | collective-permute-start | bytes 2433032 | tf_op jit(solution)/shard_map/ppermute | solution.py:270
  44.6 24.9 %collective-permute-start.6 = (bf16[4,48,4224]{2,1,0:T(8,128)(2,1)S(1)}, bf16[4,48,4224]{2,1,0:T(8,128)(2,1)S(1)}, u32[]{:S(2)}, u32[]{:S(2)}) collective-permute-start(bf16[4,48,4224]{2,1,0:T(8,128)(2,1)S(1)} %pad_maximum_fusion.4.refs_0_), channel_id=1, source_target_pairs={{0,4},{1,5},{2,6},{3,7},{4,0},{5,1},{6,2},{7,3},{8,12},{9,13},{10,... | collective-permute-start | bytes 4866056 | tf_op jit(solution)/shard_map/ppermute | solution.py:270
  49.9 19.5 %collective-permute-start.9 = (bf16[2,96,768]{2,1,0:T(8,128)(2,1)S(1)}, bf16[2,96,768]{2,1,0:T(8,128)(2,1)S(1)}, u32[]{:S(2)}, u32[]{:S(2)}) collective-permute-start(bf16[2,96,768]{2,1,0:T(8,128)(2,1)S(1)} %get-tuple-element.370), channel_id=1, source_target_pairs={{0,2},{1,3},{2,0},{3,1},{4,6},{5,7},{6,4},{7,5},{8,10},{9,11},{10,... | collective-permute-start | bytes 884744 | tf_op jit(solution)/shard_map/ppermute | solution.py:270
  51.2 18.3 %collective-permute-start.8 = (bf16[1,192,384]{2,1,0:T(8,128)(2,1)}, bf16[1,192,384]{2,1,0:T(8,128)(2,1)S(1)}, u32[]{:S(2)}, u32[]{:S(2)}) collective-permute-start(bf16[1,192,384]{2,1,0:T(8,128)(2,1)} %dynamic-slice_bitcast_fusion.7), channel_id=1, source_target_pairs={{0,1},{1,0},{2,3},{3,2},{4,5},{5,4},{6,7},{7,6},{8,9},{9,8},{10,11... | collective-permute-start | bytes 442376 | tf_op jit(solution)/shard_map/ppermute | solution.py:270
  70.2 40.7 %collective-permute-start.10 = (bf16[4,48,4224]{2,1,0:T(8,128)(2,1)S(1)}, bf16[4,48,4224]{2,1,0:T(8,128)(2,1)}, u32[]{:S(2)}, u32[]{:S(2)}) collective-permute-start(bf16[4,48,4224]{2,1,0:T(8,128)(2,1)S(1)} %pad_maximum_fusion.4.refs_0_), channel_id=1, source_target_pairs={{0,2},{1,3},{2,0},{3,1},{4,6},{5,7},{6,4},{7,5},{8,10},{9,11},{10,... | collective-permute-start | bytes 4866056 | tf_op jit(solution)/shard_map/ppermute | solution.py:270
  71.2 39.8 %collective-permute-start.11 = (bf16[4,48,4224]{2,1,0:T(8,128)(2,1)S(1)}, bf16[4,48,4224]{2,1,0:T(8,128)(2,1)}, u32[]{:S(2)}, u32[]{:S(2)}) collective-permute-start(bf16[4,48,4224]{2,1,0:T(8,128)(2,1)S(1)} %collective-permute-done.6.refs_1_), channel_id=1, source_target_pairs={{0,2},{1,3},{2,0},{3,1},{4,6},{5,7},{6,4},{7,5},{8,10},{9,11},{10,... | collective-permute-start | bytes 4866056 | tf_op jit(solution)/shard_map/ppermute | solution.py:270
  74.6 36.3 %collective-permute-start.12 = (bf16[2,96,2304]{2,1,0:T(8,128)(2,1)}, bf16[2,96,2304]{2,1,0:T(8,128)(2,1)}, u32[]{:S(2)}, u32[]{:S(2)}) collective-permute-start(bf16[2,96,2304]{2,1,0:T(8,128)(2,1)} %pad_maximum_fusion.27), channel_id=1, source_target_pairs={{0,4},{1,5},{2,6},{3,7},{4,0},{5,1},{6,2},{7,3},{8,12},{9,13},{10,... | collective-permute-start | bytes 2654216 | tf_op jit(solution)/shard_map/ppermute | solution.py:270
  79.3 17.0 %collective-permute-start.13 = (bf16[1,192,768]{2,1,0:T(8,128)(2,1)}, bf16[1,192,768]{2,1,0:T(8,128)(2,1)}, u32[]{:S(2)}, u32[]{:S(2)}) collective-permute-start(bf16[1,192,768]{2,1,0:T(8,128)(2,1)} %select_bitcast_fusion.1), channel_id=1, source_target_pairs={{0,4},{1,5},{2,6},{3,7},{4,0},{5,1},{6,2},{7,3},{8,12},{9,13},{10,... | collective-permute-start | bytes 884744 | tf_op jit(solution)/shard_map/ppermute | solution.py:270
  80.0 30.9 %collective-permute-start.14 = (bf16[2,192,384]{2,1,0:T(8,128)(2,1)}, bf16[2,192,384]{2,1,0:T(8,128)(2,1)}, u32[]{:S(2)}, u32[]{:S(2)}) collective-permute-start(bf16[2,192,384]{2,1,0:T(8,128)(2,1)} %pad_maximum_fusion.43), channel_id=1, source_target_pairs={{0,2},{1,3},{2,0},{3,1},{4,6},{5,7},{6,4},{7,5},{8,10},{9,11},{10,... | collective-permute-start | bytes 884744 | tf_op jit(solution)/shard_map/ppermute | solution.py:270
  112.1 48.7 %collective-permute-start.16 = (bf16[2,192,768]{2,1,0:T(8,128)(2,1)S(1)}, bf16[2,192,768]{2,1,0:T(8,128)(2,1)S(1)}, u32[]{:S(2)}, u32[]{:S(2)}) collective-permute-start(bf16[2,192,768]{2,1,0:T(8,128)(2,1)S(1)} %pad_maximum_fusion.36), channel_id=1, source_target_pairs={{0,1},{1,0},{2,3},{3,2},{4,5},{5,4},{6,7},{7,6},{8,9},{9,8},{10,11... | collective-permute-start | bytes 1769480 | tf_op jit(solution)/shard_map/ppermute | solution.py:270
  113.1 47.6 %collective-permute-start.17 = (bf16[4,96,768]{2,1,0:T(8,128)(2,1)S(1)}, bf16[4,96,768]{2,1,0:T(8,128)(2,1)S(1)}, u32[]{:S(2)}, u32[]{:S(2)}) collective-permute-start(bf16[4,96,768]{2,1,0:T(8,128)(2,1)S(1)} %pad_maximum_fusion.35), channel_id=1, source_target_pairs={{0,8},{1,9},{2,10},{3,11},{4,12},{5,13},{6,14},{7,15},{8,0},{9,1},... | collective-permute-start | bytes 1769480 | tf_op jit(solution)/shard_map/ppermute | solution.py:270
  115.6 45.2 %collective-permute-start.18 = (bf16[384,768]{1,0:T(8,128)(2,1)S(1)}, bf16[384,768]{1,0:T(8,128)(2,1)S(1)}, u32[]{:S(2)}, u32[]{:S(2)}) collective-permute-start(bf16[384,768]{1,0:T(8,128)(2,1)S(1)} %copy-done.141), channel_id=1, source_target_pairs={{0,8},{1,9},{2,10},{3,11},{4,12},{5,13},{6,14},{7,15},{24,16},{25,... | collective-permute-start | bytes 1769480 | tf_op jit(solution)/shard_map/ppermute | solution.py:270
  117.1 43.7 %collective-permute-start.19 = (bf16[1,96,768]{2,1,0:T(8,128)(2,1)S(1)}, bf16[1,96,768]{2,1,0:T(8,128)(2,1)S(1)}, u32[]{:S(2)}, u32[]{:S(2)}) collective-permute-start(bf16[1,96,768]{2,1,0:T(8,128)(2,1)S(1)} %copy-done.99), channel_id=1, source_target_pairs={{0,8},{1,9},{2,10},{3,11},{4,12},{5,13},{6,14},{7,15},{8,0},{9,1},... | collective-permute-start | bytes 442376 | tf_op jit(solution)/shard_map/ppermute | solution.py:270
  122.9 44.8 %collective-permute-start.15 = (bf16[4,96,2304]{2,1,0:T(8,128)(2,1)}, bf16[4,96,2304]{2,1,0:T(8,128)(2,1)}, u32[]{:S(2)}, u32[]{:S(2)}) collective-permute-start(bf16[4,96,2304]{2,1,0:T(8,128)(2,1)} %pad_maximum_fusion.3), channel_id=1, source_target_pairs={{0,1},{1,0},{2,3},{3,2},{4,5},{5,4},{6,7},{7,6},{8,9},{9,8},{10,11... | collective-permute-start | bytes 5308424 | tf_op jit(solution)/shard_map/ppermute | solution.py:270
  163.0 23.8 %collective-permute-start.22 = (bf16[4,192,768]{2,1,0:T(8,128)(2,1)S(1)}, bf16[4,192,768]{2,1,0:T(8,128)(2,1)S(1)}, u32[]{:S(2)}, u32[]{:S(2)}) collective-permute-start(bf16[4,192,768]{2,1,0:T(8,128)(2,1)S(1)} %pad_maximum_fusion.19.refs_0_.refs_1_), channel_id=1, source_target_pairs={{0,2},{1,3},{2,0},{3,1},{4,6},{5,7},{6,4},{7,5},{8,10},{9,11},{10,... | collective-permute-start | bytes 3538952 | tf_op jit(solution)/shard_map/ppermute | solution.py:270
  165.4 21.4 %collective-permute-start.23 = (bf16[1,384,768]{2,1,0:T(8,128)(2,1)S(1)}, bf16[1,384,768]{2,1,0:T(8,128)(2,1)S(1)}, u32[]{:S(2)}, u32[]{:S(2)}) collective-permute-start(bf16[1,384,768]{2,1,0:T(8,128)(2,1)S(1)} %select_bitcast_fusion.refs_0_), channel_id=1, source_target_pairs={{0,4},{1,5},{2,6},{3,7},{4,0},{5,1},{6,2},{7,3},{8,12},{9,13},{10,... | collective-permute-start | bytes 1769480 | tf_op jit(solution)/shard_map/ppermute | solution.py:270
  167.2 19.6 %collective-permute-start.24 = (bf16[2,96,768]{2,1,0:T(8,128)(2,1)}, bf16[2,96,768]{2,1,0:T(8,128)(2,1)S(1)}, u32[]{:S(2)}, u32[]{:S(2)}) collective-permute-start(bf16[2,96,768]{2,1,0:T(8,128)(2,1)} %pad_maximum_fusion.47), channel_id=1, source_target_pairs={{0,4},{1,5},{2,6},{3,7},{4,0},{5,1},{6,2},{7,3},{8,12},{9,13},{10,... | collective-permute-start | bytes 884744 | tf_op jit(solution)/shard_map/ppermute | solution.py:270
  170.9 58.8 %collective-permute-start.28 = (bf16[8,96,2304]{2,1,0:T(8,128)(2,1)S(1)}, bf16[8,96,2304]{2,1,0:T(8,128)(2,1)}, u32[]{:S(2)}, u32[]{:S(2)}) collective-permute-start(bf16[8,96,2304]{2,1,0:T(8,128)(2,1)S(1)} %pad_maximum_fusion.refs_0_.refs_1_), channel_id=1, source_target_pairs={{0,2},{1,3},{2,0},{3,1},{4,6},{5,7},{6,4},{7,5},{8,10},{9,11},{10,... | collective-permute-start | bytes 10616840 | tf_op jit(solution)/shard_map/ppermute | solution.py:270
  199.9 15.6 %collective-permute-start.29 = (bf16[4,96,768]{2,1,0:T(8,128)(2,1)S(1)}, bf16[4,96,768]{2,1,0:T(8,128)(2,1)S(1)}, u32[]{:S(2)}, u32[]{:S(2)}) collective-permute-start(bf16[4,96,768]{2,1,0:T(8,128)(2,1)S(1)} %pad_maximum_fusion.37), channel_id=1, source_target_pairs={{0,1},{1,0},{2,3},{3,2},{4,5},{5,4},{6,7},{7,6},{8,9},{9,8},{10,11... | collective-permute-start | bytes 1769480 | tf_op jit(solution)/shard_map/ppermute | solution.py:270
  201.2 27.4 %collective-permute-start.30 = (bf16[8,96,768]{2,1,0:T(8,128)(2,1)S(1)}, bf16[8,96,768]{2,1,0:T(8,128)(2,1)S(1)}, u32[]{:S(2)}, u32[]{:S(2)}) collective-permute-start(bf16[8,96,768]{2,1,0:T(8,128)(2,1)S(1)} %pad_maximum_fusion.20.refs_0_), channel_id=1, source_target_pairs={{0,4},{1,5},{2,6},{3,7},{4,0},{5,1},{6,2},{7,3},{8,12},{9,13},{10,... | collective-permute-start | bytes 3538952 | tf_op jit(solution)/shard_map/ppermute | solution.py:270
  230.8 19.2 %collective-permute-start.32 = (bf16[8,96,768]{2,1,0:T(8,128)(2,1)}, bf16[8,96,768]{2,1,0:T(8,128)(2,1)}, u32[]{:S(2)}, u32[]{:S(2)}) collective-permute-start(bf16[8,96,768]{2,1,0:T(8,128)(2,1)} %pad_maximum_fusion.22.refs_0_.refs_1_), channel_id=1, source_target_pairs={{0,2},{1,3},{2,0},{3,1},{4,6},{5,7},{6,4},{7,5},{8,10},{9,11},{10,... | collective-permute-start | bytes 3538952 | tf_op jit(solution)/shard_map/ppermute | solution.py:270
  331.0 28.0 %collective-permute-start.45 = (bf16[1,384,768]{2,1,0:T(8,128)(2,1)}, bf16[1,384,768]{2,1,0:T(8,128)(2,1)}, u32[]{:S(2)}, u32[]{:S(2)}) collective-permute-start(bf16[1,384,768]{2,1,0:T(8,128)(2,1)} %get-tuple-element.212), channel_id=1, source_target_pairs={{0,4},{1,5},{2,6},{3,7},{4,0},{5,1},{6,2},{7,3},{8,12},{9,13},{10,... | collective-permute-start | bytes 1769480 | tf_op jit(solution)/shard_map/ppermute | solution.py:270
  331.9 45.3 %collective-permute-start.49 = (bf16[8,96,768]{2,1,0:T(8,128)(2,1)}, bf16[8,96,768]{2,1,0:T(8,128)(2,1)}, u32[]{:S(2)}, u32[]{:S(2)}) collective-permute-start(bf16[8,96,768]{2,1,0:T(8,128)(2,1)} %get-tuple-element.227), channel_id=1, source_target_pairs={{0,4},{1,5},{2,6},{3,7},{4,0},{5,1},{6,2},{7,3},{8,12},{9,13},{10,... | collective-permute-start | bytes 3538952 | tf_op jit(solution)/shard_map/ppermute | solution.py:270
  340.3 18.8 %collective-permute-start.43 = (bf16[2,192,384]{2,1,0:T(8,128)(2,1)}, bf16[2,192,384]{2,1,0:T(8,128)(2,1)}, u32[]{:S(2)}, u32[]{:S(2)}) collective-permute-start(bf16[2,192,384]{2,1,0:T(8,128)(2,1)} %pad_maximum_fusion.45), channel_id=1, source_target_pairs={{0,2},{1,3},{2,0},{3,1},{4,6},{5,7},{6,4},{7,5},{8,10},{9,11},{10,... | collective-permute-start | bytes 884744 | tf_op jit(solution)/shard_map/ppermute | solution.py:270
  341.2 18.0 %collective-permute-start.44 = (bf16[8,96,768]{2,1,0:T(8,128)(2,1)}, bf16[8,96,768]{2,1,0:T(8,128)(2,1)}, u32[]{:S(2)}, u32[]{:S(2)}) collective-permute-start(bf16[8,96,768]{2,1,0:T(8,128)(2,1)} %get-tuple-element.211), channel_id=1, source_target_pairs={{0,2},{1,3},{2,0},{3,1},{4,6},{5,7},{6,4},{7,5},{8,10},{9,11},{10,... | collective-permute-start | bytes 3538952 | tf_op jit(solution)/shard_map/ppermute | solution.py:270
  359.2 53.2 %collective-permute-start.47 = (bf16[8,96,2304]{2,1,0:T(8,128)(2,1)}, bf16[8,96,2304]{2,1,0:T(8,128)(2,1)}, u32[]{:S(2)}, u32[]{:S(2)}) collective-permute-start(bf16[8,96,2304]{2,1,0:T(8,128)(2,1)} %get-tuple-element.223), channel_id=1, source_target_pairs={{0,2},{1,3},{2,0},{3,1},{4,6},{5,7},{6,4},{7,5},{8,10},{9,11},{10,... | collective-permute-start | bytes 10616840 | tf_op jit(solution)/shard_map/ppermute | solution.py:270
  361.9 15.1 %collective-permute-start.50 = (bf16[192,1536]{1,0:T(8,128)(2,1)S(1)}, bf16[192,1536]{1,0:T(8,128)(2,1)S(1)}, u32[]{:S(2)}, u32[]{:S(2)}) collective-permute-start(bf16[192,1536]{1,0:T(8,128)(2,1)S(1)} %get-tuple-element.228), channel_id=1, source_target_pairs={{0,16},{16,0},{1,17},{17,1},{2,18},{18,2},{3,19},{19,3},{4,20},{20... | collective-permute-start | bytes 1769480 | tf_op jit(solution)/shard_map/ppermute | solution.py:256
  366.1 46.2 %collective-permute-start.48 = (bf16[384,768]{1,0:T(8,128)(2,1)}, bf16[384,768]{1,0:T(8,128)(2,1)}, u32[]{:S(2)}, u32[]{:S(2)}) collective-permute-start(bf16[384,768]{1,0:T(8,128)(2,1)} %bitcast_convert_fusion), channel_id=1, source_target_pairs={{8,0},{9,1},{10,2},{11,3},{12,4},{13,5},{14,6},{15,7},{16,24},{17,... | collective-permute-start | bytes 1769480 | tf_op jit(solution)/shard_map/ppermute | solution.py:270
  374.0 38.4 %collective-permute-start.52 = (bf16[4,96,768]{2,1,0:T(8,128)(2,1)}, bf16[4,96,768]{2,1,0:T(8,128)(2,1)}, u32[]{:S(2)}, u32[]{:S(2)}) collective-permute-start(bf16[4,96,768]{2,1,0:T(8,128)(2,1)} %add_convert_fusion.7), channel_id=1, source_target_pairs={{0,1},{1,0},{2,3},{3,2},{4,5},{5,4},{6,7},{7,6},{8,9},{9,8},{10,11... | collective-permute-start | bytes 1769480 | tf_op jit(solution)/shard_map/ppermute | solution.py:270
  380.4 31.9 %collective-permute-start.51 = (bf16[4,96,768]{2,1,0:T(8,128)(2,1)}, bf16[4,96,768]{2,1,0:T(8,128)(2,1)}, u32[]{:S(2)}, u32[]{:S(2)}) collective-permute-start(bf16[4,96,768]{2,1,0:T(8,128)(2,1)} %add_convert_fusion.8), channel_id=1, source_target_pairs={{0,8},{1,9},{2,10},{3,11},{4,12},{5,13},{6,14},{7,15},{8,0},{9,1},... | collective-permute-start | bytes 1769480 | tf_op jit(solution)/shard_map/ppermute | solution.py:270
  414.5 50.0 %collective-permute-start.53 = (bf16[2,96,768]{2,1,0:T(8,128)(2,1)}, bf16[2,96,768]{2,1,0:T(8,128)(2,1)}, u32[]{:S(2)}, u32[]{:S(2)}) collective-permute-start(bf16[2,96,768]{2,1,0:T(8,128)(2,1)} %add_convert_fusion.14), channel_id=1, source_target_pairs={{0,4},{1,5},{2,6},{3,7},{4,0},{5,1},{6,2},{7,3},{8,12},{9,13},{10,... | collective-permute-start | bytes 884744 | tf_op jit(solution)/shard_map/ppermute | solution.py:270
  418.1 46.5 %collective-permute-start.54 = (bf16[2,96,768]{2,1,0:T(8,128)(2,1)}, bf16[2,96,768]{2,1,0:T(8,128)(2,1)}, u32[]{:S(2)}, u32[]{:S(2)}) collective-permute-start(bf16[2,96,768]{2,1,0:T(8,128)(2,1)} %get-tuple-element.364), channel_id=1, source_target_pairs={{0,2},{1,3},{2,0},{3,1},{4,6},{5,7},{6,4},{7,5},{8,10},{9,11},{10,... | collective-permute-start | bytes 884744 | tf_op jit(solution)/shard_map/ppermute | solution.py:270
  424.0 21.9 %collective-permute-start.55 = (bf16[4,96,2304]{2,1,0:T(8,128)(2,1)}, bf16[4,96,2304]{2,1,0:T(8,128)(2,1)S(1)}, u32[]{:S(2)}, u32[]{:S(2)}) collective-permute-start(bf16[4,96,2304]{2,1,0:T(8,128)(2,1)} %add_convert_fusion), channel_id=1, source_target_pairs={{0,1},{1,0},{2,3},{3,2},{4,5},{5,4},{6,7},{7,6},{8,9},{9,8},{10,11... | collective-permute-start | bytes 5308424 | tf_op jit(solution)/shard_map/ppermute | solution.py:270
  445.9 40.4 %collective-permute-start.58 = (bf16[8,48,2688]{2,1,0:T(8,128)(2,1)}, bf16[8,48,2688]{2,1,0:T(8,128)(2,1)}, u32[]{:S(2)}, u32[]{:S(2)}) collective-permute-start(bf16[8,48,2688]{2,1,0:T(8,128)(2,1)} %get-tuple-element.256), channel_id=1, source_target_pairs={{0,2},{1,3},{2,0},{3,1},{4,6},{5,7},{6,4},{7,5},{8,10},{9,11},{10,... | collective-permute-start | bytes 6193160 | tf_op jit(solution)/shard_map/ppermute | solution.py:270
  449.8 36.5 %collective-permute-start.60 = (bf16[2,96,2304]{2,1,0:T(8,128)(2,1)}, bf16[2,96,2304]{2,1,0:T(8,128)(2,1)}, u32[]{:S(2)}, u32[]{:S(2)}) collective-permute-start(bf16[2,96,2304]{2,1,0:T(8,128)(2,1)} %add_convert_fusion.2), channel_id=1, source_target_pairs={{0,4},{1,5},{2,6},{3,7},{4,0},{5,1},{6,2},{7,3},{8,12},{9,13},{10,... | collective-permute-start | bytes 2654216 | tf_op jit(solution)/shard_map/ppermute | solution.py:270
  450.7 35.6 %collective-permute-start.61 = (bf16[4,192,768]{2,1,0:T(8,128)(2,1)}, bf16[4,192,768]{2,1,0:T(8,128)(2,1)}, u32[]{:S(2)}, u32[]{:S(2)}) collective-permute-start(bf16[4,192,768]{2,1,0:T(8,128)(2,1)} %get-tuple-element.259), channel_id=1, source_target_pairs={{0,4},{1,5},{2,6},{3,7},{4,0},{5,1},{6,2},{7,3},{8,12},{9,13},{10,... | collective-permute-start | bytes 3538952 | tf_op jit(solution)/shard_map/ppermute | solution.py:270
  466.7 18.3 %collective-permute-start.59 = (bf16[2,96,768]{2,1,0:T(8,128)(2,1)}, bf16[2,96,768]{2,1,0:T(8,128)(2,1)S(1)}, u32[]{:S(2)}, u32[]{:S(2)}) collective-permute-start(bf16[2,96,768]{2,1,0:T(8,128)(2,1)} %get-tuple-element.362), channel_id=1, source_target_pairs={{0,1},{1,0},{2,3},{3,2},{4,5},{5,4},{6,7},{7,6},{8,9},{9,8},{10,11... | collective-permute-start | bytes 884744 | tf_op jit(solution)/shard_map/ppermute | solution.py:270
  476.4 30.9 %collective-permute-start.57 = (bf16[8,48,1152]{2,1,0:T(8,128)(2,1)}, bf16[8,48,1152]{2,1,0:T(8,128)(2,1)}, u32[]{:S(2)}, u32[]{:S(2)}) collective-permute-start(bf16[8,48,1152]{2,1,0:T(8,128)(2,1)} %get-tuple-element.254), channel_id=1, source_target_pairs={{0,2},{1,3},{2,0},{3,1},{4,6},{5,7},{6,4},{7,5},{8,10},{9,11},{10,... | collective-permute-start | bytes 2654216 | tf_op jit(solution)/shard_map/ppermute | solution.py:270
  485.0 30.9 %collective-permute-start.70 = (bf16[1,96,768]{2,1,0:T(8,128)(2,1)}, bf16[1,96,768]{2,1,0:T(8,128)(2,1)}, u32[]{:S(2)}, u32[]{:S(2)}) collective-permute-start(bf16[1,96,768]{2,1,0:T(8,128)(2,1)} %add_convert_fusion.19), channel_id=1, source_target_pairs={{0,8},{1,9},{2,10},{3,11},{4,12},{5,13},{6,14},{7,15},{8,0},{9,1},... | collective-permute-start | bytes 442376 | tf_op jit(solution)/shard_map/ppermute | solution.py:270
  488.7 21.6 %collective-permute-start.62 = (bf16[4,48,2688]{2,1,0:T(8,128)(2,1)}, bf16[4,48,2688]{2,1,0:T(8,128)(2,1)}, u32[]{:S(2)}, u32[]{:S(2)}) collective-permute-start(bf16[4,48,2688]{2,1,0:T(8,128)(2,1)} %add_convert_fusion.1), channel_id=1, source_target_pairs={{0,4},{1,5},{2,6},{3,7},{4,0},{5,1},{6,2},{7,3},{8,12},{9,13},{10,... | collective-permute-start | bytes 3096584 | tf_op jit(solution)/shard_map/ppermute | solution.py:270
  499.4 21.8 %collective-permute-start.71 = (bf16[1,96,2304]{2,1,0:T(8,128)(2,1)}, bf16[1,96,2304]{2,1,0:T(8,128)(2,1)}, u32[]{:S(2)}, u32[]{:S(2)}) collective-permute-start(bf16[1,96,2304]{2,1,0:T(8,128)(2,1)} %add_convert_fusion.11), channel_id=1, source_target_pairs={{0,8},{1,9},{2,10},{3,11},{4,12},{5,13},{6,14},{7,15},{8,0},{9,1},... | collective-permute-start | bytes 1327112 | tf_op jit(solution)/shard_map/ppermute | solution.py:270
  511.5 15.6 %collective-permute-start.65 = (bf16[4,48,1152]{2,1,0:T(8,128)(2,1)S(1)}, bf16[4,48,1152]{2,1,0:T(8,128)(2,1)S(1)}, u32[]{:S(2)}, u32[]{:S(2)}) collective-permute-start(bf16[4,48,1152]{2,1,0:T(8,128)(2,1)S(1)} %add_convert_fusion.12), channel_id=1, source_target_pairs={{0,4},{1,5},{2,6},{3,7},{4,0},{5,1},{6,2},{7,3},{8,12},{9,13},{10,... | collective-permute-start | bytes 1327112 | tf_op jit(solution)/shard_map/ppermute | solution.py:270
  523.4 18.6 %collective-permute-start.72 = (bf16[2,48,2688]{2,1,0:T(8,128)(2,1)S(1)}, bf16[2,48,2688]{2,1,0:T(8,128)(2,1)S(1)}, u32[]{:S(2)}, u32[]{:S(2)}) collective-permute-start(bf16[2,48,2688]{2,1,0:T(8,128)(2,1)S(1)} %add_convert_fusion.9), channel_id=1, source_target_pairs={{0,1},{1,0},{2,3},{3,2},{4,5},{5,4},{6,7},{7,6},{8,9},{9,8},{10,11... | collective-permute-start | bytes 1548296 | tf_op jit(solution)/shard_map/ppermute | solution.py:270
  531.8 17.7 %collective-permute-start.77 = (bf16[2,48,1152]{2,1,0:T(8,128)(2,1)S(1)}, bf16[2,48,1152]{2,1,0:T(8,128)(2,1)S(1)}, u32[]{:S(2)}, u32[]{:S(2)}) collective-permute-start(bf16[2,48,1152]{2,1,0:T(8,128)(2,1)S(1)} %add_convert_fusion.17), channel_id=1, source_target_pairs={{0,1},{1,0},{2,3},{3,2},{4,5},{5,4},{6,7},{7,6},{8,9},{9,8},{10,11... | collective-permute-start | bytes 663560 | tf_op jit(solution)/shard_map/ppermute | solution.py:270
  536.2 15.3 %collective-permute-start.80 = (bf16[192,768]{1,0:T(8,128)(2,1)S(1)}, bf16[192,768]{1,0:T(8,128)(2,1)S(1)}, u32[]{:S(2)}, u32[]{:S(2)}) collective-permute-start(bf16[192,768]{1,0:T(8,128)(2,1)S(1)} %bitcast_convert_fusion.1), channel_id=1, source_target_pairs={{8,0},{9,1},{10,2},{11,3},{12,4},{13,5},{14,6},{15,7},{16,24},{17,... | collective-permute-start | bytes 884744 | tf_op jit(solution)/shard_map/ppermute | solution.py:270
  540.9 31.2 %collective-permute-start.84 = (bf16[96,2304]{1,0:T(8,128)(2,1)S(1)}, bf16[96,2304]{1,0:T(8,128)(2,1)S(1)}, u32[]{:S(2)}, u32[]{:S(2)}) collective-permute-start(bf16[96,2304]{1,0:T(8,128)(2,1)S(1)} %fusion.45), channel_id=1, source_target_pairs={{0,16},{16,0},{1,17},{17,1},{2,18},{18,2},{3,19},{19,3},{4,20},{20... | collective-permute-start | bytes 1327112 | tf_op jit(solution)/shard_map/ppermute | solution.py:256
  545.1 16.9 %collective-permute-start.78 = (bf16[1,48,2688]{2,1,0:T(8,128)(2,1)S(1)}, bf16[1,48,2688]{2,1,0:T(8,128)(2,1)S(1)}, u32[]{:S(2)}, u32[]{:S(2)}) collective-permute-start(bf16[1,48,2688]{2,1,0:T(8,128)(2,1)S(1)} %add_convert_fusion.16), channel_id=1, source_target_pairs={{0,8},{1,9},{2,10},{3,11},{4,12},{5,13},{6,14},{7,15},{8,0},{9,1},... | collective-permute-start | bytes 774152 | tf_op jit(solution)/shard_map/ppermute | solution.py:270
  (232 other events, 1696.1 us)

commit v5 on v4

--- a/solution.py
+++ b/solution.py
@@ -537,11 +537,11 @@
 
 
 class Weight:
-    def __init__(self, parts, table, offset, width):
-        self.parts, self.table, self.offset, self.width = parts, table, offset, width
+    def __init__(self, parts, table, offset, width, tile=TILE):
+        self.parts, self.table, self.offset, self.width, self.tile = parts, table, offset, width, tile
         self.rows = parts[0].shape[1]
         self.count = sum(part.shape[0] for part in parts)
-        self.aligned = aligned(self.rows) and offset % TILE == 0 and width % TILE == 0
+        self.aligned = aligned(self.rows) and offset % tile == 0 and width % tile == 0
 
     def whole(self):
         cut = (0, self.rows, 0, self.width)
@@ -549,9 +549,9 @@
         return stack[..., self.offset : self.offset + self.width].reshape(-1, self.width)
 
     def part_specs(self):
-        first = self.offset // TILE
+        first = self.offset // self.tile
         return [
-            pl.BlockSpec((self.count // 4, self.rows, TILE), lambda i, *tables, k=k: (k, 0, first + i))
+            pl.BlockSpec((self.count // 4, self.rows, self.tile), lambda i, *tables, k=k: (k, 0, first + i))
             for _, k in quarters(self.parts)
         ]
 
@@ -569,10 +569,10 @@
             functools.partial(product_kernel, self.rows, 4, gelu),
             grid_spec=pltpu.PrefetchScalarGridSpec(
                 num_scalar_prefetch=1,
-                grid=(self.width // TILE,),
+                grid=(self.width // self.tile,),
                 in_specs=[pl.BlockSpec((tokens, depth), lambda i, t: (0, 0))] + self.part_specs(),
-                out_specs=[pl.BlockSpec((tokens, TILE), lambda i, t: (0, i))] * outs,
-                scratch_shapes=[pltpu.VMEM((depth, TILE), BF16)],
+                out_specs=[pl.BlockSpec((tokens, self.tile), lambda i, t: (0, i))] * outs,
+                scratch_shapes=[pltpu.VMEM((depth, self.tile), BF16)],
             ),
             out_shape=[shape] * outs,
             compiler_params=pltpu.CompilerParams(vmem_limit_bytes=VMEM_LIMIT),
@@ -587,19 +587,19 @@
             return dx, mm_tn(activated, grad).astype(BF16), halves
         tokens, depth = x.shape
         half = jax.ShapeDtypeStruct((self.count // 2, self.rows, lead + self.width), BF16)
-        half_spec = pl.BlockSpec((self.count // 2, self.rows, TILE), lambda i, t, p: (0, 0, lead // TILE + i))
+        half_spec = pl.BlockSpec((self.count // 2, self.rows, self.tile), lambda i, t, p: (0, 0, lead // self.tile + i))
         full = pl.BlockSpec((tokens, depth), lambda i, t, p: (0, 0))
-        units = pl.BlockSpec((tokens, TILE), lambda i, t, p: (0, i))
-        unit_rows = pl.BlockSpec((TILE, depth), lambda i, t, p: (i, 0))
+        units = pl.BlockSpec((tokens, self.tile), lambda i, t, p: (0, i))
+        unit_rows = pl.BlockSpec((self.tile, depth), lambda i, t, p: (i, 0))
         result = pl.pallas_call(
             functools.partial(feed_forward_kernel, self.rows),
             grid_spec=pltpu.PrefetchScalarGridSpec(
                 num_scalar_prefetch=2,
-                grid=(self.width // TILE,),
+                grid=(self.width // self.tile,),
                 in_specs=[full, full, unit_rows, units, units] + self.part_specs(),
                 out_specs=[full, unit_rows, half_spec, half_spec],
                 scratch_shapes=[
-                    pltpu.VMEM((depth, TILE), BF16),
+                    pltpu.VMEM((depth, self.tile), BF16),
                     pltpu.VMEM((depth, tokens), BF16),
                     pltpu.VMEM((tokens, depth), F32),
                 ],
@@ -611,10 +611,10 @@
         return result[0], result[1], result[2:]
 
     def grad_specs(self, tokens, grads):
-        ends = np.cumsum([grad.shape[1] // TILE for grad in grads])
-        bounds = [(int(end) - grad.shape[1] // TILE, int(end)) for end, grad in zip(ends, grads)]
+        ends = np.cumsum([grad.shape[1] // self.tile for grad in grads])
+        bounds = [(int(end) - grad.shape[1] // self.tile, int(end)) for end, grad in zip(ends, grads)]
         specs = [
-            pl.BlockSpec((tokens, TILE), lambda i, t, low=low, high=high: (0, jnp.clip(i, low, high - 1) - low))
+            pl.BlockSpec((tokens, self.tile), lambda i, t, low=low, high=high: (0, jnp.clip(i, low, high - 1) - low))
             for low, high in bounds
         ]
         return bounds, specs
@@ -625,15 +625,15 @@
         tokens, depth = x.shape
         bounds, specs = self.grad_specs(tokens, grads)
         half = jax.ShapeDtypeStruct((self.count // 2, self.rows, self.width), BF16)
-        half_spec = pl.BlockSpec((self.count // 2, self.rows, TILE), lambda i, t: (0, 0, i))
+        half_spec = pl.BlockSpec((self.count // 2, self.rows, self.tile), lambda i, t: (0, 0, i))
         return pl.pallas_call(
             functools.partial(outer_kernel, self.rows, bounds),
             grid_spec=pltpu.PrefetchScalarGridSpec(
                 num_scalar_prefetch=1,
-                grid=(self.width // TILE,),
+                grid=(self.width // self.tile,),
                 in_specs=[pl.BlockSpec((tokens, depth), lambda i, t: (0, 0))] + specs,
                 out_specs=[half_spec, half_spec],
-                scratch_shapes=[pltpu.VMEM((depth, TILE), BF16), pltpu.VMEM((depth, tokens), BF16)],
+                scratch_shapes=[pltpu.VMEM((depth, self.tile), BF16), pltpu.VMEM((depth, tokens), BF16)],
             ),
             out_shape=[half, half],
             compiler_params=pltpu.CompilerParams(vmem_limit_bytes=VMEM_LIMIT),
@@ -649,10 +649,10 @@
             functools.partial(inner_kernel, self.rows, bounds),
             grid_spec=pltpu.PrefetchScalarGridSpec(
                 num_scalar_prefetch=1,
-                grid=(self.width // TILE,),
+                grid=(self.width // self.tile,),
                 in_specs=self.part_specs() + specs,
                 out_specs=pl.BlockSpec((tokens, depth), lambda i, t: (0, 0)),
-                scratch_shapes=[pltpu.VMEM((depth, TILE), BF16), pltpu.VMEM((tokens, depth), F32)],
+                scratch_shapes=[pltpu.VMEM((depth, self.tile), BF16), pltpu.VMEM((tokens, depth), F32)],
             ),
             out_shape=jax.ShapeDtypeStruct((tokens, depth), BF16),
             compiler_params=pltpu.CompilerParams(vmem_limit_bytes=VMEM_LIMIT),
@@ -665,24 +665,24 @@
             halves = split_stack([mm_tn(x, grad).astype(BF16)], places, self.count)
             return mm_nt(grad, self.whole()).astype(BF16), [jnp.pad(h, ((0, 0), (0, 0), (lead, 0))) for h in halves]
         tokens, depth = x.shape
-        ends = np.cumsum([grad.shape[1] // TILE for grad in grads])
-        bounds = [(int(end) - grad.shape[1] // TILE, int(end)) for end, grad in zip(ends, grads)]
+        ends = np.cumsum([grad.shape[1] // self.tile for grad in grads])
+        bounds = [(int(end) - grad.shape[1] // self.tile, int(end)) for end, grad in zip(ends, grads)]
         half = jax.ShapeDtypeStruct((self.count // 2, self.rows, lead + self.width), BF16)
-        half_spec = pl.BlockSpec((self.count // 2, self.rows, TILE), lambda i, t, p: (0, 0, lead // TILE + i))
+        half_spec = pl.BlockSpec((self.count // 2, self.rows, self.tile), lambda i, t, p: (0, 0, lead // self.tile + i))
         result = pl.pallas_call(
             functools.partial(pullback_kernel, self.rows, 4, bounds),
             grid_spec=pltpu.PrefetchScalarGridSpec(
                 num_scalar_prefetch=2,
-                grid=(self.width // TILE,),
+                grid=(self.width // self.tile,),
                 in_specs=[pl.BlockSpec((tokens, depth), lambda i, t, p: (0, 0))]
                 + self.part_specs()
                 + [
-                    pl.BlockSpec((tokens, TILE), lambda i, t, p, low=low, high=high: (0, jnp.clip(i, low, high - 1) - low))
+                    pl.BlockSpec((tokens, self.tile), lambda i, t, p, low=low, high=high: (0, jnp.clip(i, low, high - 1) - low))
                     for low, high in bounds
                 ],
                 out_specs=[pl.BlockSpec((tokens, depth), lambda i, t, p: (0, 0)), half_spec, half_spec],
                 scratch_shapes=[
-                    pltpu.VMEM((depth, TILE), BF16),
+                    pltpu.VMEM((depth, self.tile), BF16),
                     pltpu.VMEM((depth, tokens), BF16),
                     pltpu.VMEM((tokens, depth), F32),
                 ],
@@ -847,8 +847,8 @@
     return held
 
 
-def in_square(blocks):
-    is_first = lax.axis_index("section") == 0
+def in_square(blocks, whose=0):
+    is_first = lax.axis_index("section") == whose
     middle = jnp.where(is_first, blocks[1:3], jnp.stack([blocks[2], blocks[1]]))
     return jnp.concatenate([blocks[:1], middle, blocks[3:]], axis=0)
 
@@ -1038,7 +1038,7 @@
     scale_g1 = row_scale(start_rows)
     square_top = shared(stream_top.result().reshape(4 * slots, half_l))
     scale_g1, square_top = advance([stream_g, stream_out_g, stream_up_g], (scale_g1, square_top))
-    qkv_wg = Weight(stream_g.result(), table_g, 0, qkv_width)
+    qkv_wg = Weight(stream_g.result(), table_g, 0, qkv_width, half_g)
     normed_g = (start_rows * scale_g1 * gain_one_g).astype(BF16)
     projected_g = qkv_wg.product(normed_g)
     own_mixture_g, lse_g = attention_forward(projected_g, bias_g)
@@ -1050,8 +1050,13 @@
     hidden_g = start_rows + joined(mm(mixture_g, out_wg), mm(mixture_g, out_theirs_g))
     scale_g2 = row_scale(hidden_g)
     normed_g2 = (hidden_g * scale_g2 * gain_two_g).astype(BF16)
-    square_normed = fresh(gather_in_square(half_of(normed_g2, core))).result()
-    square_normed = shared(square_normed.reshape(4 * slots, half_g))
+    near = half_of(normed_g2, core)[None]
+    near = jnp.concatenate([near, exchange(near, SQUARE[0], size)], axis=0)
+    far = exchange(near, SQUARE[1], size)
+    mine = jnp.concatenate([near, far], axis=0)
+    theirs = jnp.concatenate([swap(near), swap(far)], axis=0)
+    mine, theirs = in_square(mine), in_square(theirs, 1)
+    square_normed = joined(mine.reshape(4 * slots, half_g), theirs.reshape(4 * slots, half_g))
     (up_wg,) = stream_up_g.result()
     (down_wg,) = stream_down_g.result()
     upward_g = mm(square_normed, up_wg)
@@ -1097,7 +1102,9 @@
         normed_l2, grad_local_b, down_wl, slope_l, activated_l, table, side_l
     )
     stream_down_l = fresh(scatter_core(grad_down_l, lows_first, below, size))
-    part, up_halves = advance([stream_g, stream_down_g, stream_up_g, stream_out_g], (part, up_halves))
+    part, up_halves = advance(
+        [stream_g, stream_down_g, stream_up_g, stream_out_g], (part, up_halves), [stream_up_g, stream_out_g]
+    )
     part = summed_cores(part)
     pulled, grad_gain_l2 = norm_backward(part, hidden_l, scale_l2, gain_two_l)
     grad_hidden_l = grad_local + pulled
@@ -1105,7 +1112,7 @@
     grad_out_l = mm_tn(mixture_l, half_of(grad_hidden_lb, core)).astype(BF16)
     stream_up_l = fresh(scatter_all(split_stack([grad_out_l, grad_proj], table, size, up_halves), order_l))
     grad_mixture_l = mm_nt(grad_hidden_lb, out_own_l).astype(BF16)
-    grad_mixture_l = advance([stream_g, stream_down_l, stream_up_l], grad_mixture_l)
+    grad_mixture_l = advance([stream_g, stream_down_l, stream_up_l, stream_up_g, stream_out_g], grad_mixture_l)
     grad_projected_l = attention_backward(projected_l, bias_l, lse_l, own_mixture_l, grad_mixture_l)
     grad_projected_l = advance([stream_out_g, stream_up_g], grad_projected_l)
     stream_qkv_l = fresh(scatter_all(qkv_wl.outer(normed_l, grad_projected_l, table), order_l))
@@ -1125,10 +1132,10 @@
     hidden_out = (local_out + mm_tn(picks_live, returned.astype(BF16))).astype(BF16)[None]
     stream_gains = fresh(scatter_small(gains, size))
     input_grad = advance([stream_qkv_l, stream_up_l, stream_down_l, stream_gains], input_grad)
-    advance([stream_qkv_l, stream_gains, stream_down_l, stream_out_g, stream_g], ())
-    advance([stream_up_l, stream_gains], ())
-    advance([stream_qkv_l], ())
-    advance([stream_up_l, stream_qkv_l, stream_down_l], ())
+    advance([stream_qkv_l, stream_gains, stream_down_l, stream_out_g, stream_g], (), [stream_gains])
+    advance([stream_up_l, stream_gains, stream_down_l], ())
+    advance([stream_qkv_l, stream_gains], ())
+    advance([stream_up_l, stream_qkv_l], ())
 
     def joined_columns(mine, theirs):
         return joined(mine, theirs).astype(F32)

time: 585 us -> 569 us (0.973)
  waiting for transfers between devices: 161 us -> 139 us
  starting transfers between devices: 94.1 us -> 100 us
    ppermute x57, waiting for transfers between devices: 154 us -> 131 us  [exchange(): lax.ppermute(part, ('section', 'dp'), pairs)]
    ppermute x24 -> x25, starting transfers between devices: 19.7 us -> 25.5 us  [swap(): return lax.ppermute(array, 'section', [(0, 1), (1, 0)])]
    unnamed x410 -> x418, local copies, waits for them, and re-layouts: 37.4 us -> 36.1 us
  transfers between devices with their start and end apart: 88 -> 89, of which waited for: 28 -> 27; matrix products, arithmetic and copies ran while one was open for 25% -> 27% of each run, Pallas kernels for 19% -> 19%
where the time goes in v5:
time: 569 us; the launch traced here: 562 us
  waiting for transfers between devices  139 us (24%)
  other arithmetic  112 us (20%)
  Pallas kernels  108 us (19%)
  starting transfers between devices  100 us (18%)
  local copies, waits for them, and re-layouts  59.4 us (10%)
  matrix products  39 us (7%)
    ppermute x57, waiting for transfers between devices, exchange(): lax.ppermute(part, ('section', 'dp'), pairs)  131 us
    ppermute x57, starting transfers between devices, exchange(): lax.ppermute(part, ('section', 'dp'), pairs)  66.5 us
    unnamed x418, local copies, waits for them, and re-layouts  36.1 us
    convert_element_type x15, other arithmetic, halving(): outgoing = total_of([term[half:] for term in terms]).astype(BF16)  28.4 us
    ppermute x25, starting transfers between devices, swap(): return lax.ppermute(array, 'section', [(0, 1), (1, 0)])  25.5 us
    pallas_call x3, Pallas kernels, product(): pl.pallas_call(functools.partial(product_kernel, self.rows, 4, gelu), gri...  20.8 us
    pallas_call x2, Pallas kernels, attention_backward(): pl.pallas_call(functools.partial(attention_backward_kernel, rows, window)...  18.2 us
    pallas_call x1, Pallas kernels, feed_forward_pullback(): pl.pallas_call(functools.partial(feed_forward_kernel, self.rows), grid_sp...  17.8 us
  transfers between devices with their start and end apart: 89, of which 27 were waited for; matrix products, arithmetic and copies ran while one was open for 27% of the time, Pallas kernels for 19%

profile of v5, /device:TPU:1, one launch (start us, length us, event | category | flops | bytes accessed | tf_op | source)
XLA Modules:
  0.0 562.2 jit_solution(10634757032415932267)
XLA Ops:
  7.6 3.2 collective-permute-start.1
  18.4 10.2 %collective-permute-done.1 = bf16[1,48,4224]{2,1,0:T(8,128)(2,1)S(1)} collective-permute-done((bf16[1,48,4224]{2,1,0:T(8,128)(2,1)S(1)}, bf16[1,48,4224]{2,1,0:T(8,128)(2,1)S(1)}, u32[]{:S(2)}, u32[]{:S(2)}) %collective-permute-start.1) | collective-permute-done | bytes 405536 | tf_op jit(solution)/shard_map/ppermute | solution.py:270
  37.1 4.0 collective-permute-done.4
  41.8 2.6 collective-permute-done.2
  51.4 7.0 %collective-permute-done.7 = bf16[1,96,2304]{2,1,0:T(8,128)(2,1)} collective-permute-done((bf16[1,96,2304]{2,1,0:T(8,128)(2,1)}, bf16[1,96,2304]{2,1,0:T(8,128)(2,1)}, u32[]{:S(2)}, u32[]{:S(2)}) %collective-permute-start.7) | collective-permute-done | bytes 442400 | tf_op jit(solution)/shard_map/ppermute | solution.py:270
  58.4 11.0 %collective-permute-done.8 = bf16[1,192,384]{2,1,0:T(8,128)(2,1)S(1)} collective-permute-done((bf16[1,192,384]{2,1,0:T(8,128)(2,1)}, bf16[1,192,384]{2,1,0:T(8,128)(2,1)S(1)}, u32[]{:S(2)}, u32[]{:S(2)}) %collective-permute-start.8) | collective-permute-done | bytes 147488 | tf_op jit(solution)/shard_map/ppermute | solution.py:270
  74.6 3.2 collective-permute-start.12
  86.0 10.3 %collective-permute-done.13 = bf16[1,192,768]{2,1,0:T(8,128)(2,1)} collective-permute-done((bf16[1,192,768]{2,1,0:T(8,128)(2,1)}, bf16[1,192,768]{2,1,0:T(8,128)(2,1)}, u32[]{:S(2)}, u32[]{:S(2)}) %collective-permute-start.13) | collective-permute-done | bytes 294944 | tf_op jit(solution)/shard_map/ppermute | solution.py:270
  96.3 14.7 %collective-permute-done.14 = bf16[2,192,384]{2,1,0:T(8,128)(2,1)} collective-permute-done((bf16[2,192,384]{2,1,0:T(8,128)(2,1)}, bf16[2,192,384]{2,1,0:T(8,128)(2,1)}, u32[]{:S(2)}, u32[]{:S(2)}) %collective-permute-start.14) | collective-permute-done | bytes 294944 | tf_op jit(solution)/shard_map/ppermute | solution.py:270
  117.1 3.1 collective-permute-start.19
  120.2 2.8 pad_maximum_fusion.3
  126.3 5.8 %shard_map.452.q_ref.k_ref.v_ref = bf16[1024,1152]{1,0:T(8,128)(2,1)} custom-call(s32[16]{0:T(128)S(1)} %get-tuple-element.420.table.places, bf16[1024,768]{1,0:T(8,128)(2,1)S(1)} %fusion.2.x_ref, bf16[4,48,4224]{2,1,0:T(8,128)(2,1)S(1)} %pad_maximum_fusion.4.refs_0_, bf16[4,48,4224]{2,1,0:T(8,128)(2,1)S(1)} %collective-permute-done.6.refs_1_, ...), custom_call_target="tpu_custom_call" | custom-call | tf_op jit(solution)/shard_map/pallas_call | solution.py:568
  135.0 9.5 %shard_map.453 = (bf16[1024,384]{1,0:T(8,128)(2,1)S(1)}, f32[3,2,1024]{2,1,0:T(2,128)S(1)}) custom-call(bf16[1024,1152]{1,0:T(8,128)(2,1)S(1)} %copy-done.3, bf16[1024,1152]{1,0:T(8,128)(2,1)S(1)} %copy-done.3, bf16[1024,1152]{1,0:T(8,128)(2,1)S(1)} %copy-done.3, f32[1024,1]{1,0:T(8,128)S(1)} %fusion.45.bias_ref), custom_call_target="tpu_custom_call" | custom-call | tf_op jit(solution)/shard_map/pallas_call | solution.py:210
  144.6 16.2 %collective-permute-done.19 = bf16[1,96,768]{2,1,0:T(8,128)(2,1)S(1)} collective-permute-done((bf16[1,96,768]{2,1,0:T(8,128)(2,1)S(1)}, bf16[1,96,768]{2,1,0:T(8,128)(2,1)S(1)}, u32[]{:S(2)}, u32[]{:S(2)}) %collective-permute-start.19) | collective-permute-done | bytes 147488 | tf_op jit(solution)/shard_map/ppermute | solution.py:270
  168.1 2.8 pad_maximum_fusion.refs_0_.refs_1_
  176.6 10.2 %shard_map.454 = (bf16[1024,1536]{1,0:T(8,128)(2,1)}, bf16[1024,1536]{1,0:T(8,128)(2,1)}) custom-call(s32[16]{0:T(128)S(1)} %get-tuple-element.420.table.places, bf16[1024,768]{1,0:T(8,128)(2,1)S(1)} %multiply_convert_fusion.x_ref, bf16[4,48,4224]{2,1,0:T(8,128)(2,1)S(1)} %copy-done.5, bf16[4,48,4224]{2,1,0:T(8,128)(2,1)S(1)} %copy-done.8, ...), custom_call_target="tpu_custom_call" | custom-call | flops 99999997952 | tf_op jit(solution)/shard_map/pallas_call | solution.py:568
  187.8 5.3 fusion.134
  206.5 9.0 %collective-permute-done.29 = bf16[4,96,768]{2,1,0:T(8,128)(2,1)S(1)} collective-permute-done((bf16[4,96,768]{2,1,0:T(8,128)(2,1)S(1)}, bf16[4,96,768]{2,1,0:T(8,128)(2,1)S(1)}, u32[]{:S(2)}, u32[]{:S(2)}) %collective-permute-start.29) | collective-permute-done | bytes 589856 | tf_op jit(solution)/shard_map/ppermute | solution.py:270
  215.6 13.1 %collective-permute-done.30.refs_1_ = bf16[8,96,768]{2,1,0:T(8,128)(2,1)S(1)} collective-permute-done((bf16[8,96,768]{2,1,0:T(8,128)(2,1)S(1)}, bf16[8,96,768]{2,1,0:T(8,128)(2,1)S(1)}, u32[]{:S(2)}, u32[]{:S(2)}) %collective-permute-start.30) | collective-permute-done | bytes 1179680 | tf_op jit(solution)/shard_map/ppermute | solution.py:270
  238.4 4.8 shard_map.456.q_ref.k_ref.v_ref
  243.3 4.6 shard_map.457
  253.2 3.6 collective-permute-done.33
  263.4 4.6 collective-permute-done.35
  293.8 3.2 convolution_convert_fusion.3.refs_0_
  311.3 2.6 collective-permute-done.41
  316.3 3.7 collective-permute-done.42
  334.8 4.5 shard_map.464
  340.0 10.5 %shard_map.465 = (bf16[192,1536]{1,0:T(8,128)(2,1)S(1)}, bf16[8,96,2304]{2,1,0:T(8,128)(2,1)}, bf16[8,96,2304]{2,1,0:T(8,128)(2,1)}) custom-call(s32[16]{0:T(128)S(1)} %get-tuple-element.419.table, s32[16]{0:T(128)S(1)} %get-tuple-element.418.table.places, bf16[192,1536]{1,0:T(8,128)(2,1)S(1)} %copy-done.20, bf16[8,96,2304]{2,1,0:T(8,128)(2,1)} %copy-done.2, ...), custom_call_target="tpu_custom_call" | custom-call | tf_op jit(solution)/shard_map/pallas_call | solution.py:672
  359.1 5.9 %collective-permute-start.49 = (bf16[384,768]{1,0:T(8,128)(2,1)}, bf16[384,768]{1,0:T(8,128)(2,1)}, u32[]{:S(2)}, u32[]{:S(2)}) collective-permute-start(bf16[384,768]{1,0:T(8,128)(2,1)} %bitcast_convert_fusion), channel_id=1, source_target_pairs={{8,0},{9,1},{10,2},{11,3},{12,4},{13,5},{14,6},{15,7},{16,24},{17,... | collective-permute-start | bytes 1769480 | tf_op jit(solution)/shard_map/ppermute | solution.py:270
  377.0 5.7 %fusion.15 = (bf16[1024,768]{1,0:T(8,128)(2,1)}, f32[1024,768]{1,0:T(8,128)}) fusion(bf16[1024,384]{1,0:T(8,128)(2,1)} %copy-done.89, bf16[1024,384]{1,0:T(8,128)(2,1)S(1)} %copy-done.88, bf16[192,1536]{1,0:T(8,128)(2,1)} %add_convert_fusion.6, bf16[768,768]{1,0:T(8,128)(2,1)} %copy-done.117, bf16[768,768]{1,0:T(8,128)(2,1)} %copy-done.116, ...), kind=kOutput, calls=%fused_computation.39 | convolution fusion | flops 764755968 | bytes 9241344 | tf_op jit(solution)/shard_map/dot_general | solution.py:33
  384.2 17.8 %shard_map.466 = (bf16[1024,768]{1,0:T(8,128)(2,1)S(1)}, bf16[1536,768]{1,0:T(8,128)(2,1)}, bf16[8,48,2688]{2,1,0:T(8,128)(2,1)}, bf16[8,48,2688]{2,1,0:T(8,128)(2,1)}) custom-call(s32[16]{0:T(128)S(1)} %get-tuple-element.420.table.places, s32[16]{0:T(128)S(1)} %get-tuple-element.420.table.places, bf16[1024,768]{1,0:T(8,128)(2,1)S(1)} %copy-done.18, ...), custom_call_target="tpu_custom_call" | custom-call | tf_op jit(solution)/shard_map/pallas_call | solution.py:594
  406.1 3.6 add_convert_fusion
  420.1 2.6 fusion.122
  428.8 2.8 collective-permute-done.54
  434.3 2.7 add_convert_fusion.2
  437.4 13.7 %shard_map.469 = (bf16[1024,384]{1,0:T(8,128)(2,1)S(1)}, bf16[1024,384]{1,0:T(8,128)(2,1)S(1)}, bf16[1024,384]{1,0:T(8,128)(2,1)S(1)}) custom-call(bf16[1024,1152]{1,0:T(8,128)(2,1)} %shard_map.452.q_ref.k_ref.v_ref, bf16[1024,1152]{1,0:T(8,128)(2,1)} %shard_map.452.q_ref.k_ref.v_ref, bf16[1024,1152]{1,0:T(8,128)(2,1)} %shard_map.452.q_ref.k_ref.v_ref, ...), custom_call_target="tpu_custom_call" | custom-call | flops 99999997952 | tf_op jit(solution)/shard_map/pallas_call | solution.py:230
  457.8 5.2 shard_map.470
  463.3 5.7 %shard_map.471 = bf16[1024,768]{1,0:T(8,128)(2,1)S(1)} custom-call(s32[16]{0:T(128)S(1)} %get-tuple-element.420.table.places, bf16[4,48,4224]{2,1,0:T(8,128)(2,1)S(1)} %copy-done.6, bf16[4,48,4224]{2,1,0:T(8,128)(2,1)} %copy-done.7, bf16[4,48,4224]{2,1,0:T(8,128)(2,1)} %collective-permute-done.10.refs_2_, ...), custom_call_target="tpu_custom_call" | custom-call | tf_op jit(solution)/shard_map/pallas_call | solution.py:648
  475.7 4.1 collective-permute-start.65
  489.8 3.6 fusion.5
  495.7 3.7 fusion.30
  506.0 4.4 collective-permute-done.72
  512.3 3.9 collective-permute-done.70
  518.6 3.8 collective-permute-start.75
  529.2 2.8 collective-permute-start.77
  536.9 3.6 collective-permute-start.84
  542.7 2.6 collective-permute-start.81
  548.1 5.4 collective-permute-done.81
  (766 shorter events, 267.9 us)
Async XLA Ops:
  7.6 21.0 %collective-permute-start.1 = (bf16[1,48,4224]{2,1,0:T(8,128)(2,1)S(1)}, bf16[1,48,4224]{2,1,0:T(8,128)(2,1)S(1)}, u32[]{:S(2)}, u32[]{:S(2)}) collective-permute-start(bf16[1,48,4224]{2,1,0:T(8,128)(2,1)S(1)} %bitcast.159), channel_id=1, source_target_pairs={{0,8},{1,9},{2,10},{3,11},{4,12},{5,13},{6,14},{7,15},{8,0},{9,1},... | collective-permute-start | bytes 1216520 | tf_op jit(solution)/shard_map/ppermute | solution.py:270
  29.6 14.8 %collective-permute-start.2 = (bf16[2,48,4224]{2,1,0:T(8,128)(2,1)}, bf16[2,48,4224]{2,1,0:T(8,128)(2,1)S(1)}, u32[]{:S(2)}, u32[]{:S(2)}) collective-permute-start(bf16[2,48,4224]{2,1,0:T(8,128)(2,1)} %pad_maximum_fusion.29), channel_id=1, source_target_pairs={{0,1},{1,0},{2,3},{3,2},{4,5},{5,4},{6,7},{7,6},{8,9},{9,8},{10,11... | collective-permute-start | bytes 2433032 | tf_op jit(solution)/shard_map/ppermute | solution.py:270
  44.6 24.9 %collective-permute-start.6 = (bf16[4,48,4224]{2,1,0:T(8,128)(2,1)S(1)}, bf16[4,48,4224]{2,1,0:T(8,128)(2,1)S(1)}, u32[]{:S(2)}, u32[]{:S(2)}) collective-permute-start(bf16[4,48,4224]{2,1,0:T(8,128)(2,1)S(1)} %pad_maximum_fusion.4.refs_0_), channel_id=1, source_target_pairs={{0,4},{1,5},{2,6},{3,7},{4,0},{5,1},{6,2},{7,3},{8,12},{9,13},{10,... | collective-permute-start | bytes 4866056 | tf_op jit(solution)/shard_map/ppermute | solution.py:270
  49.9 19.5 %collective-permute-start.9 = (bf16[2,96,768]{2,1,0:T(8,128)(2,1)S(1)}, bf16[2,96,768]{2,1,0:T(8,128)(2,1)S(1)}, u32[]{:S(2)}, u32[]{:S(2)}) collective-permute-start(bf16[2,96,768]{2,1,0:T(8,128)(2,1)S(1)} %get-tuple-element.386), channel_id=1, source_target_pairs={{0,2},{1,3},{2,0},{3,1},{4,6},{5,7},{6,4},{7,5},{8,10},{9,11},{10,... | collective-permute-start | bytes 884744 | tf_op jit(solution)/shard_map/ppermute | solution.py:270
  51.2 18.3 %collective-permute-start.8 = (bf16[1,192,384]{2,1,0:T(8,128)(2,1)}, bf16[1,192,384]{2,1,0:T(8,128)(2,1)S(1)}, u32[]{:S(2)}, u32[]{:S(2)}) collective-permute-start(bf16[1,192,384]{2,1,0:T(8,128)(2,1)} %dynamic-slice_bitcast_fusion.7), channel_id=1, source_target_pairs={{0,1},{1,0},{2,3},{3,2},{4,5},{5,4},{6,7},{7,6},{8,9},{9,8},{10,11... | collective-permute-start | bytes 442376 | tf_op jit(solution)/shard_map/ppermute | solution.py:270
  70.2 40.7 %collective-permute-start.10 = (bf16[4,48,4224]{2,1,0:T(8,128)(2,1)S(1)}, bf16[4,48,4224]{2,1,0:T(8,128)(2,1)}, u32[]{:S(2)}, u32[]{:S(2)}) collective-permute-start(bf16[4,48,4224]{2,1,0:T(8,128)(2,1)S(1)} %pad_maximum_fusion.4.refs_0_), channel_id=1, source_target_pairs={{0,2},{1,3},{2,0},{3,1},{4,6},{5,7},{6,4},{7,5},{8,10},{9,11},{10,... | collective-permute-start | bytes 4866056 | tf_op jit(solution)/shard_map/ppermute | solution.py:270
  71.2 39.8 %collective-permute-start.11 = (bf16[4,48,4224]{2,1,0:T(8,128)(2,1)S(1)}, bf16[4,48,4224]{2,1,0:T(8,128)(2,1)}, u32[]{:S(2)}, u32[]{:S(2)}) collective-permute-start(bf16[4,48,4224]{2,1,0:T(8,128)(2,1)S(1)} %collective-permute-done.6.refs_1_), channel_id=1, source_target_pairs={{0,2},{1,3},{2,0},{3,1},{4,6},{5,7},{6,4},{7,5},{8,10},{9,11},{10,... | collective-permute-start | bytes 4866056 | tf_op jit(solution)/shard_map/ppermute | solution.py:270
  74.6 36.3 %collective-permute-start.12 = (bf16[2,96,2304]{2,1,0:T(8,128)(2,1)}, bf16[2,96,2304]{2,1,0:T(8,128)(2,1)}, u32[]{:S(2)}, u32[]{:S(2)}) collective-permute-start(bf16[2,96,2304]{2,1,0:T(8,128)(2,1)} %pad_maximum_fusion.28), channel_id=1, source_target_pairs={{0,4},{1,5},{2,6},{3,7},{4,0},{5,1},{6,2},{7,3},{8,12},{9,13},{10,... | collective-permute-start | bytes 2654216 | tf_op jit(solution)/shard_map/ppermute | solution.py:270
  79.3 17.0 %collective-permute-start.13 = (bf16[1,192,768]{2,1,0:T(8,128)(2,1)}, bf16[1,192,768]{2,1,0:T(8,128)(2,1)}, u32[]{:S(2)}, u32[]{:S(2)}) collective-permute-start(bf16[1,192,768]{2,1,0:T(8,128)(2,1)} %select_bitcast_fusion.1), channel_id=1, source_target_pairs={{0,4},{1,5},{2,6},{3,7},{4,0},{5,1},{6,2},{7,3},{8,12},{9,13},{10,... | collective-permute-start | bytes 884744 | tf_op jit(solution)/shard_map/ppermute | solution.py:270
  80.0 30.9 %collective-permute-start.14 = (bf16[2,192,384]{2,1,0:T(8,128)(2,1)}, bf16[2,192,384]{2,1,0:T(8,128)(2,1)}, u32[]{:S(2)}, u32[]{:S(2)}) collective-permute-start(bf16[2,192,384]{2,1,0:T(8,128)(2,1)} %pad_maximum_fusion.45), channel_id=1, source_target_pairs={{0,2},{1,3},{2,0},{3,1},{4,6},{5,7},{6,4},{7,5},{8,10},{9,11},{10,... | collective-permute-start | bytes 884744 | tf_op jit(solution)/shard_map/ppermute | solution.py:270
  112.1 48.7 %collective-permute-start.16 = (bf16[2,192,768]{2,1,0:T(8,128)(2,1)S(1)}, bf16[2,192,768]{2,1,0:T(8,128)(2,1)S(1)}, u32[]{:S(2)}, u32[]{:S(2)}) collective-permute-start(bf16[2,192,768]{2,1,0:T(8,128)(2,1)S(1)} %pad_maximum_fusion.38), channel_id=1, source_target_pairs={{0,1},{1,0},{2,3},{3,2},{4,5},{5,4},{6,7},{7,6},{8,9},{9,8},{10,11... | collective-permute-start | bytes 1769480 | tf_op jit(solution)/shard_map/ppermute | solution.py:270
  113.1 47.6 %collective-permute-start.17 = (bf16[4,96,768]{2,1,0:T(8,128)(2,1)S(1)}, bf16[4,96,768]{2,1,0:T(8,128)(2,1)S(1)}, u32[]{:S(2)}, u32[]{:S(2)}) collective-permute-start(bf16[4,96,768]{2,1,0:T(8,128)(2,1)S(1)} %pad_maximum_fusion.37), channel_id=1, source_target_pairs={{0,8},{1,9},{2,10},{3,11},{4,12},{5,13},{6,14},{7,15},{8,0},{9,1},... | collective-permute-start | bytes 1769480 | tf_op jit(solution)/shard_map/ppermute | solution.py:270
  115.6 45.2 %collective-permute-start.18 = (bf16[384,768]{1,0:T(8,128)(2,1)S(1)}, bf16[384,768]{1,0:T(8,128)(2,1)S(1)}, u32[]{:S(2)}, u32[]{:S(2)}) collective-permute-start(bf16[384,768]{1,0:T(8,128)(2,1)S(1)} %copy-done.143), channel_id=1, source_target_pairs={{0,8},{1,9},{2,10},{3,11},{4,12},{5,13},{6,14},{7,15},{24,16},{25,... | collective-permute-start | bytes 1769480 | tf_op jit(solution)/shard_map/ppermute | solution.py:270
  117.1 43.7 %collective-permute-start.19 = (bf16[1,96,768]{2,1,0:T(8,128)(2,1)S(1)}, bf16[1,96,768]{2,1,0:T(8,128)(2,1)S(1)}, u32[]{:S(2)}, u32[]{:S(2)}) collective-permute-start(bf16[1,96,768]{2,1,0:T(8,128)(2,1)S(1)} %copy-done.100), channel_id=1, source_target_pairs={{0,8},{1,9},{2,10},{3,11},{4,12},{5,13},{6,14},{7,15},{8,0},{9,1},... | collective-permute-start | bytes 442376 | tf_op jit(solution)/shard_map/ppermute | solution.py:270
  123.0 44.8 %collective-permute-start.15 = (bf16[4,96,2304]{2,1,0:T(8,128)(2,1)}, bf16[4,96,2304]{2,1,0:T(8,128)(2,1)}, u32[]{:S(2)}, u32[]{:S(2)}) collective-permute-start(bf16[4,96,2304]{2,1,0:T(8,128)(2,1)} %pad_maximum_fusion.3), channel_id=1, source_target_pairs={{0,1},{1,0},{2,3},{3,2},{4,5},{5,4},{6,7},{7,6},{8,9},{9,8},{10,11... | collective-permute-start | bytes 5308424 | tf_op jit(solution)/shard_map/ppermute | solution.py:270
  163.0 23.9 %collective-permute-start.22 = (bf16[4,192,768]{2,1,0:T(8,128)(2,1)S(1)}, bf16[4,192,768]{2,1,0:T(8,128)(2,1)S(1)}, u32[]{:S(2)}, u32[]{:S(2)}) collective-permute-start(bf16[4,192,768]{2,1,0:T(8,128)(2,1)S(1)} %pad_maximum_fusion.19.refs_0_.refs_1_), channel_id=1, source_target_pairs={{0,2},{1,3},{2,0},{3,1},{4,6},{5,7},{6,4},{7,5},{8,10},{9,11},{10,... | collective-permute-start | bytes 3538952 | tf_op jit(solution)/shard_map/ppermute | solution.py:270
  165.5 21.4 %collective-permute-start.23 = (bf16[1,384,768]{2,1,0:T(8,128)(2,1)S(1)}, bf16[1,384,768]{2,1,0:T(8,128)(2,1)S(1)}, u32[]{:S(2)}, u32[]{:S(2)}) collective-permute-start(bf16[1,384,768]{2,1,0:T(8,128)(2,1)S(1)} %select_bitcast_fusion.refs_0_), channel_id=1, source_target_pairs={{0,4},{1,5},{2,6},{3,7},{4,0},{5,1},{6,2},{7,3},{8,12},{9,13},{10,... | collective-permute-start | bytes 1769480 | tf_op jit(solution)/shard_map/ppermute | solution.py:270
  167.2 19.6 %collective-permute-start.24 = (bf16[2,96,768]{2,1,0:T(8,128)(2,1)}, bf16[2,96,768]{2,1,0:T(8,128)(2,1)S(1)}, u32[]{:S(2)}, u32[]{:S(2)}) collective-permute-start(bf16[2,96,768]{2,1,0:T(8,128)(2,1)} %pad_maximum_fusion.49), channel_id=1, source_target_pairs={{0,4},{1,5},{2,6},{3,7},{4,0},{5,1},{6,2},{7,3},{8,12},{9,13},{10,... | collective-permute-start | bytes 884744 | tf_op jit(solution)/shard_map/ppermute | solution.py:270
  170.9 58.8 %collective-permute-start.28 = (bf16[8,96,2304]{2,1,0:T(8,128)(2,1)S(1)}, bf16[8,96,2304]{2,1,0:T(8,128)(2,1)}, u32[]{:S(2)}, u32[]{:S(2)}) collective-permute-start(bf16[8,96,2304]{2,1,0:T(8,128)(2,1)S(1)} %pad_maximum_fusion.refs_0_.refs_1_), channel_id=1, source_target_pairs={{0,2},{1,3},{2,0},{3,1},{4,6},{5,7},{6,4},{7,5},{8,10},{9,11},{10,... | collective-permute-start | bytes 10616840 | tf_op jit(solution)/shard_map/ppermute | solution.py:270
  200.0 15.6 %collective-permute-start.29 = (bf16[4,96,768]{2,1,0:T(8,128)(2,1)S(1)}, bf16[4,96,768]{2,1,0:T(8,128)(2,1)S(1)}, u32[]{:S(2)}, u32[]{:S(2)}) collective-permute-start(bf16[4,96,768]{2,1,0:T(8,128)(2,1)S(1)} %pad_maximum_fusion.39), channel_id=1, source_target_pairs={{0,1},{1,0},{2,3},{3,2},{4,5},{5,4},{6,7},{7,6},{8,9},{9,8},{10,11... | collective-permute-start | bytes 1769480 | tf_op jit(solution)/shard_map/ppermute | solution.py:270
  201.3 27.4 %collective-permute-start.30 = (bf16[8,96,768]{2,1,0:T(8,128)(2,1)S(1)}, bf16[8,96,768]{2,1,0:T(8,128)(2,1)S(1)}, u32[]{:S(2)}, u32[]{:S(2)}) collective-permute-start(bf16[8,96,768]{2,1,0:T(8,128)(2,1)S(1)} %pad_maximum_fusion.20.refs_0_), channel_id=1, source_target_pairs={{0,4},{1,5},{2,6},{3,7},{4,0},{5,1},{6,2},{7,3},{8,12},{9,13},{10,... | collective-permute-start | bytes 3538952 | tf_op jit(solution)/shard_map/ppermute | solution.py:270
  230.9 17.6 %collective-permute-start.32 = (bf16[8,96,768]{2,1,0:T(8,128)(2,1)}, bf16[8,96,768]{2,1,0:T(8,128)(2,1)}, u32[]{:S(2)}, u32[]{:S(2)}) collective-permute-start(bf16[8,96,768]{2,1,0:T(8,128)(2,1)} %pad_maximum_fusion.22.refs_0_.refs_1_), channel_id=1, source_target_pairs={{0,2},{1,3},{2,0},{3,1},{4,6},{5,7},{6,4},{7,5},{8,10},{9,11},{10,... | collective-permute-start | bytes 3538952 | tf_op jit(solution)/shard_map/ppermute | solution.py:270
  324.0 26.5 %collective-permute-start.46 = (bf16[1,384,768]{2,1,0:T(8,128)(2,1)}, bf16[1,384,768]{2,1,0:T(8,128)(2,1)}, u32[]{:S(2)}, u32[]{:S(2)}) collective-permute-start(bf16[1,384,768]{2,1,0:T(8,128)(2,1)} %get-tuple-element.218), channel_id=1, source_target_pairs={{0,4},{1,5},{2,6},{3,7},{4,0},{5,1},{6,2},{7,3},{8,12},{9,13},{10,... | collective-permute-start | bytes 1769480 | tf_op jit(solution)/shard_map/ppermute | solution.py:270
  324.9 45.4 %collective-permute-start.50 = (bf16[8,96,768]{2,1,0:T(8,128)(2,1)}, bf16[8,96,768]{2,1,0:T(8,128)(2,1)}, u32[]{:S(2)}, u32[]{:S(2)}) collective-permute-start(bf16[8,96,768]{2,1,0:T(8,128)(2,1)} %get-tuple-element.232), channel_id=1, source_target_pairs={{0,4},{1,5},{2,6},{3,7},{4,0},{5,1},{6,2},{7,3},{8,12},{9,13},{10,... | collective-permute-start | bytes 3538952 | tf_op jit(solution)/shard_map/ppermute | solution.py:270
  333.3 17.2 %collective-permute-start.44 = (bf16[2,192,384]{2,1,0:T(8,128)(2,1)}, bf16[2,192,384]{2,1,0:T(8,128)(2,1)}, u32[]{:S(2)}, u32[]{:S(2)}) collective-permute-start(bf16[2,192,384]{2,1,0:T(8,128)(2,1)} %pad_maximum_fusion.47), channel_id=1, source_target_pairs={{0,2},{1,3},{2,0},{3,1},{4,6},{5,7},{6,4},{7,5},{8,10},{9,11},{10,... | collective-permute-start | bytes 884744 | tf_op jit(solution)/shard_map/ppermute | solution.py:270
  334.2 18.0 %collective-permute-start.45 = (bf16[8,96,768]{2,1,0:T(8,128)(2,1)}, bf16[8,96,768]{2,1,0:T(8,128)(2,1)}, u32[]{:S(2)}, u32[]{:S(2)}) collective-permute-start(bf16[8,96,768]{2,1,0:T(8,128)(2,1)} %get-tuple-element.217), channel_id=1, source_target_pairs={{0,2},{1,3},{2,0},{3,1},{4,6},{5,7},{6,4},{7,5},{8,10},{9,11},{10,... | collective-permute-start | bytes 3538952 | tf_op jit(solution)/shard_map/ppermute | solution.py:270
  352.1 53.9 %collective-permute-start.48 = (bf16[8,96,2304]{2,1,0:T(8,128)(2,1)}, bf16[8,96,2304]{2,1,0:T(8,128)(2,1)}, u32[]{:S(2)}, u32[]{:S(2)}) collective-permute-start(bf16[8,96,2304]{2,1,0:T(8,128)(2,1)} %get-tuple-element.228), channel_id=1, source_target_pairs={{0,2},{1,3},{2,0},{3,1},{4,6},{5,7},{6,4},{7,5},{8,10},{9,11},{10,... | collective-permute-start | bytes 10616840 | tf_op jit(solution)/shard_map/ppermute | solution.py:270
  354.9 15.2 %collective-permute-start.51 = (bf16[192,1536]{1,0:T(8,128)(2,1)S(1)}, bf16[192,1536]{1,0:T(8,128)(2,1)S(1)}, u32[]{:S(2)}, u32[]{:S(2)}) collective-permute-start(bf16[192,1536]{1,0:T(8,128)(2,1)S(1)} %get-tuple-element.233), channel_id=1, source_target_pairs={{0,16},{16,0},{1,17},{17,1},{2,18},{18,2},{3,19},{19,3},{4,20},{20... | collective-permute-start | bytes 1769480 | tf_op jit(solution)/shard_map/ppermute | solution.py:256
  359.1 46.9 %collective-permute-start.49 = (bf16[384,768]{1,0:T(8,128)(2,1)}, bf16[384,768]{1,0:T(8,128)(2,1)}, u32[]{:S(2)}, u32[]{:S(2)}) collective-permute-start(bf16[384,768]{1,0:T(8,128)(2,1)} %bitcast_convert_fusion), channel_id=1, source_target_pairs={{8,0},{9,1},{10,2},{11,3},{12,4},{13,5},{14,6},{15,7},{16,24},{17,... | collective-permute-start | bytes 1769480 | tf_op jit(solution)/shard_map/ppermute | solution.py:270
  367.0 39.0 %collective-permute-start.53 = (bf16[4,96,768]{2,1,0:T(8,128)(2,1)}, bf16[4,96,768]{2,1,0:T(8,128)(2,1)}, u32[]{:S(2)}, u32[]{:S(2)}) collective-permute-start(bf16[4,96,768]{2,1,0:T(8,128)(2,1)} %add_convert_fusion.7), channel_id=1, source_target_pairs={{0,1},{1,0},{2,3},{3,2},{4,5},{5,4},{6,7},{7,6},{8,9},{9,8},{10,11... | collective-permute-start | bytes 1769480 | tf_op jit(solution)/shard_map/ppermute | solution.py:270
  373.4 32.6 %collective-permute-start.52 = (bf16[4,96,768]{2,1,0:T(8,128)(2,1)}, bf16[4,96,768]{2,1,0:T(8,128)(2,1)}, u32[]{:S(2)}, u32[]{:S(2)}) collective-permute-start(bf16[4,96,768]{2,1,0:T(8,128)(2,1)} %add_convert_fusion.8), channel_id=1, source_target_pairs={{0,8},{1,9},{2,10},{3,11},{4,12},{5,13},{6,14},{7,15},{8,0},{9,1},... | collective-permute-start | bytes 1769480 | tf_op jit(solution)/shard_map/ppermute | solution.py:270
  409.7 21.9 %collective-permute-start.54 = (bf16[4,96,2304]{2,1,0:T(8,128)(2,1)}, bf16[4,96,2304]{2,1,0:T(8,128)(2,1)S(1)}, u32[]{:S(2)}, u32[]{:S(2)}) collective-permute-start(bf16[4,96,2304]{2,1,0:T(8,128)(2,1)} %add_convert_fusion), channel_id=1, source_target_pairs={{0,1},{1,0},{2,3},{3,2},{4,5},{5,4},{6,7},{7,6},{8,9},{9,8},{10,11... | collective-permute-start | bytes 5308424 | tf_op jit(solution)/shard_map/ppermute | solution.py:270
  431.6 19.5 %collective-permute-start.56 = (bf16[2,96,768]{2,1,0:T(8,128)(2,1)S(1)}, bf16[2,96,768]{2,1,0:T(8,128)(2,1)S(1)}, u32[]{:S(2)}, u32[]{:S(2)}) collective-permute-start(bf16[2,96,768]{2,1,0:T(8,128)(2,1)S(1)} %copy-done.158), channel_id=1, source_target_pairs={{0,4},{1,5},{2,6},{3,7},{4,0},{5,1},{6,2},{7,3},{8,12},{9,13},{10,... | collective-permute-start | bytes 884744 | tf_op jit(solution)/shard_map/ppermute | solution.py:270
  432.8 18.4 %collective-permute-start.57 = (bf16[2,96,768]{2,1,0:T(8,128)(2,1)S(1)}, bf16[2,96,768]{2,1,0:T(8,128)(2,1)S(1)}, u32[]{:S(2)}, u32[]{:S(2)}) collective-permute-start(bf16[2,96,768]{2,1,0:T(8,128)(2,1)S(1)} %copy-done.157), channel_id=1, source_target_pairs={{0,2},{1,3},{2,0},{3,1},{4,6},{5,7},{6,4},{7,5},{8,10},{9,11},{10,... | collective-permute-start | bytes 884744 | tf_op jit(solution)/shard_map/ppermute | solution.py:270
  433.2 39.0 %collective-permute-start.59 = (bf16[8,48,2688]{2,1,0:T(8,128)(2,1)}, bf16[8,48,2688]{2,1,0:T(8,128)(2,1)}, u32[]{:S(2)}, u32[]{:S(2)}) collective-permute-start(bf16[8,48,2688]{2,1,0:T(8,128)(2,1)} %get-tuple-element.264), channel_id=1, source_target_pairs={{0,2},{1,3},{2,0},{3,1},{4,6},{5,7},{6,4},{7,5},{8,10},{9,11},{10,... | collective-permute-start | bytes 6193160 | tf_op jit(solution)/shard_map/ppermute | solution.py:270
  437.0 35.1 %collective-permute-start.61 = (bf16[2,96,2304]{2,1,0:T(8,128)(2,1)}, bf16[2,96,2304]{2,1,0:T(8,128)(2,1)}, u32[]{:S(2)}, u32[]{:S(2)}) collective-permute-start(bf16[2,96,2304]{2,1,0:T(8,128)(2,1)} %add_convert_fusion.2), channel_id=1, source_target_pairs={{0,4},{1,5},{2,6},{3,7},{4,0},{5,1},{6,2},{7,3},{8,12},{9,13},{10,... | collective-permute-start | bytes 2654216 | tf_op jit(solution)/shard_map/ppermute | solution.py:270
  437.4 34.7 %collective-permute-start.62 = (bf16[4,192,768]{2,1,0:T(8,128)(2,1)}, bf16[4,192,768]{2,1,0:T(8,128)(2,1)}, u32[]{:S(2)}, u32[]{:S(2)}) collective-permute-start(bf16[4,192,768]{2,1,0:T(8,128)(2,1)} %get-tuple-element.267), channel_id=1, source_target_pairs={{0,4},{1,5},{2,6},{3,7},{4,0},{5,1},{6,2},{7,3},{8,12},{9,13},{10,... | collective-permute-start | bytes 3538952 | tf_op jit(solution)/shard_map/ppermute | solution.py:270
  452.1 18.8 %collective-permute-start.60 = (bf16[2,96,768]{2,1,0:T(8,128)(2,1)}, bf16[2,96,768]{2,1,0:T(8,128)(2,1)}, u32[]{:S(2)}, u32[]{:S(2)}) collective-permute-start(bf16[2,96,768]{2,1,0:T(8,128)(2,1)} %get-tuple-element.374), channel_id=1, source_target_pairs={{0,1},{1,0},{2,3},{3,2},{4,5},{5,4},{6,7},{7,6},{8,9},{9,8},{10,11... | collective-permute-start | bytes 884744 | tf_op jit(solution)/shard_map/ppermute | solution.py:270
  463.0 36.4 %collective-permute-start.58 = (bf16[8,48,1152]{2,1,0:T(8,128)(2,1)}, bf16[8,48,1152]{2,1,0:T(8,128)(2,1)}, u32[]{:S(2)}, u32[]{:S(2)}) collective-permute-start(bf16[8,48,1152]{2,1,0:T(8,128)(2,1)} %get-tuple-element.262), channel_id=1, source_target_pairs={{0,2},{1,3},{2,0},{3,1},{4,6},{5,7},{6,4},{7,5},{8,10},{9,11},{10,... | collective-permute-start | bytes 2654216 | tf_op jit(solution)/shard_map/ppermute | solution.py:270
  470.9 33.8 %collective-permute-start.71 = (bf16[1,96,768]{2,1,0:T(8,128)(2,1)}, bf16[1,96,768]{2,1,0:T(8,128)(2,1)}, u32[]{:S(2)}, u32[]{:S(2)}) collective-permute-start(bf16[1,96,768]{2,1,0:T(8,128)(2,1)} %add_convert_fusion.19), channel_id=1, source_target_pairs={{0,8},{1,9},{2,10},{3,11},{4,12},{5,13},{6,14},{7,15},{8,0},{9,1},... | collective-permute-start | bytes 442376 | tf_op jit(solution)/shard_map/ppermute | solution.py:270
  474.6 25.2 %collective-permute-start.63 = (bf16[4,48,2688]{2,1,0:T(8,128)(2,1)}, bf16[4,48,2688]{2,1,0:T(8,128)(2,1)}, u32[]{:S(2)}, u32[]{:S(2)}) collective-permute-start(bf16[4,48,2688]{2,1,0:T(8,128)(2,1)} %add_convert_fusion.1), channel_id=1, source_target_pairs={{0,4},{1,5},{2,6},{3,7},{4,0},{5,1},{6,2},{7,3},{8,12},{9,13},{10,... | collective-permute-start | bytes 3096584 | tf_op jit(solution)/shard_map/ppermute | solution.py:270
  488.6 21.8 %collective-permute-start.72 = (bf16[1,96,2304]{2,1,0:T(8,128)(2,1)}, bf16[1,96,2304]{2,1,0:T(8,128)(2,1)}, u32[]{:S(2)}, u32[]{:S(2)}) collective-permute-start(bf16[1,96,2304]{2,1,0:T(8,128)(2,1)} %add_convert_fusion.11), channel_id=1, source_target_pairs={{0,8},{1,9},{2,10},{3,11},{4,12},{5,13},{6,14},{7,15},{8,0},{9,1},... | collective-permute-start | bytes 1327112 | tf_op jit(solution)/shard_map/ppermute | solution.py:270
  500.9 15.3 %collective-permute-start.66 = (bf16[4,48,1152]{2,1,0:T(8,128)(2,1)S(1)}, bf16[4,48,1152]{2,1,0:T(8,128)(2,1)S(1)}, u32[]{:S(2)}, u32[]{:S(2)}) collective-permute-start(bf16[4,48,1152]{2,1,0:T(8,128)(2,1)S(1)} %add_convert_fusion.12), channel_id=1, source_target_pairs={{0,4},{1,5},{2,6},{3,7},{4,0},{5,1},{6,2},{7,3},{8,12},{9,13},{10,... | collective-permute-start | bytes 1327112 | tf_op jit(solution)/shard_map/ppermute | solution.py:270
  512.2 16.2 %collective-permute-start.74 = (bf16[2,48,2688]{2,1,0:T(8,128)(2,1)S(1)}, bf16[2,48,2688]{2,1,0:T(8,128)(2,1)S(1)}, u32[]{:S(2)}, u32[]{:S(2)}) collective-permute-start(bf16[2,48,2688]{2,1,0:T(8,128)(2,1)S(1)} %add_convert_fusion.9), channel_id=1, source_target_pairs={{0,1},{1,0},{2,3},{3,2},{4,5},{5,4},{6,7},{7,6},{8,9},{9,8},{10,11... | collective-permute-start | bytes 1548296 | tf_op jit(solution)/shard_map/ppermute | solution.py:270
  517.3 18.0 %collective-permute-start.73 = (bf16[2,48,1152]{2,1,0:T(8,128)(2,1)S(1)}, bf16[2,48,1152]{2,1,0:T(8,128)(2,1)S(1)}, u32[]{:S(2)}, u32[]{:S(2)}) collective-permute-start(bf16[2,48,1152]{2,1,0:T(8,128)(2,1)S(1)} %add_convert_fusion.17), channel_id=1, source_target_pairs={{0,1},{1,0},{2,3},{3,2},{4,5},{5,4},{6,7},{7,6},{8,9},{9,8},{10,11... | collective-permute-start | bytes 663560 | tf_op jit(solution)/shard_map/ppermute | solution.py:270
  524.2 22.3 %collective-permute-start.85 = (bf16[96,2304]{1,0:T(8,128)(2,1)S(1)}, bf16[96,2304]{1,0:T(8,128)(2,1)S(1)}, u32[]{:S(2)}, u32[]{:S(2)}) collective-permute-start(bf16[96,2304]{1,0:T(8,128)(2,1)S(1)} %fusion.46), channel_id=1, source_target_pairs={{0,16},{16,0},{1,17},{17,1},{2,18},{18,2},{3,19},{19,3},{4,20},{20... | collective-permute-start | bytes 1327112 | tf_op jit(solution)/shard_map/ppermute | solution.py:256
  535.4 18.1 %collective-permute-start.80 = (bf16[1,48,2688]{2,1,0:T(8,128)(2,1)S(1)}, bf16[1,48,2688]{2,1,0:T(8,128)(2,1)S(1)}, u32[]{:S(2)}, u32[]{:S(2)}) collective-permute-start(bf16[1,48,2688]{2,1,0:T(8,128)(2,1)S(1)} %add_convert_fusion.16), channel_id=1, source_target_pairs={{0,8},{1,9},{2,10},{3,11},{4,12},{5,13},{6,14},{7,15},{8,0},{9,1},... | collective-permute-start | bytes 774152 | tf_op jit(solution)/shard_map/ppermute | solution.py:270
  536.9 20.7 %collective-permute-start.84 = (bf16[192,768]{1,0:T(8,128)(2,1)S(1)}, bf16[192,768]{1,0:T(8,128)(2,1)S(1)}, u32[]{:S(2)}, u32[]{:S(2)}) collective-permute-start(bf16[192,768]{1,0:T(8,128)(2,1)S(1)} %fusion.44), channel_id=1, source_target_pairs={{0,16},{16,0},{1,17},{17,1},{2,18},{18,2},{3,19},{19,3},{4,20},{20... | collective-permute-start | bytes 884744 | tf_op jit(solution)/shard_map/ppermute | solution.py:256
  (237 other events, 1723.0 us)

commit v6 on v5

--- a/solution.py
+++ b/solution.py
@@ -1071,7 +1071,8 @@
     part = mm_nt(grad_up_g_rows, up_wg)
     part = half_of(part, core) + swap(half_of(part, 1 - core).astype(BF16)).astype(F32)
     part = advance([stream_down_g, stream_up_g], part)
-    part = shared(fresh(scatter_in_square(part.reshape(4, slots, half_g))).result())
+    part = fresh(scatter_in_square(part.reshape(4, slots, half_g))).result().astype(BF16)
+    part = shared(part).astype(F32)
     pulled, grad_gain_g2 = norm_backward(part, hidden_g, scale_g2, gain_two_g)
     grad_hidden_g = jnp.pad(grad_top_b.astype(F32), ((0, 0), (0, width_g - width_l))) + pulled
     grad_hidden_gb = grad_hidden_g.astype(BF16)

time: 569 us -> 567 us (level)
    unnamed x418 -> x390, local copies, waits for them, and re-layouts: 36.1 us -> 32.6 us
where the time goes in v6:
time: 567 us; the launch traced here: 560 us
  waiting for transfers between devices  140 us (25%)
  other arithmetic  113 us (20%)
  Pallas kernels  108 us (19%)
  starting transfers between devices  99.4 us (18%)
  local copies, waits for them, and re-layouts  56.9 us (10%)
  matrix products  38.5 us (7%)
    ppermute x57, waiting for transfers between devices, exchange(): lax.ppermute(part, ('section', 'dp'), pairs)  132 us
    ppermute x57, starting transfers between devices, exchange(): lax.ppermute(part, ('section', 'dp'), pairs)  66.6 us
    unnamed x390, local copies, waits for them, and re-layouts  32.6 us
    convert_element_type x15, other arithmetic, halving(): outgoing = total_of([term[half:] for term in terms]).astype(BF16)  28.3 us
    ppermute x25, starting transfers between devices, swap(): return lax.ppermute(array, 'section', [(0, 1), (1, 0)])  24.3 us
    pallas_call x3, Pallas kernels, product(): pl.pallas_call(functools.partial(product_kernel, self.rows, 4, gelu), gri...  20.9 us
    pallas_call x2, Pallas kernels, attention_backward(): pl.pallas_call(functools.partial(attention_backward_kernel, rows, window)...  18.2 us
    pallas_call x1, Pallas kernels, feed_forward_pullback(): pl.pallas_call(functools.partial(feed_forward_kernel, self.rows), grid_sp...  17.8 us
  transfers between devices with their start and end apart: 89, of which 27 were waited for; matrix products, arithmetic and copies ran while one was open for 27% of the time, Pallas kernels for 19%

profile of v6, /device:TPU:1, one launch (start us, length us, event | category | flops | bytes accessed | tf_op | source)
XLA Modules:
  0.0 560.0 jit_solution(9086682713579450157)
XLA Ops:
  7.6 3.2 collective-permute-start.1
  18.3 10.3 %collective-permute-done.1 = bf16[1,48,4224]{2,1,0:T(8,128)(2,1)S(1)} collective-permute-done((bf16[1,48,4224]{2,1,0:T(8,128)(2,1)S(1)}, bf16[1,48,4224]{2,1,0:T(8,128)(2,1)S(1)}, u32[]{:S(2)}, u32[]{:S(2)}) %collective-permute-start.1) | collective-permute-done | bytes 405536 | tf_op jit(solution)/shard_map/ppermute | solution.py:270
  37.1 4.0 collective-permute-done.4
  41.8 2.6 collective-permute-done.2
  51.4 7.0 %collective-permute-done.7 = bf16[1,96,2304]{2,1,0:T(8,128)(2,1)} collective-permute-done((bf16[1,96,2304]{2,1,0:T(8,128)(2,1)}, bf16[1,96,2304]{2,1,0:T(8,128)(2,1)}, u32[]{:S(2)}, u32[]{:S(2)}) %collective-permute-start.7) | collective-permute-done | bytes 442400 | tf_op jit(solution)/shard_map/ppermute | solution.py:270
  58.4 11.0 %collective-permute-done.8 = bf16[1,192,384]{2,1,0:T(8,128)(2,1)S(1)} collective-permute-done((bf16[1,192,384]{2,1,0:T(8,128)(2,1)}, bf16[1,192,384]{2,1,0:T(8,128)(2,1)S(1)}, u32[]{:S(2)}, u32[]{:S(2)}) %collective-permute-start.8) | collective-permute-done | bytes 147488 | tf_op jit(solution)/shard_map/ppermute | solution.py:270
  74.6 3.2 collective-permute-start.12
  85.9 10.3 %collective-permute-done.13 = bf16[1,192,768]{2,1,0:T(8,128)(2,1)} collective-permute-done((bf16[1,192,768]{2,1,0:T(8,128)(2,1)}, bf16[1,192,768]{2,1,0:T(8,128)(2,1)}, u32[]{:S(2)}, u32[]{:S(2)}) %collective-permute-start.13) | collective-permute-done | bytes 294944 | tf_op jit(solution)/shard_map/ppermute | solution.py:270
  96.3 14.7 %collective-permute-done.14 = bf16[2,192,384]{2,1,0:T(8,128)(2,1)} collective-permute-done((bf16[2,192,384]{2,1,0:T(8,128)(2,1)}, bf16[2,192,384]{2,1,0:T(8,128)(2,1)}, u32[]{:S(2)}, u32[]{:S(2)}) %collective-permute-start.14) | collective-permute-done | bytes 294944 | tf_op jit(solution)/shard_map/ppermute | solution.py:270
  117.1 3.1 collective-permute-start.19
  120.1 2.8 pad_maximum_fusion.3
  126.3 5.8 %shard_map.452.q_ref.k_ref.v_ref = bf16[1024,1152]{1,0:T(8,128)(2,1)} custom-call(s32[16]{0:T(128)S(1)} %get-tuple-element.420.table.places, bf16[1024,768]{1,0:T(8,128)(2,1)S(1)} %fusion.2.x_ref, bf16[4,48,4224]{2,1,0:T(8,128)(2,1)S(1)} %pad_maximum_fusion.4.refs_0_, bf16[4,48,4224]{2,1,0:T(8,128)(2,1)S(1)} %collective-permute-done.6.refs_1_, ...), custom_call_target="tpu_custom_call" | custom-call | tf_op jit(solution)/shard_map/pallas_call | solution.py:568
  135.0 9.5 %shard_map.453 = (bf16[1024,384]{1,0:T(8,128)(2,1)S(1)}, f32[3,2,1024]{2,1,0:T(2,128)S(1)}) custom-call(bf16[1024,1152]{1,0:T(8,128)(2,1)S(1)} %copy-done.3, bf16[1024,1152]{1,0:T(8,128)(2,1)S(1)} %copy-done.3, bf16[1024,1152]{1,0:T(8,128)(2,1)S(1)} %copy-done.3, f32[1024,1]{1,0:T(8,128)S(1)} %fusion.52.bias_ref), custom_call_target="tpu_custom_call" | custom-call | tf_op jit(solution)/shard_map/pallas_call | solution.py:210
  144.6 16.2 %collective-permute-done.19 = bf16[1,96,768]{2,1,0:T(8,128)(2,1)S(1)} collective-permute-done((bf16[1,96,768]{2,1,0:T(8,128)(2,1)S(1)}, bf16[1,96,768]{2,1,0:T(8,128)(2,1)S(1)}, u32[]{:S(2)}, u32[]{:S(2)}) %collective-permute-start.19) | collective-permute-done | bytes 147488 | tf_op jit(solution)/shard_map/ppermute | solution.py:270
  168.0 2.8 pad_maximum_fusion.refs_0_.refs_1_
  176.6 10.3 %shard_map.454 = (bf16[1024,1536]{1,0:T(8,128)(2,1)}, bf16[1024,1536]{1,0:T(8,128)(2,1)}) custom-call(s32[16]{0:T(128)S(1)} %get-tuple-element.420.table.places, bf16[1024,768]{1,0:T(8,128)(2,1)S(1)} %multiply_convert_fusion.x_ref, bf16[4,48,4224]{2,1,0:T(8,128)(2,1)S(1)} %copy-done.5, bf16[4,48,4224]{2,1,0:T(8,128)(2,1)S(1)} %copy-done.8, ...), custom_call_target="tpu_custom_call" | custom-call | flops 99999997952 | tf_op jit(solution)/shard_map/pallas_call | solution.py:568
  187.8 5.3 fusion.142
  206.5 9.0 %collective-permute-done.29 = bf16[4,96,768]{2,1,0:T(8,128)(2,1)S(1)} collective-permute-done((bf16[4,96,768]{2,1,0:T(8,128)(2,1)S(1)}, bf16[4,96,768]{2,1,0:T(8,128)(2,1)S(1)}, u32[]{:S(2)}, u32[]{:S(2)}) %collective-permute-start.29) | collective-permute-done | bytes 589856 | tf_op jit(solution)/shard_map/ppermute | solution.py:270
  215.5 13.1 %collective-permute-done.30.refs_1_ = bf16[8,96,768]{2,1,0:T(8,128)(2,1)S(1)} collective-permute-done((bf16[8,96,768]{2,1,0:T(8,128)(2,1)S(1)}, bf16[8,96,768]{2,1,0:T(8,128)(2,1)S(1)}, u32[]{:S(2)}, u32[]{:S(2)}) %collective-permute-start.30) | collective-permute-done | bytes 1179680 | tf_op jit(solution)/shard_map/ppermute | solution.py:270
  238.4 4.8 shard_map.456.q_ref.k_ref.v_ref
  243.2 4.6 shard_map.457
  253.2 3.6 collective-permute-done.33
  263.3 4.6 collective-permute-done.35
  297.2 3.3 convolution_convert_fusion.1.refs_0_
  310.2 3.7 collective-permute-done.41
  317.1 2.9 collective-permute-done.42
  332.6 4.5 shard_map.464
  337.8 10.5 %shard_map.465 = (bf16[192,1536]{1,0:T(8,128)(2,1)S(1)}, bf16[8,96,2304]{2,1,0:T(8,128)(2,1)}, bf16[8,96,2304]{2,1,0:T(8,128)(2,1)}) custom-call(s32[16]{0:T(128)S(1)} %get-tuple-element.419.table, s32[16]{0:T(128)S(1)} %get-tuple-element.418.table.places, bf16[192,1536]{1,0:T(8,128)(2,1)S(1)} %copy-done.20, bf16[8,96,2304]{2,1,0:T(8,128)(2,1)} %copy-done.2, ...), custom_call_target="tpu_custom_call" | custom-call | tf_op jit(solution)/shard_map/pallas_call | solution.py:672
  356.9 5.8 %collective-permute-start.49 = (bf16[384,768]{1,0:T(8,128)(2,1)}, bf16[384,768]{1,0:T(8,128)(2,1)}, u32[]{:S(2)}, u32[]{:S(2)}) collective-permute-start(bf16[384,768]{1,0:T(8,128)(2,1)} %bitcast_convert_fusion), channel_id=1, source_target_pairs={{8,0},{9,1},{10,2},{11,3},{12,4},{13,5},{14,6},{15,7},{16,24},{17,... | collective-permute-start | bytes 1769480 | tf_op jit(solution)/shard_map/ppermute | solution.py:270
  374.6 5.8 %fusion.15 = (bf16[1024,768]{1,0:T(8,128)(2,1)}, f32[1024,768]{1,0:T(8,128)}) fusion(bf16[1024,384]{1,0:T(8,128)(2,1)} %copy-done.85, bf16[1024,384]{1,0:T(8,128)(2,1)S(1)} %copy-done.84, bf16[192,1536]{1,0:T(8,128)(2,1)} %add_convert_fusion.6, bf16[768,768]{1,0:T(8,128)(2,1)} %copy-done.112, bf16[768,768]{1,0:T(8,128)(2,1)} %copy-done.111, ...), kind=kOutput, calls=%fused_computation.39 | convolution fusion | flops 764755968 | bytes 9241344 | tf_op jit(solution)/shard_map/dot_general | solution.py:33
  381.8 17.8 %shard_map.466 = (bf16[1024,768]{1,0:T(8,128)(2,1)S(1)}, bf16[1536,768]{1,0:T(8,128)(2,1)}, bf16[8,48,2688]{2,1,0:T(8,128)(2,1)}, bf16[8,48,2688]{2,1,0:T(8,128)(2,1)}) custom-call(s32[16]{0:T(128)S(1)} %get-tuple-element.420.table.places, s32[16]{0:T(128)S(1)} %get-tuple-element.420.table.places, bf16[1024,768]{1,0:T(8,128)(2,1)S(1)} %copy-done.18, ...), custom_call_target="tpu_custom_call" | custom-call | tf_op jit(solution)/shard_map/pallas_call | solution.py:594
  403.6 3.6 add_convert_fusion
  417.6 2.6 fusion.130
  426.3 2.9 collective-permute-done.54
  431.8 2.8 add_convert_fusion.2
  435.2 13.7 %shard_map.469 = (bf16[1024,384]{1,0:T(8,128)(2,1)S(1)}, bf16[1024,384]{1,0:T(8,128)(2,1)S(1)}, bf16[1024,384]{1,0:T(8,128)(2,1)S(1)}) custom-call(bf16[1024,1152]{1,0:T(8,128)(2,1)} %shard_map.452.q_ref.k_ref.v_ref, bf16[1024,1152]{1,0:T(8,128)(2,1)} %shard_map.452.q_ref.k_ref.v_ref, bf16[1024,1152]{1,0:T(8,128)(2,1)} %shard_map.452.q_ref.k_ref.v_ref, ...), custom_call_target="tpu_custom_call" | custom-call | flops 99999997952 | tf_op jit(solution)/shard_map/pallas_call | solution.py:230
  455.4 5.2 shard_map.470
  461.1 5.7 %shard_map.471 = bf16[1024,768]{1,0:T(8,128)(2,1)S(1)} custom-call(s32[16]{0:T(128)S(1)} %get-tuple-element.420.table.places, bf16[4,48,4224]{2,1,0:T(8,128)(2,1)S(1)} %copy-done.6, bf16[4,48,4224]{2,1,0:T(8,128)(2,1)} %copy-done.7, bf16[4,48,4224]{2,1,0:T(8,128)(2,1)} %collective-permute-done.10.refs_2_, ...), custom_call_target="tpu_custom_call" | custom-call | tf_op jit(solution)/shard_map/pallas_call | solution.py:648
  473.6 4.1 collective-permute-start.65
  487.4 3.7 fusion.5
  493.4 3.7 fusion.37
  503.9 4.5 collective-permute-done.72
  510.3 3.9 collective-permute-done.70
  516.6 3.6 collective-permute-start.75
  527.0 2.8 collective-permute-start.77
  534.7 3.3 collective-permute-start.84
  540.3 2.6 collective-permute-start.81
  545.6 5.9 %collective-permute-done.81 = bf16[1,48,1152]{2,1,0:T(8,128)(2,1)S(1)} collective-permute-done((bf16[1,48,1152]{2,1,0:T(8,128)(2,1)S(1)}, bf16[1,48,1152]{2,1,0:T(8,128)(2,1)S(1)}, u32[]{:S(2)}, u32[]{:S(2)}) %collective-permute-start.81) | collective-permute-done | bytes 110624 | tf_op jit(solution)/shard_map/ppermute | solution.py:270
  (737 shorter events, 265.1 us)
Async XLA Ops:
  7.6 21.0 %collective-permute-start.1 = (bf16[1,48,4224]{2,1,0:T(8,128)(2,1)S(1)}, bf16[1,48,4224]{2,1,0:T(8,128)(2,1)S(1)}, u32[]{:S(2)}, u32[]{:S(2)}) collective-permute-start(bf16[1,48,4224]{2,1,0:T(8,128)(2,1)S(1)} %bitcast.157), channel_id=1, source_target_pairs={{0,8},{1,9},{2,10},{3,11},{4,12},{5,13},{6,14},{7,15},{8,0},{9,1},... | collective-permute-start | bytes 1216520 | tf_op jit(solution)/shard_map/ppermute | solution.py:270
  29.6 14.8 %collective-permute-start.2 = (bf16[2,48,4224]{2,1,0:T(8,128)(2,1)}, bf16[2,48,4224]{2,1,0:T(8,128)(2,1)S(1)}, u32[]{:S(2)}, u32[]{:S(2)}) collective-permute-start(bf16[2,48,4224]{2,1,0:T(8,128)(2,1)} %pad_maximum_fusion.28), channel_id=1, source_target_pairs={{0,1},{1,0},{2,3},{3,2},{4,5},{5,4},{6,7},{7,6},{8,9},{9,8},{10,11... | collective-permute-start | bytes 2433032 | tf_op jit(solution)/shard_map/ppermute | solution.py:270
  44.6 24.9 %collective-permute-start.6 = (bf16[4,48,4224]{2,1,0:T(8,128)(2,1)S(1)}, bf16[4,48,4224]{2,1,0:T(8,128)(2,1)S(1)}, u32[]{:S(2)}, u32[]{:S(2)}) collective-permute-start(bf16[4,48,4224]{2,1,0:T(8,128)(2,1)S(1)} %pad_maximum_fusion.4.refs_0_), channel_id=1, source_target_pairs={{0,4},{1,5},{2,6},{3,7},{4,0},{5,1},{6,2},{7,3},{8,12},{9,13},{10,... | collective-permute-start | bytes 4866056 | tf_op jit(solution)/shard_map/ppermute | solution.py:270
  49.9 19.5 %collective-permute-start.9 = (bf16[2,96,768]{2,1,0:T(8,128)(2,1)S(1)}, bf16[2,96,768]{2,1,0:T(8,128)(2,1)S(1)}, u32[]{:S(2)}, u32[]{:S(2)}) collective-permute-start(bf16[2,96,768]{2,1,0:T(8,128)(2,1)S(1)} %get-tuple-element.386), channel_id=1, source_target_pairs={{0,2},{1,3},{2,0},{3,1},{4,6},{5,7},{6,4},{7,5},{8,10},{9,11},{10,... | collective-permute-start | bytes 884744 | tf_op jit(solution)/shard_map/ppermute | solution.py:270
  51.2 18.3 %collective-permute-start.8 = (bf16[1,192,384]{2,1,0:T(8,128)(2,1)}, bf16[1,192,384]{2,1,0:T(8,128)(2,1)S(1)}, u32[]{:S(2)}, u32[]{:S(2)}) collective-permute-start(bf16[1,192,384]{2,1,0:T(8,128)(2,1)} %dynamic-slice_bitcast_fusion.7), channel_id=1, source_target_pairs={{0,1},{1,0},{2,3},{3,2},{4,5},{5,4},{6,7},{7,6},{8,9},{9,8},{10,11... | collective-permute-start | bytes 442376 | tf_op jit(solution)/shard_map/ppermute | solution.py:270
  70.2 40.7 %collective-permute-start.10 = (bf16[4,48,4224]{2,1,0:T(8,128)(2,1)S(1)}, bf16[4,48,4224]{2,1,0:T(8,128)(2,1)}, u32[]{:S(2)}, u32[]{:S(2)}) collective-permute-start(bf16[4,48,4224]{2,1,0:T(8,128)(2,1)S(1)} %pad_maximum_fusion.4.refs_0_), channel_id=1, source_target_pairs={{0,2},{1,3},{2,0},{3,1},{4,6},{5,7},{6,4},{7,5},{8,10},{9,11},{10,... | collective-permute-start | bytes 4866056 | tf_op jit(solution)/shard_map/ppermute | solution.py:270
  71.2 39.8 %collective-permute-start.11 = (bf16[4,48,4224]{2,1,0:T(8,128)(2,1)S(1)}, bf16[4,48,4224]{2,1,0:T(8,128)(2,1)}, u32[]{:S(2)}, u32[]{:S(2)}) collective-permute-start(bf16[4,48,4224]{2,1,0:T(8,128)(2,1)S(1)} %collective-permute-done.6.refs_1_), channel_id=1, source_target_pairs={{0,2},{1,3},{2,0},{3,1},{4,6},{5,7},{6,4},{7,5},{8,10},{9,11},{10,... | collective-permute-start | bytes 4866056 | tf_op jit(solution)/shard_map/ppermute | solution.py:270
  74.6 36.3 %collective-permute-start.12 = (bf16[2,96,2304]{2,1,0:T(8,128)(2,1)}, bf16[2,96,2304]{2,1,0:T(8,128)(2,1)}, u32[]{:S(2)}, u32[]{:S(2)}) collective-permute-start(bf16[2,96,2304]{2,1,0:T(8,128)(2,1)} %pad_maximum_fusion.27), channel_id=1, source_target_pairs={{0,4},{1,5},{2,6},{3,7},{4,0},{5,1},{6,2},{7,3},{8,12},{9,13},{10,... | collective-permute-start | bytes 2654216 | tf_op jit(solution)/shard_map/ppermute | solution.py:270
  79.3 17.0 %collective-permute-start.13 = (bf16[1,192,768]{2,1,0:T(8,128)(2,1)}, bf16[1,192,768]{2,1,0:T(8,128)(2,1)}, u32[]{:S(2)}, u32[]{:S(2)}) collective-permute-start(bf16[1,192,768]{2,1,0:T(8,128)(2,1)} %select_bitcast_fusion.1), channel_id=1, source_target_pairs={{0,4},{1,5},{2,6},{3,7},{4,0},{5,1},{6,2},{7,3},{8,12},{9,13},{10,... | collective-permute-start | bytes 884744 | tf_op jit(solution)/shard_map/ppermute | solution.py:270
  80.0 30.9 %collective-permute-start.14 = (bf16[2,192,384]{2,1,0:T(8,128)(2,1)}, bf16[2,192,384]{2,1,0:T(8,128)(2,1)}, u32[]{:S(2)}, u32[]{:S(2)}) collective-permute-start(bf16[2,192,384]{2,1,0:T(8,128)(2,1)} %pad_maximum_fusion.45), channel_id=1, source_target_pairs={{0,2},{1,3},{2,0},{3,1},{4,6},{5,7},{6,4},{7,5},{8,10},{9,11},{10,... | collective-permute-start | bytes 884744 | tf_op jit(solution)/shard_map/ppermute | solution.py:270
  112.1 48.7 %collective-permute-start.16 = (bf16[2,192,768]{2,1,0:T(8,128)(2,1)S(1)}, bf16[2,192,768]{2,1,0:T(8,128)(2,1)S(1)}, u32[]{:S(2)}, u32[]{:S(2)}) collective-permute-start(bf16[2,192,768]{2,1,0:T(8,128)(2,1)S(1)} %pad_maximum_fusion.37), channel_id=1, source_target_pairs={{0,1},{1,0},{2,3},{3,2},{4,5},{5,4},{6,7},{7,6},{8,9},{9,8},{10,11... | collective-permute-start | bytes 1769480 | tf_op jit(solution)/shard_map/ppermute | solution.py:270
  113.1 47.6 %collective-permute-start.17 = (bf16[4,96,768]{2,1,0:T(8,128)(2,1)S(1)}, bf16[4,96,768]{2,1,0:T(8,128)(2,1)S(1)}, u32[]{:S(2)}, u32[]{:S(2)}) collective-permute-start(bf16[4,96,768]{2,1,0:T(8,128)(2,1)S(1)} %pad_maximum_fusion.36), channel_id=1, source_target_pairs={{0,8},{1,9},{2,10},{3,11},{4,12},{5,13},{6,14},{7,15},{8,0},{9,1},... | collective-permute-start | bytes 1769480 | tf_op jit(solution)/shard_map/ppermute | solution.py:270
  115.6 45.2 %collective-permute-start.18 = (bf16[384,768]{1,0:T(8,128)(2,1)S(1)}, bf16[384,768]{1,0:T(8,128)(2,1)S(1)}, u32[]{:S(2)}, u32[]{:S(2)}) collective-permute-start(bf16[384,768]{1,0:T(8,128)(2,1)S(1)} %copy-done.136), channel_id=1, source_target_pairs={{0,8},{1,9},{2,10},{3,11},{4,12},{5,13},{6,14},{7,15},{24,16},{25,... | collective-permute-start | bytes 1769480 | tf_op jit(solution)/shard_map/ppermute | solution.py:270
  117.1 43.7 %collective-permute-start.19 = (bf16[1,96,768]{2,1,0:T(8,128)(2,1)S(1)}, bf16[1,96,768]{2,1,0:T(8,128)(2,1)S(1)}, u32[]{:S(2)}, u32[]{:S(2)}) collective-permute-start(bf16[1,96,768]{2,1,0:T(8,128)(2,1)S(1)} %copy-done.95), channel_id=1, source_target_pairs={{0,8},{1,9},{2,10},{3,11},{4,12},{5,13},{6,14},{7,15},{8,0},{9,1},... | collective-permute-start | bytes 442376 | tf_op jit(solution)/shard_map/ppermute | solution.py:270
  122.9 44.7 %collective-permute-start.15 = (bf16[4,96,2304]{2,1,0:T(8,128)(2,1)}, bf16[4,96,2304]{2,1,0:T(8,128)(2,1)}, u32[]{:S(2)}, u32[]{:S(2)}) collective-permute-start(bf16[4,96,2304]{2,1,0:T(8,128)(2,1)} %pad_maximum_fusion.3), channel_id=1, source_target_pairs={{0,1},{1,0},{2,3},{3,2},{4,5},{5,4},{6,7},{7,6},{8,9},{9,8},{10,11... | collective-permute-start | bytes 5308424 | tf_op jit(solution)/shard_map/ppermute | solution.py:270
  163.0 23.9 %collective-permute-start.22 = (bf16[4,192,768]{2,1,0:T(8,128)(2,1)S(1)}, bf16[4,192,768]{2,1,0:T(8,128)(2,1)S(1)}, u32[]{:S(2)}, u32[]{:S(2)}) collective-permute-start(bf16[4,192,768]{2,1,0:T(8,128)(2,1)S(1)} %pad_maximum_fusion.19.refs_0_.refs_1_), channel_id=1, source_target_pairs={{0,2},{1,3},{2,0},{3,1},{4,6},{5,7},{6,4},{7,5},{8,10},{9,11},{10,... | collective-permute-start | bytes 3538952 | tf_op jit(solution)/shard_map/ppermute | solution.py:270
  165.4 21.5 %collective-permute-start.23 = (bf16[1,384,768]{2,1,0:T(8,128)(2,1)S(1)}, bf16[1,384,768]{2,1,0:T(8,128)(2,1)S(1)}, u32[]{:S(2)}, u32[]{:S(2)}) collective-permute-start(bf16[1,384,768]{2,1,0:T(8,128)(2,1)S(1)} %select_bitcast_fusion.refs_0_), channel_id=1, source_target_pairs={{0,4},{1,5},{2,6},{3,7},{4,0},{5,1},{6,2},{7,3},{8,12},{9,13},{10,... | collective-permute-start | bytes 1769480 | tf_op jit(solution)/shard_map/ppermute | solution.py:270
  167.2 19.7 %collective-permute-start.24 = (bf16[2,96,768]{2,1,0:T(8,128)(2,1)}, bf16[2,96,768]{2,1,0:T(8,128)(2,1)S(1)}, u32[]{:S(2)}, u32[]{:S(2)}) collective-permute-start(bf16[2,96,768]{2,1,0:T(8,128)(2,1)} %pad_maximum_fusion.49), channel_id=1, source_target_pairs={{0,4},{1,5},{2,6},{3,7},{4,0},{5,1},{6,2},{7,3},{8,12},{9,13},{10,... | collective-permute-start | bytes 884744 | tf_op jit(solution)/shard_map/ppermute | solution.py:270
  170.8 58.9 %collective-permute-start.28 = (bf16[8,96,2304]{2,1,0:T(8,128)(2,1)S(1)}, bf16[8,96,2304]{2,1,0:T(8,128)(2,1)}, u32[]{:S(2)}, u32[]{:S(2)}) collective-permute-start(bf16[8,96,2304]{2,1,0:T(8,128)(2,1)S(1)} %pad_maximum_fusion.refs_0_.refs_1_), channel_id=1, source_target_pairs={{0,2},{1,3},{2,0},{3,1},{4,6},{5,7},{6,4},{7,5},{8,10},{9,11},{10,... | collective-permute-start | bytes 10616840 | tf_op jit(solution)/shard_map/ppermute | solution.py:270
  199.9 15.6 %collective-permute-start.29 = (bf16[4,96,768]{2,1,0:T(8,128)(2,1)S(1)}, bf16[4,96,768]{2,1,0:T(8,128)(2,1)S(1)}, u32[]{:S(2)}, u32[]{:S(2)}) collective-permute-start(bf16[4,96,768]{2,1,0:T(8,128)(2,1)S(1)} %pad_maximum_fusion.38), channel_id=1, source_target_pairs={{0,1},{1,0},{2,3},{3,2},{4,5},{5,4},{6,7},{7,6},{8,9},{9,8},{10,11... | collective-permute-start | bytes 1769480 | tf_op jit(solution)/shard_map/ppermute | solution.py:270
  201.3 27.4 %collective-permute-start.30 = (bf16[8,96,768]{2,1,0:T(8,128)(2,1)S(1)}, bf16[8,96,768]{2,1,0:T(8,128)(2,1)S(1)}, u32[]{:S(2)}, u32[]{:S(2)}) collective-permute-start(bf16[8,96,768]{2,1,0:T(8,128)(2,1)S(1)} %pad_maximum_fusion.20.refs_0_), channel_id=1, source_target_pairs={{0,4},{1,5},{2,6},{3,7},{4,0},{5,1},{6,2},{7,3},{8,12},{9,13},{10,... | collective-permute-start | bytes 3538952 | tf_op jit(solution)/shard_map/ppermute | solution.py:270
  230.9 17.5 %collective-permute-start.32 = (bf16[8,96,768]{2,1,0:T(8,128)(2,1)}, bf16[8,96,768]{2,1,0:T(8,128)(2,1)}, u32[]{:S(2)}, u32[]{:S(2)}) collective-permute-start(bf16[8,96,768]{2,1,0:T(8,128)(2,1)} %pad_maximum_fusion.22.refs_0_.refs_1_), channel_id=1, source_target_pairs={{0,2},{1,3},{2,0},{3,1},{4,6},{5,7},{6,4},{7,5},{8,10},{9,11},{10,... | collective-permute-start | bytes 3538952 | tf_op jit(solution)/shard_map/ppermute | solution.py:270
  322.6 25.7 %collective-permute-start.46 = (bf16[1,384,768]{2,1,0:T(8,128)(2,1)}, bf16[1,384,768]{2,1,0:T(8,128)(2,1)}, u32[]{:S(2)}, u32[]{:S(2)}) collective-permute-start(bf16[1,384,768]{2,1,0:T(8,128)(2,1)} %get-tuple-element.218), channel_id=1, source_target_pairs={{0,4},{1,5},{2,6},{3,7},{4,0},{5,1},{6,2},{7,3},{8,12},{9,13},{10,... | collective-permute-start | bytes 1769480 | tf_op jit(solution)/shard_map/ppermute | solution.py:270
  323.5 44.5 %collective-permute-start.50 = (bf16[8,96,768]{2,1,0:T(8,128)(2,1)}, bf16[8,96,768]{2,1,0:T(8,128)(2,1)}, u32[]{:S(2)}, u32[]{:S(2)}) collective-permute-start(bf16[8,96,768]{2,1,0:T(8,128)(2,1)} %get-tuple-element.232), channel_id=1, source_target_pairs={{0,4},{1,5},{2,6},{3,7},{4,0},{5,1},{6,2},{7,3},{8,12},{9,13},{10,... | collective-permute-start | bytes 3538952 | tf_op jit(solution)/shard_map/ppermute | solution.py:270
  331.1 17.3 %collective-permute-start.44 = (bf16[2,192,384]{2,1,0:T(8,128)(2,1)}, bf16[2,192,384]{2,1,0:T(8,128)(2,1)}, u32[]{:S(2)}, u32[]{:S(2)}) collective-permute-start(bf16[2,192,384]{2,1,0:T(8,128)(2,1)} %pad_maximum_fusion.47), channel_id=1, source_target_pairs={{0,2},{1,3},{2,0},{3,1},{4,6},{5,7},{6,4},{7,5},{8,10},{9,11},{10,... | collective-permute-start | bytes 884744 | tf_op jit(solution)/shard_map/ppermute | solution.py:270
  332.0 18.0 %collective-permute-start.45 = (bf16[8,96,768]{2,1,0:T(8,128)(2,1)}, bf16[8,96,768]{2,1,0:T(8,128)(2,1)}, u32[]{:S(2)}, u32[]{:S(2)}) collective-permute-start(bf16[8,96,768]{2,1,0:T(8,128)(2,1)} %get-tuple-element.217), channel_id=1, source_target_pairs={{0,2},{1,3},{2,0},{3,1},{4,6},{5,7},{6,4},{7,5},{8,10},{9,11},{10,... | collective-permute-start | bytes 3538952 | tf_op jit(solution)/shard_map/ppermute | solution.py:270
  350.0 53.6 %collective-permute-start.48 = (bf16[8,96,2304]{2,1,0:T(8,128)(2,1)}, bf16[8,96,2304]{2,1,0:T(8,128)(2,1)}, u32[]{:S(2)}, u32[]{:S(2)}) collective-permute-start(bf16[8,96,2304]{2,1,0:T(8,128)(2,1)} %get-tuple-element.228), channel_id=1, source_target_pairs={{0,2},{1,3},{2,0},{3,1},{4,6},{5,7},{6,4},{7,5},{8,10},{9,11},{10,... | collective-permute-start | bytes 10616840 | tf_op jit(solution)/shard_map/ppermute | solution.py:270
  352.7 15.1 %collective-permute-start.51 = (bf16[192,1536]{1,0:T(8,128)(2,1)S(1)}, bf16[192,1536]{1,0:T(8,128)(2,1)S(1)}, u32[]{:S(2)}, u32[]{:S(2)}) collective-permute-start(bf16[192,1536]{1,0:T(8,128)(2,1)S(1)} %get-tuple-element.233), channel_id=1, source_target_pairs={{0,16},{16,0},{1,17},{17,1},{2,18},{18,2},{3,19},{19,3},{4,20},{20... | collective-permute-start | bytes 1769480 | tf_op jit(solution)/shard_map/ppermute | solution.py:256
  356.9 46.7 %collective-permute-start.49 = (bf16[384,768]{1,0:T(8,128)(2,1)}, bf16[384,768]{1,0:T(8,128)(2,1)}, u32[]{:S(2)}, u32[]{:S(2)}) collective-permute-start(bf16[384,768]{1,0:T(8,128)(2,1)} %bitcast_convert_fusion), channel_id=1, source_target_pairs={{8,0},{9,1},{10,2},{11,3},{12,4},{13,5},{14,6},{15,7},{16,24},{17,... | collective-permute-start | bytes 1769480 | tf_op jit(solution)/shard_map/ppermute | solution.py:270
  364.7 38.8 %collective-permute-start.53 = (bf16[4,96,768]{2,1,0:T(8,128)(2,1)}, bf16[4,96,768]{2,1,0:T(8,128)(2,1)}, u32[]{:S(2)}, u32[]{:S(2)}) collective-permute-start(bf16[4,96,768]{2,1,0:T(8,128)(2,1)} %add_convert_fusion.7), channel_id=1, source_target_pairs={{0,1},{1,0},{2,3},{3,2},{4,5},{5,4},{6,7},{7,6},{8,9},{9,8},{10,11... | collective-permute-start | bytes 1769480 | tf_op jit(solution)/shard_map/ppermute | solution.py:270
  371.1 32.5 %collective-permute-start.52 = (bf16[4,96,768]{2,1,0:T(8,128)(2,1)}, bf16[4,96,768]{2,1,0:T(8,128)(2,1)}, u32[]{:S(2)}, u32[]{:S(2)}) collective-permute-start(bf16[4,96,768]{2,1,0:T(8,128)(2,1)} %add_convert_fusion.8), channel_id=1, source_target_pairs={{0,8},{1,9},{2,10},{3,11},{4,12},{5,13},{6,14},{7,15},{8,0},{9,1},... | collective-permute-start | bytes 1769480 | tf_op jit(solution)/shard_map/ppermute | solution.py:270
  407.3 21.9 %collective-permute-start.54 = (bf16[4,96,2304]{2,1,0:T(8,128)(2,1)}, bf16[4,96,2304]{2,1,0:T(8,128)(2,1)S(1)}, u32[]{:S(2)}, u32[]{:S(2)}) collective-permute-start(bf16[4,96,2304]{2,1,0:T(8,128)(2,1)} %add_convert_fusion), channel_id=1, source_target_pairs={{0,1},{1,0},{2,3},{3,2},{4,5},{5,4},{6,7},{7,6},{8,9},{9,8},{10,11... | collective-permute-start | bytes 5308424 | tf_op jit(solution)/shard_map/ppermute | solution.py:270
  429.2 19.8 %collective-permute-start.56 = (bf16[2,96,768]{2,1,0:T(8,128)(2,1)S(1)}, bf16[2,96,768]{2,1,0:T(8,128)(2,1)S(1)}, u32[]{:S(2)}, u32[]{:S(2)}) collective-permute-start(bf16[2,96,768]{2,1,0:T(8,128)(2,1)S(1)} %copy-done.151), channel_id=1, source_target_pairs={{0,4},{1,5},{2,6},{3,7},{4,0},{5,1},{6,2},{7,3},{8,12},{9,13},{10,... | collective-permute-start | bytes 884744 | tf_op jit(solution)/shard_map/ppermute | solution.py:270
  430.4 18.6 %collective-permute-start.57 = (bf16[2,96,768]{2,1,0:T(8,128)(2,1)S(1)}, bf16[2,96,768]{2,1,0:T(8,128)(2,1)S(1)}, u32[]{:S(2)}, u32[]{:S(2)}) collective-permute-start(bf16[2,96,768]{2,1,0:T(8,128)(2,1)S(1)} %copy-done.150), channel_id=1, source_target_pairs={{0,2},{1,3},{2,0},{3,1},{4,6},{5,7},{6,4},{7,5},{8,10},{9,11},{10,... | collective-permute-start | bytes 884744 | tf_op jit(solution)/shard_map/ppermute | solution.py:270
  430.7 39.2 %collective-permute-start.59 = (bf16[8,48,2688]{2,1,0:T(8,128)(2,1)}, bf16[8,48,2688]{2,1,0:T(8,128)(2,1)}, u32[]{:S(2)}, u32[]{:S(2)}) collective-permute-start(bf16[8,48,2688]{2,1,0:T(8,128)(2,1)} %get-tuple-element.264), channel_id=1, source_target_pairs={{0,2},{1,3},{2,0},{3,1},{4,6},{5,7},{6,4},{7,5},{8,10},{9,11},{10,... | collective-permute-start | bytes 6193160 | tf_op jit(solution)/shard_map/ppermute | solution.py:270
  434.6 35.3 %collective-permute-start.61 = (bf16[2,96,2304]{2,1,0:T(8,128)(2,1)}, bf16[2,96,2304]{2,1,0:T(8,128)(2,1)}, u32[]{:S(2)}, u32[]{:S(2)}) collective-permute-start(bf16[2,96,2304]{2,1,0:T(8,128)(2,1)} %add_convert_fusion.2), channel_id=1, source_target_pairs={{0,4},{1,5},{2,6},{3,7},{4,0},{5,1},{6,2},{7,3},{8,12},{9,13},{10,... | collective-permute-start | bytes 2654216 | tf_op jit(solution)/shard_map/ppermute | solution.py:270
  434.9 35.0 %collective-permute-start.62 = (bf16[4,192,768]{2,1,0:T(8,128)(2,1)}, bf16[4,192,768]{2,1,0:T(8,128)(2,1)}, u32[]{:S(2)}, u32[]{:S(2)}) collective-permute-start(bf16[4,192,768]{2,1,0:T(8,128)(2,1)} %get-tuple-element.267), channel_id=1, source_target_pairs={{0,4},{1,5},{2,6},{3,7},{4,0},{5,1},{6,2},{7,3},{8,12},{9,13},{10,... | collective-permute-start | bytes 3538952 | tf_op jit(solution)/shard_map/ppermute | solution.py:270
  449.9 18.7 %collective-permute-start.60 = (bf16[2,96,768]{2,1,0:T(8,128)(2,1)}, bf16[2,96,768]{2,1,0:T(8,128)(2,1)}, u32[]{:S(2)}, u32[]{:S(2)}) collective-permute-start(bf16[2,96,768]{2,1,0:T(8,128)(2,1)} %get-tuple-element.372), channel_id=1, source_target_pairs={{0,1},{1,0},{2,3},{3,2},{4,5},{5,4},{6,7},{7,6},{8,9},{9,8},{10,11... | collective-permute-start | bytes 884744 | tf_op jit(solution)/shard_map/ppermute | solution.py:270
  460.6 36.4 %collective-permute-start.58 = (bf16[8,48,1152]{2,1,0:T(8,128)(2,1)}, bf16[8,48,1152]{2,1,0:T(8,128)(2,1)}, u32[]{:S(2)}, u32[]{:S(2)}) collective-permute-start(bf16[8,48,1152]{2,1,0:T(8,128)(2,1)} %get-tuple-element.262), channel_id=1, source_target_pairs={{0,2},{1,3},{2,0},{3,1},{4,6},{5,7},{6,4},{7,5},{8,10},{9,11},{10,... | collective-permute-start | bytes 2654216 | tf_op jit(solution)/shard_map/ppermute | solution.py:270
  468.6 34.0 %collective-permute-start.71 = (bf16[1,96,768]{2,1,0:T(8,128)(2,1)}, bf16[1,96,768]{2,1,0:T(8,128)(2,1)}, u32[]{:S(2)}, u32[]{:S(2)}) collective-permute-start(bf16[1,96,768]{2,1,0:T(8,128)(2,1)} %add_convert_fusion.19), channel_id=1, source_target_pairs={{0,8},{1,9},{2,10},{3,11},{4,12},{5,13},{6,14},{7,15},{8,0},{9,1},... | collective-permute-start | bytes 442376 | tf_op jit(solution)/shard_map/ppermute | solution.py:270
  472.4 25.2 %collective-permute-start.63 = (bf16[4,48,2688]{2,1,0:T(8,128)(2,1)}, bf16[4,48,2688]{2,1,0:T(8,128)(2,1)}, u32[]{:S(2)}, u32[]{:S(2)}) collective-permute-start(bf16[4,48,2688]{2,1,0:T(8,128)(2,1)} %add_convert_fusion.1), channel_id=1, source_target_pairs={{0,4},{1,5},{2,6},{3,7},{4,0},{5,1},{6,2},{7,3},{8,12},{9,13},{10,... | collective-permute-start | bytes 3096584 | tf_op jit(solution)/shard_map/ppermute | solution.py:270
  486.5 21.9 %collective-permute-start.72 = (bf16[1,96,2304]{2,1,0:T(8,128)(2,1)}, bf16[1,96,2304]{2,1,0:T(8,128)(2,1)}, u32[]{:S(2)}, u32[]{:S(2)}) collective-permute-start(bf16[1,96,2304]{2,1,0:T(8,128)(2,1)} %add_convert_fusion.11), channel_id=1, source_target_pairs={{0,8},{1,9},{2,10},{3,11},{4,12},{5,13},{6,14},{7,15},{8,0},{9,1},... | collective-permute-start | bytes 1327112 | tf_op jit(solution)/shard_map/ppermute | solution.py:270
  498.8 15.5 %collective-permute-start.66 = (bf16[4,48,1152]{2,1,0:T(8,128)(2,1)S(1)}, bf16[4,48,1152]{2,1,0:T(8,128)(2,1)S(1)}, u32[]{:S(2)}, u32[]{:S(2)}) collective-permute-start(bf16[4,48,1152]{2,1,0:T(8,128)(2,1)S(1)} %add_convert_fusion.12), channel_id=1, source_target_pairs={{0,4},{1,5},{2,6},{3,7},{4,0},{5,1},{6,2},{7,3},{8,12},{9,13},{10,... | collective-permute-start | bytes 1327112 | tf_op jit(solution)/shard_map/ppermute | solution.py:270
  510.2 16.0 %collective-permute-start.74 = (bf16[2,48,2688]{2,1,0:T(8,128)(2,1)S(1)}, bf16[2,48,2688]{2,1,0:T(8,128)(2,1)S(1)}, u32[]{:S(2)}, u32[]{:S(2)}) collective-permute-start(bf16[2,48,2688]{2,1,0:T(8,128)(2,1)S(1)} %add_convert_fusion.9), channel_id=1, source_target_pairs={{0,1},{1,0},{2,3},{3,2},{4,5},{5,4},{6,7},{7,6},{8,9},{9,8},{10,11... | collective-permute-start | bytes 1548296 | tf_op jit(solution)/shard_map/ppermute | solution.py:270
  515.3 17.9 %collective-permute-start.73 = (bf16[2,48,1152]{2,1,0:T(8,128)(2,1)S(1)}, bf16[2,48,1152]{2,1,0:T(8,128)(2,1)S(1)}, u32[]{:S(2)}, u32[]{:S(2)}) collective-permute-start(bf16[2,48,1152]{2,1,0:T(8,128)(2,1)S(1)} %add_convert_fusion.17), channel_id=1, source_target_pairs={{0,1},{1,0},{2,3},{3,2},{4,5},{5,4},{6,7},{7,6},{8,9},{9,8},{10,11... | collective-permute-start | bytes 663560 | tf_op jit(solution)/shard_map/ppermute | solution.py:270
  522.0 22.1 %collective-permute-start.85 = (bf16[96,2304]{1,0:T(8,128)(2,1)S(1)}, bf16[96,2304]{1,0:T(8,128)(2,1)S(1)}, u32[]{:S(2)}, u32[]{:S(2)}) collective-permute-start(bf16[96,2304]{1,0:T(8,128)(2,1)S(1)} %fusion.53), channel_id=1, source_target_pairs={{0,16},{16,0},{1,17},{17,1},{2,18},{18,2},{3,19},{19,3},{4,20},{20... | collective-permute-start | bytes 1327112 | tf_op jit(solution)/shard_map/ppermute | solution.py:256
  533.1 18.4 %collective-permute-start.80 = (bf16[1,48,2688]{2,1,0:T(8,128)(2,1)S(1)}, bf16[1,48,2688]{2,1,0:T(8,128)(2,1)S(1)}, u32[]{:S(2)}, u32[]{:S(2)}) collective-permute-start(bf16[1,48,2688]{2,1,0:T(8,128)(2,1)S(1)} %add_convert_fusion.16), channel_id=1, source_target_pairs={{0,8},{1,9},{2,10},{3,11},{4,12},{5,13},{6,14},{7,15},{8,0},{9,1},... | collective-permute-start | bytes 774152 | tf_op jit(solution)/shard_map/ppermute | solution.py:270
  534.7 20.7 %collective-permute-start.84 = (bf16[192,768]{1,0:T(8,128)(2,1)S(1)}, bf16[192,768]{1,0:T(8,128)(2,1)S(1)}, u32[]{:S(2)}, u32[]{:S(2)}) collective-permute-start(bf16[192,768]{1,0:T(8,128)(2,1)S(1)} %fusion.51), channel_id=1, source_target_pairs={{0,16},{16,0},{1,17},{17,1},{2,18},{18,2},{3,19},{19,3},{4,20},{20... | collective-permute-start | bytes 884744 | tf_op jit(solution)/shard_map/ppermute | solution.py:256
  (223 other events, 1679.8 us)

commit v7 on v6

--- a/solution.py
+++ b/solution.py
@@ -1069,9 +1069,13 @@
     grad_up_g = mm_tn(square_normed, grad_up_g_rows).astype(BF16)
     stream_up_g = fresh(scatter_square(grad_up_g, plane, every))
     part = mm_nt(grad_up_g_rows, up_wg)
-    part = half_of(part, core) + swap(half_of(part, 1 - core).astype(BF16)).astype(F32)
-    part = advance([stream_down_g, stream_up_g], part)
-    part = fresh(scatter_in_square(part.reshape(4, slots, half_g))).result().astype(BF16)
+    mine = in_square(half_of(part, core).reshape(4, slots, half_g))
+    theirs = in_square(half_of(part, 1 - core).astype(BF16).reshape(4, slots, half_g), 1)
+    mine, theirs = advance([stream_down_g, stream_up_g], (mine, theirs))
+    outgoing = (mine[2:] + swap(theirs[2:]).astype(F32)).astype(BF16)
+    kept = mine[:2] + swap(theirs[:2]).astype(F32)
+    kept = kept + exchange(outgoing, SQUARE[1], size).astype(F32)
+    part = (kept[0] + exchange(kept[1].astype(BF16), SQUARE[0], size).astype(F32)).astype(BF16)
     part = shared(part).astype(F32)
     pulled, grad_gain_g2 = norm_backward(part, hidden_g, scale_g2, gain_two_g)
     grad_hidden_g = jnp.pad(grad_top_b.astype(F32), ((0, 0), (0, width_g - width_l))) + pulled

time: 567 us -> 569 us (level)
    ppermute x25 -> x26, starting transfers between devices: 24.3 us -> 24.7 us  [swap(): return lax.ppermute(array, 'section', [(0, 1), (1, 0)])]
    unnamed x390 -> x396, local copies, waits for them, and re-layouts: 32.6 us -> 32.3 us
  transfers between devices with their start and end apart: 89 -> 90, of which waited for: 27 -> 28; matrix products, arithmetic and copies ran while one was open for 27% -> 26% of each run, Pallas kernels for 19% -> 18%
where the time goes in v7:
time: 569 us; the launch traced here: 562 us
  waiting for transfers between devices  141 us (25%)
  other arithmetic  113 us (20%)
  Pallas kernels  108 us (19%)
  starting transfers between devices  100 us (18%)
  local copies, waits for them, and re-layouts  56.7 us (10%)
  matrix products  39.4 us (7%)
    ppermute x57, waiting for transfers between devices, exchange(): lax.ppermute(part, ('section', 'dp'), pairs)  133 us
    ppermute x57, starting transfers between devices, exchange(): lax.ppermute(part, ('section', 'dp'), pairs)  66.9 us
    unnamed x396, local copies, waits for them, and re-layouts  32.3 us
    convert_element_type x15, other arithmetic, halving(): outgoing = total_of([term[half:] for term in terms]).astype(BF16)  28.2 us
    ppermute x26, starting transfers between devices, swap(): return lax.ppermute(array, 'section', [(0, 1), (1, 0)])  24.7 us
    pallas_call x3, Pallas kernels, product(): pl.pallas_call(functools.partial(product_kernel, self.rows, 4, gelu), gri...  20.8 us
    pallas_call x2, Pallas kernels, attention_backward(): pl.pallas_call(functools.partial(attention_backward_kernel, rows, window)...  18.2 us
    dot_general x9, matrix products, mm(): return jnp.dot(left, right, preferred_element_type=F32)  18.2 us
  transfers between devices with their start and end apart: 90, of which 28 were waited for; matrix products, arithmetic and copies ran while one was open for 26% of the time, Pallas kernels for 18%

profile of v7, /device:TPU:1, one launch (start us, length us, event | category | flops | bytes accessed | tf_op | source)
XLA Modules:
  0.0 562.1 jit_solution(11650989644990467081)
XLA Ops:
  7.6 3.2 collective-permute-start.1
  18.4 10.2 %collective-permute-done.1 = bf16[1,48,4224]{2,1,0:T(8,128)(2,1)S(1)} collective-permute-done((bf16[1,48,4224]{2,1,0:T(8,128)(2,1)S(1)}, bf16[1,48,4224]{2,1,0:T(8,128)(2,1)S(1)}, u32[]{:S(2)}, u32[]{:S(2)}) %collective-permute-start.1) | collective-permute-done | bytes 405536 | tf_op jit(solution)/shard_map/ppermute | solution.py:270
  37.1 4.0 collective-permute-done.4
  41.8 2.6 collective-permute-done.2
  51.4 7.0 %collective-permute-done.7 = bf16[1,96,2304]{2,1,0:T(8,128)(2,1)} collective-permute-done((bf16[1,96,2304]{2,1,0:T(8,128)(2,1)}, bf16[1,96,2304]{2,1,0:T(8,128)(2,1)}, u32[]{:S(2)}, u32[]{:S(2)}) %collective-permute-start.7) | collective-permute-done | bytes 442400 | tf_op jit(solution)/shard_map/ppermute | solution.py:270
  58.4 11.0 %collective-permute-done.8 = bf16[1,192,384]{2,1,0:T(8,128)(2,1)S(1)} collective-permute-done((bf16[1,192,384]{2,1,0:T(8,128)(2,1)}, bf16[1,192,384]{2,1,0:T(8,128)(2,1)S(1)}, u32[]{:S(2)}, u32[]{:S(2)}) %collective-permute-start.8) | collective-permute-done | bytes 147488 | tf_op jit(solution)/shard_map/ppermute | solution.py:270
  74.6 3.2 collective-permute-start.12
  86.0 10.3 %collective-permute-done.13 = bf16[1,192,768]{2,1,0:T(8,128)(2,1)} collective-permute-done((bf16[1,192,768]{2,1,0:T(8,128)(2,1)}, bf16[1,192,768]{2,1,0:T(8,128)(2,1)}, u32[]{:S(2)}, u32[]{:S(2)}) %collective-permute-start.13) | collective-permute-done | bytes 294944 | tf_op jit(solution)/shard_map/ppermute | solution.py:270
  96.3 14.7 %collective-permute-done.14 = bf16[2,192,384]{2,1,0:T(8,128)(2,1)} collective-permute-done((bf16[2,192,384]{2,1,0:T(8,128)(2,1)}, bf16[2,192,384]{2,1,0:T(8,128)(2,1)}, u32[]{:S(2)}, u32[]{:S(2)}) %collective-permute-start.14) | collective-permute-done | bytes 294944 | tf_op jit(solution)/shard_map/ppermute | solution.py:270
  117.1 3.1 collective-permute-start.19
  120.2 2.8 pad_maximum_fusion.4
  126.3 5.8 %shard_map.452.q_ref.k_ref.v_ref = bf16[1024,1152]{1,0:T(8,128)(2,1)} custom-call(s32[16]{0:T(128)S(1)} %get-tuple-element.427.table.places, bf16[1024,768]{1,0:T(8,128)(2,1)S(1)} %fusion.2.x_ref, bf16[4,48,4224]{2,1,0:T(8,128)(2,1)S(1)} %pad_maximum_fusion.5.refs_0_, bf16[4,48,4224]{2,1,0:T(8,128)(2,1)S(1)} %collective-permute-done.6.refs_1_, ...), custom_call_target="tpu_custom_call" | custom-call | tf_op jit(solution)/shard_map/pallas_call | solution.py:568
  135.0 9.5 %shard_map.453 = (bf16[1024,384]{1,0:T(8,128)(2,1)S(1)}, f32[3,2,1024]{2,1,0:T(2,128)S(1)}) custom-call(bf16[1024,1152]{1,0:T(8,128)(2,1)S(1)} %copy-done.3, bf16[1024,1152]{1,0:T(8,128)(2,1)S(1)} %copy-done.3, bf16[1024,1152]{1,0:T(8,128)(2,1)S(1)} %copy-done.3, f32[1024,1]{1,0:T(8,128)S(1)} %fusion.52.bias_ref), custom_call_target="tpu_custom_call" | custom-call | tf_op jit(solution)/shard_map/pallas_call | solution.py:210
  144.5 16.2 %collective-permute-done.19 = bf16[1,96,768]{2,1,0:T(8,128)(2,1)S(1)} collective-permute-done((bf16[1,96,768]{2,1,0:T(8,128)(2,1)S(1)}, bf16[1,96,768]{2,1,0:T(8,128)(2,1)S(1)}, u32[]{:S(2)}, u32[]{:S(2)}) %collective-permute-start.19) | collective-permute-done | bytes 147488 | tf_op jit(solution)/shard_map/ppermute | solution.py:270
  168.1 2.8 pad_maximum_fusion.refs_0_.refs_1_
  176.6 10.2 %shard_map.454 = (bf16[1024,1536]{1,0:T(8,128)(2,1)}, bf16[1024,1536]{1,0:T(8,128)(2,1)}) custom-call(s32[16]{0:T(128)S(1)} %get-tuple-element.427.table.places, bf16[1024,768]{1,0:T(8,128)(2,1)S(1)} %multiply_convert_fusion.x_ref, bf16[4,48,4224]{2,1,0:T(8,128)(2,1)S(1)} %copy-done.5, bf16[4,48,4224]{2,1,0:T(8,128)(2,1)S(1)} %copy-done.8, ...), custom_call_target="tpu_custom_call" | custom-call | flops 99999997952 | tf_op jit(solution)/shard_map/pallas_call | solution.py:568
  187.7 5.3 fusion.141
  206.5 9.0 %collective-permute-done.29 = bf16[4,96,768]{2,1,0:T(8,128)(2,1)S(1)} collective-permute-done((bf16[4,96,768]{2,1,0:T(8,128)(2,1)S(1)}, bf16[4,96,768]{2,1,0:T(8,128)(2,1)S(1)}, u32[]{:S(2)}, u32[]{:S(2)}) %collective-permute-start.29) | collective-permute-done | bytes 589856 | tf_op jit(solution)/shard_map/ppermute | solution.py:270
  215.5 13.1 %collective-permute-done.30.refs_1_ = bf16[8,96,768]{2,1,0:T(8,128)(2,1)S(1)} collective-permute-done((bf16[8,96,768]{2,1,0:T(8,128)(2,1)S(1)}, bf16[8,96,768]{2,1,0:T(8,128)(2,1)S(1)}, u32[]{:S(2)}, u32[]{:S(2)}) %collective-permute-start.30) | collective-permute-done | bytes 1179680 | tf_op jit(solution)/shard_map/ppermute | solution.py:270
  238.3 4.8 shard_map.456.q_ref.k_ref.v_ref
  243.2 4.6 shard_map.457
  253.1 3.6 collective-permute-done.33
  263.2 4.6 collective-permute-done.35
  302.0 3.7 fusion.126
  312.3 4.8 collective-permute-done.42
  320.3 3.0 collective-permute-done.43
  335.1 4.5 shard_map.464
  340.3 10.5 %shard_map.465 = (bf16[192,1536]{1,0:T(8,128)(2,1)S(1)}, bf16[8,96,2304]{2,1,0:T(8,128)(2,1)}, bf16[8,96,2304]{2,1,0:T(8,128)(2,1)}) custom-call(s32[16]{0:T(128)S(1)} %get-tuple-element.426.table, s32[16]{0:T(128)S(1)} %get-tuple-element.425.table.places, bf16[192,1536]{1,0:T(8,128)(2,1)S(1)} %copy-done.20, bf16[8,96,2304]{2,1,0:T(8,128)(2,1)} %copy-done.2, ...), custom_call_target="tpu_custom_call" | custom-call | tf_op jit(solution)/shard_map/pallas_call | solution.py:672
  359.2 5.9 %collective-permute-start.50 = (bf16[384,768]{1,0:T(8,128)(2,1)}, bf16[384,768]{1,0:T(8,128)(2,1)}, u32[]{:S(2)}, u32[]{:S(2)}) collective-permute-start(bf16[384,768]{1,0:T(8,128)(2,1)} %bitcast_convert_fusion), channel_id=1, source_target_pairs={{8,0},{9,1},{10,2},{11,3},{12,4},{13,5},{14,6},{15,7},{16,24},{17,... | collective-permute-start | bytes 1769480 | tf_op jit(solution)/shard_map/ppermute | solution.py:270
  377.0 5.8 %fusion.15 = (bf16[1024,768]{1,0:T(8,128)(2,1)}, f32[1024,768]{1,0:T(8,128)}) fusion(bf16[1024,384]{1,0:T(8,128)(2,1)} %copy-done.88, bf16[1024,384]{1,0:T(8,128)(2,1)S(1)} %copy-done.87, bf16[192,1536]{1,0:T(8,128)(2,1)} %add_convert_fusion.6, bf16[768,768]{1,0:T(8,128)(2,1)} %copy-done.115, bf16[768,768]{1,0:T(8,128)(2,1)} %copy-done.114, ...), kind=kOutput, calls=%fused_computation.39 | convolution fusion | flops 764755968 | bytes 9241344 | tf_op jit(solution)/shard_map/dot_general | solution.py:33
  384.1 17.8 %shard_map.466 = (bf16[1024,768]{1,0:T(8,128)(2,1)S(1)}, bf16[1536,768]{1,0:T(8,128)(2,1)}, bf16[8,48,2688]{2,1,0:T(8,128)(2,1)}, bf16[8,48,2688]{2,1,0:T(8,128)(2,1)}) custom-call(s32[16]{0:T(128)S(1)} %get-tuple-element.427.table.places, s32[16]{0:T(128)S(1)} %get-tuple-element.427.table.places, bf16[1024,768]{1,0:T(8,128)(2,1)S(1)} %copy-done.18, ...), custom_call_target="tpu_custom_call" | custom-call | tf_op jit(solution)/shard_map/pallas_call | solution.py:594
  406.0 3.6 add_convert_fusion
  420.0 2.6 fusion.129
  428.6 2.9 collective-permute-done.55
  434.2 2.7 add_convert_fusion.2
  437.5 13.7 %shard_map.469 = (bf16[1024,384]{1,0:T(8,128)(2,1)S(1)}, bf16[1024,384]{1,0:T(8,128)(2,1)S(1)}, bf16[1024,384]{1,0:T(8,128)(2,1)S(1)}) custom-call(bf16[1024,1152]{1,0:T(8,128)(2,1)} %shard_map.452.q_ref.k_ref.v_ref, bf16[1024,1152]{1,0:T(8,128)(2,1)} %shard_map.452.q_ref.k_ref.v_ref, bf16[1024,1152]{1,0:T(8,128)(2,1)} %shard_map.452.q_ref.k_ref.v_ref, ...), custom_call_target="tpu_custom_call" | custom-call | flops 99999997952 | tf_op jit(solution)/shard_map/pallas_call | solution.py:230
  457.7 5.1 shard_map.470
  463.3 5.7 %shard_map.471 = bf16[1024,768]{1,0:T(8,128)(2,1)S(1)} custom-call(s32[16]{0:T(128)S(1)} %get-tuple-element.427.table.places, bf16[4,48,4224]{2,1,0:T(8,128)(2,1)S(1)} %copy-done.6, bf16[4,48,4224]{2,1,0:T(8,128)(2,1)} %copy-done.7, bf16[4,48,4224]{2,1,0:T(8,128)(2,1)} %collective-permute-done.10.refs_2_, ...), custom_call_target="tpu_custom_call" | custom-call | tf_op jit(solution)/shard_map/pallas_call | solution.py:648
  475.7 4.1 collective-permute-start.66
  489.5 3.6 fusion.5
  495.5 3.7 fusion.36
  506.0 4.4 collective-permute-done.73
  512.4 3.9 collective-permute-done.71
  518.6 3.9 collective-permute-start.76
  529.3 2.8 collective-permute-start.78
  536.8 3.5 collective-permute-start.85
  542.6 2.6 collective-permute-start.82
  548.0 5.4 collective-permute-done.82
  (750 shorter events, 265.9 us)
Async XLA Ops:
  7.6 21.0 %collective-permute-start.1 = (bf16[1,48,4224]{2,1,0:T(8,128)(2,1)S(1)}, bf16[1,48,4224]{2,1,0:T(8,128)(2,1)S(1)}, u32[]{:S(2)}, u32[]{:S(2)}) collective-permute-start(bf16[1,48,4224]{2,1,0:T(8,128)(2,1)S(1)} %bitcast.173), channel_id=1, source_target_pairs={{0,8},{1,9},{2,10},{3,11},{4,12},{5,13},{6,14},{7,15},{8,0},{9,1},... | collective-permute-start | bytes 1216520 | tf_op jit(solution)/shard_map/ppermute | solution.py:270
  29.6 14.8 %collective-permute-start.2 = (bf16[2,48,4224]{2,1,0:T(8,128)(2,1)}, bf16[2,48,4224]{2,1,0:T(8,128)(2,1)S(1)}, u32[]{:S(2)}, u32[]{:S(2)}) collective-permute-start(bf16[2,48,4224]{2,1,0:T(8,128)(2,1)} %pad_maximum_fusion.29), channel_id=1, source_target_pairs={{0,1},{1,0},{2,3},{3,2},{4,5},{5,4},{6,7},{7,6},{8,9},{9,8},{10,11... | collective-permute-start | bytes 2433032 | tf_op jit(solution)/shard_map/ppermute | solution.py:270
  44.6 24.9 %collective-permute-start.6 = (bf16[4,48,4224]{2,1,0:T(8,128)(2,1)S(1)}, bf16[4,48,4224]{2,1,0:T(8,128)(2,1)S(1)}, u32[]{:S(2)}, u32[]{:S(2)}) collective-permute-start(bf16[4,48,4224]{2,1,0:T(8,128)(2,1)S(1)} %pad_maximum_fusion.5.refs_0_), channel_id=1, source_target_pairs={{0,4},{1,5},{2,6},{3,7},{4,0},{5,1},{6,2},{7,3},{8,12},{9,13},{10,... | collective-permute-start | bytes 4866056 | tf_op jit(solution)/shard_map/ppermute | solution.py:270
  49.9 19.5 %collective-permute-start.9 = (bf16[2,96,768]{2,1,0:T(8,128)(2,1)S(1)}, bf16[2,96,768]{2,1,0:T(8,128)(2,1)S(1)}, u32[]{:S(2)}, u32[]{:S(2)}) collective-permute-start(bf16[2,96,768]{2,1,0:T(8,128)(2,1)S(1)} %get-tuple-element.393), channel_id=1, source_target_pairs={{0,2},{1,3},{2,0},{3,1},{4,6},{5,7},{6,4},{7,5},{8,10},{9,11},{10,... | collective-permute-start | bytes 884744 | tf_op jit(solution)/shard_map/ppermute | solution.py:270
  51.2 18.3 %collective-permute-start.8 = (bf16[1,192,384]{2,1,0:T(8,128)(2,1)}, bf16[1,192,384]{2,1,0:T(8,128)(2,1)S(1)}, u32[]{:S(2)}, u32[]{:S(2)}) collective-permute-start(bf16[1,192,384]{2,1,0:T(8,128)(2,1)} %dynamic-slice_bitcast_fusion.11), channel_id=1, source_target_pairs={{0,1},{1,0},{2,3},{3,2},{4,5},{5,4},{6,7},{7,6},{8,9},{9,8},{10,11... | collective-permute-start | bytes 442376 | tf_op jit(solution)/shard_map/ppermute | solution.py:270
  70.2 40.7 %collective-permute-start.10 = (bf16[4,48,4224]{2,1,0:T(8,128)(2,1)S(1)}, bf16[4,48,4224]{2,1,0:T(8,128)(2,1)}, u32[]{:S(2)}, u32[]{:S(2)}) collective-permute-start(bf16[4,48,4224]{2,1,0:T(8,128)(2,1)S(1)} %pad_maximum_fusion.5.refs_0_), channel_id=1, source_target_pairs={{0,2},{1,3},{2,0},{3,1},{4,6},{5,7},{6,4},{7,5},{8,10},{9,11},{10,... | collective-permute-start | bytes 4866056 | tf_op jit(solution)/shard_map/ppermute | solution.py:270
  71.2 39.8 %collective-permute-start.11 = (bf16[4,48,4224]{2,1,0:T(8,128)(2,1)S(1)}, bf16[4,48,4224]{2,1,0:T(8,128)(2,1)}, u32[]{:S(2)}, u32[]{:S(2)}) collective-permute-start(bf16[4,48,4224]{2,1,0:T(8,128)(2,1)S(1)} %collective-permute-done.6.refs_1_), channel_id=1, source_target_pairs={{0,2},{1,3},{2,0},{3,1},{4,6},{5,7},{6,4},{7,5},{8,10},{9,11},{10,... | collective-permute-start | bytes 4866056 | tf_op jit(solution)/shard_map/ppermute | solution.py:270
  74.6 36.3 %collective-permute-start.12 = (bf16[2,96,2304]{2,1,0:T(8,128)(2,1)}, bf16[2,96,2304]{2,1,0:T(8,128)(2,1)}, u32[]{:S(2)}, u32[]{:S(2)}) collective-permute-start(bf16[2,96,2304]{2,1,0:T(8,128)(2,1)} %pad_maximum_fusion.28), channel_id=1, source_target_pairs={{0,4},{1,5},{2,6},{3,7},{4,0},{5,1},{6,2},{7,3},{8,12},{9,13},{10,... | collective-permute-start | bytes 2654216 | tf_op jit(solution)/shard_map/ppermute | solution.py:270
  79.3 17.0 %collective-permute-start.13 = (bf16[1,192,768]{2,1,0:T(8,128)(2,1)}, bf16[1,192,768]{2,1,0:T(8,128)(2,1)}, u32[]{:S(2)}, u32[]{:S(2)}) collective-permute-start(bf16[1,192,768]{2,1,0:T(8,128)(2,1)} %select_bitcast_fusion.1), channel_id=1, source_target_pairs={{0,4},{1,5},{2,6},{3,7},{4,0},{5,1},{6,2},{7,3},{8,12},{9,13},{10,... | collective-permute-start | bytes 884744 | tf_op jit(solution)/shard_map/ppermute | solution.py:270
  80.0 30.9 %collective-permute-start.14 = (bf16[2,192,384]{2,1,0:T(8,128)(2,1)}, bf16[2,192,384]{2,1,0:T(8,128)(2,1)}, u32[]{:S(2)}, u32[]{:S(2)}) collective-permute-start(bf16[2,192,384]{2,1,0:T(8,128)(2,1)} %pad_maximum_fusion.45), channel_id=1, source_target_pairs={{0,2},{1,3},{2,0},{3,1},{4,6},{5,7},{6,4},{7,5},{8,10},{9,11},{10,... | collective-permute-start | bytes 884744 | tf_op jit(solution)/shard_map/ppermute | solution.py:270
  112.1 48.7 %collective-permute-start.16 = (bf16[2,192,768]{2,1,0:T(8,128)(2,1)S(1)}, bf16[2,192,768]{2,1,0:T(8,128)(2,1)S(1)}, u32[]{:S(2)}, u32[]{:S(2)}) collective-permute-start(bf16[2,192,768]{2,1,0:T(8,128)(2,1)S(1)} %pad_maximum_fusion.37), channel_id=1, source_target_pairs={{0,1},{1,0},{2,3},{3,2},{4,5},{5,4},{6,7},{7,6},{8,9},{9,8},{10,11... | collective-permute-start | bytes 1769480 | tf_op jit(solution)/shard_map/ppermute | solution.py:270
  113.1 47.6 %collective-permute-start.17 = (bf16[4,96,768]{2,1,0:T(8,128)(2,1)S(1)}, bf16[4,96,768]{2,1,0:T(8,128)(2,1)S(1)}, u32[]{:S(2)}, u32[]{:S(2)}) collective-permute-start(bf16[4,96,768]{2,1,0:T(8,128)(2,1)S(1)} %pad_maximum_fusion.36), channel_id=1, source_target_pairs={{0,8},{1,9},{2,10},{3,11},{4,12},{5,13},{6,14},{7,15},{8,0},{9,1},... | collective-permute-start | bytes 1769480 | tf_op jit(solution)/shard_map/ppermute | solution.py:270
  115.6 45.2 %collective-permute-start.18 = (bf16[384,768]{1,0:T(8,128)(2,1)S(1)}, bf16[384,768]{1,0:T(8,128)(2,1)S(1)}, u32[]{:S(2)}, u32[]{:S(2)}) collective-permute-start(bf16[384,768]{1,0:T(8,128)(2,1)S(1)} %copy-done.139), channel_id=1, source_target_pairs={{0,8},{1,9},{2,10},{3,11},{4,12},{5,13},{6,14},{7,15},{24,16},{25,... | collective-permute-start | bytes 1769480 | tf_op jit(solution)/shard_map/ppermute | solution.py:270
  117.1 43.7 %collective-permute-start.19 = (bf16[1,96,768]{2,1,0:T(8,128)(2,1)S(1)}, bf16[1,96,768]{2,1,0:T(8,128)(2,1)S(1)}, u32[]{:S(2)}, u32[]{:S(2)}) collective-permute-start(bf16[1,96,768]{2,1,0:T(8,128)(2,1)S(1)} %copy-done.98), channel_id=1, source_target_pairs={{0,8},{1,9},{2,10},{3,11},{4,12},{5,13},{6,14},{7,15},{8,0},{9,1},... | collective-permute-start | bytes 442376 | tf_op jit(solution)/shard_map/ppermute | solution.py:270
  123.0 44.8 %collective-permute-start.15 = (bf16[4,96,2304]{2,1,0:T(8,128)(2,1)}, bf16[4,96,2304]{2,1,0:T(8,128)(2,1)}, u32[]{:S(2)}, u32[]{:S(2)}) collective-permute-start(bf16[4,96,2304]{2,1,0:T(8,128)(2,1)} %pad_maximum_fusion.4), channel_id=1, source_target_pairs={{0,1},{1,0},{2,3},{3,2},{4,5},{5,4},{6,7},{7,6},{8,9},{9,8},{10,11... | collective-permute-start | bytes 5308424 | tf_op jit(solution)/shard_map/ppermute | solution.py:270
  163.0 23.8 %collective-permute-start.22 = (bf16[4,192,768]{2,1,0:T(8,128)(2,1)S(1)}, bf16[4,192,768]{2,1,0:T(8,128)(2,1)S(1)}, u32[]{:S(2)}, u32[]{:S(2)}) collective-permute-start(bf16[4,192,768]{2,1,0:T(8,128)(2,1)S(1)} %pad_maximum_fusion.19.refs_0_.refs_1_), channel_id=1, source_target_pairs={{0,2},{1,3},{2,0},{3,1},{4,6},{5,7},{6,4},{7,5},{8,10},{9,11},{10,... | collective-permute-start | bytes 3538952 | tf_op jit(solution)/shard_map/ppermute | solution.py:270
  165.5 21.4 %collective-permute-start.23 = (bf16[1,384,768]{2,1,0:T(8,128)(2,1)S(1)}, bf16[1,384,768]{2,1,0:T(8,128)(2,1)S(1)}, u32[]{:S(2)}, u32[]{:S(2)}) collective-permute-start(bf16[1,384,768]{2,1,0:T(8,128)(2,1)S(1)} %select_bitcast_fusion.refs_0_), channel_id=1, source_target_pairs={{0,4},{1,5},{2,6},{3,7},{4,0},{5,1},{6,2},{7,3},{8,12},{9,13},{10,... | collective-permute-start | bytes 1769480 | tf_op jit(solution)/shard_map/ppermute | solution.py:270
  167.2 19.6 %collective-permute-start.24 = (bf16[2,96,768]{2,1,0:T(8,128)(2,1)}, bf16[2,96,768]{2,1,0:T(8,128)(2,1)S(1)}, u32[]{:S(2)}, u32[]{:S(2)}) collective-permute-start(bf16[2,96,768]{2,1,0:T(8,128)(2,1)} %pad_maximum_fusion.49), channel_id=1, source_target_pairs={{0,4},{1,5},{2,6},{3,7},{4,0},{5,1},{6,2},{7,3},{8,12},{9,13},{10,... | collective-permute-start | bytes 884744 | tf_op jit(solution)/shard_map/ppermute | solution.py:270
  170.9 58.8 %collective-permute-start.28 = (bf16[8,96,2304]{2,1,0:T(8,128)(2,1)S(1)}, bf16[8,96,2304]{2,1,0:T(8,128)(2,1)}, u32[]{:S(2)}, u32[]{:S(2)}) collective-permute-start(bf16[8,96,2304]{2,1,0:T(8,128)(2,1)S(1)} %pad_maximum_fusion.refs_0_.refs_1_), channel_id=1, source_target_pairs={{0,2},{1,3},{2,0},{3,1},{4,6},{5,7},{6,4},{7,5},{8,10},{9,11},{10,... | collective-permute-start | bytes 10616840 | tf_op jit(solution)/shard_map/ppermute | solution.py:270
  199.9 15.6 %collective-permute-start.29 = (bf16[4,96,768]{2,1,0:T(8,128)(2,1)S(1)}, bf16[4,96,768]{2,1,0:T(8,128)(2,1)S(1)}, u32[]{:S(2)}, u32[]{:S(2)}) collective-permute-start(bf16[4,96,768]{2,1,0:T(8,128)(2,1)S(1)} %pad_maximum_fusion.38), channel_id=1, source_target_pairs={{0,1},{1,0},{2,3},{3,2},{4,5},{5,4},{6,7},{7,6},{8,9},{9,8},{10,11... | collective-permute-start | bytes 1769480 | tf_op jit(solution)/shard_map/ppermute | solution.py:270
  201.2 27.4 %collective-permute-start.30 = (bf16[8,96,768]{2,1,0:T(8,128)(2,1)S(1)}, bf16[8,96,768]{2,1,0:T(8,128)(2,1)S(1)}, u32[]{:S(2)}, u32[]{:S(2)}) collective-permute-start(bf16[8,96,768]{2,1,0:T(8,128)(2,1)S(1)} %pad_maximum_fusion.20.refs_0_), channel_id=1, source_target_pairs={{0,4},{1,5},{2,6},{3,7},{4,0},{5,1},{6,2},{7,3},{8,12},{9,13},{10,... | collective-permute-start | bytes 3538952 | tf_op jit(solution)/shard_map/ppermute | solution.py:270
  230.8 17.5 %collective-permute-start.32 = (bf16[8,96,768]{2,1,0:T(8,128)(2,1)}, bf16[8,96,768]{2,1,0:T(8,128)(2,1)}, u32[]{:S(2)}, u32[]{:S(2)}) collective-permute-start(bf16[8,96,768]{2,1,0:T(8,128)(2,1)} %pad_maximum_fusion.22.refs_0_.refs_1_), channel_id=1, source_target_pairs={{0,2},{1,3},{2,0},{3,1},{4,6},{5,7},{6,4},{7,5},{8,10},{9,11},{10,... | collective-permute-start | bytes 3538952 | tf_op jit(solution)/shard_map/ppermute | solution.py:270
  310.7 40.1 %collective-permute-start.47 = (bf16[1,384,768]{2,1,0:T(8,128)(2,1)}, bf16[1,384,768]{2,1,0:T(8,128)(2,1)}, u32[]{:S(2)}, u32[]{:S(2)}) collective-permute-start(bf16[1,384,768]{2,1,0:T(8,128)(2,1)} %get-tuple-element.220), channel_id=1, source_target_pairs={{0,4},{1,5},{2,6},{3,7},{4,0},{5,1},{6,2},{7,3},{8,12},{9,13},{10,... | collective-permute-start | bytes 1769480 | tf_op jit(solution)/shard_map/ppermute | solution.py:270
  311.5 58.8 %collective-permute-start.51 = (bf16[8,96,768]{2,1,0:T(8,128)(2,1)}, bf16[8,96,768]{2,1,0:T(8,128)(2,1)}, u32[]{:S(2)}, u32[]{:S(2)}) collective-permute-start(bf16[8,96,768]{2,1,0:T(8,128)(2,1)} %get-tuple-element.234), channel_id=1, source_target_pairs={{0,4},{1,5},{2,6},{3,7},{4,0},{5,1},{6,2},{7,3},{8,12},{9,13},{10,... | collective-permute-start | bytes 3538952 | tf_op jit(solution)/shard_map/ppermute | solution.py:270
  333.6 17.3 %collective-permute-start.45 = (bf16[2,192,384]{2,1,0:T(8,128)(2,1)}, bf16[2,192,384]{2,1,0:T(8,128)(2,1)}, u32[]{:S(2)}, u32[]{:S(2)}) collective-permute-start(bf16[2,192,384]{2,1,0:T(8,128)(2,1)} %pad_maximum_fusion.47), channel_id=1, source_target_pairs={{0,2},{1,3},{2,0},{3,1},{4,6},{5,7},{6,4},{7,5},{8,10},{9,11},{10,... | collective-permute-start | bytes 884744 | tf_op jit(solution)/shard_map/ppermute | solution.py:270
  334.5 18.0 %collective-permute-start.46 = (bf16[8,96,768]{2,1,0:T(8,128)(2,1)}, bf16[8,96,768]{2,1,0:T(8,128)(2,1)}, u32[]{:S(2)}, u32[]{:S(2)}) collective-permute-start(bf16[8,96,768]{2,1,0:T(8,128)(2,1)} %get-tuple-element.219), channel_id=1, source_target_pairs={{0,2},{1,3},{2,0},{3,1},{4,6},{5,7},{6,4},{7,5},{8,10},{9,11},{10,... | collective-permute-start | bytes 3538952 | tf_op jit(solution)/shard_map/ppermute | solution.py:270
  352.5 53.4 %collective-permute-start.49 = (bf16[8,96,2304]{2,1,0:T(8,128)(2,1)}, bf16[8,96,2304]{2,1,0:T(8,128)(2,1)}, u32[]{:S(2)}, u32[]{:S(2)}) collective-permute-start(bf16[8,96,2304]{2,1,0:T(8,128)(2,1)} %get-tuple-element.230), channel_id=1, source_target_pairs={{0,2},{1,3},{2,0},{3,1},{4,6},{5,7},{6,4},{7,5},{8,10},{9,11},{10,... | collective-permute-start | bytes 10616840 | tf_op jit(solution)/shard_map/ppermute | solution.py:270
  355.2 14.9 %collective-permute-start.52 = (bf16[192,1536]{1,0:T(8,128)(2,1)S(1)}, bf16[192,1536]{1,0:T(8,128)(2,1)S(1)}, u32[]{:S(2)}, u32[]{:S(2)}) collective-permute-start(bf16[192,1536]{1,0:T(8,128)(2,1)S(1)} %get-tuple-element.235), channel_id=1, source_target_pairs={{0,16},{16,0},{1,17},{17,1},{2,18},{18,2},{3,19},{19,3},{4,20},{20... | collective-permute-start | bytes 1769480 | tf_op jit(solution)/shard_map/ppermute | solution.py:256
  359.2 46.7 %collective-permute-start.50 = (bf16[384,768]{1,0:T(8,128)(2,1)}, bf16[384,768]{1,0:T(8,128)(2,1)}, u32[]{:S(2)}, u32[]{:S(2)}) collective-permute-start(bf16[384,768]{1,0:T(8,128)(2,1)} %bitcast_convert_fusion), channel_id=1, source_target_pairs={{8,0},{9,1},{10,2},{11,3},{12,4},{13,5},{14,6},{15,7},{16,24},{17,... | collective-permute-start | bytes 1769480 | tf_op jit(solution)/shard_map/ppermute | solution.py:270
  367.0 38.8 %collective-permute-start.54 = (bf16[4,96,768]{2,1,0:T(8,128)(2,1)}, bf16[4,96,768]{2,1,0:T(8,128)(2,1)}, u32[]{:S(2)}, u32[]{:S(2)}) collective-permute-start(bf16[4,96,768]{2,1,0:T(8,128)(2,1)} %add_convert_fusion.7), channel_id=1, source_target_pairs={{0,1},{1,0},{2,3},{3,2},{4,5},{5,4},{6,7},{7,6},{8,9},{9,8},{10,11... | collective-permute-start | bytes 1769480 | tf_op jit(solution)/shard_map/ppermute | solution.py:270
  373.4 32.5 %collective-permute-start.53 = (bf16[4,96,768]{2,1,0:T(8,128)(2,1)}, bf16[4,96,768]{2,1,0:T(8,128)(2,1)}, u32[]{:S(2)}, u32[]{:S(2)}) collective-permute-start(bf16[4,96,768]{2,1,0:T(8,128)(2,1)} %add_convert_fusion.8), channel_id=1, source_target_pairs={{0,8},{1,9},{2,10},{3,11},{4,12},{5,13},{6,14},{7,15},{8,0},{9,1},... | collective-permute-start | bytes 1769480 | tf_op jit(solution)/shard_map/ppermute | solution.py:270
  409.6 21.9 %collective-permute-start.55 = (bf16[4,96,2304]{2,1,0:T(8,128)(2,1)}, bf16[4,96,2304]{2,1,0:T(8,128)(2,1)S(1)}, u32[]{:S(2)}, u32[]{:S(2)}) collective-permute-start(bf16[4,96,2304]{2,1,0:T(8,128)(2,1)} %add_convert_fusion), channel_id=1, source_target_pairs={{0,1},{1,0},{2,3},{3,2},{4,5},{5,4},{6,7},{7,6},{8,9},{9,8},{10,11... | collective-permute-start | bytes 5308424 | tf_op jit(solution)/shard_map/ppermute | solution.py:270
  431.5 19.7 %collective-permute-start.57 = (bf16[2,96,768]{2,1,0:T(8,128)(2,1)S(1)}, bf16[2,96,768]{2,1,0:T(8,128)(2,1)S(1)}, u32[]{:S(2)}, u32[]{:S(2)}) collective-permute-start(bf16[2,96,768]{2,1,0:T(8,128)(2,1)S(1)} %copy-done.154), channel_id=1, source_target_pairs={{0,4},{1,5},{2,6},{3,7},{4,0},{5,1},{6,2},{7,3},{8,12},{9,13},{10,... | collective-permute-start | bytes 884744 | tf_op jit(solution)/shard_map/ppermute | solution.py:270
  432.7 18.5 %collective-permute-start.58 = (bf16[2,96,768]{2,1,0:T(8,128)(2,1)S(1)}, bf16[2,96,768]{2,1,0:T(8,128)(2,1)S(1)}, u32[]{:S(2)}, u32[]{:S(2)}) collective-permute-start(bf16[2,96,768]{2,1,0:T(8,128)(2,1)S(1)} %copy-done.153), channel_id=1, source_target_pairs={{0,2},{1,3},{2,0},{3,1},{4,6},{5,7},{6,4},{7,5},{8,10},{9,11},{10,... | collective-permute-start | bytes 884744 | tf_op jit(solution)/shard_map/ppermute | solution.py:270
  433.0 39.1 %collective-permute-start.60 = (bf16[8,48,2688]{2,1,0:T(8,128)(2,1)}, bf16[8,48,2688]{2,1,0:T(8,128)(2,1)}, u32[]{:S(2)}, u32[]{:S(2)}) collective-permute-start(bf16[8,48,2688]{2,1,0:T(8,128)(2,1)} %get-tuple-element.266), channel_id=1, source_target_pairs={{0,2},{1,3},{2,0},{3,1},{4,6},{5,7},{6,4},{7,5},{8,10},{9,11},{10,... | collective-permute-start | bytes 6193160 | tf_op jit(solution)/shard_map/ppermute | solution.py:270
  436.9 35.3 %collective-permute-start.62 = (bf16[2,96,2304]{2,1,0:T(8,128)(2,1)}, bf16[2,96,2304]{2,1,0:T(8,128)(2,1)}, u32[]{:S(2)}, u32[]{:S(2)}) collective-permute-start(bf16[2,96,2304]{2,1,0:T(8,128)(2,1)} %add_convert_fusion.2), channel_id=1, source_target_pairs={{0,4},{1,5},{2,6},{3,7},{4,0},{5,1},{6,2},{7,3},{8,12},{9,13},{10,... | collective-permute-start | bytes 2654216 | tf_op jit(solution)/shard_map/ppermute | solution.py:270
  437.2 34.9 %collective-permute-start.63 = (bf16[4,192,768]{2,1,0:T(8,128)(2,1)}, bf16[4,192,768]{2,1,0:T(8,128)(2,1)}, u32[]{:S(2)}, u32[]{:S(2)}) collective-permute-start(bf16[4,192,768]{2,1,0:T(8,128)(2,1)} %get-tuple-element.269), channel_id=1, source_target_pairs={{0,4},{1,5},{2,6},{3,7},{4,0},{5,1},{6,2},{7,3},{8,12},{9,13},{10,... | collective-permute-start | bytes 3538952 | tf_op jit(solution)/shard_map/ppermute | solution.py:270
  452.1 18.7 %collective-permute-start.61 = (bf16[2,96,768]{2,1,0:T(8,128)(2,1)}, bf16[2,96,768]{2,1,0:T(8,128)(2,1)}, u32[]{:S(2)}, u32[]{:S(2)}) collective-permute-start(bf16[2,96,768]{2,1,0:T(8,128)(2,1)} %get-tuple-element.379), channel_id=1, source_target_pairs={{0,1},{1,0},{2,3},{3,2},{4,5},{5,4},{6,7},{7,6},{8,9},{9,8},{10,11... | collective-permute-start | bytes 884744 | tf_op jit(solution)/shard_map/ppermute | solution.py:270
  462.9 36.3 %collective-permute-start.59 = (bf16[8,48,1152]{2,1,0:T(8,128)(2,1)}, bf16[8,48,1152]{2,1,0:T(8,128)(2,1)}, u32[]{:S(2)}, u32[]{:S(2)}) collective-permute-start(bf16[8,48,1152]{2,1,0:T(8,128)(2,1)} %get-tuple-element.264), channel_id=1, source_target_pairs={{0,2},{1,3},{2,0},{3,1},{4,6},{5,7},{6,4},{7,5},{8,10},{9,11},{10,... | collective-permute-start | bytes 2654216 | tf_op jit(solution)/shard_map/ppermute | solution.py:270
  470.8 33.9 %collective-permute-start.72 = (bf16[1,96,768]{2,1,0:T(8,128)(2,1)}, bf16[1,96,768]{2,1,0:T(8,128)(2,1)}, u32[]{:S(2)}, u32[]{:S(2)}) collective-permute-start(bf16[1,96,768]{2,1,0:T(8,128)(2,1)} %add_convert_fusion.20), channel_id=1, source_target_pairs={{0,8},{1,9},{2,10},{3,11},{4,12},{5,13},{6,14},{7,15},{8,0},{9,1},... | collective-permute-start | bytes 442376 | tf_op jit(solution)/shard_map/ppermute | solution.py:270
  474.6 25.2 %collective-permute-start.64 = (bf16[4,48,2688]{2,1,0:T(8,128)(2,1)}, bf16[4,48,2688]{2,1,0:T(8,128)(2,1)}, u32[]{:S(2)}, u32[]{:S(2)}) collective-permute-start(bf16[4,48,2688]{2,1,0:T(8,128)(2,1)} %add_convert_fusion.1), channel_id=1, source_target_pairs={{0,4},{1,5},{2,6},{3,7},{4,0},{5,1},{6,2},{7,3},{8,12},{9,13},{10,... | collective-permute-start | bytes 3096584 | tf_op jit(solution)/shard_map/ppermute | solution.py:270
  488.6 21.8 %collective-permute-start.73 = (bf16[1,96,2304]{2,1,0:T(8,128)(2,1)}, bf16[1,96,2304]{2,1,0:T(8,128)(2,1)}, u32[]{:S(2)}, u32[]{:S(2)}) collective-permute-start(bf16[1,96,2304]{2,1,0:T(8,128)(2,1)} %add_convert_fusion.12), channel_id=1, source_target_pairs={{0,8},{1,9},{2,10},{3,11},{4,12},{5,13},{6,14},{7,15},{8,0},{9,1},... | collective-permute-start | bytes 1327112 | tf_op jit(solution)/shard_map/ppermute | solution.py:270
  500.9 15.4 %collective-permute-start.67 = (bf16[4,48,1152]{2,1,0:T(8,128)(2,1)S(1)}, bf16[4,48,1152]{2,1,0:T(8,128)(2,1)S(1)}, u32[]{:S(2)}, u32[]{:S(2)}) collective-permute-start(bf16[4,48,1152]{2,1,0:T(8,128)(2,1)S(1)} %add_convert_fusion.13), channel_id=1, source_target_pairs={{0,4},{1,5},{2,6},{3,7},{4,0},{5,1},{6,2},{7,3},{8,12},{9,13},{10,... | collective-permute-start | bytes 1327112 | tf_op jit(solution)/shard_map/ppermute | solution.py:270
  512.3 16.0 %collective-permute-start.75 = (bf16[2,48,2688]{2,1,0:T(8,128)(2,1)S(1)}, bf16[2,48,2688]{2,1,0:T(8,128)(2,1)S(1)}, u32[]{:S(2)}, u32[]{:S(2)}) collective-permute-start(bf16[2,48,2688]{2,1,0:T(8,128)(2,1)S(1)} %add_convert_fusion.10), channel_id=1, source_target_pairs={{0,1},{1,0},{2,3},{3,2},{4,5},{5,4},{6,7},{7,6},{8,9},{9,8},{10,11... | collective-permute-start | bytes 1548296 | tf_op jit(solution)/shard_map/ppermute | solution.py:270
  517.3 17.9 %collective-permute-start.74 = (bf16[2,48,1152]{2,1,0:T(8,128)(2,1)S(1)}, bf16[2,48,1152]{2,1,0:T(8,128)(2,1)S(1)}, u32[]{:S(2)}, u32[]{:S(2)}) collective-permute-start(bf16[2,48,1152]{2,1,0:T(8,128)(2,1)S(1)} %add_convert_fusion.18), channel_id=1, source_target_pairs={{0,1},{1,0},{2,3},{3,2},{4,5},{5,4},{6,7},{7,6},{8,9},{9,8},{10,11... | collective-permute-start | bytes 663560 | tf_op jit(solution)/shard_map/ppermute | solution.py:270
  524.4 22.1 %collective-permute-start.86 = (bf16[96,2304]{1,0:T(8,128)(2,1)S(1)}, bf16[96,2304]{1,0:T(8,128)(2,1)S(1)}, u32[]{:S(2)}, u32[]{:S(2)}) collective-permute-start(bf16[96,2304]{1,0:T(8,128)(2,1)S(1)} %fusion.53), channel_id=1, source_target_pairs={{0,16},{16,0},{1,17},{17,1},{2,18},{18,2},{3,19},{19,3},{4,20},{20... | collective-permute-start | bytes 1327112 | tf_op jit(solution)/shard_map/ppermute | solution.py:256
  535.3 18.2 %collective-permute-start.81 = (bf16[1,48,2688]{2,1,0:T(8,128)(2,1)S(1)}, bf16[1,48,2688]{2,1,0:T(8,128)(2,1)S(1)}, u32[]{:S(2)}, u32[]{:S(2)}) collective-permute-start(bf16[1,48,2688]{2,1,0:T(8,128)(2,1)S(1)} %add_convert_fusion.17), channel_id=1, source_target_pairs={{0,8},{1,9},{2,10},{3,11},{4,12},{5,13},{6,14},{7,15},{8,0},{9,1},... | collective-permute-start | bytes 774152 | tf_op jit(solution)/shard_map/ppermute | solution.py:270
  536.8 20.7 %collective-permute-start.85 = (bf16[192,768]{1,0:T(8,128)(2,1)S(1)}, bf16[192,768]{1,0:T(8,128)(2,1)S(1)}, u32[]{:S(2)}, u32[]{:S(2)}) collective-permute-start(bf16[192,768]{1,0:T(8,128)(2,1)S(1)} %fusion.51), channel_id=1, source_target_pairs={{0,16},{16,0},{1,17},{17,1},{2,18},{18,2},{3,19},{19,3},{4,20},{20... | collective-permute-start | bytes 884744 | tf_op jit(solution)/shard_map/ppermute | solution.py:256
  (228 other events, 1687.8 us)
